TPU v7x, 128 devices: a whole 4x4x4 slice. The times are simulated.
128 devices in a mesh: inner: 8 (over z, core), outer: 8 (over x, y_lo), head: 2 (over y_hi).
Axes of the slice: x: 4, y: 4 (y_hi: 2, y_lo: 2; y = y_hi * 2 + y_lo), z: 4, core: 2. Of those that a mesh axis runs over, the one named last changes fastest.
Arguments:
- queries: bfloat16 [8192, 2048], P(('inner', 'outer'), 'head'), parts along dimension 1, may hold values from -120 to 120
- keys: bfloat16 [8192, 256], P(('inner', 'outer'), 'head'), parts along dimension 1, may hold values from -6 to 6
- values: bfloat16 [8192, 256], P(('inner', 'outer'), 'head'), parts along dimension 1, may hold values from -6 to 6
- grad_out: bfloat16 [8192, 2048], P(('inner', 'outer'), 'head'), parts along dimension 1, may hold values from -6 to 6
- block_docs: int32 [64], P(('inner', 'outer')), may hold values from 0 to 7, never falling along the last dimension, each value on 1 to 40 neighbouring positions
Outputs:
- grad_queries: bfloat16 [8192, 2048], P(('inner', 'outer'), 'head'), parts along dimension 1
- grad_keys: bfloat16 [8192, 256], P(('inner', 'outer'), 'head'), parts along dimension 1
- grad_values: bfloat16 [8192, 256], P(('inner', 'outer'), 'head'), parts along dimension 1
There are 2 independent parts, one for each index of `head`. A program takes and returns all parts, laid end to end along the dimension named above; an argument that names none is the same for every part. Nothing has to cross between parts.
Inputs may be any that keep to these rules, and one draw needn't show every extreme that they name: `block_docs`: documents are runs of whole blocks in order; the longest has 40 blocks.
All inputs are finite; a program needn't handle non-finite values.
Results may differ from a plain program's by a relative error of at most 0.0065.
Values may be sent and summed in bfloat16 or wider, within the bound.
No kernel may reach another device: no remote copies, remote signals or barrier semaphores. Data moves between devices by JAX's collectives and lax.ppermute only.
A program may use at most 64 MiB of HBM per device.

v0:
```python
import jax
import jax.numpy as jnp
from jax import lax
from jax.sharding import PartitionSpec as P

NEG = -1e30


def passed_along(value, axis, steps):
    count = lax.axis_size(axis)
    leading, last = (max(0, -steps), min(count, count - steps))
    return lax.ppermute(value, axis, [(source, source + steps) for source in range(leading, last)])


def shifted(shard, axis, by):
    length = lax.axis_size(axis)
    return lax.ppermute(shard, axis, [(i, (i + by) % length) for i in range(length)])


def permitted(row_pos, row_doc, key_pos, key_doc):
    return (key_pos[None, :] <= row_pos[:, None]) & (key_doc[None, :] == row_doc[:, None])


def per_device(queries, keys, values, grad_out, block_docs):
    rows, width = queries.shape
    head_dim = keys.shape[1]
    heads = width // head_dim
    scale = float(head_dim) ** (-0.5)
    per_block = rows // block_docs.shape[0]
    row_doc = jnp.repeat(block_docs, per_block, total_repeat_length=rows)
    offsets = lax.iota(jnp.int32, rows)
    devices = lax.axis_size(("inner", "outer"))
    position = lax.axis_index(("inner", "outer"))
    row_pos = position * rows + offsets
    q3 = queries.reshape(rows, heads, head_dim)
    d3 = grad_out.reshape(rows, heads, head_dim)

    def masked_scores(key_rows, mask):
        s = jnp.einsum("rhd,kd->hrk", q3, key_rows, preferred_element_type=jnp.float32) * scale
        return jnp.where(mask[None], s, NEG)

    start_state = (
        jnp.full((heads, rows), NEG, jnp.float32),
        jnp.zeros((heads, rows), jnp.float32),
        jnp.zeros((heads, rows), jnp.float32),
    )
    key_piece = lax.all_gather(keys, ("inner", "outer"), axis=0, tiled=True)
    value_piece = lax.all_gather(values, ("inner", "outer"), axis=0, tiled=True)
    doc_piece = lax.all_gather(row_doc, ("inner", "outer"), axis=0, tiled=True)
    length = key_piece.shape[0]
    span = min(length, rows)

    def visit_keys(index, state):
        first = index * span
        key_rows = lax.dynamic_slice_in_dim(key_piece, first, span, 0)
        value_rows = lax.dynamic_slice_in_dim(value_piece, first, span, 0)
        key_doc = lax.dynamic_slice_in_dim(doc_piece, first, span, 0)
        key_pos = first + lax.iota(jnp.int32, span)
        mask = permitted(row_pos, row_doc, key_pos, key_doc)

        def update(current):
            top, total, weighted = current
            s = masked_scores(key_rows, mask)
            new_top = jnp.maximum(top, jnp.max(s, axis=-1))
            probs = jnp.where(mask[None], jnp.exp(s - new_top[:, :, None]), 0.0)
            dprobs = jnp.einsum("rhd,kd->hrk", d3, value_rows, preferred_element_type=jnp.float32)
            factor = jnp.exp(top - new_top)
            return (
                new_top,
                total * factor + jnp.sum(probs, axis=-1),
                weighted * factor + jnp.sum(probs * dprobs, axis=-1),
            )

        return lax.cond(jnp.any(mask), update, lambda current: current, state)

    top, total, weighted = lax.fori_loop(0, length // span, visit_keys, start_state)
    lse = top + jnp.log(total)
    delta = weighted / total

    def visit(key_rows, value_rows, key_doc, source, accum):
        key_pos = source * rows + offsets
        mask = permitted(row_pos, row_doc, key_pos, key_doc) & True

        def work(current):
            dq, dk, dv = current
            s = masked_scores(key_rows, mask)
            probs = jnp.where(mask[None], jnp.exp(s - lse[:, :, None]), 0.0)
            dprobs = jnp.einsum("rhd,kd->hrk", d3, value_rows, preferred_element_type=jnp.float32)
            dscores = probs * (dprobs - delta[:, :, None])
            probs_low = probs.astype(jnp.bfloat16)
            dscores_low = dscores.astype(jnp.bfloat16)
            dq = dq + jnp.einsum(
                "hrk,kd->rhd", dscores_low, key_rows, preferred_element_type=jnp.float32
            )
            dk = dk + jnp.einsum("hrk,rhd->kd", dscores_low, q3, preferred_element_type=jnp.float32)
            dv = dv + jnp.einsum("hrk,rhd->kd", probs_low, d3, preferred_element_type=jnp.float32)
            return (dq, dk, dv)

        return lax.cond(jnp.any(mask), work, lambda current: current, accum)

    zero_dq = jnp.zeros((rows, heads, head_dim), jnp.float32)
    zero_kv = jnp.zeros((rows, head_dim), jnp.float32)
    initial = (keys, values, row_doc, zero_dq, zero_kv, zero_kv)

    def circle_step(step, state):
        key_rows, value_rows, key_doc, dq, dk, dv = state
        source = (position - step) % devices
        dq, dk, dv = visit(key_rows, value_rows, key_doc, source, (dq, dk, dv))
        key_rows, value_rows, key_doc = passed_along(
            (key_rows, value_rows, key_doc), ("inner", "outer"), 1
        )
        dk, dv = shifted((dk, dv), ("inner", "outer"), 1)
        return (key_rows, value_rows, key_doc, dq, dk, dv)

    final = lax.fori_loop(0, devices, circle_step, initial)
    dq, dk, dv = (final[3], final[4], final[5])
    grad_queries = (scale * dq).reshape(rows, width).astype(jnp.bfloat16)
    grad_keys = (scale * dk).astype(jnp.bfloat16)
    grad_values = dv.astype(jnp.bfloat16)
    return (grad_queries, grad_keys, grad_values)


def solution(mesh):
    placed = (
        P(("inner", "outer"), "head"),
        P(("inner", "outer"), "head"),
        P(("inner", "outer"), "head"),
        P(("inner", "outer"), "head"),
        P(("inner", "outer")),
    )
    return jax.shard_map(
        per_device,
        mesh=mesh,
        in_specs=placed,
        out_specs=(
            P(("inner", "outer"), "head"),
            P(("inner", "outer"), "head"),
            P(("inner", "outer"), "head"),
        ),
        check_vma=False,
    )
```

profile of v0, /device:TPU:1, one launch (start us, length us, event | category | flops | bytes accessed | tf_op | source)
XLA Modules:
  0.0 1667.1 jit_solution(14962822528104116848)
XLA Ops:
  14.0 131.6 %all-gather = s32[64,1,128]{2,1,0:T(1,128)S(1)} all-gather(s32[1,1,128]{2,1,0:T(1,128)S(1)} %broadcast.93), channel_id=1, replica_groups=mesh['inner'=8,'outer'=8,'head'=2] {'inner','outer'}, dimensions={0}, use_global_device_ids=true | all-gather | bytes 33280 | tf_op jit(solution)/shard_map/all_gather | solution.py:49
  145.7 25.2 %all-gather.4.cloned.1.call-done = bf16[8192,128]{1,0:T(8,128)(2,1)} async-done(((bf16[128,128]{1,0:T(8,128)(2,1)}), bf16[8192,128]{1,0:T(8,128)(2,1)}) %all-gather.4.cloned.1.call-update) | async-done | bytes 2097168 | tf_op jit(solution)/shard_map/all_gather | solution.py:47
  170.9 157.5 %all-gather.6.cloned.1.call-done = bf16[8192,128]{1,0:T(8,128)(2,1)} async-done(((bf16[128,128]{1,0:T(8,128)(2,1)}), bf16[8192,128]{1,0:T(8,128)(2,1)}) %all-gather.6.cloned.1.call-update) | async-done | bytes 2097168 | tf_op jit(solution)/shard_map/all_gather | solution.py:48
  328.4 157.8 %while.46 = (s32[]{:T(128)}, f32[8,128]{1,0:T(8,128)S(1)}, f32[8,128]{1,0:T(8,128)S(1)}, f32[8,128]{1,0:T(8,128)S(1)}, s32[8192]{0:T(1024)S(1)}, /*index=5*/bf16...) while((s32[]{:T(128)}, f32[8,128]{1,0:T(8,128)S(1)}, ...), condition=%wide.region_7.8_spmd.clone, body=%wide.region_0.7_spmd.clone.sunk | while | flops 68472200 | bytes 2306129 | solution.py:76
  486.3 1172.0 %while.47 = (s32[]{:T(128)}, bf16[128,128]{1,0:T(8,128)(2,1)S(1)}, bf16[128,128]{1,0:T(8,128)(2,1)S(1)}, s32[128]{0:T(128)S(1)}, f32[128,8,128]{2,0,1:T(8,128)S(...) while((s32[]{:T(128)}, bf16[128,128]{1,0:T(8,128)(2,1)S(1)}, ...), condition=%wide.region_12.13_spmd.clone, body=%wide.region_8.12_spmd.clone.sunk | while | flops 169034128 | bytes 6044052 | solution.py:115
  496.3 5.7 collective-permute-start
  502.0 5.6 collective-permute-start.1
  522.7 5.5 collective-permute-start
  528.2 5.7 collective-permute-start.1
  533.9 6.4 collective-permute-start.2
  550.8 7.1 collective-permute-start
  562.6 5.0 collective-permute-start.2
  577.9 7.1 collective-permute-start
  589.7 4.9 collective-permute-start.2
  605.3 7.1 collective-permute-start
  616.9 5.2 collective-permute-start.2
  633.2 7.1 collective-permute-start
  644.9 5.0 collective-permute-start.2
  660.5 7.1 collective-permute-start
  685.4 7.2 collective-permute-start
  760.9 4.9 collective-permute-done.2
  776.2 4.9 collective-permute-done.2
  805.2 5.2 collective-permute-done.2
  820.5 5.2 collective-permute-done.2
  865.2 5.1 collective-permute-done.2
  879.9 5.0 collective-permute-start.2
  894.5 7.1 collective-permute-start
  920.5 7.1 collective-permute-start
  945.1 7.1 collective-permute-start
  967.0 7.1 collective-permute-start
  980.7 5.2 collective-permute-done.2
  1131.1 5.2 collective-permute-done.2
  1162.3 5.1 collective-permute-start.2
  1176.6 7.1 collective-permute-start
  1201.2 7.1 collective-permute-start
  1222.2 7.0 collective-permute-start
  1243.8 7.2 collective-permute-start
  1257.5 4.9 collective-permute-done.2
  1346.7 5.2 collective-permute-done.2
  1406.8 5.2 collective-permute-done.2
  1421.0 5.2 collective-permute-done.2
  1430.1 7.1 collective-permute-start
  1454.7 7.1 collective-permute-start
  1476.7 7.1 collective-permute-start
  1490.4 5.2 collective-permute-done.2
  1497.9 6.6 collective-permute-start
  1519.2 7.2 collective-permute-start
  1622.5 5.2 collective-permute-done.2
  (1618 shorter events, 1015.4 us)
Async XLA Ops:
  7.2 163.7 %all-gather.4.cloned.1.call-start = ((), (), s32[]{:S(2)}) async-start(), calls=%async_computation | async-start | bytes 2129920 | tf_op jit(solution)/shard_map/all_gather | solution.py:47
  10.0 318.4 %all-gather.6.cloned.1.call-start = ((), (), s32[]{:S(2)}) async-start(), calls=%async_computation.1 | async-start | bytes 2129920 | tf_op jit(solution)/shard_map/all_gather | solution.py:48
  489.7 22.1 %collective-permute-start.3 = (f32[128,128]{1,0:T(8,128)S(1)}, f32[128,128]{1,0:T(8,128)S(1)}, u32[]{:S(2)}, u32[]{:S(2)}) collective-permute-start(f32[128,128]{1,0:T(8,128)S(1)} %get-tuple-element.1058), channel_id=1, source_target_pairs={{0,2},{2,4},{4,6},{6,8},{8,10},{10,12},{12,14},{14,16},{16,18},{18... | collective-permute-start | bytes 196616 | tf_op jit(solution)/shard_map/while/body/eval_jaxpr/ppermute | solution.py:17
  493.4 18.4 %collective-permute-start.4 = (f32[128,128]{1,0:T(8,128)S(1)}, f32[128,128]{1,0:T(8,128)S(1)}, u32[]{:S(2)}, u32[]{:S(2)}) collective-permute-start(f32[128,128]{1,0:T(8,128)S(1)} %get-tuple-element.1059), channel_id=1, source_target_pairs={{0,2},{2,4},{4,6},{6,8},{8,10},{10,12},{12,14},{14,16},{16,18},{18... | collective-permute-start | bytes 196616 | tf_op jit(solution)/shard_map/while/body/eval_jaxpr/ppermute | solution.py:17
  496.3 18.2 %collective-permute-start = (bf16[128,128]{1,0:T(8,128)(2,1)S(1)}, bf16[128,128]{1,0:T(8,128)(2,1)S(1)}, u32[]{:S(2)}, u32[]{:S(2)}) collective-permute-start(bf16[128,128]{1,0:T(8,128)(2,1)S(1)} %copy.61), channel_id=1, source_target_pairs={{0,2},{2,4},{4,6},{6,8},{8,10},{10,12},{12,14},{14,16},{16,18},{18... | collective-permute-start | bytes 98312 | tf_op jit(solution)/shard_map/while/body/eval_jaxpr/ppermute | solution.py:12
  517.9 22.4 %collective-permute-start.3 = (f32[128,128]{1,0:T(8,128)S(1)}, f32[128,128]{1,0:T(8,128)S(1)}, u32[]{:S(2)}, u32[]{:S(2)}) collective-permute-start(f32[128,128]{1,0:T(8,128)S(1)} %get-tuple-element.1058), channel_id=1, source_target_pairs={{0,2},{2,4},{4,6},{6,8},{8,10},{10,12},{12,14},{14,16},{16,18},{18... | collective-permute-start | bytes 196616 | tf_op jit(solution)/shard_map/while/body/eval_jaxpr/ppermute | solution.py:17
  519.4 20.9 %collective-permute-start.4 = (f32[128,128]{1,0:T(8,128)S(1)}, f32[128,128]{1,0:T(8,128)S(1)}, u32[]{:S(2)}, u32[]{:S(2)}) collective-permute-start(f32[128,128]{1,0:T(8,128)S(1)} %get-tuple-element.1059), channel_id=1, source_target_pairs={{0,2},{2,4},{4,6},{6,8},{8,10},{10,12},{12,14},{14,16},{16,18},{18... | collective-permute-start | bytes 196616 | tf_op jit(solution)/shard_map/while/body/eval_jaxpr/ppermute | solution.py:17
  522.7 18.3 %collective-permute-start = (bf16[128,128]{1,0:T(8,128)(2,1)S(1)}, bf16[128,128]{1,0:T(8,128)(2,1)S(1)}, u32[]{:S(2)}, u32[]{:S(2)}) collective-permute-start(bf16[128,128]{1,0:T(8,128)(2,1)S(1)} %copy.61), channel_id=1, source_target_pairs={{0,2},{2,4},{4,6},{6,8},{8,10},{10,12},{12,14},{14,16},{16,18},{18... | collective-permute-start | bytes 98312 | tf_op jit(solution)/shard_map/while/body/eval_jaxpr/ppermute | solution.py:12
  544.4 23.3 %collective-permute-start.3 = (f32[128,128]{1,0:T(8,128)S(1)}, f32[128,128]{1,0:T(8,128)S(1)}, u32[]{:S(2)}, u32[]{:S(2)}) collective-permute-start(f32[128,128]{1,0:T(8,128)S(1)} %get-tuple-element.1058), channel_id=1, source_target_pairs={{0,2},{2,4},{4,6},{6,8},{8,10},{10,12},{12,14},{14,16},{16,18},{18... | collective-permute-start | bytes 196616 | tf_op jit(solution)/shard_map/while/body/eval_jaxpr/ppermute | solution.py:17
  547.0 20.7 %collective-permute-start.4 = (f32[128,128]{1,0:T(8,128)S(1)}, f32[128,128]{1,0:T(8,128)S(1)}, u32[]{:S(2)}, u32[]{:S(2)}) collective-permute-start(f32[128,128]{1,0:T(8,128)S(1)} %get-tuple-element.1059), channel_id=1, source_target_pairs={{0,2},{2,4},{4,6},{6,8},{8,10},{10,12},{12,14},{14,16},{16,18},{18... | collective-permute-start | bytes 196616 | tf_op jit(solution)/shard_map/while/body/eval_jaxpr/ppermute | solution.py:17
  550.8 18.8 %collective-permute-start = (bf16[128,128]{1,0:T(8,128)(2,1)S(1)}, bf16[128,128]{1,0:T(8,128)(2,1)S(1)}, u32[]{:S(2)}, u32[]{:S(2)}) collective-permute-start(bf16[128,128]{1,0:T(8,128)(2,1)S(1)} %copy.61), channel_id=1, source_target_pairs={{0,2},{2,4},{4,6},{6,8},{8,10},{10,12},{12,14},{14,16},{16,18},{18... | collective-permute-start | bytes 98312 | tf_op jit(solution)/shard_map/while/body/eval_jaxpr/ppermute | solution.py:12
  573.0 21.6 %collective-permute-start.3 = (f32[128,128]{1,0:T(8,128)S(1)}, f32[128,128]{1,0:T(8,128)S(1)}, u32[]{:S(2)}, u32[]{:S(2)}) collective-permute-start(f32[128,128]{1,0:T(8,128)S(1)} %get-tuple-element.1058), channel_id=1, source_target_pairs={{0,2},{2,4},{4,6},{6,8},{8,10},{10,12},{12,14},{14,16},{16,18},{18... | collective-permute-start | bytes 196616 | tf_op jit(solution)/shard_map/while/body/eval_jaxpr/ppermute | solution.py:17
  574.4 20.2 %collective-permute-start.4 = (f32[128,128]{1,0:T(8,128)S(1)}, f32[128,128]{1,0:T(8,128)S(1)}, u32[]{:S(2)}, u32[]{:S(2)}) collective-permute-start(f32[128,128]{1,0:T(8,128)S(1)} %get-tuple-element.1059), channel_id=1, source_target_pairs={{0,2},{2,4},{4,6},{6,8},{8,10},{10,12},{12,14},{14,16},{16,18},{18... | collective-permute-start | bytes 196616 | tf_op jit(solution)/shard_map/while/body/eval_jaxpr/ppermute | solution.py:17
  577.9 18.7 %collective-permute-start = (bf16[128,128]{1,0:T(8,128)(2,1)S(1)}, bf16[128,128]{1,0:T(8,128)(2,1)S(1)}, u32[]{:S(2)}, u32[]{:S(2)}) collective-permute-start(bf16[128,128]{1,0:T(8,128)(2,1)S(1)} %copy.61), channel_id=1, source_target_pairs={{0,2},{2,4},{4,6},{6,8},{8,10},{10,12},{12,14},{14,16},{16,18},{18... | collective-permute-start | bytes 98312 | tf_op jit(solution)/shard_map/while/body/eval_jaxpr/ppermute | solution.py:12
  600.0 22.1 %collective-permute-start.3 = (f32[128,128]{1,0:T(8,128)S(1)}, f32[128,128]{1,0:T(8,128)S(1)}, u32[]{:S(2)}, u32[]{:S(2)}) collective-permute-start(f32[128,128]{1,0:T(8,128)S(1)} %get-tuple-element.1058), channel_id=1, source_target_pairs={{0,2},{2,4},{4,6},{6,8},{8,10},{10,12},{12,14},{14,16},{16,18},{18... | collective-permute-start | bytes 196616 | tf_op jit(solution)/shard_map/while/body/eval_jaxpr/ppermute | solution.py:17
  602.2 20.0 %collective-permute-start.4 = (f32[128,128]{1,0:T(8,128)S(1)}, f32[128,128]{1,0:T(8,128)S(1)}, u32[]{:S(2)}, u32[]{:S(2)}) collective-permute-start(f32[128,128]{1,0:T(8,128)S(1)} %get-tuple-element.1059), channel_id=1, source_target_pairs={{0,2},{2,4},{4,6},{6,8},{8,10},{10,12},{12,14},{14,16},{16,18},{18... | collective-permute-start | bytes 196616 | tf_op jit(solution)/shard_map/while/body/eval_jaxpr/ppermute | solution.py:17
  605.3 18.6 %collective-permute-start = (bf16[128,128]{1,0:T(8,128)(2,1)S(1)}, bf16[128,128]{1,0:T(8,128)(2,1)S(1)}, u32[]{:S(2)}, u32[]{:S(2)}) collective-permute-start(bf16[128,128]{1,0:T(8,128)(2,1)S(1)} %copy.61), channel_id=1, source_target_pairs={{0,2},{2,4},{4,6},{6,8},{8,10},{10,12},{12,14},{14,16},{16,18},{18... | collective-permute-start | bytes 98312 | tf_op jit(solution)/shard_map/while/body/eval_jaxpr/ppermute | solution.py:12
  627.3 22.7 %collective-permute-start.3 = (f32[128,128]{1,0:T(8,128)S(1)}, f32[128,128]{1,0:T(8,128)S(1)}, u32[]{:S(2)}, u32[]{:S(2)}) collective-permute-start(f32[128,128]{1,0:T(8,128)S(1)} %get-tuple-element.1058), channel_id=1, source_target_pairs={{0,2},{2,4},{4,6},{6,8},{8,10},{10,12},{12,14},{14,16},{16,18},{18... | collective-permute-start | bytes 196616 | tf_op jit(solution)/shard_map/while/body/eval_jaxpr/ppermute | solution.py:17
  630.1 19.9 %collective-permute-start.4 = (f32[128,128]{1,0:T(8,128)S(1)}, f32[128,128]{1,0:T(8,128)S(1)}, u32[]{:S(2)}, u32[]{:S(2)}) collective-permute-start(f32[128,128]{1,0:T(8,128)S(1)} %get-tuple-element.1059), channel_id=1, source_target_pairs={{0,2},{2,4},{4,6},{6,8},{8,10},{10,12},{12,14},{14,16},{16,18},{18... | collective-permute-start | bytes 196616 | tf_op jit(solution)/shard_map/while/body/eval_jaxpr/ppermute | solution.py:17
  633.2 18.7 %collective-permute-start = (bf16[128,128]{1,0:T(8,128)(2,1)S(1)}, bf16[128,128]{1,0:T(8,128)(2,1)S(1)}, u32[]{:S(2)}, u32[]{:S(2)}) collective-permute-start(bf16[128,128]{1,0:T(8,128)(2,1)S(1)} %copy.61), channel_id=1, source_target_pairs={{0,2},{2,4},{4,6},{6,8},{8,10},{10,12},{12,14},{14,16},{16,18},{18... | collective-permute-start | bytes 98312 | tf_op jit(solution)/shard_map/while/body/eval_jaxpr/ppermute | solution.py:12
  655.3 19.6 %collective-permute-start.3 = (f32[128,128]{1,0:T(8,128)S(1)}, f32[128,128]{1,0:T(8,128)S(1)}, u32[]{:S(2)}, u32[]{:S(2)}) collective-permute-start(f32[128,128]{1,0:T(8,128)S(1)} %get-tuple-element.1058), channel_id=1, source_target_pairs={{0,2},{2,4},{4,6},{6,8},{8,10},{10,12},{12,14},{14,16},{16,18},{18... | collective-permute-start | bytes 196616 | tf_op jit(solution)/shard_map/while/body/eval_jaxpr/ppermute | solution.py:17
  657.4 17.6 %collective-permute-start.4 = (f32[128,128]{1,0:T(8,128)S(1)}, f32[128,128]{1,0:T(8,128)S(1)}, u32[]{:S(2)}, u32[]{:S(2)}) collective-permute-start(f32[128,128]{1,0:T(8,128)S(1)} %get-tuple-element.1059), channel_id=1, source_target_pairs={{0,2},{2,4},{4,6},{6,8},{8,10},{10,12},{12,14},{14,16},{16,18},{18... | collective-permute-start | bytes 196616 | tf_op jit(solution)/shard_map/while/body/eval_jaxpr/ppermute | solution.py:17
  660.5 18.6 %collective-permute-start = (bf16[128,128]{1,0:T(8,128)(2,1)S(1)}, bf16[128,128]{1,0:T(8,128)(2,1)S(1)}, u32[]{:S(2)}, u32[]{:S(2)}) collective-permute-start(bf16[128,128]{1,0:T(8,128)(2,1)S(1)} %copy.61), channel_id=1, source_target_pairs={{0,2},{2,4},{4,6},{6,8},{8,10},{10,12},{12,14},{14,16},{16,18},{18... | collective-permute-start | bytes 98312 | tf_op jit(solution)/shard_map/while/body/eval_jaxpr/ppermute | solution.py:12
  685.4 18.6 %collective-permute-start = (bf16[128,128]{1,0:T(8,128)(2,1)S(1)}, bf16[128,128]{1,0:T(8,128)(2,1)S(1)}, u32[]{:S(2)}, u32[]{:S(2)}) collective-permute-start(bf16[128,128]{1,0:T(8,128)(2,1)S(1)} %copy.61), channel_id=1, source_target_pairs={{0,2},{2,4},{4,6},{6,8},{8,10},{10,12},{12,14},{14,16},{16,18},{18... | collective-permute-start | bytes 98312 | tf_op jit(solution)/shard_map/while/body/eval_jaxpr/ppermute | solution.py:12
  889.0 21.1 %collective-permute-start.3 = (f32[128,128]{1,0:T(8,128)S(1)}, f32[128,128]{1,0:T(8,128)S(1)}, u32[]{:S(2)}, u32[]{:S(2)}) collective-permute-start(f32[128,128]{1,0:T(8,128)S(1)} %get-tuple-element.1058), channel_id=1, source_target_pairs={{0,2},{2,4},{4,6},{6,8},{8,10},{10,12},{12,14},{14,16},{16,18},{18... | collective-permute-start | bytes 196616 | tf_op jit(solution)/shard_map/while/body/eval_jaxpr/ppermute | solution.py:17
  891.4 18.7 %collective-permute-start.4 = (f32[128,128]{1,0:T(8,128)S(1)}, f32[128,128]{1,0:T(8,128)S(1)}, u32[]{:S(2)}, u32[]{:S(2)}) collective-permute-start(f32[128,128]{1,0:T(8,128)S(1)} %get-tuple-element.1059), channel_id=1, source_target_pairs={{0,2},{2,4},{4,6},{6,8},{8,10},{10,12},{12,14},{14,16},{16,18},{18... | collective-permute-start | bytes 196616 | tf_op jit(solution)/shard_map/while/body/eval_jaxpr/ppermute | solution.py:17
  894.5 19.2 %collective-permute-start = (bf16[128,128]{1,0:T(8,128)(2,1)S(1)}, bf16[128,128]{1,0:T(8,128)(2,1)S(1)}, u32[]{:S(2)}, u32[]{:S(2)}) collective-permute-start(bf16[128,128]{1,0:T(8,128)(2,1)S(1)} %copy.61), channel_id=1, source_target_pairs={{0,2},{2,4},{4,6},{6,8},{8,10},{10,12},{12,14},{14,16},{16,18},{18... | collective-permute-start | bytes 98312 | tf_op jit(solution)/shard_map/while/body/eval_jaxpr/ppermute | solution.py:12
  915.9 18.7 %collective-permute-start.3 = (f32[128,128]{1,0:T(8,128)S(1)}, f32[128,128]{1,0:T(8,128)S(1)}, u32[]{:S(2)}, u32[]{:S(2)}) collective-permute-start(f32[128,128]{1,0:T(8,128)S(1)} %get-tuple-element.1058), channel_id=1, source_target_pairs={{0,2},{2,4},{4,6},{6,8},{8,10},{10,12},{12,14},{14,16},{16,18},{18... | collective-permute-start | bytes 196616 | tf_op jit(solution)/shard_map/while/body/eval_jaxpr/ppermute | solution.py:17
  917.4 17.2 %collective-permute-start.4 = (f32[128,128]{1,0:T(8,128)S(1)}, f32[128,128]{1,0:T(8,128)S(1)}, u32[]{:S(2)}, u32[]{:S(2)}) collective-permute-start(f32[128,128]{1,0:T(8,128)S(1)} %get-tuple-element.1059), channel_id=1, source_target_pairs={{0,2},{2,4},{4,6},{6,8},{8,10},{10,12},{12,14},{14,16},{16,18},{18... | collective-permute-start | bytes 196616 | tf_op jit(solution)/shard_map/while/body/eval_jaxpr/ppermute | solution.py:17
  920.5 18.6 %collective-permute-start = (bf16[128,128]{1,0:T(8,128)(2,1)S(1)}, bf16[128,128]{1,0:T(8,128)(2,1)S(1)}, u32[]{:S(2)}, u32[]{:S(2)}) collective-permute-start(bf16[128,128]{1,0:T(8,128)(2,1)S(1)} %copy.61), channel_id=1, source_target_pairs={{0,2},{2,4},{4,6},{6,8},{8,10},{10,12},{12,14},{14,16},{16,18},{18... | collective-permute-start | bytes 98312 | tf_op jit(solution)/shard_map/while/body/eval_jaxpr/ppermute | solution.py:12
  941.3 17.5 %collective-permute-start.3 = (f32[128,128]{1,0:T(8,128)S(1)}, f32[128,128]{1,0:T(8,128)S(1)}, u32[]{:S(2)}, u32[]{:S(2)}) collective-permute-start(f32[128,128]{1,0:T(8,128)S(1)} %get-tuple-element.1058), channel_id=1, source_target_pairs={{0,2},{2,4},{4,6},{6,8},{8,10},{10,12},{12,14},{14,16},{16,18},{18... | collective-permute-start | bytes 196616 | tf_op jit(solution)/shard_map/while/body/eval_jaxpr/ppermute | solution.py:17
  941.4 17.5 %collective-permute-start.4 = (f32[128,128]{1,0:T(8,128)S(1)}, f32[128,128]{1,0:T(8,128)S(1)}, u32[]{:S(2)}, u32[]{:S(2)}) collective-permute-start(f32[128,128]{1,0:T(8,128)S(1)} %get-tuple-element.1059), channel_id=1, source_target_pairs={{0,2},{2,4},{4,6},{6,8},{8,10},{10,12},{12,14},{14,16},{16,18},{18... | collective-permute-start | bytes 196616 | tf_op jit(solution)/shard_map/while/body/eval_jaxpr/ppermute | solution.py:17
  945.1 18.7 %collective-permute-start = (bf16[128,128]{1,0:T(8,128)(2,1)S(1)}, bf16[128,128]{1,0:T(8,128)(2,1)S(1)}, u32[]{:S(2)}, u32[]{:S(2)}) collective-permute-start(bf16[128,128]{1,0:T(8,128)(2,1)S(1)} %copy.61), channel_id=1, source_target_pairs={{0,2},{2,4},{4,6},{6,8},{8,10},{10,12},{12,14},{14,16},{16,18},{18... | collective-permute-start | bytes 98312 | tf_op jit(solution)/shard_map/while/body/eval_jaxpr/ppermute | solution.py:12
  967.0 18.9 %collective-permute-start = (bf16[128,128]{1,0:T(8,128)(2,1)S(1)}, bf16[128,128]{1,0:T(8,128)(2,1)S(1)}, u32[]{:S(2)}, u32[]{:S(2)}) collective-permute-start(bf16[128,128]{1,0:T(8,128)(2,1)S(1)} %copy.61), channel_id=1, source_target_pairs={{0,2},{2,4},{4,6},{6,8},{8,10},{10,12},{12,14},{14,16},{16,18},{18... | collective-permute-start | bytes 98312 | tf_op jit(solution)/shard_map/while/body/eval_jaxpr/ppermute | solution.py:12
  1171.4 20.4 %collective-permute-start.3 = (f32[128,128]{1,0:T(8,128)S(1)}, f32[128,128]{1,0:T(8,128)S(1)}, u32[]{:S(2)}, u32[]{:S(2)}) collective-permute-start(f32[128,128]{1,0:T(8,128)S(1)} %get-tuple-element.1058), channel_id=1, source_target_pairs={{0,2},{2,4},{4,6},{6,8},{8,10},{10,12},{12,14},{14,16},{16,18},{18... | collective-permute-start | bytes 196616 | tf_op jit(solution)/shard_map/while/body/eval_jaxpr/ppermute | solution.py:17
  1173.5 18.3 %collective-permute-start.4 = (f32[128,128]{1,0:T(8,128)S(1)}, f32[128,128]{1,0:T(8,128)S(1)}, u32[]{:S(2)}, u32[]{:S(2)}) collective-permute-start(f32[128,128]{1,0:T(8,128)S(1)} %get-tuple-element.1059), channel_id=1, source_target_pairs={{0,2},{2,4},{4,6},{6,8},{8,10},{10,12},{12,14},{14,16},{16,18},{18... | collective-permute-start | bytes 196616 | tf_op jit(solution)/shard_map/while/body/eval_jaxpr/ppermute | solution.py:17
  1176.6 18.7 %collective-permute-start = (bf16[128,128]{1,0:T(8,128)(2,1)S(1)}, bf16[128,128]{1,0:T(8,128)(2,1)S(1)}, u32[]{:S(2)}, u32[]{:S(2)}) collective-permute-start(bf16[128,128]{1,0:T(8,128)(2,1)S(1)} %copy.61), channel_id=1, source_target_pairs={{0,2},{2,4},{4,6},{6,8},{8,10},{10,12},{12,14},{14,16},{16,18},{18... | collective-permute-start | bytes 98312 | tf_op jit(solution)/shard_map/while/body/eval_jaxpr/ppermute | solution.py:12
  1197.4 17.5 %collective-permute-start.3 = (f32[128,128]{1,0:T(8,128)S(1)}, f32[128,128]{1,0:T(8,128)S(1)}, u32[]{:S(2)}, u32[]{:S(2)}) collective-permute-start(f32[128,128]{1,0:T(8,128)S(1)} %get-tuple-element.1058), channel_id=1, source_target_pairs={{0,2},{2,4},{4,6},{6,8},{8,10},{10,12},{12,14},{14,16},{16,18},{18... | collective-permute-start | bytes 196616 | tf_op jit(solution)/shard_map/while/body/eval_jaxpr/ppermute | solution.py:17
  1201.2 18.7 %collective-permute-start = (bf16[128,128]{1,0:T(8,128)(2,1)S(1)}, bf16[128,128]{1,0:T(8,128)(2,1)S(1)}, u32[]{:S(2)}, u32[]{:S(2)}) collective-permute-start(bf16[128,128]{1,0:T(8,128)(2,1)S(1)} %copy.61), channel_id=1, source_target_pairs={{0,2},{2,4},{4,6},{6,8},{8,10},{10,12},{12,14},{14,16},{16,18},{18... | collective-permute-start | bytes 98312 | tf_op jit(solution)/shard_map/while/body/eval_jaxpr/ppermute | solution.py:12
  1222.2 18.4 %collective-permute-start = (bf16[128,128]{1,0:T(8,128)(2,1)S(1)}, bf16[128,128]{1,0:T(8,128)(2,1)S(1)}, u32[]{:S(2)}, u32[]{:S(2)}) collective-permute-start(bf16[128,128]{1,0:T(8,128)(2,1)S(1)} %copy.61), channel_id=1, source_target_pairs={{0,2},{2,4},{4,6},{6,8},{8,10},{10,12},{12,14},{14,16},{16,18},{18... | collective-permute-start | bytes 98312 | tf_op jit(solution)/shard_map/while/body/eval_jaxpr/ppermute | solution.py:12
  1243.8 18.6 %collective-permute-start = (bf16[128,128]{1,0:T(8,128)(2,1)S(1)}, bf16[128,128]{1,0:T(8,128)(2,1)S(1)}, u32[]{:S(2)}, u32[]{:S(2)}) collective-permute-start(bf16[128,128]{1,0:T(8,128)(2,1)S(1)} %copy.61), channel_id=1, source_target_pairs={{0,2},{2,4},{4,6},{6,8},{8,10},{10,12},{12,14},{14,16},{16,18},{18... | collective-permute-start | bytes 98312 | tf_op jit(solution)/shard_map/while/body/eval_jaxpr/ppermute | solution.py:12
  1428.4 17.1 %collective-permute-start.3 = (f32[128,128]{1,0:T(8,128)S(1)}, f32[128,128]{1,0:T(8,128)S(1)}, u32[]{:S(2)}, u32[]{:S(2)}) collective-permute-start(f32[128,128]{1,0:T(8,128)S(1)} %get-tuple-element.1058), channel_id=1, source_target_pairs={{0,2},{2,4},{4,6},{6,8},{8,10},{10,12},{12,14},{14,16},{16,18},{18... | collective-permute-start | bytes 196616 | tf_op jit(solution)/shard_map/while/body/eval_jaxpr/ppermute | solution.py:17
  1430.1 18.6 %collective-permute-start = (bf16[128,128]{1,0:T(8,128)(2,1)S(1)}, bf16[128,128]{1,0:T(8,128)(2,1)S(1)}, u32[]{:S(2)}, u32[]{:S(2)}) collective-permute-start(bf16[128,128]{1,0:T(8,128)(2,1)S(1)} %copy.61), channel_id=1, source_target_pairs={{0,2},{2,4},{4,6},{6,8},{8,10},{10,12},{12,14},{14,16},{16,18},{18... | collective-permute-start | bytes 98312 | tf_op jit(solution)/shard_map/while/body/eval_jaxpr/ppermute | solution.py:12
  1450.8 17.5 %collective-permute-start.3 = (f32[128,128]{1,0:T(8,128)S(1)}, f32[128,128]{1,0:T(8,128)S(1)}, u32[]{:S(2)}, u32[]{:S(2)}) collective-permute-start(f32[128,128]{1,0:T(8,128)S(1)} %get-tuple-element.1058), channel_id=1, source_target_pairs={{0,2},{2,4},{4,6},{6,8},{8,10},{10,12},{12,14},{14,16},{16,18},{18... | collective-permute-start | bytes 196616 | tf_op jit(solution)/shard_map/while/body/eval_jaxpr/ppermute | solution.py:17
  1454.7 18.7 %collective-permute-start = (bf16[128,128]{1,0:T(8,128)(2,1)S(1)}, bf16[128,128]{1,0:T(8,128)(2,1)S(1)}, u32[]{:S(2)}, u32[]{:S(2)}) collective-permute-start(bf16[128,128]{1,0:T(8,128)(2,1)S(1)} %copy.61), channel_id=1, source_target_pairs={{0,2},{2,4},{4,6},{6,8},{8,10},{10,12},{12,14},{14,16},{16,18},{18... | collective-permute-start | bytes 98312 | tf_op jit(solution)/shard_map/while/body/eval_jaxpr/ppermute | solution.py:12
  1476.7 18.9 %collective-permute-start = (bf16[128,128]{1,0:T(8,128)(2,1)S(1)}, bf16[128,128]{1,0:T(8,128)(2,1)S(1)}, u32[]{:S(2)}, u32[]{:S(2)}) collective-permute-start(bf16[128,128]{1,0:T(8,128)(2,1)S(1)} %copy.61), channel_id=1, source_target_pairs={{0,2},{2,4},{4,6},{6,8},{8,10},{10,12},{12,14},{14,16},{16,18},{18... | collective-permute-start | bytes 98312 | tf_op jit(solution)/shard_map/while/body/eval_jaxpr/ppermute | solution.py:12
  1497.9 18.1 %collective-permute-start = (bf16[128,128]{1,0:T(8,128)(2,1)S(1)}, bf16[128,128]{1,0:T(8,128)(2,1)S(1)}, u32[]{:S(2)}, u32[]{:S(2)}) collective-permute-start(bf16[128,128]{1,0:T(8,128)(2,1)S(1)} %copy.61), channel_id=1, source_target_pairs={{0,2},{2,4},{4,6},{6,8},{8,10},{10,12},{12,14},{14,16},{16,18},{18... | collective-permute-start | bytes 98312 | tf_op jit(solution)/shard_map/while/body/eval_jaxpr/ppermute | solution.py:12
  1519.2 18.9 %collective-permute-start = (bf16[128,128]{1,0:T(8,128)(2,1)S(1)}, bf16[128,128]{1,0:T(8,128)(2,1)S(1)}, u32[]{:S(2)}, u32[]{:S(2)}) collective-permute-start(bf16[128,128]{1,0:T(8,128)(2,1)S(1)} %copy.61), channel_id=1, source_target_pairs={{0,2},{2,4},{4,6},{6,8},{8,10},{10,12},{12,14},{14,16},{16,18},{18... | collective-permute-start | bytes 98312 | tf_op jit(solution)/shard_map/while/body/eval_jaxpr/ppermute | solution.py:12
  (276 other events, 2970.6 us)
Sparse Core Ops, SparseCore 0:
  10.2 160.5 all-gather.3
  173.1 155.2 all-gather.5
where the time goes:
time: 1690 us; the launch traced here: 1670 us
  starting transfers between devices  732 us (43%)
  waiting for transfers between devices  471 us (28%)
  other arithmetic  187 us (11%)
  blocking collectives  132 us (8%)
  loops' own time  94.4 us (6%)
  matrix products  29.1 us (2%)
    ppermute x192, starting transfers between devices, passed_along(): lax.ppermute(value, axis, [(source, source + steps) for source in range(l...  649 us
    ppermute x192, waiting for transfers between devices, passed_along(): lax.ppermute(value, axis, [(source, source + steps) for source in range(l...  287 us
    all_gather x1, waiting for transfers between devices, per_device(): value_piece = lax.all_gather(values, ('inner', 'outer'), axis=0, tiled=True)  158 us
    all_gather x1, blocking collectives, per_device(): doc_piece = lax.all_gather(row_doc, ('inner', 'outer'), axis=0, tiled=True)  132 us
    and x128, other arithmetic, permitted(): (key_pos[None, :] <= row_pos[:, None]) & (key_doc[None, :] == row_doc[:,...  95.1 us
    eq x128, other arithmetic, permitted(): key_doc[None, :] == row_doc[:, None]  88.3 us
    ppermute x128, starting transfers between devices, shifted(): lax.ppermute(shard, axis, [(i, (i + by) % length) for i in range(length)])  82.3 us
    another operation x1, loops' own time, per_device(): final = lax.fori_loop(0, devices, circle_step, initial)  49.3 us
  transfers between devices with their start and end apart: 322, of which 66 were waited for; matrix products, arithmetic and copies ran while one was open for 0% of the time, Pallas kernels for 0%

commit v1 on v0

v1 whole, which is shorter than its diff:
```python
import math

import jax
import jax.numpy as jnp
from jax import lax
from jax.experimental import pallas as pl
from jax.experimental.pallas import tpu as pltpu
from jax.sharding import PartitionSpec as P

NEG = -1e30
HEAD = 128
BLOCK = 128
DOC_ROWS = 16
CHUNK_BLOCKS = 4
CHUNK = CHUNK_BLOCKS * BLOCK
LONGEST = 40
SCALE = float(HEAD) ** (-0.5)
TO_EXP2 = SCALE * math.log2(math.e)
CONTEXT = ("inner", "outer")


def dot(lhs, rhs, over):
    return lax.dot_general(lhs, rhs, ((over[:1], over[1:]), ((), ())), preferred_element_type=jnp.float32)


def attention_grads(sizes, *refs):
    nz, nx = sizes
    place_ref, q_ref, g_ref = refs[:3]
    k_pieces = (refs[3 : 3 + nx], refs[3 + nx : 3 + 2 * nx])
    refs = refs[3 + 2 * nx :]
    v_pieces = (refs[:nz], refs[nz : 2 * nz])
    refs = refs[2 * nz :]
    dq_ref, dk_own, dk_sib, dv_own, dv_sib = refs[:5]
    q_rows, g_rows, k_all, v_all, scores, dprobs, dk_total, dv_total, sem = refs[5:]
    blocks = k_all.shape[0]
    tiles, part, width = q_ref.shape
    heads = width // HEAD
    rows = heads * part
    z, x, y, core = (place_ref[i] for i in range(4))

    def block_of(dz, dx, dc):
        c = core if dc == 0 else 1 - core
        return (lax.rem(z + dz, nz) * 2 + c) * (2 * nx) + lax.rem(x + dx, nx) * 2

    copies = []
    for dc in range(2):
        for dx in range(nx):
            for dz in range(nz):
                to = pl.ds(block_of(nz - dz, nx - dx, dc), 2)
                for piece, whole in ((k_pieces[dc][dx].at[dz], k_all), (v_pieces[dc][dz].at[dx], v_all)):
                    copies.append(pltpu.make_async_copy(piece, whole.at[to], sem.at[len(copies)]))
    for copy in copies:
        copy.start()
    dk_total[...] = jnp.zeros_like(dk_total)
    dv_total[...] = jnp.zeros_like(dv_total)
    row_token = z * part + lax.rem(lax.broadcasted_iota(jnp.int32, (CHUNK, rows), 1), part)
    key_token = lax.broadcasted_iota(jnp.int32, (CHUNK, rows), 0)
    for copy in copies:
        copy.wait()

    def fold(value, combine):
        return combine(value.reshape(CHUNK // 8, 8, rows), axis=0)

    def tile(j, carry):
        block = (lax.rem(z + nz - j, nz) * 2 + core) * (2 * nx) + x * 2 + y
        docs = k_all[:, BLOCK:, :].astype(jnp.float32)
        mine = k_all[pl.ds(block, 1), BLOCK:, :].astype(jnp.float32)
        before = jnp.sum(jnp.where(docs < mine, 1.0, 0.0), axis=0)
        first = jnp.max(before).astype(jnp.int32)
        for h in range(heads):
            q_rows[h * part : (h + 1) * part, :] = q_ref[j, :, h * HEAD : (h + 1) * HEAD]
            g_rows[h * part : (h + 1) * part, :] = g_ref[j, :, h * HEAD : (h + 1) * HEAD]
        q = q_rows[...]
        g = g_rows[...]
        chunks = lax.div(block - first + CHUNK_BLOCKS, CHUNK_BLOCKS)

        def keys_at(t):
            return jnp.minimum(first + t * CHUNK_BLOCKS, blocks - CHUNK_BLOCKS)

        def key_rows(t):
            return k_all[pl.ds(keys_at(t), CHUNK_BLOCKS), :BLOCK, :].reshape(CHUNK, HEAD)

        def slot(t):
            return pl.ds(pl.multiple_of(t * CHUNK, CHUNK), CHUNK)

        def full_scores(t, top):
            s = dot(key_rows(t), q, (1, 1))
            scores[slot(t), :] = s
            return jnp.maximum(top, fold(s, jnp.max))

        last = chunks - 1
        top = lax.fori_loop(0, last, full_scores, jnp.full((8, rows), NEG, jnp.float32))
        begin = keys_at(last)
        skipped = (first + last * CHUNK_BLOCKS - begin) * BLOCK
        mask = (key_token <= row_token + (block - begin) * BLOCK) & (key_token >= skipped)
        s = jnp.where(mask, dot(key_rows(last), q, (1, 1)), NEG)
        scores[slot(last), :] = s
        top = jnp.max(jnp.maximum(top, fold(s, jnp.max)), axis=0, keepdims=True) * TO_EXP2

        def sums(t, state):
            norm, weighted = state
            e = jnp.exp2(scores[slot(t), :] * TO_EXP2 - top)
            scores[slot(t), :] = e
            value_rows = v_all[pl.ds(keys_at(t), CHUNK_BLOCKS)].reshape(CHUNK, HEAD)
            dp = dot(value_rows, g, (1, 1))
            dprobs[slot(t), :] = dp
            return norm + fold(e, jnp.sum), weighted + fold(e * dp, jnp.sum)

        zeros = jnp.zeros((8, rows), jnp.float32)
        norm, weighted = lax.fori_loop(0, chunks, sums, (zeros, zeros))
        inverse = 1.0 / jnp.sum(norm, axis=0, keepdims=True)
        delta = jnp.sum(weighted, axis=0, keepdims=True) * inverse

        def grads(t, dq):
            keys = pl.ds(pl.multiple_of(keys_at(t) * BLOCK, BLOCK), CHUNK)
            p = scores[slot(t), :] * inverse
            ds = p * (dprobs[slot(t), :] - delta)
            p_low = p.astype(jnp.bfloat16)
            ds_low = ds.astype(jnp.bfloat16)
            dk_total[keys, :] += dot(ds_low, q, (1, 0))
            dv_total[keys, :] += dot(p_low, g, (1, 0))
            return dq + dot(key_rows(t), ds_low, (0, 0))

        dq = lax.fori_loop(0, chunks, grads, jnp.zeros((HEAD, rows), jnp.float32))
        dq = (dq * SCALE).T.astype(jnp.bfloat16)
        for h in range(heads):
            dq_ref[j, :, h * HEAD : (h + 1) * HEAD] = dq[h * part : (h + 1) * part, :]
        return carry

    lax.fori_loop(0, tiles, tile, 0)
    for dc, dk_out, dv_out in ((0, dk_own, dv_own), (1, dk_sib, dv_sib)):
        for dx in range(nx):
            for dz in range(nz):
                begin = pl.multiple_of(block_of(dz, dx, dc) * BLOCK, BLOCK)
                dk_out[dx, dz] = dk_total[pl.ds(begin, 2 * BLOCK), :].astype(jnp.bfloat16)
                dv_out[dz, dx] = dv_total[pl.ds(begin, 2 * BLOCK), :].astype(jnp.bfloat16)


def grads_call(place, q, g, k_own, k_sib, v_own, v_sib):
    part, width = q.shape[1:]
    rows = part * width // HEAD
    nx, nz = len(k_own), len(v_own)
    blocks = nx * nz * 4
    pieces = [*k_own, *k_sib, *v_own, *v_sib]
    whole = pl.BlockSpec(memory_space=pltpu.VMEM)
    dk_shape = jax.ShapeDtypeStruct((nx, nz, 2 * BLOCK, HEAD), jnp.bfloat16)
    dv_shape = jax.ShapeDtypeStruct((nz, nx, 2 * BLOCK, HEAD), jnp.bfloat16)
    return pl.pallas_call(
        lambda *refs: attention_grads((nz, nx), *refs),
        name="attention_grads",
        out_shape=(jax.ShapeDtypeStruct(q.shape, jnp.bfloat16), dk_shape, dk_shape, dv_shape, dv_shape),
        in_specs=[pl.BlockSpec(memory_space=pltpu.SMEM), whole, whole]
        + [pl.BlockSpec(memory_space=pl.ANY)] * len(pieces),
        out_specs=(whole,) * 5,
        scratch_shapes=[
            pltpu.VMEM((rows, HEAD), jnp.bfloat16),
            pltpu.VMEM((rows, HEAD), jnp.bfloat16),
            pltpu.VMEM((blocks, BLOCK + DOC_ROWS, HEAD), jnp.bfloat16),
            pltpu.VMEM((blocks, BLOCK, HEAD), jnp.bfloat16),
            pltpu.VMEM((LONGEST * BLOCK, rows), jnp.float32),
            pltpu.VMEM((LONGEST * BLOCK, rows), jnp.float32),
            pltpu.VMEM((blocks * BLOCK, HEAD), jnp.float32),
            pltpu.VMEM((blocks * BLOCK, HEAD), jnp.float32),
            pltpu.SemaphoreType.DMA((blocks,)),
        ],
        compiler_params=pltpu.CompilerParams(vmem_limit_bytes=48 * 1024 * 1024),
        cost_estimate=pl.CostEstimate(
            flops=10 * 20 * 1024 * 128 * 128, bytes_accessed=16 * 1024 * 1024, transcendentals=0
        ),
    )(place, q, g, *pieces)


def per_device(queries, keys, values, grad_out, block_docs):
    rows, width = queries.shape
    inner_size, outer_size = lax.axis_size("inner"), lax.axis_size("outer")
    nz, nx = inner_size // 2, outer_size // 2
    inner, outer = lax.axis_index("inner"), lax.axis_index("outer")
    z, core = lax.div(inner, 2), lax.rem(inner, 2)
    x, y = lax.div(outer, 2), lax.rem(outer, 2)
    part = rows // nz

    def moved(value, dz=0, dx=0, dy=0, dc=0):
        hops = []
        for source in range(inner_size * outer_size):
            i, o = divmod(source, outer_size)
            to_inner = (i // 2 + dz) % nz * 2 + (i % 2 + dc) % 2
            to_outer = (o // 2 + dx) % nx * 2 + (o % 2 + dy) % 2
            hops.append((source, to_inner * outer_size + to_outer))
        return lax.ppermute(value, CONTEXT, hops)

    doc_rows = jnp.broadcast_to(block_docs.astype(jnp.bfloat16)[:, None], (DOC_ROWS, HEAD))
    packed = jnp.concatenate([keys, doc_rows, values])
    other = moved(packed, dy=1)
    pair = jnp.where(y == 0, jnp.stack([packed, other]), jnp.stack([other, packed]))
    split = BLOCK + DOC_ROWS
    k_pair, v_pair = pair[:, :split], pair[:, split:]

    both = jnp.concatenate([queries, grad_out], axis=1)

    def piece_for(peer):
        return lax.dynamic_slice_in_dim(both, lax.rem(peer, nz) * part, part, 0)

    pieces = [piece_for(z)] + [moved(piece_for(z + by), dz=by) for by in range(1, nz)]
    q = jnp.stack([piece[:, :width] for piece in pieces])
    g = jnp.stack([piece[:, width:] for piece in pieces])

    k_line = jnp.stack([k_pair] + [moved(k_pair, dz=by) for by in range(1, nz)])
    v_line = jnp.stack([v_pair] + [moved(v_pair, dx=by) for by in range(1, nx)])
    k_own = [k_line] + [moved(k_line, dx=by) for by in range(1, nx)]
    v_own = [v_line] + [moved(v_line, dz=by) for by in range(1, nz)]
    k_sib = [moved(piece, dc=1) for piece in k_own]
    v_sib = [moved(piece, dc=1) for piece in v_own]

    place = jnp.stack([z, x, y, core]).astype(jnp.int32)
    dq, dk_own, dk_sib, dv_own, dv_sib = grads_call(place, q, g, k_own, k_sib, v_own, v_sib)

    returned = jnp.stack([dq[0]] + [moved(dq[by], dz=-by) for by in range(1, nz)])
    order = lax.rem(jnp.arange(nz) - z + nz, nz)
    grad_queries = jnp.take(returned, order, axis=0).reshape(rows, width)

    def added(terms):
        total = terms[0].astype(jnp.float32)
        for term in terms[1:]:
            total = total + term.astype(jnp.float32)
        return total

    def low(value):
        return value.astype(jnp.bfloat16)

    def line_sum(value, **axis):
        ((name, count),) = axis.items()
        return added([value[0]] + [moved(value[by], **{name: by}) for by in range(1, count)])

    dk = low(added([dk_own, moved(dk_sib, dc=1)]))
    dv = low(added([dv_own, moved(dv_sib, dc=1)]))
    dk = low(line_sum(dk, dx=nx))
    dv = low(line_sum(dv, dz=nz))
    dk = low(line_sum(dk, dz=nz))
    dv = low(line_sum(dv, dx=nx))
    sums = jnp.concatenate([dk, dv], axis=1).reshape(2, BLOCK, 2 * HEAD)
    keep = jnp.where(y == 0, sums[0], sums[1])
    send = jnp.where(y == 0, sums[1], sums[0])
    total = added([keep, moved(send, dy=1)])
    return grad_queries, low(SCALE * total[:, :HEAD]), low(total[:, HEAD:])


def solution(mesh):
    wide = P(CONTEXT, "head")
    return jax.shard_map(
        per_device,
        mesh=mesh,
        in_specs=(wide, wide, wide, wide, P(CONTEXT)),
        out_specs=(wide, wide, wide),
        check_vma=False,
    )
```

time: 1690 us -> 135 us (0.08)
  the two profiles are of different devices: /device:TPU:1 before, /device:TPU:0 now
where the time goes in v1:
time: 135 us; the launch traced here: 134 us
  starting transfers between devices  53.5 us (40%)
  waiting for transfers between devices  46.5 us (34%)
  Pallas kernels  24.3 us (18%)
  other arithmetic  4.79 us (4%)
  local copies, waits for them, and re-layouts  3.58 us (3%)
  between operations  1.62 us (1%)
    ppermute x42, starting transfers between devices, moved(): return lax.ppermute(value, CONTEXT, hops)  53.5 us
    ppermute x42, waiting for transfers between devices, moved(): return lax.ppermute(value, CONTEXT, hops)  46.5 us
    pallas_call x1, Pallas kernels, grads_call(): pl.pallas_call(lambda *refs: attention_grads((nz, nx), *refs), name='atte...  24.3 us
    convert_element_type x7, other arithmetic, low(): return value.astype(jnp.bfloat16)  2.77 us
  transfers between devices with their start and end apart: 42, of which 22 were waited for; matrix products, arithmetic and copies ran while one was open for 5% of the time, Pallas kernels for 0%

profile of v1, /device:TPU:0, one launch (start us, length us, event | category | flops | bytes accessed | tf_op | source)
XLA Modules:
  0.0 134.3 jit_solution(17014328248945795273)
XLA Ops:
  1.3 0.9 fusion.17
  2.2 1.7 %collective-permute-start.3 = (bf16[272,128]{1,0:T(8,128)(2,1)S(1)}, bf16[272,128]{1,0:T(8,128)(2,1)S(1)}, u32[]{:S(2)}, u32[]{:S(2)}) collective-permute-start(bf16[272,128]{1,0:T(8,128)(2,1)S(1)} %get-tuple-element.45), channel_id=1, source_target_pairs={{0,2},{2,0},{4,6},{6,4},{8,10},{10,8},{12,14},{14,12},{16,18},{18,... | collective-permute-start | bytes 208904 | tf_op jit(solution)/shard_map/ppermute | solution.py:189
  3.9 1.0 constant_dynamic-update-slice_fusion.1
  4.9 1.0 constant_dynamic-update-slice_fusion
  5.9 2.0 %collective-permute-start = (bf16[32,2048]{1,0:T(8,128)(2,1)S(1)}, bf16[32,2048]{1,0:T(8,128)(2,1)S(1)}, u32[]{:S(2)}, u32[]{:S(2)}) collective-permute-start(bf16[32,2048]{1,0:T(8,128)(2,1)S(1)} %get-tuple-element.21), channel_id=1, source_target_pairs={{0,32},{2,34},{4,36},{6,38},{8,40},{10,42},{12,44},{14,46},{16,48}... | collective-permute-start | bytes 393224 | tf_op jit(solution)/shard_map/ppermute | solution.py:189
  7.9 3.6 %collective-permute-start.1 = (bf16[32,2048]{1,0:T(8,128)(2,1)S(1)}, bf16[32,2048]{1,0:T(8,128)(2,1)S(1)}, u32[]{:S(2)}, u32[]{:S(2)}) collective-permute-start(bf16[32,2048]{1,0:T(8,128)(2,1)S(1)} %get-tuple-element.23), channel_id=1, source_target_pairs={{0,64},{2,66},{4,68},{6,70},{8,72},{10,74},{12,76},{14,78},{16,80}... | collective-permute-start | bytes 393224 | tf_op jit(solution)/shard_map/ppermute | solution.py:189
  11.6 1.6 %collective-permute-start.14 = (bf16[2,128,128]{2,1,0:T(8,128)(2,1)S(1)}, bf16[2,128,128]{2,1,0:T(8,128)(2,1)S(1)}, u32[]{:S(2)}, u32[]{:S(2)}) collective-permute-start(bf16[2,128,128]{2,1,0:T(8,128)(2,1)S(1)} %get-tuple-element.35), channel_id=1, source_target_pairs={{0,4},{2,6},{4,8},{6,10},{8,12},{10,14},{12,0},{14,2},{16,20},{18,... | collective-permute-start | bytes 196616 | tf_op jit(solution)/shard_map/ppermute | solution.py:189
  13.1 2.7 %collective-permute-start.15 = (bf16[2,128,128]{2,1,0:T(8,128)(2,1)S(1)}, bf16[2,128,128]{2,1,0:T(8,128)(2,1)S(1)}, u32[]{:S(2)}, u32[]{:S(2)}) collective-permute-start(bf16[2,128,128]{2,1,0:T(8,128)(2,1)S(1)} %get-tuple-element.35), channel_id=1, source_target_pairs={{0,8},{2,10},{4,12},{6,14},{8,0},{10,2},{12,4},{14,6},{16,24},{18,... | collective-permute-start | bytes 196616 | tf_op jit(solution)/shard_map/ppermute | solution.py:189
  15.8 1.4 %collective-permute-start.16 = (bf16[2,128,128]{2,1,0:T(8,128)(2,1)S(1)}, bf16[2,128,128]{2,1,0:T(8,128)(2,1)S(1)}, u32[]{:S(2)}, u32[]{:S(2)}) collective-permute-start(bf16[2,128,128]{2,1,0:T(8,128)(2,1)S(1)} %get-tuple-element.35), channel_id=1, source_target_pairs={{0,12},{2,14},{4,0},{6,2},{8,4},{10,6},{12,8},{14,10},{16,28},{18,... | collective-permute-start | bytes 196616 | tf_op jit(solution)/shard_map/ppermute | solution.py:189
  17.5 1.4 %collective-permute-done.15 = bf16[2,128,128]{2,1,0:T(8,128)(2,1)S(1)} collective-permute-done((bf16[2,128,128]{2,1,0:T(8,128)(2,1)S(1)}, bf16[2,128,128]{2,1,0:T(8,128)(2,1)S(1)}, u32[]{:S(2)}, u32[]{:S(2)}) %collective-permute-start.15) | collective-permute-done | bytes 65568 | tf_op jit(solution)/shard_map/ppermute | solution.py:189
  18.9 1.1 collective-permute-start.5
  20.1 1.0 collective-permute-start.6
  21.2 1.1 collective-permute-start.17
  22.3 2.3 %collective-permute-start.18 = (bf16[4,2,128,128]{3,2,1,0:T(8,128)(2,1)S(1)}, bf16[4,2,128,128]{3,2,1,0:T(8,128)(2,1)S(1)}, u32[]{:S(2)}, u32[]{:S(2)}) collective-permute-start(bf16[4,2,128,128]{3,2,1,0:T(8,128)(2,1)S(1)} %pad_maximum_fusion.3.refs_11_), channel_id=1, source_target_pairs={{0,64},{2,66},{4,68},{6,70},{8,72},{10,74},{12,76},{14,78},{16,80}... | collective-permute-start | bytes 786440 | tf_op jit(solution)/shard_map/ppermute | solution.py:189
  24.6 1.9 %collective-permute-start.19 = (bf16[4,2,128,128]{3,2,1,0:T(8,128)(2,1)S(1)}, bf16[4,2,128,128]{3,2,1,0:T(8,128)(2,1)S(1)}, u32[]{:S(2)}, u32[]{:S(2)}) collective-permute-start(bf16[4,2,128,128]{3,2,1,0:T(8,128)(2,1)S(1)} %pad_maximum_fusion.3.refs_11_), channel_id=1, source_target_pairs={{0,96},{2,98},{4,100},{6,102},{8,104},{10,106},{12,108},{14,110},{... | collective-permute-start | bytes 786440 | tf_op jit(solution)/shard_map/ppermute | solution.py:189
  26.5 1.5 %collective-permute-done.6 = bf16[2,144,128]{2,1,0:T(8,128)(2,1)S(1)} collective-permute-done((bf16[2,144,128]{2,1,0:T(8,128)(2,1)S(1)}, bf16[2,144,128]{2,1,0:T(8,128)(2,1)S(1)}, u32[]{:S(2)}, u32[]{:S(2)}) %collective-permute-start.6) | collective-permute-done | bytes 73760 | tf_op jit(solution)/shard_map/ppermute | solution.py:189
  28.0 4.2 %collective-permute-start.2 = (bf16[32,2048]{1,0:T(8,128)(2,1)S(1)}, bf16[32,2048]{1,0:T(8,128)(2,1)S(1)}, u32[]{:S(2)}, u32[]{:S(2)}) collective-permute-start(bf16[32,2048]{1,0:T(8,128)(2,1)S(1)} %get-tuple-element.22), channel_id=1, source_target_pairs={{0,96},{2,98},{4,100},{6,102},{8,104},{10,106},{12,108},{14,110},{... | collective-permute-start | bytes 393224 | tf_op jit(solution)/shard_map/ppermute | solution.py:189
  32.3 6.5 %collective-permute-done.2 = bf16[32,2048]{1,0:T(8,128)(2,1)S(1)} collective-permute-done((bf16[32,2048]{1,0:T(8,128)(2,1)S(1)}, bf16[32,2048]{1,0:T(8,128)(2,1)S(1)}, u32[]{:S(2)}, u32[]{:S(2)}) %collective-permute-start.2) | collective-permute-done | bytes 131104 | tf_op jit(solution)/shard_map/ppermute | solution.py:189
  38.8 0.7 collective-permute-start.7
  39.5 2.7 %collective-permute-start.8 = (bf16[4,2,144,128]{3,2,1,0:T(8,128)(2,1)S(1)}, bf16[4,2,144,128]{3,2,1,0:T(8,128)(2,1)S(1)}, u32[]{:S(2)}, u32[]{:S(2)}) collective-permute-start(bf16[4,2,144,128]{3,2,1,0:T(8,128)(2,1)S(1)} %pad_maximum_fusion.refs_3_), channel_id=1, source_target_pairs={{0,8},{2,10},{4,12},{6,14},{8,0},{10,2},{12,4},{14,6},{16,24},{18,... | collective-permute-start | bytes 884744 | tf_op jit(solution)/shard_map/ppermute | solution.py:189
  42.2 1.1 collective-permute-start.9
  43.4 0.5 collective-permute-start.21
  43.9 5.8 %collective-permute-done.7.refs_4_ = bf16[4,2,144,128]{3,2,1,0:T(8,128)(2,1)S(1)} collective-permute-done((bf16[4,2,144,128]{3,2,1,0:T(8,128)(2,1)S(1)}, bf16[4,2,144,128]{3,2,1,0:T(8,128)(2,1)S(1)}, u32[]{:S(2)}, u32[]{:S(2)}) %collective-permute-start.7) | collective-permute-done | bytes 294944 | tf_op jit(solution)/shard_map/ppermute | solution.py:189
  49.7 4.2 %collective-permute-done.8.refs_5_ = bf16[4,2,144,128]{3,2,1,0:T(8,128)(2,1)S(1)} collective-permute-done((bf16[4,2,144,128]{3,2,1,0:T(8,128)(2,1)S(1)}, bf16[4,2,144,128]{3,2,1,0:T(8,128)(2,1)S(1)}, u32[]{:S(2)}, u32[]{:S(2)}) %collective-permute-start.8) | collective-permute-done | bytes 294944 | tf_op jit(solution)/shard_map/ppermute | solution.py:189
  55.4 0.4 collective-permute-done.11.refs_8_
  56.7 24.3 %attention_grads.1 = (bf16[4,32,1024]{2,1,0:T(8,128)(2,1)S(1)}, bf16[4,4,256,128]{3,2,1,0:T(8,128)(2,1)}, bf16[4,4,256,128]{3,2,1,0:T(8,128)(2,1)}, bf16[4,4,256...) custom-call(s32[4]{0:T(128)S(1)} %pad_add_fusion.refs_0_, bf16[4,32,1024]{2,1,0:T(8,128)(2,1)S(1)} %get-tuple-element.46.refs_1_, ...), custom_call_target="tpu_custom_call" | custom-call | flops 3355443200 | bytes 16777216 | tf_op jit(solution)/shard_map/attention_grads/pallas_call | solution.py:148
  81.0 4.4 %collective-permute-start.27 = (bf16[4,4,256,128]{3,2,1,0:T(8,128)(2,1)}, bf16[4,4,256,128]{3,2,1,0:T(8,128)(2,1)}, u32[]{:S(2)}, u32[]{:S(2)}) collective-permute-start(bf16[4,4,256,128]{3,2,1,0:T(8,128)(2,1)} %get-tuple-element.10), channel_id=1, source_target_pairs={{0,16},{2,18},{4,20},{6,22},{8,24},{10,26},{12,28},{14,30},{16,0},... | collective-permute-start | bytes 3145736 | tf_op jit(solution)/shard_map/ppermute | solution.py:189
  85.7 4.0 %collective-permute-start.24 = (bf16[32,1024]{1,0:T(8,128)(2,1)S(1)}, bf16[32,1024]{1,0:T(8,128)(2,1)S(1)}, u32[]{:S(2)}, u32[]{:S(2)}) collective-permute-start(bf16[32,1024]{1,0:T(8,128)(2,1)S(1)} %get-tuple-element.33), channel_id=1, source_target_pairs={{0,96},{2,98},{4,100},{6,102},{8,104},{10,106},{12,108},{14,110},{... | collective-permute-start | bytes 196616 | tf_op jit(solution)/shard_map/ppermute | solution.py:189
  89.8 0.8 collective-permute-start.26
  90.7 2.5 %collective-permute-done.24 = bf16[32,1024]{1,0:T(8,128)(2,1)S(1)} collective-permute-done((bf16[32,1024]{1,0:T(8,128)(2,1)S(1)}, bf16[32,1024]{1,0:T(8,128)(2,1)S(1)}, u32[]{:S(2)}, u32[]{:S(2)}) %collective-permute-start.24) | collective-permute-done | bytes 65568 | tf_op jit(solution)/shard_map/ppermute | solution.py:189
  93.1 3.0 %collective-permute-done.25 = bf16[32,1024]{1,0:T(8,128)(2,1)S(1)} collective-permute-done((bf16[32,1024]{1,0:T(8,128)(2,1)S(1)}, bf16[32,1024]{1,0:T(8,128)(2,1)S(1)}, u32[]{:S(2)}, u32[]{:S(2)}) %collective-permute-start.25) | collective-permute-done | bytes 65568 | tf_op jit(solution)/shard_map/ppermute | solution.py:189
  96.6 0.6 gather_fusion
  97.2 1.5 %add_convert_fusion.1 = bf16[4,4,256,128]{3,2,1,0:T(8,128)(2,1)S(1)} fusion(bf16[4,4,256,128]{3,2,1,0:T(8,128)(2,1)} %collective-permute-done.27, bf16[4,4,256,128]{3,2,1,0:T(8,128)(2,1)S(1)} %copy-done.1), kind=kLoop, calls=%fused_computation.2 | loop fusion | flops 2097152 | bytes 3145728 | tf_op jit(solution)/shard_map/convert_element_type | solution.py:228
  98.8 4.0 %collective-permute-start.29 = (bf16[4,256,128]{2,1,0:T(8,128)(2,1)S(1)}, bf16[4,256,128]{2,1,0:T(8,128)(2,1)S(1)}, u32[]{:S(2)}, u32[]{:S(2)}) collective-permute-start(bf16[4,256,128]{2,1,0:T(8,128)(2,1)S(1)} %get-tuple-element.15), channel_id=1, source_target_pairs={{0,8},{2,10},{4,12},{6,14},{8,0},{10,2},{12,4},{14,6},{16,24},{18,... | collective-permute-start | bytes 786440 | tf_op jit(solution)/shard_map/ppermute | solution.py:189
  103.2 2.3 %collective-permute-start.36 = (bf16[4,256,128]{2,1,0:T(8,128)(2,1)S(1)}, bf16[4,256,128]{2,1,0:T(8,128)(2,1)S(1)}, u32[]{:S(2)}, u32[]{:S(2)}) collective-permute-start(bf16[4,256,128]{2,1,0:T(8,128)(2,1)S(1)} %get-tuple-element.18), channel_id=1, source_target_pairs={{0,64},{2,66},{4,68},{6,70},{8,72},{10,74},{12,76},{14,78},{16,80}... | collective-permute-start | bytes 786440 | tf_op jit(solution)/shard_map/ppermute | solution.py:189
  105.5 8.1 %collective-permute-done.28 = bf16[4,256,128]{2,1,0:T(8,128)(2,1)S(1)} collective-permute-done((bf16[4,256,128]{2,1,0:T(8,128)(2,1)S(1)}, bf16[4,256,128]{2,1,0:T(8,128)(2,1)S(1)}, u32[]{:S(2)}, u32[]{:S(2)}) %collective-permute-start.28) | collective-permute-done | bytes 262176 | tf_op jit(solution)/shard_map/ppermute | solution.py:189
  113.6 0.6 collective-permute-done.30
  114.4 1.5 %collective-permute-start.31 = (bf16[256,128]{1,0:T(8,128)(2,1)S(1)}, bf16[256,128]{1,0:T(8,128)(2,1)S(1)}, u32[]{:S(2)}, u32[]{:S(2)}) collective-permute-start(bf16[256,128]{1,0:T(8,128)(2,1)S(1)} %get-tuple-element.24), channel_id=1, source_target_pairs={{0,32},{2,34},{4,36},{6,38},{8,40},{10,42},{12,44},{14,46},{16,48}... | collective-permute-start | bytes 196616 | tf_op jit(solution)/shard_map/ppermute | solution.py:189
  115.9 0.5 collective-permute-start.32
  116.7 1.9 %collective-permute-start.33 = (bf16[256,128]{1,0:T(8,128)(2,1)S(1)}, bf16[256,128]{1,0:T(8,128)(2,1)S(1)}, u32[]{:S(2)}, u32[]{:S(2)}) collective-permute-start(bf16[256,128]{1,0:T(8,128)(2,1)S(1)} %get-tuple-element.25), channel_id=1, source_target_pairs={{0,96},{2,98},{4,100},{6,102},{8,104},{10,106},{12,108},{14,110},{... | collective-permute-start | bytes 196616 | tf_op jit(solution)/shard_map/ppermute | solution.py:189
  118.6 2.7 %collective-permute-done.37 = bf16[4,256,128]{2,1,0:T(8,128)(2,1)S(1)} collective-permute-done((bf16[4,256,128]{2,1,0:T(8,128)(2,1)S(1)}, bf16[4,256,128]{2,1,0:T(8,128)(2,1)S(1)}, u32[]{:S(2)}, u32[]{:S(2)}) %collective-permute-start.37) | collective-permute-done | bytes 262176 | tf_op jit(solution)/shard_map/ppermute | solution.py:189
  121.7 3.1 %collective-permute-start.40 = (bf16[256,128]{1,0:T(8,128)(2,1)S(1)}, bf16[256,128]{1,0:T(8,128)(2,1)S(1)}, u32[]{:S(2)}, u32[]{:S(2)}) collective-permute-start(bf16[256,128]{1,0:T(8,128)(2,1)S(1)} %get-tuple-element.28), channel_id=1, source_target_pairs={{0,12},{2,14},{4,0},{6,2},{8,4},{10,6},{12,8},{14,10},{16,28},{18,... | collective-permute-start | bytes 196616 | tf_op jit(solution)/shard_map/ppermute | solution.py:189
  124.9 2.9 %collective-permute-done.38 = bf16[256,128]{1,0:T(8,128)(2,1)S(1)} collective-permute-done((bf16[256,128]{1,0:T(8,128)(2,1)S(1)}, bf16[256,128]{1,0:T(8,128)(2,1)S(1)}, u32[]{:S(2)}, u32[]{:S(2)}) %collective-permute-start.38) | collective-permute-done | bytes 65568 | tf_op jit(solution)/shard_map/ppermute | solution.py:189
  127.8 0.9 collective-permute-done.40
  128.8 0.8 bitcast_select_fusion
  129.6 3.5 %collective-permute-done.41 = bf16[128,256]{1,0:T(8,128)(2,1)S(1)} collective-permute-done((bf16[128,256]{1,0:T(8,128)(2,1)S(1)}, bf16[128,256]{1,0:T(8,128)(2,1)S(1)}, u32[]{:S(2)}, u32[]{:S(2)}) %collective-permute-start.41) | collective-permute-done | bytes 65568 | tf_op jit(solution)/shard_map/ppermute | solution.py:189
  133.1 0.6 fusion.13
  133.7 0.6 slice.224
  (81 shorter events, 5.5 us)
Async XLA Ops:
  2.2 9.3 %collective-permute-start.3 = (bf16[272,128]{1,0:T(8,128)(2,1)S(1)}, bf16[272,128]{1,0:T(8,128)(2,1)S(1)}, u32[]{:S(2)}, u32[]{:S(2)}) collective-permute-start(bf16[272,128]{1,0:T(8,128)(2,1)S(1)} %get-tuple-element.45), channel_id=1, source_target_pairs={{0,2},{2,0},{4,6},{6,4},{8,10},{10,8},{12,14},{14,12},{16,18},{18,... | collective-permute-start | bytes 208904 | tf_op jit(solution)/shard_map/ppermute | solution.py:189
  5.9 15.2 %collective-permute-start = (bf16[32,2048]{1,0:T(8,128)(2,1)S(1)}, bf16[32,2048]{1,0:T(8,128)(2,1)S(1)}, u32[]{:S(2)}, u32[]{:S(2)}) collective-permute-start(bf16[32,2048]{1,0:T(8,128)(2,1)S(1)} %get-tuple-element.21), channel_id=1, source_target_pairs={{0,32},{2,34},{4,36},{6,38},{8,40},{10,42},{12,44},{14,46},{16,48}... | collective-permute-start | bytes 393224 | tf_op jit(solution)/shard_map/ppermute | solution.py:189
  7.9 14.3 %collective-permute-start.1 = (bf16[32,2048]{1,0:T(8,128)(2,1)S(1)}, bf16[32,2048]{1,0:T(8,128)(2,1)S(1)}, u32[]{:S(2)}, u32[]{:S(2)}) collective-permute-start(bf16[32,2048]{1,0:T(8,128)(2,1)S(1)} %get-tuple-element.23), channel_id=1, source_target_pairs={{0,64},{2,66},{4,68},{6,70},{8,72},{10,74},{12,76},{14,78},{16,80}... | collective-permute-start | bytes 393224 | tf_op jit(solution)/shard_map/ppermute | solution.py:189
  11.6 6.0 %collective-permute-start.14 = (bf16[2,128,128]{2,1,0:T(8,128)(2,1)S(1)}, bf16[2,128,128]{2,1,0:T(8,128)(2,1)S(1)}, u32[]{:S(2)}, u32[]{:S(2)}) collective-permute-start(bf16[2,128,128]{2,1,0:T(8,128)(2,1)S(1)} %get-tuple-element.35), channel_id=1, source_target_pairs={{0,4},{2,6},{4,8},{6,10},{8,12},{10,14},{12,0},{14,2},{16,20},{18,... | collective-permute-start | bytes 196616 | tf_op jit(solution)/shard_map/ppermute | solution.py:189
  13.1 5.8 %collective-permute-start.15 = (bf16[2,128,128]{2,1,0:T(8,128)(2,1)S(1)}, bf16[2,128,128]{2,1,0:T(8,128)(2,1)S(1)}, u32[]{:S(2)}, u32[]{:S(2)}) collective-permute-start(bf16[2,128,128]{2,1,0:T(8,128)(2,1)S(1)} %get-tuple-element.35), channel_id=1, source_target_pairs={{0,8},{2,10},{4,12},{6,14},{8,0},{10,2},{12,4},{14,6},{16,24},{18,... | collective-permute-start | bytes 196616 | tf_op jit(solution)/shard_map/ppermute | solution.py:189
  15.8 4.3 %collective-permute-start.16 = (bf16[2,128,128]{2,1,0:T(8,128)(2,1)S(1)}, bf16[2,128,128]{2,1,0:T(8,128)(2,1)S(1)}, u32[]{:S(2)}, u32[]{:S(2)}) collective-permute-start(bf16[2,128,128]{2,1,0:T(8,128)(2,1)S(1)} %get-tuple-element.35), channel_id=1, source_target_pairs={{0,12},{2,14},{4,0},{6,2},{8,4},{10,6},{12,8},{14,10},{16,28},{18,... | collective-permute-start | bytes 196616 | tf_op jit(solution)/shard_map/ppermute | solution.py:189
  17.5 7.1 %collective-permute-start.4 = (bf16[2,144,128]{2,1,0:T(8,128)(2,1)S(1)}, bf16[2,144,128]{2,1,0:T(8,128)(2,1)S(1)}, u32[]{:S(2)}, u32[]{:S(2)}) collective-permute-start(bf16[2,144,128]{2,1,0:T(8,128)(2,1)S(1)} %get-tuple-element.37), channel_id=1, source_target_pairs={{0,32},{2,34},{4,36},{6,38},{8,40},{10,42},{12,44},{14,46},{16,48}... | collective-permute-start | bytes 221192 | tf_op jit(solution)/shard_map/ppermute | solution.py:189
  18.9 7.6 %collective-permute-start.5 = (bf16[2,144,128]{2,1,0:T(8,128)(2,1)S(1)}, bf16[2,144,128]{2,1,0:T(8,128)(2,1)S(1)}, u32[]{:S(2)}, u32[]{:S(2)}) collective-permute-start(bf16[2,144,128]{2,1,0:T(8,128)(2,1)S(1)} %get-tuple-element.37), channel_id=1, source_target_pairs={{0,64},{2,66},{4,68},{6,70},{8,72},{10,74},{12,76},{14,78},{16,80}... | collective-permute-start | bytes 221192 | tf_op jit(solution)/shard_map/ppermute | solution.py:189
  20.1 7.9 %collective-permute-start.6 = (bf16[2,144,128]{2,1,0:T(8,128)(2,1)S(1)}, bf16[2,144,128]{2,1,0:T(8,128)(2,1)S(1)}, u32[]{:S(2)}, u32[]{:S(2)}) collective-permute-start(bf16[2,144,128]{2,1,0:T(8,128)(2,1)S(1)} %get-tuple-element.37), channel_id=1, source_target_pairs={{0,96},{2,98},{4,100},{6,102},{8,104},{10,106},{12,108},{14,110},{... | collective-permute-start | bytes 221192 | tf_op jit(solution)/shard_map/ppermute | solution.py:189
  21.2 18.3 %collective-permute-start.17 = (bf16[4,2,128,128]{3,2,1,0:T(8,128)(2,1)S(1)}, bf16[4,2,128,128]{3,2,1,0:T(8,128)(2,1)S(1)}, u32[]{:S(2)}, u32[]{:S(2)}) collective-permute-start(bf16[4,2,128,128]{3,2,1,0:T(8,128)(2,1)S(1)} %pad_maximum_fusion.3.refs_11_), channel_id=1, source_target_pairs={{0,32},{2,34},{4,36},{6,38},{8,40},{10,42},{12,44},{14,46},{16,48}... | collective-permute-start | bytes 786440 | tf_op jit(solution)/shard_map/ppermute | solution.py:189
  22.3 20.0 %collective-permute-start.18 = (bf16[4,2,128,128]{3,2,1,0:T(8,128)(2,1)S(1)}, bf16[4,2,128,128]{3,2,1,0:T(8,128)(2,1)S(1)}, u32[]{:S(2)}, u32[]{:S(2)}) collective-permute-start(bf16[4,2,128,128]{3,2,1,0:T(8,128)(2,1)S(1)} %pad_maximum_fusion.3.refs_11_), channel_id=1, source_target_pairs={{0,64},{2,66},{4,68},{6,70},{8,72},{10,74},{12,76},{14,78},{16,80}... | collective-permute-start | bytes 786440 | tf_op jit(solution)/shard_map/ppermute | solution.py:189
  24.6 18.8 %collective-permute-start.19 = (bf16[4,2,128,128]{3,2,1,0:T(8,128)(2,1)S(1)}, bf16[4,2,128,128]{3,2,1,0:T(8,128)(2,1)S(1)}, u32[]{:S(2)}, u32[]{:S(2)}) collective-permute-start(bf16[4,2,128,128]{3,2,1,0:T(8,128)(2,1)S(1)} %pad_maximum_fusion.3.refs_11_), channel_id=1, source_target_pairs={{0,96},{2,98},{4,100},{6,102},{8,104},{10,106},{12,108},{14,110},{... | collective-permute-start | bytes 786440 | tf_op jit(solution)/shard_map/ppermute | solution.py:189
  26.4 16.9 %collective-permute-start.20 = (bf16[4,2,128,128]{3,2,1,0:T(8,128)(2,1)S(1)}, bf16[4,2,128,128]{3,2,1,0:T(8,128)(2,1)S(1)}, u32[]{:S(2)}, u32[]{:S(2)}) collective-permute-start(bf16[4,2,128,128]{3,2,1,0:T(8,128)(2,1)S(1)} %pad_maximum_fusion.3.refs_11_), channel_id=1, source_target_pairs={{0,16},{2,18},{4,20},{6,22},{8,24},{10,26},{12,28},{14,30},{16,0},... | collective-permute-start | bytes 786440 | tf_op jit(solution)/shard_map/ppermute | solution.py:189
  28.0 10.8 %collective-permute-start.2 = (bf16[32,2048]{1,0:T(8,128)(2,1)S(1)}, bf16[32,2048]{1,0:T(8,128)(2,1)S(1)}, u32[]{:S(2)}, u32[]{:S(2)}) collective-permute-start(bf16[32,2048]{1,0:T(8,128)(2,1)S(1)} %get-tuple-element.22), channel_id=1, source_target_pairs={{0,96},{2,98},{4,100},{6,102},{8,104},{10,106},{12,108},{14,110},{... | collective-permute-start | bytes 393224 | tf_op jit(solution)/shard_map/ppermute | solution.py:189
  38.8 10.9 %collective-permute-start.7 = (bf16[4,2,144,128]{3,2,1,0:T(8,128)(2,1)S(1)}, bf16[4,2,144,128]{3,2,1,0:T(8,128)(2,1)S(1)}, u32[]{:S(2)}, u32[]{:S(2)}) collective-permute-start(bf16[4,2,144,128]{3,2,1,0:T(8,128)(2,1)S(1)} %pad_maximum_fusion.refs_3_), channel_id=1, source_target_pairs={{0,4},{2,6},{4,8},{6,10},{8,12},{10,14},{12,0},{14,2},{16,20},{18,... | collective-permute-start | bytes 884744 | tf_op jit(solution)/shard_map/ppermute | solution.py:189
  39.5 14.3 %collective-permute-start.8 = (bf16[4,2,144,128]{3,2,1,0:T(8,128)(2,1)S(1)}, bf16[4,2,144,128]{3,2,1,0:T(8,128)(2,1)S(1)}, u32[]{:S(2)}, u32[]{:S(2)}) collective-permute-start(bf16[4,2,144,128]{3,2,1,0:T(8,128)(2,1)S(1)} %pad_maximum_fusion.refs_3_), channel_id=1, source_target_pairs={{0,8},{2,10},{4,12},{6,14},{8,0},{10,2},{12,4},{14,6},{16,24},{18,... | collective-permute-start | bytes 884744 | tf_op jit(solution)/shard_map/ppermute | solution.py:189
  42.2 12.0 %collective-permute-start.9 = (bf16[4,2,144,128]{3,2,1,0:T(8,128)(2,1)S(1)}, bf16[4,2,144,128]{3,2,1,0:T(8,128)(2,1)S(1)}, u32[]{:S(2)}, u32[]{:S(2)}) collective-permute-start(bf16[4,2,144,128]{3,2,1,0:T(8,128)(2,1)S(1)} %pad_maximum_fusion.refs_3_), channel_id=1, source_target_pairs={{0,12},{2,14},{4,0},{6,2},{8,4},{10,6},{12,8},{14,10},{16,28},{18,... | collective-permute-start | bytes 884744 | tf_op jit(solution)/shard_map/ppermute | solution.py:189
  43.4 11.0 %collective-permute-start.10 = (bf16[4,2,144,128]{3,2,1,0:T(8,128)(2,1)S(1)}, bf16[4,2,144,128]{3,2,1,0:T(8,128)(2,1)S(1)}, u32[]{:S(2)}, u32[]{:S(2)}) collective-permute-start(bf16[4,2,144,128]{3,2,1,0:T(8,128)(2,1)S(1)} %pad_maximum_fusion.refs_3_), channel_id=1, source_target_pairs={{0,16},{2,18},{4,20},{6,22},{8,24},{10,26},{12,28},{14,30},{16,0},... | collective-permute-start | bytes 884744 | tf_op jit(solution)/shard_map/ppermute | solution.py:189
  43.4 11.4 %collective-permute-start.21 = (bf16[4,2,128,128]{3,2,1,0:T(8,128)(2,1)S(1)}, bf16[4,2,128,128]{3,2,1,0:T(8,128)(2,1)S(1)}, u32[]{:S(2)}, u32[]{:S(2)}) collective-permute-start(bf16[4,2,128,128]{3,2,1,0:T(8,128)(2,1)S(1)} %collective-permute-done.17.refs_12_), channel_id=1, source_target_pairs={{0,16},{2,18},{4,20},{6,22},{8,24},{10,26},{12,28},{14,30},{16,0},... | collective-permute-start | bytes 786440 | tf_op jit(solution)/shard_map/ppermute | solution.py:189
  49.7 5.3 %collective-permute-start.22 = (bf16[4,2,128,128]{3,2,1,0:T(8,128)(2,1)S(1)}, bf16[4,2,128,128]{3,2,1,0:T(8,128)(2,1)S(1)}, u32[]{:S(2)}, u32[]{:S(2)}) collective-permute-start(bf16[4,2,128,128]{3,2,1,0:T(8,128)(2,1)S(1)} %collective-permute-done.18.refs_13_), channel_id=1, source_target_pairs={{0,16},{2,18},{4,20},{6,22},{8,24},{10,26},{12,28},{14,30},{16,0},... | collective-permute-start | bytes 786440 | tf_op jit(solution)/shard_map/ppermute | solution.py:189
  53.9 1.5 %collective-permute-start.23 = (bf16[4,2,128,128]{3,2,1,0:T(8,128)(2,1)S(1)}, bf16[4,2,128,128]{3,2,1,0:T(8,128)(2,1)S(1)}, u32[]{:S(2)}, u32[]{:S(2)}) collective-permute-start(bf16[4,2,128,128]{3,2,1,0:T(8,128)(2,1)S(1)} %collective-permute-done.19.refs_14_), channel_id=1, source_target_pairs={{0,16},{2,18},{4,20},{6,22},{8,24},{10,26},{12,28},{14,30},{16,0},... | collective-permute-start | bytes 786440 | tf_op jit(solution)/shard_map/ppermute | solution.py:189
  54.2 1.6 %collective-permute-start.11 = (bf16[4,2,144,128]{3,2,1,0:T(8,128)(2,1)S(1)}, bf16[4,2,144,128]{3,2,1,0:T(8,128)(2,1)S(1)}, u32[]{:S(2)}, u32[]{:S(2)}) collective-permute-start(bf16[4,2,144,128]{3,2,1,0:T(8,128)(2,1)S(1)} %collective-permute-done.7.refs_4_), channel_id=1, source_target_pairs={{0,16},{2,18},{4,20},{6,22},{8,24},{10,26},{12,28},{14,30},{16,0},... | collective-permute-start | bytes 884744 | tf_op jit(solution)/shard_map/ppermute | solution.py:189
  54.4 1.9 %collective-permute-start.12 = (bf16[4,2,144,128]{3,2,1,0:T(8,128)(2,1)S(1)}, bf16[4,2,144,128]{3,2,1,0:T(8,128)(2,1)S(1)}, u32[]{:S(2)}, u32[]{:S(2)}) collective-permute-start(bf16[4,2,144,128]{3,2,1,0:T(8,128)(2,1)S(1)} %collective-permute-done.8.refs_5_), channel_id=1, source_target_pairs={{0,16},{2,18},{4,20},{6,22},{8,24},{10,26},{12,28},{14,30},{16,0},... | collective-permute-start | bytes 884744 | tf_op jit(solution)/shard_map/ppermute | solution.py:189
  54.8 1.9 %collective-permute-start.13 = (bf16[4,2,144,128]{3,2,1,0:T(8,128)(2,1)S(1)}, bf16[4,2,144,128]{3,2,1,0:T(8,128)(2,1)S(1)}, u32[]{:S(2)}, u32[]{:S(2)}) collective-permute-start(bf16[4,2,144,128]{3,2,1,0:T(8,128)(2,1)S(1)} %collective-permute-done.9.refs_6_), channel_id=1, source_target_pairs={{0,16},{2,18},{4,20},{6,22},{8,24},{10,26},{12,28},{14,30},{16,0},... | collective-permute-start | bytes 884744 | tf_op jit(solution)/shard_map/ppermute | solution.py:189
  81.0 16.1 %copy-start.1 = (bf16[4,4,256,128]{3,2,1,0:T(8,128)(2,1)S(1)}, bf16[4,4,256,128]{3,2,1,0:T(8,128)(2,1)}, u32[]{:S(2)}) copy-start(bf16[4,4,256,128]{3,2,1,0:T(8,128)(2,1)} %get-tuple-element.9) | copy-start | bytes 3145732
  81.0 16.1 %collective-permute-start.27 = (bf16[4,4,256,128]{3,2,1,0:T(8,128)(2,1)}, bf16[4,4,256,128]{3,2,1,0:T(8,128)(2,1)}, u32[]{:S(2)}, u32[]{:S(2)}) collective-permute-start(bf16[4,4,256,128]{3,2,1,0:T(8,128)(2,1)} %get-tuple-element.10), channel_id=1, source_target_pairs={{0,16},{2,18},{4,20},{6,22},{8,24},{10,26},{12,28},{14,30},{16,0},... | collective-permute-start | bytes 3145736 | tf_op jit(solution)/shard_map/ppermute | solution.py:189
  85.4 17.3 %collective-permute-start.34 = (bf16[4,4,256,128]{3,2,1,0:T(8,128)(2,1)}, bf16[4,4,256,128]{3,2,1,0:T(8,128)(2,1)S(1)}, u32[]{:S(2)}, u32[]{:S(2)}) collective-permute-start(bf16[4,4,256,128]{3,2,1,0:T(8,128)(2,1)} %get-tuple-element.12), channel_id=1, source_target_pairs={{0,16},{2,18},{4,20},{6,22},{8,24},{10,26},{12,28},{14,30},{16,0},... | collective-permute-start | bytes 3145736 | tf_op jit(solution)/shard_map/ppermute | solution.py:189
  85.7 7.4 %collective-permute-start.24 = (bf16[32,1024]{1,0:T(8,128)(2,1)S(1)}, bf16[32,1024]{1,0:T(8,128)(2,1)S(1)}, u32[]{:S(2)}, u32[]{:S(2)}) collective-permute-start(bf16[32,1024]{1,0:T(8,128)(2,1)S(1)} %get-tuple-element.33), channel_id=1, source_target_pairs={{0,96},{2,98},{4,100},{6,102},{8,104},{10,106},{12,108},{14,110},{... | collective-permute-start | bytes 196616 | tf_op jit(solution)/shard_map/ppermute | solution.py:189
  89.7 6.4 %collective-permute-start.25 = (bf16[32,1024]{1,0:T(8,128)(2,1)S(1)}, bf16[32,1024]{1,0:T(8,128)(2,1)S(1)}, u32[]{:S(2)}, u32[]{:S(2)}) collective-permute-start(bf16[32,1024]{1,0:T(8,128)(2,1)S(1)} %get-tuple-element.32), channel_id=1, source_target_pairs={{0,64},{2,66},{4,68},{6,70},{8,72},{10,74},{12,76},{14,78},{16,80}... | collective-permute-start | bytes 196616 | tf_op jit(solution)/shard_map/ppermute | solution.py:189
  89.8 6.7 %collective-permute-start.26 = (bf16[32,1024]{1,0:T(8,128)(2,1)S(1)}, bf16[32,1024]{1,0:T(8,128)(2,1)S(1)}, u32[]{:S(2)}, u32[]{:S(2)}) collective-permute-start(bf16[32,1024]{1,0:T(8,128)(2,1)S(1)} %get-tuple-element.31), channel_id=1, source_target_pairs={{0,32},{2,34},{4,36},{6,38},{8,40},{10,42},{12,44},{14,46},{16,48}... | collective-permute-start | bytes 196616 | tf_op jit(solution)/shard_map/ppermute | solution.py:189
  98.7 4.1 %copy-start = (bf16[4,4,256,128]{3,2,1,0:T(8,128)(2,1)S(1)}, bf16[4,4,256,128]{3,2,1,0:T(8,128)(2,1)}, u32[]{:S(2)}) copy-start(bf16[4,4,256,128]{3,2,1,0:T(8,128)(2,1)} %get-tuple-element.11) | copy-start | bytes 3145732
  98.7 14.9 %collective-permute-start.28 = (bf16[4,256,128]{2,1,0:T(8,128)(2,1)S(1)}, bf16[4,256,128]{2,1,0:T(8,128)(2,1)S(1)}, u32[]{:S(2)}, u32[]{:S(2)}) collective-permute-start(bf16[4,256,128]{2,1,0:T(8,128)(2,1)S(1)} %get-tuple-element.13), channel_id=1, source_target_pairs={{0,4},{2,6},{4,8},{6,10},{8,12},{10,14},{12,0},{14,2},{16,20},{18,... | collective-permute-start | bytes 786440 | tf_op jit(solution)/shard_map/ppermute | solution.py:189
  98.8 14.8 %collective-permute-start.29 = (bf16[4,256,128]{2,1,0:T(8,128)(2,1)S(1)}, bf16[4,256,128]{2,1,0:T(8,128)(2,1)S(1)}, u32[]{:S(2)}, u32[]{:S(2)}) collective-permute-start(bf16[4,256,128]{2,1,0:T(8,128)(2,1)S(1)} %get-tuple-element.15), channel_id=1, source_target_pairs={{0,8},{2,10},{4,12},{6,14},{8,0},{10,2},{12,4},{14,6},{16,24},{18,... | collective-permute-start | bytes 786440 | tf_op jit(solution)/shard_map/ppermute | solution.py:189
  102.8 11.4 %collective-permute-start.30 = (bf16[4,256,128]{2,1,0:T(8,128)(2,1)S(1)}, bf16[4,256,128]{2,1,0:T(8,128)(2,1)S(1)}, u32[]{:S(2)}, u32[]{:S(2)}) collective-permute-start(bf16[4,256,128]{2,1,0:T(8,128)(2,1)S(1)} %get-tuple-element.14), channel_id=1, source_target_pairs={{0,12},{2,14},{4,0},{6,2},{8,4},{10,6},{12,8},{14,10},{16,28},{18,... | collective-permute-start | bytes 786440 | tf_op jit(solution)/shard_map/ppermute | solution.py:189
  103.1 13.6 %collective-permute-start.35 = (bf16[4,256,128]{2,1,0:T(8,128)(2,1)S(1)}, bf16[4,256,128]{2,1,0:T(8,128)(2,1)S(1)}, u32[]{:S(2)}, u32[]{:S(2)}) collective-permute-start(bf16[4,256,128]{2,1,0:T(8,128)(2,1)S(1)} %get-tuple-element.16), channel_id=1, source_target_pairs={{0,32},{2,34},{4,36},{6,38},{8,40},{10,42},{12,44},{14,46},{16,48}... | collective-permute-start | bytes 786440 | tf_op jit(solution)/shard_map/ppermute | solution.py:189
  103.2 15.4 %collective-permute-start.36 = (bf16[4,256,128]{2,1,0:T(8,128)(2,1)S(1)}, bf16[4,256,128]{2,1,0:T(8,128)(2,1)S(1)}, u32[]{:S(2)}, u32[]{:S(2)}) collective-permute-start(bf16[4,256,128]{2,1,0:T(8,128)(2,1)S(1)} %get-tuple-element.18), channel_id=1, source_target_pairs={{0,64},{2,66},{4,68},{6,70},{8,72},{10,74},{12,76},{14,78},{16,80}... | collective-permute-start | bytes 786440 | tf_op jit(solution)/shard_map/ppermute | solution.py:189
  113.6 7.8 %collective-permute-start.37 = (bf16[4,256,128]{2,1,0:T(8,128)(2,1)S(1)}, bf16[4,256,128]{2,1,0:T(8,128)(2,1)S(1)}, u32[]{:S(2)}, u32[]{:S(2)}) collective-permute-start(bf16[4,256,128]{2,1,0:T(8,128)(2,1)S(1)} %get-tuple-element.17), channel_id=1, source_target_pairs={{0,96},{2,98},{4,100},{6,102},{8,104},{10,106},{12,108},{14,110},{... | collective-permute-start | bytes 786440 | tf_op jit(solution)/shard_map/ppermute | solution.py:189
  114.4 7.4 %collective-permute-start.31 = (bf16[256,128]{1,0:T(8,128)(2,1)S(1)}, bf16[256,128]{1,0:T(8,128)(2,1)S(1)}, u32[]{:S(2)}, u32[]{:S(2)}) collective-permute-start(bf16[256,128]{1,0:T(8,128)(2,1)S(1)} %get-tuple-element.24), channel_id=1, source_target_pairs={{0,32},{2,34},{4,36},{6,38},{8,40},{10,42},{12,44},{14,46},{16,48}... | collective-permute-start | bytes 196616 | tf_op jit(solution)/shard_map/ppermute | solution.py:189
  115.9 9.0 %collective-permute-start.32 = (bf16[256,128]{1,0:T(8,128)(2,1)S(1)}, bf16[256,128]{1,0:T(8,128)(2,1)S(1)}, u32[]{:S(2)}, u32[]{:S(2)}) collective-permute-start(bf16[256,128]{1,0:T(8,128)(2,1)S(1)} %get-tuple-element.26), channel_id=1, source_target_pairs={{0,64},{2,66},{4,68},{6,70},{8,72},{10,74},{12,76},{14,78},{16,80}... | collective-permute-start | bytes 196616 | tf_op jit(solution)/shard_map/ppermute | solution.py:189
  116.7 8.2 %collective-permute-start.33 = (bf16[256,128]{1,0:T(8,128)(2,1)S(1)}, bf16[256,128]{1,0:T(8,128)(2,1)S(1)}, u32[]{:S(2)}, u32[]{:S(2)}) collective-permute-start(bf16[256,128]{1,0:T(8,128)(2,1)S(1)} %get-tuple-element.25), channel_id=1, source_target_pairs={{0,96},{2,98},{4,100},{6,102},{8,104},{10,106},{12,108},{14,110},{... | collective-permute-start | bytes 196616 | tf_op jit(solution)/shard_map/ppermute | solution.py:189
  121.5 6.2 %collective-permute-start.38 = (bf16[256,128]{1,0:T(8,128)(2,1)S(1)}, bf16[256,128]{1,0:T(8,128)(2,1)S(1)}, u32[]{:S(2)}, u32[]{:S(2)}) collective-permute-start(bf16[256,128]{1,0:T(8,128)(2,1)S(1)} %get-tuple-element.27), channel_id=1, source_target_pairs={{0,4},{2,6},{4,8},{6,10},{8,12},{10,14},{12,0},{14,2},{16,20},{18,... | collective-permute-start | bytes 196616 | tf_op jit(solution)/shard_map/ppermute | solution.py:189
  121.6 6.2 %collective-permute-start.39 = (bf16[256,128]{1,0:T(8,128)(2,1)S(1)}, bf16[256,128]{1,0:T(8,128)(2,1)S(1)}, u32[]{:S(2)}, u32[]{:S(2)}) collective-permute-start(bf16[256,128]{1,0:T(8,128)(2,1)S(1)} %get-tuple-element.29), channel_id=1, source_target_pairs={{0,8},{2,10},{4,12},{6,14},{8,0},{10,2},{12,4},{14,6},{16,24},{18,... | collective-permute-start | bytes 196616 | tf_op jit(solution)/shard_map/ppermute | solution.py:189
  121.7 6.9 %collective-permute-start.40 = (bf16[256,128]{1,0:T(8,128)(2,1)S(1)}, bf16[256,128]{1,0:T(8,128)(2,1)S(1)}, u32[]{:S(2)}, u32[]{:S(2)}) collective-permute-start(bf16[256,128]{1,0:T(8,128)(2,1)S(1)} %get-tuple-element.28), channel_id=1, source_target_pairs={{0,12},{2,14},{4,0},{6,2},{8,4},{10,6},{12,8},{14,10},{16,28},{18,... | collective-permute-start | bytes 196616 | tf_op jit(solution)/shard_map/ppermute | solution.py:189
  128.7 4.3 %collective-permute-start.41 = (bf16[128,256]{1,0:T(8,128)(2,1)S(1)}, bf16[128,256]{1,0:T(8,128)(2,1)S(1)}, u32[]{:S(2)}, u32[]{:S(2)}) collective-permute-start(bf16[128,256]{1,0:T(8,128)(2,1)S(1)} %broadcast_select_fusion), channel_id=1, source_target_pairs={{0,2},{2,0},{4,6},{6,4},{8,10},{10,8},{12,14},{14,12},{16,18},{18,... | collective-permute-start | bytes 196616 | tf_op jit(solution)/shard_map/ppermute | solution.py:189

commit v2 on v1

v2 whole, which is shorter than its diff:
```python
import math

import jax
import jax.numpy as jnp
from jax import lax
from jax.experimental import pallas as pl
from jax.experimental.pallas import tpu as pltpu
from jax.sharding import PartitionSpec as P

NEG = -1e30
HEAD = 128
BLOCK = 128
DOC_ROWS = 16
CHUNK_BLOCKS = 4
CHUNK = CHUNK_BLOCKS * BLOCK
LONGEST = 40
SCALE = float(HEAD) ** (-0.5)
TO_EXP2 = SCALE * math.log2(math.e)
CONTEXT = ("inner", "outer")


def dot(lhs, rhs, over):
    return lax.dot_general(lhs, rhs, ((over[:1], over[1:]), ((), ())), preferred_element_type=jnp.float32)


def attention_grads(sizes, *refs):
    nz, nx = sizes
    lines = nz
    place_ref, q_ref, g_ref = refs[:3]
    pieces = (refs[3 : 3 + lines], refs[3 + lines : 3 + 2 * lines])
    dq_ref, keep_ref, send_ref = refs[3 + 2 * lines : 6 + 2 * lines]
    q_rows, g_rows, kv_all, scores, dprobs, totals, sem = refs[6 + 2 * lines :]
    blocks = kv_all.shape[1]
    tiles, part, width = q_ref.shape
    heads = width // HEAD
    rows = heads * part
    z, x, y, core = (place_ref[i] for i in range(4))
    k_all = kv_all.at[0]
    v_all = kv_all.at[1]
    dk_total = totals.at[0]
    dv_total = totals.at[1]

    def block_of(dz, dx, c):
        return (lax.rem(z + dz, nz) * 2 + c) * (2 * nx) + lax.rem(x + dx, nx) * 2

    def ordered(which, i, j):
        return jnp.where(which == 0, j, i), jnp.where(which == 0, i, j)

    copies = []
    for which, arrived in ((core, pieces[0]), (1 - core, pieces[1])):
        for i in range(lines):
            for j in range(lines):
                dz, dx = ordered(which, lines - i, lines - j)
                for c in range(2):
                    to = kv_all.at[which, pl.ds(block_of(dz, dx, c), 2)]
                    copies.append(pltpu.make_async_copy(arrived[i].at[j, c], to, sem.at[len(copies)]))
    for copy in copies:
        copy.start()
    totals[...] = jnp.zeros_like(totals)
    row_token = z * part + lax.rem(lax.broadcasted_iota(jnp.int32, (CHUNK, rows), 1), part)
    key_token = lax.broadcasted_iota(jnp.int32, (CHUNK, rows), 0)
    for copy in copies:
        copy.wait()

    def fold(value, combine):
        return combine(value.reshape(CHUNK // 8, 8, rows), axis=0)

    def tile(j, carry):
        block = (lax.rem(z + nz - j, nz) * 2 + core) * (2 * nx) + x * 2 + y
        docs = k_all[:, BLOCK:, :].astype(jnp.float32)
        mine = k_all[pl.ds(block, 1), BLOCK:, :].astype(jnp.float32)
        before = jnp.sum(jnp.where(docs < mine, 1.0, 0.0), axis=0)
        first = jnp.max(before).astype(jnp.int32)
        for h in range(heads):
            q_rows[h * part : (h + 1) * part, :] = q_ref[j, :, h * HEAD : (h + 1) * HEAD]
            g_rows[h * part : (h + 1) * part, :] = g_ref[j, :, h * HEAD : (h + 1) * HEAD]
        q = q_rows[...]
        g = g_rows[...]
        chunks = lax.div(block - first + CHUNK_BLOCKS, CHUNK_BLOCKS)

        def keys_at(t):
            return jnp.minimum(first + t * CHUNK_BLOCKS, blocks - CHUNK_BLOCKS)

        def key_rows(t):
            return k_all[pl.ds(keys_at(t), CHUNK_BLOCKS), :BLOCK, :].reshape(CHUNK, HEAD)

        def slot(t):
            return pl.ds(pl.multiple_of(t * CHUNK, CHUNK), CHUNK)

        def full_scores(t, top):
            s = dot(key_rows(t), q, (1, 1))
            scores[slot(t), :] = s
            return jnp.maximum(top, fold(s, jnp.max))

        last = chunks - 1
        top = lax.fori_loop(0, last, full_scores, jnp.full((8, rows), NEG, jnp.float32))
        begin = keys_at(last)
        skipped = (first + last * CHUNK_BLOCKS - begin) * BLOCK
        mask = (key_token <= row_token + (block - begin) * BLOCK) & (key_token >= skipped)
        s = jnp.where(mask, dot(key_rows(last), q, (1, 1)), NEG)
        scores[slot(last), :] = s
        top = jnp.max(jnp.maximum(top, fold(s, jnp.max)), axis=0, keepdims=True) * TO_EXP2

        def sums(t, state):
            norm, weighted = state
            e = jnp.exp2(scores[slot(t), :] * TO_EXP2 - top)
            scores[slot(t), :] = e
            value_rows = v_all[pl.ds(keys_at(t), CHUNK_BLOCKS), :BLOCK, :].reshape(CHUNK, HEAD)
            dp = dot(value_rows, g, (1, 1))
            dprobs[slot(t), :] = dp
            return norm + fold(e, jnp.sum), weighted + fold(e * dp, jnp.sum)

        zeros = jnp.zeros((8, rows), jnp.float32)
        norm, weighted = lax.fori_loop(0, chunks, sums, (zeros, zeros))
        inverse = 1.0 / jnp.sum(norm, axis=0, keepdims=True)
        delta = jnp.sum(weighted, axis=0, keepdims=True) * inverse

        def grads(t, dq):
            keys = pl.ds(pl.multiple_of(keys_at(t) * BLOCK, BLOCK), CHUNK)
            p = scores[slot(t), :] * inverse
            ds = p * (dprobs[slot(t), :] - delta)
            p_low = p.astype(jnp.bfloat16)
            ds_low = ds.astype(jnp.bfloat16)
            dk_total[keys, :] += dot(ds_low, q, (1, 0))
            dv_total[keys, :] += dot(p_low, g, (1, 0))
            return dq + dot(key_rows(t), ds_low, (0, 0))

        dq = lax.fori_loop(0, chunks, grads, jnp.zeros((HEAD, rows), jnp.float32))
        dq = (dq * SCALE).T.astype(jnp.bfloat16)
        for h in range(heads):
            dq_ref[j, :, h * HEAD : (h + 1) * HEAD] = dq[h * part : (h + 1) * part, :]
        return carry

    lax.fori_loop(0, tiles, tile, 0)
    for which, out in ((core, keep_ref), (1 - core, send_ref)):
        for i in range(lines):
            for j in range(lines):
                dz, dx = ordered(which, i, j)
                for c in range(2):
                    begin = pl.multiple_of(block_of(dz, dx, c) * BLOCK, BLOCK)
                    out[i, j, c] = totals[which, pl.ds(begin, 2 * BLOCK), :].astype(jnp.bfloat16)


def grads_call(sizes, place, q, g, mine, theirs):
    part, width = q.shape[1:]
    rows = part * width // HEAD
    nz, nx = sizes
    blocks = nx * nz * 4
    pieces = [*mine, *theirs]
    whole = pl.BlockSpec(memory_space=pltpu.VMEM)
    sums_shape = jax.ShapeDtypeStruct((nz, nx, 2, 2 * BLOCK, HEAD), jnp.bfloat16)
    return pl.pallas_call(
        lambda *refs: attention_grads(sizes, *refs),
        name="attention_grads",
        out_shape=(jax.ShapeDtypeStruct(q.shape, jnp.bfloat16), sums_shape, sums_shape),
        in_specs=[pl.BlockSpec(memory_space=pltpu.SMEM), whole, whole]
        + [pl.BlockSpec(memory_space=pl.ANY)] * len(pieces),
        out_specs=(whole,) * 3,
        scratch_shapes=[
            pltpu.VMEM((rows, HEAD), jnp.bfloat16),
            pltpu.VMEM((rows, HEAD), jnp.bfloat16),
            pltpu.VMEM((2, blocks, BLOCK + DOC_ROWS, HEAD), jnp.bfloat16),
            pltpu.VMEM((LONGEST * BLOCK, rows), jnp.float32),
            pltpu.VMEM((LONGEST * BLOCK, rows), jnp.float32),
            pltpu.VMEM((2, blocks * BLOCK, HEAD), jnp.float32),
            pltpu.SemaphoreType.DMA((blocks,)),
        ],
        compiler_params=pltpu.CompilerParams(vmem_limit_bytes=48 * 1024 * 1024),
        cost_estimate=pl.CostEstimate(
            flops=10 * 20 * 1024 * 128 * 128, bytes_accessed=16 * 1024 * 1024, transcendentals=0
        ),
    )(place, q, g, *pieces)


def low(value):
    return value.astype(jnp.bfloat16)


def added(terms):
    total = terms[0].astype(jnp.float32)
    for term in terms[1:]:
        total = total + term.astype(jnp.float32)
    return total


def per_device(queries, keys, values, grad_out, block_docs):
    rows, width = queries.shape
    inner_size, outer_size = lax.axis_size("inner"), lax.axis_size("outer")
    nz, nx = inner_size // 2, outer_size // 2
    inner, outer = lax.axis_index("inner"), lax.axis_index("outer")
    z, core = lax.div(inner, 2), lax.rem(inner, 2)
    x, y = lax.div(outer, 2), lax.rem(outer, 2)
    part = rows // nz
    lines = nz

    def moved(value, step):
        hops = []
        for source in range(inner_size * outer_size):
            i, o = divmod(source, outer_size)
            dz, dx, dy, dc = step(i % 2)
            to_inner = (i // 2 + dz) % nz * 2 + (i % 2 + dc) % 2
            to_outer = (o // 2 + dx) % nx * 2 + (o % 2 + dy) % 2
            hops.append((source, to_inner * outer_size + to_outer))
        return lax.ppermute(value, CONTEXT, hops)

    def other_core(value):
        return moved(value, lambda c: (0, 0, 0, 1))

    def other_y(value):
        return moved(value, lambda c: (0, 0, 1, 0))

    def along_z(value, by):
        return moved(value, lambda c: (by, 0, 0, 0))

    def along_first(value, by):
        return moved(value, lambda c: (0, by, 0, 0) if c else (by, 0, 0, 0))

    def along_second(value, by):
        return moved(value, lambda c: (by, 0, 0, 0) if c else (0, by, 0, 0))

    def in_order(index, mine, theirs, axis):
        return jnp.where(
            index == 0, jnp.stack([mine, theirs], axis=axis), jnp.stack([theirs, mine], axis=axis)
        )

    docs = jnp.broadcast_to(low(block_docs)[:, None], (DOC_ROWS, HEAD))
    k_rows, v_rows = jnp.concatenate([keys, docs]), jnp.concatenate([values, docs])
    kept = jnp.where(core == 0, k_rows, v_rows)
    given = jnp.where(core == 0, v_rows, k_rows)
    unit = in_order(core, kept, other_core(given), 0)
    unit = in_order(y, unit, other_y(unit), 1)
    line = jnp.stack([unit] + [along_first(unit, by) for by in range(1, lines)])
    mine = [line] + [along_second(line, by) for by in range(1, lines)]
    theirs = [other_core(piece) for piece in mine]

    both = jnp.concatenate([queries, grad_out], axis=1)

    def piece_for(peer):
        return lax.dynamic_slice_in_dim(both, lax.rem(peer, nz) * part, part, 0)

    pieces = [piece_for(z)] + [along_z(piece_for(z + by), by) for by in range(1, nz)]
    q = jnp.stack([piece[:, :width] for piece in pieces])
    g = jnp.stack([piece[:, width:] for piece in pieces])

    place = jnp.stack([z, x, y, core]).astype(jnp.int32)
    dq, keep, send = grads_call((nz, nx), place, q, g, mine, theirs)

    total = low(added([keep, other_core(send)]))
    arrived = [along_second(total[by], by) for by in range(1, lines)]
    dq, arrived[0] = lax.optimization_barrier((dq, arrived[0]))
    returned = jnp.stack([dq[0]] + [along_z(dq[by], -by) for by in range(1, nz)])
    total = low(added([total[0]] + arrived))
    total = low(added([total[0]] + [along_first(total[by], by) for by in range(1, lines)]))
    total = total.reshape(2, 2, BLOCK, HEAD)
    ours = jnp.where(y == 0, total[:, 0], total[:, 1])
    far = jnp.where(y == 0, total[:, 1], total[:, 0])
    total = added([ours, other_y(far)])
    total = low(jnp.where(core == 0, SCALE * total, total))
    mine = jnp.where(core == 0, total[0], total[1])
    theirs = other_core(jnp.where(core == 0, total[1], total[0]))
    grad_keys = jnp.where(core == 0, mine, theirs)
    grad_values = jnp.where(core == 0, theirs, mine)

    order = lax.rem(jnp.arange(nz) - z + nz, nz)
    grad_queries = jnp.take(returned, order, axis=0).reshape(rows, width)
    return grad_queries, grad_keys, grad_values


def solution(mesh):
    wide = P(CONTEXT, "head")
    return jax.shard_map(
        per_device,
        mesh=mesh,
        in_specs=(wide, wide, wide, wide, P(CONTEXT)),
        out_specs=(wide, wide, wide),
        check_vma=False,
    )
```

time: 135 us -> 118 us (0.87)
  the two profiles are of different devices: /device:TPU:0 before, /device:TPU:1 now
where the time goes in v2:
time: 118 us; the launch traced here: 117 us
  waiting for transfers between devices  42.2 us (36%)
  starting transfers between devices  40.7 us (34%)
  Pallas kernels  23.4 us (20%)
  other arithmetic  6.32 us (5%)
  local copies, waits for them, and re-layouts  2.75 us (2%)
  between operations  1.62 us (1%)
    ppermute x27, waiting for transfers between devices, moved(): return lax.ppermute(value, CONTEXT, hops)  42.2 us
    ppermute x27, starting transfers between devices, moved(): return lax.ppermute(value, CONTEXT, hops)  40.7 us
    pallas_call x1, Pallas kernels, grads_call(): pl.pallas_call(lambda *refs: attention_grads(sizes, *refs), name='attenti...  23.4 us
    convert_element_type x4, other arithmetic, low(): return value.astype(jnp.bfloat16)  3.76 us
  transfers between devices with their start and end apart: 27, of which 15 were waited for; matrix products, arithmetic and copies ran while one was open for 2% of the time, Pallas kernels for 0%

profile of v2, /device:TPU:1, one launch (start us, length us, event | category | flops | bytes accessed | tf_op | source)
XLA Modules:
  0.0 117.0 jit_solution(1923349275485840498)
XLA Ops:
  1.4 0.8 fusion.8
  2.2 1.5 %collective-permute-start.3 = (bf16[144,128]{1,0:T(8,128)(2,1)S(1)}, bf16[144,128]{1,0:T(8,128)(2,1)S(1)}, u32[]{:S(2)}, u32[]{:S(2)}) collective-permute-start(bf16[144,128]{1,0:T(8,128)(2,1)S(1)} %get-tuple-element.38), channel_id=1, source_target_pairs={{0,16},{2,18},{4,20},{6,22},{8,24},{10,26},{12,28},{14,30},{16,0},... | collective-permute-start | bytes 110600 | tf_op jit(solution)/shard_map/ppermute | solution.py:204
  3.7 0.9 collective-permute-done.3
  4.5 1.5 %collective-permute-start.4 = (bf16[2,144,128]{2,1,0:T(8,128)(2,1)S(1)}, bf16[2,144,128]{2,1,0:T(8,128)(2,1)S(1)}, u32[]{:S(2)}, u32[]{:S(2)}) collective-permute-start(bf16[2,144,128]{2,1,0:T(8,128)(2,1)S(1)} %maximum_select_fusion.3), channel_id=1, source_target_pairs={{0,2},{2,0},{4,6},{6,4},{8,10},{10,8},{12,14},{14,12},{16,18},{18,... | collective-permute-start | bytes 221192 | tf_op jit(solution)/shard_map/ppermute | solution.py:204
  6.0 1.8 %collective-permute-done.4 = bf16[2,144,128]{2,1,0:T(8,128)(2,1)S(1)} collective-permute-done((bf16[2,144,128]{2,1,0:T(8,128)(2,1)S(1)}, bf16[2,144,128]{2,1,0:T(8,128)(2,1)S(1)}, u32[]{:S(2)}, u32[]{:S(2)}) %collective-permute-start.4) | collective-permute-done | bytes 73760 | tf_op jit(solution)/shard_map/ppermute | solution.py:204
  7.8 1.4 %collective-permute-start.5 = (bf16[2,2,144,128]{3,2,1,0:T(8,128)(2,1)S(1)}, bf16[2,2,144,128]{3,2,1,0:T(8,128)(2,1)S(1)}, u32[]{:S(2)}, u32[]{:S(2)}) collective-permute-start(bf16[2,2,144,128]{3,2,1,0:T(8,128)(2,1)S(1)} %maximum_select_fusion.1), channel_id=1, source_target_pairs={{0,32},{2,34},{4,36},{6,38},{8,40},{10,42},{12,44},{14,46},{16,20}... | collective-permute-start | bytes 442376 | tf_op jit(solution)/shard_map/ppermute | solution.py:204
  9.2 2.5 %collective-permute-start.6 = (bf16[2,2,144,128]{3,2,1,0:T(8,128)(2,1)S(1)}, bf16[2,2,144,128]{3,2,1,0:T(8,128)(2,1)S(1)}, u32[]{:S(2)}, u32[]{:S(2)}) collective-permute-start(bf16[2,2,144,128]{3,2,1,0:T(8,128)(2,1)S(1)} %maximum_select_fusion.1), channel_id=1, source_target_pairs={{0,64},{2,66},{4,68},{6,70},{8,72},{10,74},{12,76},{14,78},{16,24}... | collective-permute-start | bytes 442376 | tf_op jit(solution)/shard_map/ppermute | solution.py:204
  11.7 1.2 collective-permute-start.7
  12.8 0.3 collective-permute-done.5
  13.1 2.6 %collective-permute-done.6 = bf16[2,2,144,128]{3,2,1,0:T(8,128)(2,1)S(1)} collective-permute-done((bf16[2,2,144,128]{3,2,1,0:T(8,128)(2,1)S(1)}, bf16[2,2,144,128]{3,2,1,0:T(8,128)(2,1)S(1)}, u32[]{:S(2)}, u32[]{:S(2)}) %collective-permute-start.6) | collective-permute-done | bytes 147488 | tf_op jit(solution)/shard_map/ppermute | solution.py:204
  15.8 0.2 collective-permute-done.7
  16.0 1.7 %collective-permute-start.8 = (bf16[4,2,2,144,128]{4,3,2,1,0:T(8,128)(2,1)S(1)}, bf16[4,2,2,144,128]{4,3,2,1,0:T(8,128)(2,1)S(1)}, u32[]{:S(2)}, u32[]{:S(2)}) collective-permute-start(bf16[4,2,2,144,128]{4,3,2,1,0:T(8,128)(2,1)S(1)} %pad_maximum_fusion.refs_3_), channel_id=1, source_target_pairs={{0,4},{2,6},{4,8},{6,10},{8,12},{10,14},{12,0},{14,2},{16,48},{18,... | collective-permute-start | bytes 1769480 | tf_op jit(solution)/shard_map/ppermute | solution.py:204
  17.7 3.2 %collective-permute-start.9 = (bf16[4,2,2,144,128]{4,3,2,1,0:T(8,128)(2,1)S(1)}, bf16[4,2,2,144,128]{4,3,2,1,0:T(8,128)(2,1)S(1)}, u32[]{:S(2)}, u32[]{:S(2)}) collective-permute-start(bf16[4,2,2,144,128]{4,3,2,1,0:T(8,128)(2,1)S(1)} %pad_maximum_fusion.refs_3_), channel_id=1, source_target_pairs={{0,8},{2,10},{4,12},{6,14},{8,0},{10,2},{12,4},{14,6},{16,80},{18,... | collective-permute-start | bytes 1769480 | tf_op jit(solution)/shard_map/ppermute | solution.py:204
  20.9 0.8 collective-permute-start.10
  21.9 0.7 constant_dynamic-slice_fusion.2
  22.5 0.6 collective-permute-start
  23.2 0.6 collective-permute-start.1
  23.8 11.3 %collective-permute-done = bf16[32,2048]{1,0:T(8,128)(2,1)S(1)} collective-permute-done((bf16[32,2048]{1,0:T(8,128)(2,1)S(1)}, bf16[32,2048]{1,0:T(8,128)(2,1)S(1)}, u32[]{:S(2)}, u32[]{:S(2)}) %collective-permute-start) | collective-permute-done | bytes 131104 | tf_op jit(solution)/shard_map/ppermute | solution.py:204
  35.1 3.1 %collective-permute-start.11 = (bf16[4,2,2,144,128]{4,3,2,1,0:T(8,128)(2,1)S(1)}, bf16[4,2,2,144,128]{4,3,2,1,0:T(8,128)(2,1)S(1)}, u32[]{:S(2)}, u32[]{:S(2)}) collective-permute-start(bf16[4,2,2,144,128]{4,3,2,1,0:T(8,128)(2,1)S(1)} %pad_maximum_fusion.refs_3_), channel_id=1, source_target_pairs={{0,16},{2,18},{4,20},{6,22},{8,24},{10,26},{12,28},{14,30},{16,0},... | collective-permute-start | bytes 1769480 | tf_op jit(solution)/shard_map/ppermute | solution.py:204
  38.2 0.5 collective-permute-start.13
  38.8 1.3 %collective-permute-done.1 = bf16[32,2048]{1,0:T(8,128)(2,1)S(1)} collective-permute-done((bf16[32,2048]{1,0:T(8,128)(2,1)}, bf16[32,2048]{1,0:T(8,128)(2,1)S(1)}, u32[]{:S(2)}, u32[]{:S(2)}) %collective-permute-start.1) | collective-permute-done | bytes 131104 | tf_op jit(solution)/shard_map/ppermute | solution.py:204
  40.2 0.5 collective-permute-start.2
  40.7 4.3 %collective-permute-done.2 = bf16[32,2048]{1,0:T(8,128)(2,1)S(1)} collective-permute-done((bf16[32,2048]{1,0:T(8,128)(2,1)S(1)}, bf16[32,2048]{1,0:T(8,128)(2,1)S(1)}, u32[]{:S(2)}, u32[]{:S(2)}) %collective-permute-start.2) | collective-permute-done | bytes 131104 | tf_op jit(solution)/shard_map/ppermute | solution.py:204
  45.2 23.4 %attention_grads.1 = (bf16[4,32,1024]{2,1,0:T(8,128)(2,1)S(1)}, bf16[4,4,2,256,128]{4,3,2,1,0:T(8,128)(2,1)}, bf16[4,4,2,256,128]{4,3,2,1,0:T(8,128)(2,1)}) custom-call(s32[4]{0:T(128)S(1)} %pad_add_fusion.refs_0_, bf16[4,32,1024]{2,1,0:T(8,128)(2,1)S(1)} %get-tuple-element.39.refs_1_, bf16[4,32,1024]{2,1,0:T(8,128)(2,1)S(1)} %get-tuple-element.40.refs_2_, ...), custom_call_target="tpu_custom_call" | custom-call | flops 3355443200 | bytes 16777216 | tf_op jit(solution)/shard_map/attention_grads/pallas_call | solution.py:152
  68.6 3.8 %collective-permute-start.15 = (bf16[4,4,2,256,128]{4,3,2,1,0:T(8,128)(2,1)}, bf16[4,4,2,256,128]{4,3,2,1,0:T(8,128)(2,1)S(1)}, u32[]{:S(2)}, u32[]{:S(2)}) collective-permute-start(bf16[4,4,2,256,128]{4,3,2,1,0:T(8,128)(2,1)} %get-tuple-element.10), channel_id=1, source_target_pairs={{0,16},{2,18},{4,20},{6,22},{8,24},{10,26},{12,28},{14,30},{16,0},... | collective-permute-start | bytes 6291464 | tf_op jit(solution)/shard_map/ppermute | solution.py:204
  72.5 4.0 %collective-permute-done.15 = bf16[4,4,2,256,128]{4,3,2,1,0:T(8,128)(2,1)S(1)} collective-permute-done((bf16[4,4,2,256,128]{4,3,2,1,0:T(8,128)(2,1)}, bf16[4,4,2,256,128]{4,3,2,1,0:T(8,128)(2,1)S(1)}, u32[]{:S(2)}, u32[]{:S(2)}) %collective-permute-start.15) | collective-permute-done | bytes 2097184 | tf_op jit(solution)/shard_map/ppermute | solution.py:204
  76.5 2.3 %add_convert_fusion = bf16[4,4,2,256,128]{4,3,2,1,0:T(8,128)(2,1)S(1)} fusion(bf16[4,4,2,256,128]{4,3,2,1,0:T(8,128)(2,1)S(1)} %collective-permute-done.15, bf16[4,4,2,256,128]{4,3,2,1,0:T(8,128)(2,1)} %get-tuple-element.9), kind=kLoop, calls=%fused_computation.1 | loop fusion | flops 4194304 | bytes 6291456 | tf_op jit(solution)/shard_map/convert_element_type | solution.py:176
  78.8 1.2 %slice_bitcast_fusion.1 = (bf16[4,2,256,128]{3,2,1,0:T(8,128)(2,1)}, bf16[4,2,256,128]{3,2,1,0:T(8,128)(2,1)}, bf16[4,2,256,128]{3,2,1,0:T(8,128)(2,1)}) fusion(bf16[4,4,2,256,128]{4,3,2,1,0:T(8,128)(2,1)S(1)} %add_convert_fusion), kind=kLoop, calls=%fused_computation.8 | loop fusion | bytes 3145728 | tf_op jit(solution)/shard_map/squeeze | solution.py:249
  80.0 0.1 collective-permute-start.16
  80.1 3.4 %collective-permute-start.20 = (bf16[4,2,256,128]{3,2,1,0:T(8,128)(2,1)}, bf16[4,2,256,128]{3,2,1,0:T(8,128)(2,1)S(1)}, u32[]{:S(2)}, u32[]{:S(2)}) collective-permute-start(bf16[4,2,256,128]{3,2,1,0:T(8,128)(2,1)} %get-tuple-element.13), channel_id=1, source_target_pairs={{0,8},{2,10},{4,12},{6,14},{8,0},{10,2},{12,4},{14,6},{16,80},{18,... | collective-permute-start | bytes 1572872 | tf_op jit(solution)/shard_map/ppermute | solution.py:204
  83.5 0.5 collective-permute-start.21
  84.1 0.1 broadcast_in_dim.21
  84.2 5.5 %collective-permute-done.16 = bf16[4,2,256,128]{3,2,1,0:T(8,128)(2,1)S(1)} collective-permute-done((bf16[4,2,256,128]{3,2,1,0:T(8,128)(2,1)}, bf16[4,2,256,128]{3,2,1,0:T(8,128)(2,1)S(1)}, u32[]{:S(2)}, u32[]{:S(2)}) %collective-permute-start.16) | collective-permute-done | bytes 524320 | tf_op jit(solution)/shard_map/ppermute | solution.py:204
  89.7 6.5 %collective-permute-done.20 = bf16[4,2,256,128]{3,2,1,0:T(8,128)(2,1)S(1)} collective-permute-done((bf16[4,2,256,128]{3,2,1,0:T(8,128)(2,1)}, bf16[4,2,256,128]{3,2,1,0:T(8,128)(2,1)S(1)}, u32[]{:S(2)}, u32[]{:S(2)}) %collective-permute-start.20) | collective-permute-done | bytes 524320 | tf_op jit(solution)/shard_map/ppermute | solution.py:204
  96.2 1.3 %fusion.2 = bf16[4,2,256,128]{3,2,1,0:T(8,128)(2,1)S(1)} fusion(bf16[4,2,256,128]{3,2,1,0:T(8,128)(2,1)} %collective-permute-done.21, bf16[4,2,256,128]{3,2,1,0:T(8,128)(2,1)S(1)} %collective-permute-done.20, bf16[4,2,256,128]{3,2,1,0:T(8,128)(2,1)S(1)} %collective-permute-done.16, bf16[4,4,2,256,128]{4,3,2,1,0:T(8,128)(2,1)S(1)} %add_convert_fusion), kind=kLoop, calls=%fused_computation.5 | loop fusion | flops 2097152 | bytes 2621440 | tf_op jit(solution)/shard_map/convert_element_type | solution.py:176
  97.6 3.9 %collective-permute-start.22 = (bf16[2,256,128]{2,1,0:T(8,128)(2,1)S(1)}, bf16[2,256,128]{2,1,0:T(8,128)(2,1)S(1)}, u32[]{:S(2)}, u32[]{:S(2)}) collective-permute-start(bf16[2,256,128]{2,1,0:T(8,128)(2,1)S(1)} %get-tuple-element.16), channel_id=1, source_target_pairs={{0,32},{2,34},{4,36},{6,38},{8,40},{10,42},{12,44},{14,46},{16,20}... | collective-permute-start | bytes 393224 | tf_op jit(solution)/shard_map/ppermute | solution.py:204
  101.5 1.2 collective-permute-start.23
  102.6 2.0 %collective-permute-start.24 = (bf16[2,256,128]{2,1,0:T(8,128)(2,1)S(1)}, bf16[2,256,128]{2,1,0:T(8,128)(2,1)S(1)}, u32[]{:S(2)}, u32[]{:S(2)}) collective-permute-start(bf16[2,256,128]{2,1,0:T(8,128)(2,1)S(1)} %get-tuple-element.17), channel_id=1, source_target_pairs={{0,96},{2,98},{4,100},{6,102},{8,104},{10,106},{12,108},{14,110},{... | collective-permute-start | bytes 393224 | tf_op jit(solution)/shard_map/ppermute | solution.py:204
  104.6 2.1 %collective-permute-start.17 = (bf16[32,1024]{1,0:T(8,128)(2,1)S(1)}, bf16[32,1024]{1,0:T(8,128)(2,1)S(1)}, u32[]{:S(2)}, u32[]{:S(2)}) collective-permute-start(bf16[32,1024]{1,0:T(8,128)(2,1)S(1)} %get-tuple-element.27), channel_id=1, source_target_pairs={{0,96},{2,98},{4,100},{6,102},{8,104},{10,106},{12,108},{14,110},{... | collective-permute-start | bytes 196616 | tf_op jit(solution)/shard_map/ppermute | solution.py:204
  106.8 0.8 collective-permute-start.18
  107.7 1.0 collective-permute-start.25
  108.8 0.6 collective-permute-done.17
  109.4 2.0 %collective-permute-done.18 = bf16[32,1024]{1,0:T(8,128)(2,1)S(1)} collective-permute-done((bf16[32,1024]{1,0:T(8,128)(2,1)S(1)}, bf16[32,1024]{1,0:T(8,128)(2,1)S(1)}, u32[]{:S(2)}, u32[]{:S(2)}) %collective-permute-start.18) | collective-permute-done | bytes 65568 | tf_op jit(solution)/shard_map/ppermute | solution.py:204
  111.4 0.7 collective-permute-done.19
  112.1 0.6 gather_fusion
  112.8 2.7 %collective-permute-start.26 = (bf16[128,128]{1,0:T(8,128)(2,1)S(1)}, bf16[128,128]{1,0:T(8,128)(2,1)S(1)}, u32[]{:S(2)}, u32[]{:S(2)}) collective-permute-start(bf16[128,128]{1,0:T(8,128)(2,1)S(1)} %select_bitcast_fusion.1), channel_id=1, source_target_pairs={{0,16},{2,18},{4,20},{6,22},{8,24},{10,26},{12,28},{14,30},{16,0},... | collective-permute-start | bytes 98312 | tf_op jit(solution)/shard_map/ppermute | solution.py:204
  115.5 0.8 bitcast_select_fusion
  116.4 0.6 bitcast_select_fusion.1
  (44 shorter events, 0.8 us)
Async XLA Ops:
  0.6 21.1 %copy-start = (bf16[128,1024]{1,0:T(8,128)(2,1)S(1)}, bf16[128,1024]{1,0:T(8,128)(2,1)}, u32[]{:S(2)}) copy-start(bf16[128,1024]{1,0:T(8,128)(2,1)} %param.5) | copy-start | bytes 786436
  0.6 21.2 %copy-start.1 = (bf16[128,1024]{1,0:T(8,128)(2,1)S(1)}, bf16[128,1024]{1,0:T(8,128)(2,1)}, u32[]{:S(2)}) copy-start(bf16[128,1024]{1,0:T(8,128)(2,1)} %param.8) | copy-start | bytes 786436
  2.2 2.4 %collective-permute-start.3 = (bf16[144,128]{1,0:T(8,128)(2,1)S(1)}, bf16[144,128]{1,0:T(8,128)(2,1)S(1)}, u32[]{:S(2)}, u32[]{:S(2)}) collective-permute-start(bf16[144,128]{1,0:T(8,128)(2,1)S(1)} %get-tuple-element.38), channel_id=1, source_target_pairs={{0,16},{2,18},{4,20},{6,22},{8,24},{10,26},{12,28},{14,30},{16,0},... | collective-permute-start | bytes 110600 | tf_op jit(solution)/shard_map/ppermute | solution.py:204
  4.5 3.3 %collective-permute-start.4 = (bf16[2,144,128]{2,1,0:T(8,128)(2,1)S(1)}, bf16[2,144,128]{2,1,0:T(8,128)(2,1)S(1)}, u32[]{:S(2)}, u32[]{:S(2)}) collective-permute-start(bf16[2,144,128]{2,1,0:T(8,128)(2,1)S(1)} %maximum_select_fusion.3), channel_id=1, source_target_pairs={{0,2},{2,0},{4,6},{6,4},{8,10},{10,8},{12,14},{14,12},{16,18},{18,... | collective-permute-start | bytes 221192 | tf_op jit(solution)/shard_map/ppermute | solution.py:204
  7.8 5.3 %collective-permute-start.5 = (bf16[2,2,144,128]{3,2,1,0:T(8,128)(2,1)S(1)}, bf16[2,2,144,128]{3,2,1,0:T(8,128)(2,1)S(1)}, u32[]{:S(2)}, u32[]{:S(2)}) collective-permute-start(bf16[2,2,144,128]{3,2,1,0:T(8,128)(2,1)S(1)} %maximum_select_fusion.1), channel_id=1, source_target_pairs={{0,32},{2,34},{4,36},{6,38},{8,40},{10,42},{12,44},{14,46},{16,20}... | collective-permute-start | bytes 442376 | tf_op jit(solution)/shard_map/ppermute | solution.py:204
  9.2 6.6 %collective-permute-start.6 = (bf16[2,2,144,128]{3,2,1,0:T(8,128)(2,1)S(1)}, bf16[2,2,144,128]{3,2,1,0:T(8,128)(2,1)S(1)}, u32[]{:S(2)}, u32[]{:S(2)}) collective-permute-start(bf16[2,2,144,128]{3,2,1,0:T(8,128)(2,1)S(1)} %maximum_select_fusion.1), channel_id=1, source_target_pairs={{0,64},{2,66},{4,68},{6,70},{8,72},{10,74},{12,76},{14,78},{16,24}... | collective-permute-start | bytes 442376 | tf_op jit(solution)/shard_map/ppermute | solution.py:204
  11.7 4.3 %collective-permute-start.7 = (bf16[2,2,144,128]{3,2,1,0:T(8,128)(2,1)S(1)}, bf16[2,2,144,128]{3,2,1,0:T(8,128)(2,1)S(1)}, u32[]{:S(2)}, u32[]{:S(2)}) collective-permute-start(bf16[2,2,144,128]{3,2,1,0:T(8,128)(2,1)S(1)} %maximum_select_fusion.1), channel_id=1, source_target_pairs={{0,96},{2,98},{4,100},{6,102},{8,104},{10,106},{12,108},{14,110},{... | collective-permute-start | bytes 442376 | tf_op jit(solution)/shard_map/ppermute | solution.py:204
  16.0 22.2 %collective-permute-start.8 = (bf16[4,2,2,144,128]{4,3,2,1,0:T(8,128)(2,1)S(1)}, bf16[4,2,2,144,128]{4,3,2,1,0:T(8,128)(2,1)S(1)}, u32[]{:S(2)}, u32[]{:S(2)}) collective-permute-start(bf16[4,2,2,144,128]{4,3,2,1,0:T(8,128)(2,1)S(1)} %pad_maximum_fusion.refs_3_), channel_id=1, source_target_pairs={{0,4},{2,6},{4,8},{6,10},{8,12},{10,14},{12,0},{14,2},{16,48},{18,... | collective-permute-start | bytes 1769480 | tf_op jit(solution)/shard_map/ppermute | solution.py:204
  17.7 20.5 %collective-permute-start.9 = (bf16[4,2,2,144,128]{4,3,2,1,0:T(8,128)(2,1)S(1)}, bf16[4,2,2,144,128]{4,3,2,1,0:T(8,128)(2,1)S(1)}, u32[]{:S(2)}, u32[]{:S(2)}) collective-permute-start(bf16[4,2,2,144,128]{4,3,2,1,0:T(8,128)(2,1)S(1)} %pad_maximum_fusion.refs_3_), channel_id=1, source_target_pairs={{0,8},{2,10},{4,12},{6,14},{8,0},{10,2},{12,4},{14,6},{16,80},{18,... | collective-permute-start | bytes 1769480 | tf_op jit(solution)/shard_map/ppermute | solution.py:204
  20.9 17.8 %collective-permute-start.10 = (bf16[4,2,2,144,128]{4,3,2,1,0:T(8,128)(2,1)S(1)}, bf16[4,2,2,144,128]{4,3,2,1,0:T(8,128)(2,1)S(1)}, u32[]{:S(2)}, u32[]{:S(2)}) collective-permute-start(bf16[4,2,2,144,128]{4,3,2,1,0:T(8,128)(2,1)S(1)} %pad_maximum_fusion.refs_3_), channel_id=1, source_target_pairs={{0,12},{2,14},{4,0},{6,2},{8,4},{10,6},{12,8},{14,10},{16,112},{18... | collective-permute-start | bytes 1769480 | tf_op jit(solution)/shard_map/ppermute | solution.py:204
  22.5 12.6 %collective-permute-start = (bf16[32,2048]{1,0:T(8,128)(2,1)S(1)}, bf16[32,2048]{1,0:T(8,128)(2,1)S(1)}, u32[]{:S(2)}, u32[]{:S(2)}) collective-permute-start(bf16[32,2048]{1,0:T(8,128)(2,1)S(1)} %get-tuple-element.21), channel_id=1, source_target_pairs={{0,32},{2,34},{4,36},{6,38},{8,40},{10,42},{12,44},{14,46},{16,48}... | collective-permute-start | bytes 393224 | tf_op jit(solution)/shard_map/ppermute | solution.py:204
  23.2 17.0 %collective-permute-start.1 = (bf16[32,2048]{1,0:T(8,128)(2,1)}, bf16[32,2048]{1,0:T(8,128)(2,1)S(1)}, u32[]{:S(2)}, u32[]{:S(2)}) collective-permute-start(bf16[32,2048]{1,0:T(8,128)(2,1)} %get-tuple-element.23), channel_id=1, source_target_pairs={{0,64},{2,66},{4,68},{6,70},{8,72},{10,74},{12,76},{14,78},{16,80}... | collective-permute-start | bytes 393224 | tf_op jit(solution)/shard_map/ppermute | solution.py:204
  35.1 10.0 %collective-permute-start.11 = (bf16[4,2,2,144,128]{4,3,2,1,0:T(8,128)(2,1)S(1)}, bf16[4,2,2,144,128]{4,3,2,1,0:T(8,128)(2,1)S(1)}, u32[]{:S(2)}, u32[]{:S(2)}) collective-permute-start(bf16[4,2,2,144,128]{4,3,2,1,0:T(8,128)(2,1)S(1)} %pad_maximum_fusion.refs_3_), channel_id=1, source_target_pairs={{0,16},{2,18},{4,20},{6,22},{8,24},{10,26},{12,28},{14,30},{16,0},... | collective-permute-start | bytes 1769480 | tf_op jit(solution)/shard_map/ppermute | solution.py:204
  38.2 6.9 %collective-permute-start.12 = (bf16[4,2,2,144,128]{4,3,2,1,0:T(8,128)(2,1)S(1)}, bf16[4,2,2,144,128]{4,3,2,1,0:T(8,128)(2,1)S(1)}, u32[]{:S(2)}, u32[]{:S(2)}) collective-permute-start(bf16[4,2,2,144,128]{4,3,2,1,0:T(8,128)(2,1)S(1)} %collective-permute-done.8.refs_4_), channel_id=1, source_target_pairs={{0,16},{2,18},{4,20},{6,22},{8,24},{10,26},{12,28},{14,30},{16,0},... | collective-permute-start | bytes 1769480 | tf_op jit(solution)/shard_map/ppermute | solution.py:204
  38.2 6.9 %collective-permute-start.13 = (bf16[4,2,2,144,128]{4,3,2,1,0:T(8,128)(2,1)S(1)}, bf16[4,2,2,144,128]{4,3,2,1,0:T(8,128)(2,1)S(1)}, u32[]{:S(2)}, u32[]{:S(2)}) collective-permute-start(bf16[4,2,2,144,128]{4,3,2,1,0:T(8,128)(2,1)S(1)} %collective-permute-done.9.refs_5_), channel_id=1, source_target_pairs={{0,16},{2,18},{4,20},{6,22},{8,24},{10,26},{12,28},{14,30},{16,0},... | collective-permute-start | bytes 1769480 | tf_op jit(solution)/shard_map/ppermute | solution.py:204
  38.7 6.4 %collective-permute-start.14 = (bf16[4,2,2,144,128]{4,3,2,1,0:T(8,128)(2,1)S(1)}, bf16[4,2,2,144,128]{4,3,2,1,0:T(8,128)(2,1)S(1)}, u32[]{:S(2)}, u32[]{:S(2)}) collective-permute-start(bf16[4,2,2,144,128]{4,3,2,1,0:T(8,128)(2,1)S(1)} %collective-permute-done.10.refs_6_), channel_id=1, source_target_pairs={{0,16},{2,18},{4,20},{6,22},{8,24},{10,26},{12,28},{14,30},{16,0},... | collective-permute-start | bytes 1769480 | tf_op jit(solution)/shard_map/ppermute | solution.py:204
  40.2 4.9 %collective-permute-start.2 = (bf16[32,2048]{1,0:T(8,128)(2,1)S(1)}, bf16[32,2048]{1,0:T(8,128)(2,1)S(1)}, u32[]{:S(2)}, u32[]{:S(2)}) collective-permute-start(bf16[32,2048]{1,0:T(8,128)(2,1)S(1)} %get-tuple-element.22), channel_id=1, source_target_pairs={{0,96},{2,98},{4,100},{6,102},{8,104},{10,106},{12,108},{14,110},{... | collective-permute-start | bytes 393224 | tf_op jit(solution)/shard_map/ppermute | solution.py:204
  68.6 7.8 %collective-permute-start.15 = (bf16[4,4,2,256,128]{4,3,2,1,0:T(8,128)(2,1)}, bf16[4,4,2,256,128]{4,3,2,1,0:T(8,128)(2,1)S(1)}, u32[]{:S(2)}, u32[]{:S(2)}) collective-permute-start(bf16[4,4,2,256,128]{4,3,2,1,0:T(8,128)(2,1)} %get-tuple-element.10), channel_id=1, source_target_pairs={{0,16},{2,18},{4,20},{6,22},{8,24},{10,26},{12,28},{14,30},{16,0},... | collective-permute-start | bytes 6291464 | tf_op jit(solution)/shard_map/ppermute | solution.py:204
  80.0 9.7 %collective-permute-start.16 = (bf16[4,2,256,128]{3,2,1,0:T(8,128)(2,1)}, bf16[4,2,256,128]{3,2,1,0:T(8,128)(2,1)S(1)}, u32[]{:S(2)}, u32[]{:S(2)}) collective-permute-start(bf16[4,2,256,128]{3,2,1,0:T(8,128)(2,1)} %get-tuple-element.15), channel_id=1, source_target_pairs={{0,4},{2,6},{4,8},{6,10},{8,12},{10,14},{12,0},{14,2},{16,48},{18,... | collective-permute-start | bytes 1572872 | tf_op jit(solution)/shard_map/ppermute | solution.py:204
  80.1 16.1 %collective-permute-start.20 = (bf16[4,2,256,128]{3,2,1,0:T(8,128)(2,1)}, bf16[4,2,256,128]{3,2,1,0:T(8,128)(2,1)S(1)}, u32[]{:S(2)}, u32[]{:S(2)}) collective-permute-start(bf16[4,2,256,128]{3,2,1,0:T(8,128)(2,1)} %get-tuple-element.13), channel_id=1, source_target_pairs={{0,8},{2,10},{4,12},{6,14},{8,0},{10,2},{12,4},{14,6},{16,80},{18,... | collective-permute-start | bytes 1572872 | tf_op jit(solution)/shard_map/ppermute | solution.py:204
  83.5 12.7 %collective-permute-start.21 = (bf16[4,2,256,128]{3,2,1,0:T(8,128)(2,1)}, bf16[4,2,256,128]{3,2,1,0:T(8,128)(2,1)}, u32[]{:S(2)}, u32[]{:S(2)}) collective-permute-start(bf16[4,2,256,128]{3,2,1,0:T(8,128)(2,1)} %get-tuple-element.14), channel_id=1, source_target_pairs={{0,12},{2,14},{4,0},{6,2},{8,4},{10,6},{12,8},{14,10},{16,112},{18... | collective-permute-start | bytes 1572872 | tf_op jit(solution)/shard_map/ppermute | solution.py:204
  97.6 10.0 %collective-permute-start.22 = (bf16[2,256,128]{2,1,0:T(8,128)(2,1)S(1)}, bf16[2,256,128]{2,1,0:T(8,128)(2,1)S(1)}, u32[]{:S(2)}, u32[]{:S(2)}) collective-permute-start(bf16[2,256,128]{2,1,0:T(8,128)(2,1)S(1)} %get-tuple-element.16), channel_id=1, source_target_pairs={{0,32},{2,34},{4,36},{6,38},{8,40},{10,42},{12,44},{14,46},{16,20}... | collective-permute-start | bytes 393224 | tf_op jit(solution)/shard_map/ppermute | solution.py:204
  101.5 6.1 %collective-permute-start.23 = (bf16[2,256,128]{2,1,0:T(8,128)(2,1)S(1)}, bf16[2,256,128]{2,1,0:T(8,128)(2,1)S(1)}, u32[]{:S(2)}, u32[]{:S(2)}) collective-permute-start(bf16[2,256,128]{2,1,0:T(8,128)(2,1)S(1)} %get-tuple-element.18), channel_id=1, source_target_pairs={{0,64},{2,66},{4,68},{6,70},{8,72},{10,74},{12,76},{14,78},{16,24}... | collective-permute-start | bytes 393224 | tf_op jit(solution)/shard_map/ppermute | solution.py:204
  102.6 5.0 %collective-permute-start.24 = (bf16[2,256,128]{2,1,0:T(8,128)(2,1)S(1)}, bf16[2,256,128]{2,1,0:T(8,128)(2,1)S(1)}, u32[]{:S(2)}, u32[]{:S(2)}) collective-permute-start(bf16[2,256,128]{2,1,0:T(8,128)(2,1)S(1)} %get-tuple-element.17), channel_id=1, source_target_pairs={{0,96},{2,98},{4,100},{6,102},{8,104},{10,106},{12,108},{14,110},{... | collective-permute-start | bytes 393224 | tf_op jit(solution)/shard_map/ppermute | solution.py:204
  104.6 4.7 %collective-permute-start.17 = (bf16[32,1024]{1,0:T(8,128)(2,1)S(1)}, bf16[32,1024]{1,0:T(8,128)(2,1)S(1)}, u32[]{:S(2)}, u32[]{:S(2)}) collective-permute-start(bf16[32,1024]{1,0:T(8,128)(2,1)S(1)} %get-tuple-element.27), channel_id=1, source_target_pairs={{0,96},{2,98},{4,100},{6,102},{8,104},{10,106},{12,108},{14,110},{... | collective-permute-start | bytes 196616 | tf_op jit(solution)/shard_map/ppermute | solution.py:204
  106.8 4.6 %collective-permute-start.18 = (bf16[32,1024]{1,0:T(8,128)(2,1)S(1)}, bf16[32,1024]{1,0:T(8,128)(2,1)S(1)}, u32[]{:S(2)}, u32[]{:S(2)}) collective-permute-start(bf16[32,1024]{1,0:T(8,128)(2,1)S(1)} %get-tuple-element.26), channel_id=1, source_target_pairs={{0,64},{2,66},{4,68},{6,70},{8,72},{10,74},{12,76},{14,78},{16,80}... | collective-permute-start | bytes 196616 | tf_op jit(solution)/shard_map/ppermute | solution.py:204
  107.6 4.5 %collective-permute-start.19 = (bf16[32,1024]{1,0:T(8,128)(2,1)S(1)}, bf16[32,1024]{1,0:T(8,128)(2,1)S(1)}, u32[]{:S(2)}, u32[]{:S(2)}) collective-permute-start(bf16[32,1024]{1,0:T(8,128)(2,1)S(1)} %get-tuple-element.25), channel_id=1, source_target_pairs={{0,32},{2,34},{4,36},{6,38},{8,40},{10,42},{12,44},{14,46},{16,48}... | collective-permute-start | bytes 196616 | tf_op jit(solution)/shard_map/ppermute | solution.py:204
  107.7 5.0 %collective-permute-start.25 = (bf16[2,128,128]{2,1,0:T(8,128)(2,1)S(1)}, bf16[2,128,128]{2,1,0:T(8,128)(2,1)S(1)}, u32[]{:S(2)}, u32[]{:S(2)}) collective-permute-start(bf16[2,128,128]{2,1,0:T(8,128)(2,1)S(1)} %select_bitcast_fusion), channel_id=1, source_target_pairs={{0,2},{2,0},{4,6},{6,4},{8,10},{10,8},{12,14},{14,12},{16,18},{18,... | collective-permute-start | bytes 196616 | tf_op jit(solution)/shard_map/ppermute | solution.py:204
  112.8 3.6 %collective-permute-start.26 = (bf16[128,128]{1,0:T(8,128)(2,1)S(1)}, bf16[128,128]{1,0:T(8,128)(2,1)S(1)}, u32[]{:S(2)}, u32[]{:S(2)}) collective-permute-start(bf16[128,128]{1,0:T(8,128)(2,1)S(1)} %select_bitcast_fusion.1), channel_id=1, source_target_pairs={{0,16},{2,18},{4,20},{6,22},{8,24},{10,26},{12,28},{14,30},{16,0},... | collective-permute-start | bytes 98312 | tf_op jit(solution)/shard_map/ppermute | solution.py:204

commit v3 on v2

--- a/solution.py
+++ b/solution.py
@@ -11,7 +11,7 @@
 HEAD = 128
 BLOCK = 128
 DOC_ROWS = 16
-CHUNK_BLOCKS = 4
+CHUNK_BLOCKS = 8
 CHUNK = CHUNK_BLOCKS * BLOCK
 LONGEST = 40
 SCALE = float(HEAD) ** (-0.5)
@@ -28,8 +28,10 @@
     lines = nz
     place_ref, q_ref, g_ref = refs[:3]
     pieces = (refs[3 : 3 + lines], refs[3 + lines : 3 + 2 * lines])
-    dq_ref, keep_ref, send_ref = refs[3 + 2 * lines : 6 + 2 * lines]
-    q_rows, g_rows, kv_all, scores, dprobs, totals, sem = refs[6 + 2 * lines :]
+    refs = refs[3 + 2 * lines :]
+    dq_ref = refs[0]
+    sums = (refs[1 : 1 + lines], refs[1 + lines : 1 + 2 * lines])
+    q_rows, g_rows, q_cols, g_cols, docs_all, kv_all, scores, dprobs, totals = refs[1 + 2 * lines :]
     blocks = kv_all.shape[1]
     tiles, part, width = q_ref.shape
     heads = width // HEAD
@@ -40,55 +42,62 @@
     dk_total = totals.at[0]
     dv_total = totals.at[1]
 
-    def block_of(dz, dx, c):
-        return (lax.rem(z + dz, nz) * 2 + c) * (2 * nx) + lax.rem(x + dx, nx) * 2
-
-    def ordered(which, i, j):
-        return jnp.where(which == 0, j, i), jnp.where(which == 0, i, j)
-
-    copies = []
-    for which, arrived in ((core, pieces[0]), (1 - core, pieces[1])):
-        for i in range(lines):
-            for j in range(lines):
-                dz, dx = ordered(which, lines - i, lines - j)
+    steps = range(lines)
+    z_at = [lax.rem(z + by, nz) * (4 * nx) for by in steps]
+    x_at = [lax.rem(x + by, nx) * 2 for by in steps]
+
+    def places(which):
+        return [
+            [
+                jnp.where(which == 0, x_at[i], z_at[i]) + jnp.where(which == 0, z_at[j], x_at[j])
+                for j in steps
+            ]
+            for i in steps
+        ]
+
+    spots = (places(core), places(1 - core))
+
+    for which, arrived, spot in ((core, pieces[0], spots[0]), (1 - core, pieces[1], spots[1])):
+        for i in steps:
+            for j in steps:
                 for c in range(2):
-                    to = kv_all.at[which, pl.ds(block_of(dz, dx, c), 2)]
-                    copies.append(pltpu.make_async_copy(arrived[i].at[j, c], to, sem.at[len(copies)]))
-    for copy in copies:
-        copy.start()
+                    rows_of = arrived[i][j, 2 * c * BLOCK : 2 * (c + 1) * BLOCK]
+                    kv_all[which, pl.ds(spot[-i][-j] + 2 * nx * c, 2)] = rows_of.reshape(2, BLOCK, HEAD)
+    for i in steps:
+        for j in steps:
+            docs_all[i * lines + j] = pieces[0][i][j, 4 * BLOCK :].astype(jnp.float32)
     totals[...] = jnp.zeros_like(totals)
     row_token = z * part + lax.rem(lax.broadcasted_iota(jnp.int32, (CHUNK, rows), 1), part)
     key_token = lax.broadcasted_iota(jnp.int32, (CHUNK, rows), 0)
-    for copy in copies:
-        copy.wait()
 
     def fold(value, combine):
         return combine(value.reshape(CHUNK // 8, 8, rows), axis=0)
 
     def tile(j, carry):
         block = (lax.rem(z + nz - j, nz) * 2 + core) * (2 * nx) + x * 2 + y
-        docs = k_all[:, BLOCK:, :].astype(jnp.float32)
-        mine = k_all[pl.ds(block, 1), BLOCK:, :].astype(jnp.float32)
-        before = jnp.sum(jnp.where(docs < mine, 1.0, 0.0), axis=0)
+        doc = docs_all[jnp.where(core == 0, j, j * lines), pl.ds(4 * (2 * core + y), 1), :]
+        before = jnp.sum(jnp.where(docs_all[...] < doc, 0.25, 0.0), axis=(0, 1))
         first = jnp.max(before).astype(jnp.int32)
         for h in range(heads):
             q_rows[h * part : (h + 1) * part, :] = q_ref[j, :, h * HEAD : (h + 1) * HEAD]
             g_rows[h * part : (h + 1) * part, :] = g_ref[j, :, h * HEAD : (h + 1) * HEAD]
         q = q_rows[...]
         g = g_rows[...]
+        q_cols[...] = q.T
+        g_cols[...] = g.T
         chunks = lax.div(block - first + CHUNK_BLOCKS, CHUNK_BLOCKS)
 
         def keys_at(t):
             return jnp.minimum(first + t * CHUNK_BLOCKS, blocks - CHUNK_BLOCKS)
 
         def key_rows(t):
-            return k_all[pl.ds(keys_at(t), CHUNK_BLOCKS), :BLOCK, :].reshape(CHUNK, HEAD)
+            return k_all[pl.ds(keys_at(t), CHUNK_BLOCKS)].reshape(CHUNK, HEAD)
 
         def slot(t):
             return pl.ds(pl.multiple_of(t * CHUNK, CHUNK), CHUNK)
 
         def full_scores(t, top):
-            s = dot(key_rows(t), q, (1, 1))
+            s = dot(key_rows(t), q_cols[...], (1, 0))
             scores[slot(t), :] = s
             return jnp.maximum(top, fold(s, jnp.max))
 
@@ -97,7 +106,7 @@
         begin = keys_at(last)
         skipped = (first + last * CHUNK_BLOCKS - begin) * BLOCK
         mask = (key_token <= row_token + (block - begin) * BLOCK) & (key_token >= skipped)
-        s = jnp.where(mask, dot(key_rows(last), q, (1, 1)), NEG)
+        s = jnp.where(mask, dot(key_rows(last), q_cols[...], (1, 0)), NEG)
         scores[slot(last), :] = s
         top = jnp.max(jnp.maximum(top, fold(s, jnp.max)), axis=0, keepdims=True) * TO_EXP2
 
@@ -105,8 +114,8 @@
             norm, weighted = state
             e = jnp.exp2(scores[slot(t), :] * TO_EXP2 - top)
             scores[slot(t), :] = e
-            value_rows = v_all[pl.ds(keys_at(t), CHUNK_BLOCKS), :BLOCK, :].reshape(CHUNK, HEAD)
-            dp = dot(value_rows, g, (1, 1))
+            value_rows = v_all[pl.ds(keys_at(t), CHUNK_BLOCKS)].reshape(CHUNK, HEAD)
+            dp = dot(value_rows, g_cols[...], (1, 0))
             dprobs[slot(t), :] = dp
             return norm + fold(e, jnp.sum), weighted + fold(e * dp, jnp.sum)
 
@@ -132,13 +141,12 @@
         return carry
 
     lax.fori_loop(0, tiles, tile, 0)
-    for which, out in ((core, keep_ref), (1 - core, send_ref)):
-        for i in range(lines):
-            for j in range(lines):
-                dz, dx = ordered(which, i, j)
+    for which, out, spot in ((core, sums[0], spots[0]), (1 - core, sums[1], spots[1])):
+        for i in steps:
+            for j in steps:
                 for c in range(2):
-                    begin = pl.multiple_of(block_of(dz, dx, c) * BLOCK, BLOCK)
-                    out[i, j, c] = totals[which, pl.ds(begin, 2 * BLOCK), :].astype(jnp.bfloat16)
+                    begin = pl.multiple_of((spot[i][j] + 2 * nx * c) * BLOCK, BLOCK)
+                    out[i][j, c] = totals[which, pl.ds(begin, 2 * BLOCK), :].astype(jnp.bfloat16)
 
 
 def grads_call(sizes, place, q, g, mine, theirs):
@@ -148,22 +156,23 @@
     blocks = nx * nz * 4
     pieces = [*mine, *theirs]
     whole = pl.BlockSpec(memory_space=pltpu.VMEM)
-    sums_shape = jax.ShapeDtypeStruct((nz, nx, 2, 2 * BLOCK, HEAD), jnp.bfloat16)
+    sums_shape = jax.ShapeDtypeStruct((nx, 2, 2 * BLOCK, HEAD), jnp.bfloat16)
     return pl.pallas_call(
         lambda *refs: attention_grads(sizes, *refs),
         name="attention_grads",
-        out_shape=(jax.ShapeDtypeStruct(q.shape, jnp.bfloat16), sums_shape, sums_shape),
-        in_specs=[pl.BlockSpec(memory_space=pltpu.SMEM), whole, whole]
-        + [pl.BlockSpec(memory_space=pl.ANY)] * len(pieces),
-        out_specs=(whole,) * 3,
+        out_shape=(jax.ShapeDtypeStruct(q.shape, jnp.bfloat16),) + (sums_shape,) * len(pieces),
+        in_specs=[pl.BlockSpec(memory_space=pltpu.SMEM)] + [whole] * (2 + len(pieces)),
+        out_specs=(whole,) * (1 + len(pieces)),
         scratch_shapes=[
             pltpu.VMEM((rows, HEAD), jnp.bfloat16),
             pltpu.VMEM((rows, HEAD), jnp.bfloat16),
-            pltpu.VMEM((2, blocks, BLOCK + DOC_ROWS, HEAD), jnp.bfloat16),
+            pltpu.VMEM((HEAD, rows), jnp.bfloat16),
+            pltpu.VMEM((HEAD, rows), jnp.bfloat16),
+            pltpu.VMEM((nz * nx, DOC_ROWS, HEAD), jnp.float32),
+            pltpu.VMEM((2, blocks, BLOCK, HEAD), jnp.bfloat16),
             pltpu.VMEM((LONGEST * BLOCK, rows), jnp.float32),
             pltpu.VMEM((LONGEST * BLOCK, rows), jnp.float32),
             pltpu.VMEM((2, blocks * BLOCK, HEAD), jnp.float32),
-            pltpu.SemaphoreType.DMA((blocks,)),
         ],
         compiler_params=pltpu.CompilerParams(vmem_limit_bytes=48 * 1024 * 1024),
         cost_estimate=pl.CostEstimate(
@@ -223,33 +232,40 @@
             index == 0, jnp.stack([mine, theirs], axis=axis), jnp.stack([theirs, mine], axis=axis)
         )
 
+    both = jnp.concatenate([queries, grad_out], axis=1)
+
+    def piece_for(peer):
+        return lax.dynamic_slice_in_dim(both, lax.rem(peer, nz) * part, part, 0)
+
+    pieces = [piece_for(z)] + [along_z(piece_for(z + by), by) for by in range(1, nz)]
     docs = jnp.broadcast_to(low(block_docs)[:, None], (DOC_ROWS, HEAD))
     k_rows, v_rows = jnp.concatenate([keys, docs]), jnp.concatenate([values, docs])
     kept = jnp.where(core == 0, k_rows, v_rows)
     given = jnp.where(core == 0, v_rows, k_rows)
     unit = in_order(core, kept, other_core(given), 0)
     unit = in_order(y, unit, other_y(unit), 1)
+    unit = jnp.concatenate(
+        [unit[:, :, :BLOCK].reshape(4 * BLOCK, HEAD), unit[:, :, BLOCK : BLOCK + 4].reshape(DOC_ROWS, HEAD)]
+    )
     line = jnp.stack([unit] + [along_first(unit, by) for by in range(1, lines)])
+    line, *pieces = lax.optimization_barrier((line, *pieces))
+    q = jnp.stack([piece[:, :width] for piece in pieces])
+    g = jnp.stack([piece[:, width:] for piece in pieces])
     mine = [line] + [along_second(line, by) for by in range(1, lines)]
     theirs = [other_core(piece) for piece in mine]
 
-    both = jnp.concatenate([queries, grad_out], axis=1)
-
-    def piece_for(peer):
-        return lax.dynamic_slice_in_dim(both, lax.rem(peer, nz) * part, part, 0)
-
-    pieces = [piece_for(z)] + [along_z(piece_for(z + by), by) for by in range(1, nz)]
-    q = jnp.stack([piece[:, :width] for piece in pieces])
-    g = jnp.stack([piece[:, width:] for piece in pieces])
-
     place = jnp.stack([z, x, y, core]).astype(jnp.int32)
-    dq, keep, send = grads_call((nz, nx), place, q, g, mine, theirs)
-
-    total = low(added([keep, other_core(send)]))
-    arrived = [along_second(total[by], by) for by in range(1, lines)]
-    dq, arrived[0] = lax.optimization_barrier((dq, arrived[0]))
-    returned = jnp.stack([dq[0]] + [along_z(dq[by], -by) for by in range(1, nz)])
-    total = low(added([total[0]] + arrived))
+    dq, *sums = grads_call((nz, nx), place, q, g, mine, theirs)
+    keep, send = sums[:lines], sums[lines:]
+
+    totals = [None] * lines
+    for by in [*range(1, lines), 0]:
+        totals[by] = low(added([keep[by], other_core(send[by])]))
+    arrived = [along_second(totals[by], by) for by in range(1, lines)]
+    dq, totals[0] = lax.optimization_barrier((dq, totals[0]))
+    returned = [dq[0]] + [along_z(dq[by], -by) for by in range(1, nz)]
+    arrived, returned = lax.optimization_barrier((arrived, returned))
+    total = low(added([totals[0]] + arrived))
     total = low(added([total[0]] + [along_first(total[by], by) for by in range(1, lines)]))
     total = total.reshape(2, 2, BLOCK, HEAD)
     ours = jnp.where(y == 0, total[:, 0], total[:, 1])
@@ -262,7 +278,7 @@
     grad_values = jnp.where(core == 0, theirs, mine)
 
     order = lax.rem(jnp.arange(nz) - z + nz, nz)
-    grad_queries = jnp.take(returned, order, axis=0).reshape(rows, width)
+    grad_queries = jnp.take(jnp.stack(returned), order, axis=0).reshape(rows, width)
     return grad_queries, grad_keys, grad_values
 
 

time: 118 us -> 103 us (0.87)
  Pallas kernels: 23.4 us -> 16.4 us
  waiting for transfers between devices: 42.2 us -> 38.3 us
  other arithmetic: 6.32 us -> 3.55 us
    pallas_call x1, Pallas kernels: 23.4 us -> 16.4 us  [grads_call(): pl.pallas_call(lambda *refs: attention_grads(sizes, *refs), name='attenti...]
    ppermute x27 -> x30, waiting for transfers between devices: 42.2 us -> 38.3 us  [moved(): return lax.ppermute(value, CONTEXT, hops)]
    convert_element_type x4 -> x7, other arithmetic: 3.76 us -> 0.96 us  [low(): return value.astype(jnp.bfloat16)]
    unnamed x5 -> x15, local copies, waits for them, and re-layouts: 0.03 us -> 1.94 us
    ppermute x27 -> x30, starting transfers between devices: 40.7 us -> 39.8 us  [moved(): return lax.ppermute(value, CONTEXT, hops)]
  transfers between devices with their start and end apart: 27 -> 30, of which waited for: 15 -> 16; matrix products, arithmetic and copies ran while one was open for 2% -> 3% of each run, Pallas kernels for 0% -> 0%
where the time goes in v3:
time: 103 us; the launch traced here: 102 us
  starting transfers between devices  39.8 us (39%)
  waiting for transfers between devices  38.3 us (37%)
  Pallas kernels  16.4 us (16%)
  other arithmetic  3.55 us (3%)
  local copies, waits for them, and re-layouts  2.84 us (3%)
  between operations  1.64 us (2%)
    ppermute x30, starting transfers between devices, moved(): return lax.ppermute(value, CONTEXT, hops)  39.8 us
    ppermute x30, waiting for transfers between devices, moved(): return lax.ppermute(value, CONTEXT, hops)  38.3 us
    pallas_call x1, Pallas kernels, grads_call(): pl.pallas_call(lambda *refs: attention_grads(sizes, *refs), name='attenti...  16.4 us
  transfers between devices with their start and end apart: 30, of which 16 were waited for; matrix products, arithmetic and copies ran while one was open for 3% of the time, Pallas kernels for 0%

profile of v3, /device:TPU:1, one launch (start us, length us, event | category | flops | bytes accessed | tf_op | source)
XLA Modules:
  0.0 102.5 jit_solution(15420282634615986692)
XLA Ops:
  1.3 0.8 fusion.5
  2.1 1.5 %collective-permute-start = (bf16[144,128]{1,0:T(8,128)(2,1)S(1)}, bf16[144,128]{1,0:T(8,128)(2,1)S(1)}, u32[]{:S(2)}, u32[]{:S(2)}) collective-permute-start(bf16[144,128]{1,0:T(8,128)(2,1)S(1)} %get-tuple-element.74), channel_id=1, source_target_pairs={{0,16},{2,18},{4,20},{6,22},{8,24},{10,26},{12,28},{14,30},{16,0},... | collective-permute-start | bytes 110600 | tf_op jit(solution)/shard_map/ppermute | solution.py:213
  3.6 1.0 constant_dynamic-update-slice_fusion.1
  4.7 1.5 %collective-permute-start.1 = (bf16[2,144,128]{2,1,0:T(8,128)(2,1)S(1)}, bf16[2,144,128]{2,1,0:T(8,128)(2,1)S(1)}, u32[]{:S(2)}, u32[]{:S(2)}) collective-permute-start(bf16[2,144,128]{2,1,0:T(8,128)(2,1)S(1)} %maximum_select_fusion.2), channel_id=1, source_target_pairs={{0,2},{2,0},{4,6},{6,4},{8,10},{10,8},{12,14},{14,12},{16,18},{18,... | collective-permute-start | bytes 221192 | tf_op jit(solution)/shard_map/ppermute | solution.py:213
  6.2 2.3 %collective-permute-done.1 = bf16[2,144,128]{2,1,0:T(8,128)(2,1)S(1)} collective-permute-done((bf16[2,144,128]{2,1,0:T(8,128)(2,1)S(1)}, bf16[2,144,128]{2,1,0:T(8,128)(2,1)S(1)}, u32[]{:S(2)}, u32[]{:S(2)}) %collective-permute-start.1) | collective-permute-done | bytes 73760 | tf_op jit(solution)/shard_map/ppermute | solution.py:213
  8.6 1.4 %collective-permute-start.2 = (bf16[528,128]{1,0:T(8,128)(2,1)S(1)}, bf16[528,128]{1,0:T(8,128)(2,1)S(1)}, u32[]{:S(2)}, u32[]{:S(2)}) collective-permute-start(bf16[528,128]{1,0:T(8,128)(2,1)S(1)} %get-tuple-element.61), channel_id=1, source_target_pairs={{0,32},{2,34},{4,36},{6,38},{8,40},{10,42},{12,44},{14,46},{16,20}... | collective-permute-start | bytes 405512 | tf_op jit(solution)/shard_map/ppermute | solution.py:213
  10.0 2.5 %collective-permute-start.3 = (bf16[528,128]{1,0:T(8,128)(2,1)S(1)}, bf16[528,128]{1,0:T(8,128)(2,1)S(1)}, u32[]{:S(2)}, u32[]{:S(2)}) collective-permute-start(bf16[528,128]{1,0:T(8,128)(2,1)S(1)} %get-tuple-element.61), channel_id=1, source_target_pairs={{0,64},{2,66},{4,68},{6,70},{8,72},{10,74},{12,76},{14,78},{16,24}... | collective-permute-start | bytes 405512 | tf_op jit(solution)/shard_map/ppermute | solution.py:213
  12.4 1.2 %collective-permute-start.4 = (bf16[528,128]{1,0:T(8,128)(2,1)S(1)}, bf16[528,128]{1,0:T(8,128)(2,1)S(1)}, u32[]{:S(2)}, u32[]{:S(2)}) collective-permute-start(bf16[528,128]{1,0:T(8,128)(2,1)S(1)} %get-tuple-element.61), channel_id=1, source_target_pairs={{0,96},{2,98},{4,100},{6,102},{8,104},{10,106},{12,108},{14,110},{... | collective-permute-start | bytes 405512 | tf_op jit(solution)/shard_map/ppermute | solution.py:213
  13.6 1.7 %collective-permute-start.5 = (bf16[32,2048]{1,0:T(8,128)(2,1)S(1)}, bf16[32,2048]{1,0:T(8,128)(2,1)S(1)}, u32[]{:S(2)}, u32[]{:S(2)}) collective-permute-start(bf16[32,2048]{1,0:T(8,128)(2,1)S(1)} %get-tuple-element.54), channel_id=1, source_target_pairs={{0,32},{2,34},{4,36},{6,38},{8,40},{10,42},{12,44},{14,46},{16,48}... | collective-permute-start | bytes 393224 | tf_op jit(solution)/shard_map/ppermute | solution.py:213
  15.3 3.3 %collective-permute-start.6 = (bf16[32,2048]{1,0:T(8,128)(2,1)S(1)}, bf16[32,2048]{1,0:T(8,128)(2,1)S(1)}, u32[]{:S(2)}, u32[]{:S(2)}) collective-permute-start(bf16[32,2048]{1,0:T(8,128)(2,1)S(1)} %get-tuple-element.53), channel_id=1, source_target_pairs={{0,64},{2,66},{4,68},{6,70},{8,72},{10,74},{12,76},{14,78},{16,80}... | collective-permute-start | bytes 393224 | tf_op jit(solution)/shard_map/ppermute | solution.py:213
  18.7 0.7 collective-permute-start.7
  19.5 0.9 collective-permute-done.5
  20.4 4.5 %collective-permute-done.6 = bf16[32,2048]{1,0:T(8,128)(2,1)S(1)} collective-permute-done((bf16[32,2048]{1,0:T(8,128)(2,1)S(1)}, bf16[32,2048]{1,0:T(8,128)(2,1)S(1)}, u32[]{:S(2)}, u32[]{:S(2)}) %collective-permute-start.6) | collective-permute-done | bytes 131104 | tf_op jit(solution)/shard_map/ppermute | solution.py:213
  24.9 1.1 %collective-permute-start.8 = (bf16[4,528,128]{2,1,0:T(8,128)(2,1)S(1)}, bf16[4,528,128]{2,1,0:T(8,128)(2,1)S(1)}, u32[]{:S(2)}, u32[]{:S(2)}) collective-permute-start(bf16[4,528,128]{2,1,0:T(8,128)(2,1)S(1)} %pad_maximum_fusion.refs_3_), channel_id=1, source_target_pairs={{0,4},{2,6},{4,8},{6,10},{8,12},{10,14},{12,0},{14,2},{16,48},{18,... | collective-permute-start | bytes 1622024 | tf_op jit(solution)/shard_map/ppermute | solution.py:213
  25.9 2.6 %collective-permute-start.9 = (bf16[4,528,128]{2,1,0:T(8,128)(2,1)S(1)}, bf16[4,528,128]{2,1,0:T(8,128)(2,1)S(1)}, u32[]{:S(2)}, u32[]{:S(2)}) collective-permute-start(bf16[4,528,128]{2,1,0:T(8,128)(2,1)S(1)} %pad_maximum_fusion.refs_3_), channel_id=1, source_target_pairs={{0,8},{2,10},{4,12},{6,14},{8,0},{10,2},{12,4},{14,6},{16,80},{18,... | collective-permute-start | bytes 1622024 | tf_op jit(solution)/shard_map/ppermute | solution.py:213
  28.6 0.3 collective-permute-start.10
  29.0 2.0 %collective-permute-start.11 = (bf16[4,528,128]{2,1,0:T(8,128)(2,1)S(1)}, bf16[4,528,128]{2,1,0:T(8,128)(2,1)S(1)}, u32[]{:S(2)}, u32[]{:S(2)}) collective-permute-start(bf16[4,528,128]{2,1,0:T(8,128)(2,1)S(1)} %pad_maximum_fusion.refs_3_), channel_id=1, source_target_pairs={{0,16},{2,18},{4,20},{6,22},{8,24},{10,26},{12,28},{14,30},{16,0},... | collective-permute-start | bytes 1622024 | tf_op jit(solution)/shard_map/ppermute | solution.py:213
  31.0 3.5 %collective-permute-done.8.refs_4_ = bf16[4,528,128]{2,1,0:T(8,128)(2,1)S(1)} collective-permute-done((bf16[4,528,128]{2,1,0:T(8,128)(2,1)S(1)}, bf16[4,528,128]{2,1,0:T(8,128)(2,1)S(1)}, u32[]{:S(2)}, u32[]{:S(2)}) %collective-permute-start.8) | collective-permute-done | bytes 540704 | tf_op jit(solution)/shard_map/ppermute | solution.py:213
  34.6 2.0 %collective-permute-start.12 = (bf16[4,528,128]{2,1,0:T(8,128)(2,1)S(1)}, bf16[4,528,128]{2,1,0:T(8,128)(2,1)S(1)}, u32[]{:S(2)}, u32[]{:S(2)}) collective-permute-start(bf16[4,528,128]{2,1,0:T(8,128)(2,1)S(1)} %collective-permute-done.8.refs_4_), channel_id=1, source_target_pairs={{0,16},{2,18},{4,20},{6,22},{8,24},{10,26},{12,28},{14,30},{16,0},... | collective-permute-start | bytes 1622024 | tf_op jit(solution)/shard_map/ppermute | solution.py:213
  36.5 4.9 %collective-permute-done.9.refs_5_ = bf16[4,528,128]{2,1,0:T(8,128)(2,1)S(1)} collective-permute-done((bf16[4,528,128]{2,1,0:T(8,128)(2,1)S(1)}, bf16[4,528,128]{2,1,0:T(8,128)(2,1)S(1)}, u32[]{:S(2)}, u32[]{:S(2)}) %collective-permute-start.9) | collective-permute-done | bytes 540704 | tf_op jit(solution)/shard_map/ppermute | solution.py:213
  41.4 1.2 %collective-permute-start.13 = (bf16[4,528,128]{2,1,0:T(8,128)(2,1)S(1)}, bf16[4,528,128]{2,1,0:T(8,128)(2,1)S(1)}, u32[]{:S(2)}, u32[]{:S(2)}) collective-permute-start(bf16[4,528,128]{2,1,0:T(8,128)(2,1)S(1)} %collective-permute-done.9.refs_5_), channel_id=1, source_target_pairs={{0,16},{2,18},{4,20},{6,22},{8,24},{10,26},{12,28},{14,30},{16,0},... | collective-permute-start | bytes 1622024 | tf_op jit(solution)/shard_map/ppermute | solution.py:213
  42.6 0.6 collective-permute-start.14
  43.5 0.6 collective-permute-done.13.refs_9_
  44.2 0.8 collective-permute-done.14.refs_10_
  45.0 0.8 copy-done.6
  45.8 16.4 %attention_grads.1 = (bf16[4,32,1024]{2,1,0:T(8,128)(2,1)S(1)}, bf16[4,2,256,128]{3,2,1,0:T(8,128)(2,1)S(1)}, bf16[4,2,256,128]{3,2,1,0:T(8,128)(2,1)S(1)}, bf16...) custom-call(s32[4]{0:T(128)S(1)} %pad_add_fusion.refs_0_, ...), custom_call_target="tpu_custom_call" | custom-call | flops 3355443200 | bytes 16777216 | tf_op jit(solution)/shard_map/attention_grads/pallas_call | solution.py:160
  62.3 0.5 collective-permute-start.17
  62.9 0.4 collective-permute-start.15
  63.3 0.9 collective-permute-done.19
  64.3 2.2 %collective-permute-start.20 = (bf16[4,2,256,128]{3,2,1,0:T(8,128)(2,1)S(1)}, bf16[4,2,256,128]{3,2,1,0:T(8,128)(2,1)S(1)}, u32[]{:S(2)}, u32[]{:S(2)}) collective-permute-start(bf16[4,2,256,128]{3,2,1,0:T(8,128)(2,1)S(1)} %add_convert_fusion.2), channel_id=1, source_target_pairs={{0,12},{2,14},{4,0},{6,2},{8,4},{10,6},{12,8},{14,10},{16,112},{18... | collective-permute-start | bytes 1572872 | tf_op jit(solution)/shard_map/ppermute | solution.py:213
  66.6 1.0 %collective-permute-start.18 = (bf16[4,2,256,128]{3,2,1,0:T(8,128)(2,1)S(1)}, bf16[4,2,256,128]{3,2,1,0:T(8,128)(2,1)S(1)}, u32[]{:S(2)}, u32[]{:S(2)}) collective-permute-start(bf16[4,2,256,128]{3,2,1,0:T(8,128)(2,1)S(1)} %add_convert_fusion.3), channel_id=1, source_target_pairs={{0,8},{2,10},{4,12},{6,14},{8,0},{10,2},{12,4},{14,6},{16,80},{18,... | collective-permute-start | bytes 1572872 | tf_op jit(solution)/shard_map/ppermute | solution.py:213
  68.2 2.6 %collective-permute-start.22 = (bf16[32,1024]{1,0:T(8,128)(2,1)S(1)}, bf16[32,1024]{1,0:T(8,128)(2,1)S(1)}, u32[]{:S(2)}, u32[]{:S(2)}) collective-permute-start(bf16[32,1024]{1,0:T(8,128)(2,1)S(1)} %get-tuple-element.58), channel_id=1, source_target_pairs={{0,96},{2,98},{4,100},{6,102},{8,104},{10,106},{12,108},{14,110},{... | collective-permute-start | bytes 196616 | tf_op jit(solution)/shard_map/ppermute | solution.py:213
  70.8 0.8 collective-permute-start.23
  71.6 9.4 %collective-permute-done.22 = bf16[32,1024]{1,0:T(8,128)(2,1)S(1)} collective-permute-done((bf16[32,1024]{1,0:T(8,128)(2,1)S(1)}, bf16[32,1024]{1,0:T(8,128)(2,1)S(1)}, u32[]{:S(2)}, u32[]{:S(2)}) %collective-permute-start.22) | collective-permute-done | bytes 65568 | tf_op jit(solution)/shard_map/ppermute | solution.py:213
  81.0 0.7 collective-permute-start.24
  81.7 1.6 %collective-permute-done.23 = bf16[32,1024]{1,0:T(8,128)(2,1)S(1)} collective-permute-done((bf16[32,1024]{1,0:T(8,128)(2,1)S(1)}, bf16[32,1024]{1,0:T(8,128)(2,1)S(1)}, u32[]{:S(2)}, u32[]{:S(2)}) %collective-permute-start.23) | collective-permute-done | bytes 65568 | tf_op jit(solution)/shard_map/ppermute | solution.py:213
  83.3 3.5 %collective-permute-done.24 = bf16[32,1024]{1,0:T(8,128)(2,1)S(1)} collective-permute-done((bf16[32,1024]{1,0:T(8,128)(2,1)S(1)}, bf16[32,1024]{1,0:T(8,128)(2,1)S(1)}, u32[]{:S(2)}, u32[]{:S(2)}) %collective-permute-start.24) | collective-permute-done | bytes 65568 | tf_op jit(solution)/shard_map/ppermute | solution.py:213
  86.9 0.3 add_convert_fusion
  87.2 0.8 collective-permute-start.25
  88.0 2.7 %collective-permute-start.26 = (bf16[2,256,128]{2,1,0:T(8,128)(2,1)S(1)}, bf16[2,256,128]{2,1,0:T(8,128)(2,1)S(1)}, u32[]{:S(2)}, u32[]{:S(2)}) collective-permute-start(bf16[2,256,128]{2,1,0:T(8,128)(2,1)S(1)} %get-tuple-element.51), channel_id=1, source_target_pairs={{0,64},{2,66},{4,68},{6,70},{8,72},{10,74},{12,76},{14,78},{16,24}... | collective-permute-start | bytes 393224 | tf_op jit(solution)/shard_map/ppermute | solution.py:213
  90.9 1.7 %collective-permute-done.25 = bf16[2,256,128]{2,1,0:T(8,128)(2,1)S(1)} collective-permute-done((bf16[2,256,128]{2,1,0:T(8,128)(2,1)S(1)}, bf16[2,256,128]{2,1,0:T(8,128)(2,1)S(1)}, u32[]{:S(2)}, u32[]{:S(2)}) %collective-permute-start.25) | collective-permute-done | bytes 131104 | tf_op jit(solution)/shard_map/ppermute | solution.py:213
  92.6 2.2 %collective-permute-done.26 = bf16[2,256,128]{2,1,0:T(8,128)(2,1)S(1)} collective-permute-done((bf16[2,256,128]{2,1,0:T(8,128)(2,1)S(1)}, bf16[2,256,128]{2,1,0:T(8,128)(2,1)S(1)}, u32[]{:S(2)}, u32[]{:S(2)}) %collective-permute-start.26) | collective-permute-done | bytes 131104 | tf_op jit(solution)/shard_map/ppermute | solution.py:213
  94.9 1.3 %collective-permute-start.28 = (bf16[2,128,128]{2,1,0:T(8,128)(2,1)S(1)}, bf16[2,128,128]{2,1,0:T(8,128)(2,1)S(1)}, u32[]{:S(2)}, u32[]{:S(2)}) collective-permute-start(bf16[2,128,128]{2,1,0:T(8,128)(2,1)S(1)} %select_bitcast_fusion), channel_id=1, source_target_pairs={{0,2},{2,0},{4,6},{6,4},{8,10},{10,8},{12,14},{14,12},{16,18},{18,... | collective-permute-start | bytes 196616 | tf_op jit(solution)/shard_map/ppermute | solution.py:213
  96.3 0.6 gather_fusion
  96.9 1.2 %collective-permute-done.28 = bf16[2,128,128]{2,1,0:T(8,128)(2,1)S(1)} collective-permute-done((bf16[2,128,128]{2,1,0:T(8,128)(2,1)S(1)}, bf16[2,128,128]{2,1,0:T(8,128)(2,1)S(1)}, u32[]{:S(2)}, u32[]{:S(2)}) %collective-permute-start.28) | collective-permute-done | bytes 65568 | tf_op jit(solution)/shard_map/ppermute | solution.py:213
  98.2 2.8 %collective-permute-start.29 = (bf16[128,128]{1,0:T(8,128)(2,1)S(1)}, bf16[128,128]{1,0:T(8,128)(2,1)S(1)}, u32[]{:S(2)}, u32[]{:S(2)}) collective-permute-start(bf16[128,128]{1,0:T(8,128)(2,1)S(1)} %select_bitcast_fusion.1), channel_id=1, source_target_pairs={{0,16},{2,18},{4,20},{6,22},{8,24},{10,26},{12,28},{14,30},{16,0},... | collective-permute-start | bytes 98312 | tf_op jit(solution)/shard_map/ppermute | solution.py:213
  101.0 0.8 bitcast_select_fusion
  101.8 0.6 bitcast_select_fusion.1
  (65 shorter events, 2.1 us)
Async XLA Ops:
  2.1 2.5 %copy-start = (bf16[128,1024]{1,0:T(8,128)(2,1)S(1)}, bf16[128,1024]{1,0:T(8,128)(2,1)}, u32[]{:S(2)}) copy-start(bf16[128,1024]{1,0:T(8,128)(2,1)} %param.8) | copy-start | bytes 786436
  2.1 2.6 %collective-permute-start = (bf16[144,128]{1,0:T(8,128)(2,1)S(1)}, bf16[144,128]{1,0:T(8,128)(2,1)S(1)}, u32[]{:S(2)}, u32[]{:S(2)}) collective-permute-start(bf16[144,128]{1,0:T(8,128)(2,1)S(1)} %get-tuple-element.74), channel_id=1, source_target_pairs={{0,16},{2,18},{4,20},{6,22},{8,24},{10,26},{12,28},{14,30},{16,0},... | collective-permute-start | bytes 110600 | tf_op jit(solution)/shard_map/ppermute | solution.py:213
  4.7 3.8 %collective-permute-start.1 = (bf16[2,144,128]{2,1,0:T(8,128)(2,1)S(1)}, bf16[2,144,128]{2,1,0:T(8,128)(2,1)S(1)}, u32[]{:S(2)}, u32[]{:S(2)}) collective-permute-start(bf16[2,144,128]{2,1,0:T(8,128)(2,1)S(1)} %maximum_select_fusion.2), channel_id=1, source_target_pairs={{0,2},{2,0},{4,6},{6,4},{8,10},{10,8},{12,14},{14,12},{16,18},{18,... | collective-permute-start | bytes 221192 | tf_op jit(solution)/shard_map/ppermute | solution.py:213
  8.6 10.0 %collective-permute-start.2 = (bf16[528,128]{1,0:T(8,128)(2,1)S(1)}, bf16[528,128]{1,0:T(8,128)(2,1)S(1)}, u32[]{:S(2)}, u32[]{:S(2)}) collective-permute-start(bf16[528,128]{1,0:T(8,128)(2,1)S(1)} %get-tuple-element.61), channel_id=1, source_target_pairs={{0,32},{2,34},{4,36},{6,38},{8,40},{10,42},{12,44},{14,46},{16,20}... | collective-permute-start | bytes 405512 | tf_op jit(solution)/shard_map/ppermute | solution.py:213
  10.0 9.4 %collective-permute-start.3 = (bf16[528,128]{1,0:T(8,128)(2,1)S(1)}, bf16[528,128]{1,0:T(8,128)(2,1)S(1)}, u32[]{:S(2)}, u32[]{:S(2)}) collective-permute-start(bf16[528,128]{1,0:T(8,128)(2,1)S(1)} %get-tuple-element.61), channel_id=1, source_target_pairs={{0,64},{2,66},{4,68},{6,70},{8,72},{10,74},{12,76},{14,78},{16,24}... | collective-permute-start | bytes 405512 | tf_op jit(solution)/shard_map/ppermute | solution.py:213
  12.4 6.9 %collective-permute-start.4 = (bf16[528,128]{1,0:T(8,128)(2,1)S(1)}, bf16[528,128]{1,0:T(8,128)(2,1)S(1)}, u32[]{:S(2)}, u32[]{:S(2)}) collective-permute-start(bf16[528,128]{1,0:T(8,128)(2,1)S(1)} %get-tuple-element.61), channel_id=1, source_target_pairs={{0,96},{2,98},{4,100},{6,102},{8,104},{10,106},{12,108},{14,110},{... | collective-permute-start | bytes 405512 | tf_op jit(solution)/shard_map/ppermute | solution.py:213
  13.6 6.7 %collective-permute-start.5 = (bf16[32,2048]{1,0:T(8,128)(2,1)S(1)}, bf16[32,2048]{1,0:T(8,128)(2,1)S(1)}, u32[]{:S(2)}, u32[]{:S(2)}) collective-permute-start(bf16[32,2048]{1,0:T(8,128)(2,1)S(1)} %get-tuple-element.54), channel_id=1, source_target_pairs={{0,32},{2,34},{4,36},{6,38},{8,40},{10,42},{12,44},{14,46},{16,48}... | collective-permute-start | bytes 393224 | tf_op jit(solution)/shard_map/ppermute | solution.py:213
  15.3 9.5 %collective-permute-start.6 = (bf16[32,2048]{1,0:T(8,128)(2,1)S(1)}, bf16[32,2048]{1,0:T(8,128)(2,1)S(1)}, u32[]{:S(2)}, u32[]{:S(2)}) collective-permute-start(bf16[32,2048]{1,0:T(8,128)(2,1)S(1)} %get-tuple-element.53), channel_id=1, source_target_pairs={{0,64},{2,66},{4,68},{6,70},{8,72},{10,74},{12,76},{14,78},{16,80}... | collective-permute-start | bytes 393224 | tf_op jit(solution)/shard_map/ppermute | solution.py:213
  18.7 6.2 %collective-permute-start.7 = (bf16[32,2048]{1,0:T(8,128)(2,1)S(1)}, bf16[32,2048]{1,0:T(8,128)(2,1)S(1)}, u32[]{:S(2)}, u32[]{:S(2)}) collective-permute-start(bf16[32,2048]{1,0:T(8,128)(2,1)S(1)} %get-tuple-element.52), channel_id=1, source_target_pairs={{0,96},{2,98},{4,100},{6,102},{8,104},{10,106},{12,108},{14,110},{... | collective-permute-start | bytes 393224 | tf_op jit(solution)/shard_map/ppermute | solution.py:213
  24.9 9.7 %collective-permute-start.8 = (bf16[4,528,128]{2,1,0:T(8,128)(2,1)S(1)}, bf16[4,528,128]{2,1,0:T(8,128)(2,1)S(1)}, u32[]{:S(2)}, u32[]{:S(2)}) collective-permute-start(bf16[4,528,128]{2,1,0:T(8,128)(2,1)S(1)} %pad_maximum_fusion.refs_3_), channel_id=1, source_target_pairs={{0,4},{2,6},{4,8},{6,10},{8,12},{10,14},{12,0},{14,2},{16,48},{18,... | collective-permute-start | bytes 1622024 | tf_op jit(solution)/shard_map/ppermute | solution.py:213
  25.9 15.5 %collective-permute-start.9 = (bf16[4,528,128]{2,1,0:T(8,128)(2,1)S(1)}, bf16[4,528,128]{2,1,0:T(8,128)(2,1)S(1)}, u32[]{:S(2)}, u32[]{:S(2)}) collective-permute-start(bf16[4,528,128]{2,1,0:T(8,128)(2,1)S(1)} %pad_maximum_fusion.refs_3_), channel_id=1, source_target_pairs={{0,8},{2,10},{4,12},{6,14},{8,0},{10,2},{12,4},{14,6},{16,80},{18,... | collective-permute-start | bytes 1622024 | tf_op jit(solution)/shard_map/ppermute | solution.py:213
  28.6 14.1 %collective-permute-start.10 = (bf16[4,528,128]{2,1,0:T(8,128)(2,1)S(1)}, bf16[4,528,128]{2,1,0:T(8,128)(2,1)S(1)}, u32[]{:S(2)}, u32[]{:S(2)}) collective-permute-start(bf16[4,528,128]{2,1,0:T(8,128)(2,1)S(1)} %pad_maximum_fusion.refs_3_), channel_id=1, source_target_pairs={{0,12},{2,14},{4,0},{6,2},{8,4},{10,6},{12,8},{14,10},{16,112},{18... | collective-permute-start | bytes 1622024 | tf_op jit(solution)/shard_map/ppermute | solution.py:213
  29.0 14.5 %collective-permute-start.11 = (bf16[4,528,128]{2,1,0:T(8,128)(2,1)S(1)}, bf16[4,528,128]{2,1,0:T(8,128)(2,1)S(1)}, u32[]{:S(2)}, u32[]{:S(2)}) collective-permute-start(bf16[4,528,128]{2,1,0:T(8,128)(2,1)S(1)} %pad_maximum_fusion.refs_3_), channel_id=1, source_target_pairs={{0,16},{2,18},{4,20},{6,22},{8,24},{10,26},{12,28},{14,30},{16,0},... | collective-permute-start | bytes 1622024 | tf_op jit(solution)/shard_map/ppermute | solution.py:213
  34.6 9.0 %collective-permute-start.12 = (bf16[4,528,128]{2,1,0:T(8,128)(2,1)S(1)}, bf16[4,528,128]{2,1,0:T(8,128)(2,1)S(1)}, u32[]{:S(2)}, u32[]{:S(2)}) collective-permute-start(bf16[4,528,128]{2,1,0:T(8,128)(2,1)S(1)} %collective-permute-done.8.refs_4_), channel_id=1, source_target_pairs={{0,16},{2,18},{4,20},{6,22},{8,24},{10,26},{12,28},{14,30},{16,0},... | collective-permute-start | bytes 1622024 | tf_op jit(solution)/shard_map/ppermute | solution.py:213
  41.4 1.9 %copy-start.1 = (bf16[4,528,128]{2,1,0:T(8,128)(2,1)}, bf16[4,528,128]{2,1,0:T(8,128)(2,1)S(1)}, u32[]{:S(2)}) copy-start(bf16[4,528,128]{2,1,0:T(8,128)(2,1)S(1)} %collective-permute-done.9.refs_5_) | copy-start | bytes 1622020
  41.4 2.8 %collective-permute-start.13 = (bf16[4,528,128]{2,1,0:T(8,128)(2,1)S(1)}, bf16[4,528,128]{2,1,0:T(8,128)(2,1)S(1)}, u32[]{:S(2)}, u32[]{:S(2)}) collective-permute-start(bf16[4,528,128]{2,1,0:T(8,128)(2,1)S(1)} %collective-permute-done.9.refs_5_), channel_id=1, source_target_pairs={{0,16},{2,18},{4,20},{6,22},{8,24},{10,26},{12,28},{14,30},{16,0},... | collective-permute-start | bytes 1622024 | tf_op jit(solution)/shard_map/ppermute | solution.py:213
  42.6 0.8 copy-start.2
  42.6 2.3 %collective-permute-start.14 = (bf16[4,528,128]{2,1,0:T(8,128)(2,1)S(1)}, bf16[4,528,128]{2,1,0:T(8,128)(2,1)S(1)}, u32[]{:S(2)}, u32[]{:S(2)}) collective-permute-start(bf16[4,528,128]{2,1,0:T(8,128)(2,1)S(1)} %collective-permute-done.10.refs_6_), channel_id=1, source_target_pairs={{0,16},{2,18},{4,20},{6,22},{8,24},{10,26},{12,28},{14,30},{16,0},... | collective-permute-start | bytes 1622024 | tf_op jit(solution)/shard_map/ppermute | solution.py:213
  43.5 1.4 %copy-start.3 = (bf16[4,528,128]{2,1,0:T(8,128)(2,1)}, bf16[4,528,128]{2,1,0:T(8,128)(2,1)S(1)}, u32[]{:S(2)}) copy-start(bf16[4,528,128]{2,1,0:T(8,128)(2,1)S(1)} %collective-permute-done.11.refs_7_) | copy-start | bytes 1622020
  43.5 1.4 %copy-start.4 = (bf16[4,528,128]{2,1,0:T(8,128)(2,1)}, bf16[4,528,128]{2,1,0:T(8,128)(2,1)S(1)}, u32[]{:S(2)}) copy-start(bf16[4,528,128]{2,1,0:T(8,128)(2,1)S(1)} %collective-permute-done.12.refs_8_) | copy-start | bytes 1622020
  44.2 0.8 copy-start.5
  45.0 0.8 copy-start.6
  62.2 2.0 %collective-permute-start.19 = (bf16[4,2,256,128]{3,2,1,0:T(8,128)(2,1)S(1)}, bf16[4,2,256,128]{3,2,1,0:T(8,128)(2,1)S(1)}, u32[]{:S(2)}, u32[]{:S(2)}) collective-permute-start(bf16[4,2,256,128]{3,2,1,0:T(8,128)(2,1)S(1)} %get-tuple-element.36), channel_id=1, source_target_pairs={{0,16},{2,18},{4,20},{6,22},{8,24},{10,26},{12,28},{14,30},{16,0},... | collective-permute-start | bytes 1572872 | tf_op jit(solution)/shard_map/ppermute | solution.py:213
  62.3 4.2 %collective-permute-start.17 = (bf16[4,2,256,128]{3,2,1,0:T(8,128)(2,1)S(1)}, bf16[4,2,256,128]{3,2,1,0:T(8,128)(2,1)S(1)}, u32[]{:S(2)}, u32[]{:S(2)}) collective-permute-start(bf16[4,2,256,128]{3,2,1,0:T(8,128)(2,1)S(1)} %get-tuple-element.34), channel_id=1, source_target_pairs={{0,16},{2,18},{4,20},{6,22},{8,24},{10,26},{12,28},{14,30},{16,0},... | collective-permute-start | bytes 1572872 | tf_op jit(solution)/shard_map/ppermute | solution.py:213
  62.8 5.3 %collective-permute-start.21 = (bf16[4,2,256,128]{3,2,1,0:T(8,128)(2,1)S(1)}, bf16[4,2,256,128]{3,2,1,0:T(8,128)(2,1)S(1)}, u32[]{:S(2)}, u32[]{:S(2)}) collective-permute-start(bf16[4,2,256,128]{3,2,1,0:T(8,128)(2,1)S(1)} %get-tuple-element.39), channel_id=1, source_target_pairs={{0,16},{2,18},{4,20},{6,22},{8,24},{10,26},{12,28},{14,30},{16,0},... | collective-permute-start | bytes 1572872 | tf_op jit(solution)/shard_map/ppermute | solution.py:213
  62.9 4.8 %collective-permute-start.15 = (bf16[4,2,256,128]{3,2,1,0:T(8,128)(2,1)S(1)}, bf16[4,2,256,128]{3,2,1,0:T(8,128)(2,1)S(1)}, u32[]{:S(2)}, u32[]{:S(2)}) collective-permute-start(bf16[4,2,256,128]{3,2,1,0:T(8,128)(2,1)S(1)} %get-tuple-element.32), channel_id=1, source_target_pairs={{0,16},{2,18},{4,20},{6,22},{8,24},{10,26},{12,28},{14,30},{16,0},... | collective-permute-start | bytes 1572872 | tf_op jit(solution)/shard_map/ppermute | solution.py:213
  64.3 22.5 %collective-permute-start.20 = (bf16[4,2,256,128]{3,2,1,0:T(8,128)(2,1)S(1)}, bf16[4,2,256,128]{3,2,1,0:T(8,128)(2,1)S(1)}, u32[]{:S(2)}, u32[]{:S(2)}) collective-permute-start(bf16[4,2,256,128]{3,2,1,0:T(8,128)(2,1)S(1)} %add_convert_fusion.2), channel_id=1, source_target_pairs={{0,12},{2,14},{4,0},{6,2},{8,4},{10,6},{12,8},{14,10},{16,112},{18... | collective-permute-start | bytes 1572872 | tf_op jit(solution)/shard_map/ppermute | solution.py:213
  66.6 20.2 %collective-permute-start.18 = (bf16[4,2,256,128]{3,2,1,0:T(8,128)(2,1)S(1)}, bf16[4,2,256,128]{3,2,1,0:T(8,128)(2,1)S(1)}, u32[]{:S(2)}, u32[]{:S(2)}) collective-permute-start(bf16[4,2,256,128]{3,2,1,0:T(8,128)(2,1)S(1)} %add_convert_fusion.3), channel_id=1, source_target_pairs={{0,8},{2,10},{4,12},{6,14},{8,0},{10,2},{12,4},{14,6},{16,80},{18,... | collective-permute-start | bytes 1572872 | tf_op jit(solution)/shard_map/ppermute | solution.py:213
  67.8 19.0 %collective-permute-start.16 = (bf16[4,2,256,128]{3,2,1,0:T(8,128)(2,1)S(1)}, bf16[4,2,256,128]{3,2,1,0:T(8,128)(2,1)S(1)}, u32[]{:S(2)}, u32[]{:S(2)}) collective-permute-start(bf16[4,2,256,128]{3,2,1,0:T(8,128)(2,1)S(1)} %add_convert_fusion.4), channel_id=1, source_target_pairs={{0,4},{2,6},{4,8},{6,10},{8,12},{10,14},{12,0},{14,2},{16,48},{18,... | collective-permute-start | bytes 1572872 | tf_op jit(solution)/shard_map/ppermute | solution.py:213
  68.2 12.8 %collective-permute-start.22 = (bf16[32,1024]{1,0:T(8,128)(2,1)S(1)}, bf16[32,1024]{1,0:T(8,128)(2,1)S(1)}, u32[]{:S(2)}, u32[]{:S(2)}) collective-permute-start(bf16[32,1024]{1,0:T(8,128)(2,1)S(1)} %get-tuple-element.58), channel_id=1, source_target_pairs={{0,96},{2,98},{4,100},{6,102},{8,104},{10,106},{12,108},{14,110},{... | collective-permute-start | bytes 196616 | tf_op jit(solution)/shard_map/ppermute | solution.py:213
  70.8 12.5 %collective-permute-start.23 = (bf16[32,1024]{1,0:T(8,128)(2,1)S(1)}, bf16[32,1024]{1,0:T(8,128)(2,1)S(1)}, u32[]{:S(2)}, u32[]{:S(2)}) collective-permute-start(bf16[32,1024]{1,0:T(8,128)(2,1)S(1)} %get-tuple-element.57), channel_id=1, source_target_pairs={{0,64},{2,66},{4,68},{6,70},{8,72},{10,74},{12,76},{14,78},{16,80}... | collective-permute-start | bytes 196616 | tf_op jit(solution)/shard_map/ppermute | solution.py:213
  81.0 5.8 %collective-permute-start.24 = (bf16[32,1024]{1,0:T(8,128)(2,1)S(1)}, bf16[32,1024]{1,0:T(8,128)(2,1)S(1)}, u32[]{:S(2)}, u32[]{:S(2)}) collective-permute-start(bf16[32,1024]{1,0:T(8,128)(2,1)S(1)} %get-tuple-element.56), channel_id=1, source_target_pairs={{0,32},{2,34},{4,36},{6,38},{8,40},{10,42},{12,44},{14,46},{16,48}... | collective-permute-start | bytes 196616 | tf_op jit(solution)/shard_map/ppermute | solution.py:213
  87.2 5.4 %collective-permute-start.25 = (bf16[2,256,128]{2,1,0:T(8,128)(2,1)S(1)}, bf16[2,256,128]{2,1,0:T(8,128)(2,1)S(1)}, u32[]{:S(2)}, u32[]{:S(2)}) collective-permute-start(bf16[2,256,128]{2,1,0:T(8,128)(2,1)S(1)} %get-tuple-element.49), channel_id=1, source_target_pairs={{0,32},{2,34},{4,36},{6,38},{8,40},{10,42},{12,44},{14,46},{16,20}... | collective-permute-start | bytes 393224 | tf_op jit(solution)/shard_map/ppermute | solution.py:213
  88.0 6.8 %collective-permute-start.26 = (bf16[2,256,128]{2,1,0:T(8,128)(2,1)S(1)}, bf16[2,256,128]{2,1,0:T(8,128)(2,1)S(1)}, u32[]{:S(2)}, u32[]{:S(2)}) collective-permute-start(bf16[2,256,128]{2,1,0:T(8,128)(2,1)S(1)} %get-tuple-element.51), channel_id=1, source_target_pairs={{0,64},{2,66},{4,68},{6,70},{8,72},{10,74},{12,76},{14,78},{16,24}... | collective-permute-start | bytes 393224 | tf_op jit(solution)/shard_map/ppermute | solution.py:213
  90.7 4.1 %collective-permute-start.27 = (bf16[2,256,128]{2,1,0:T(8,128)(2,1)S(1)}, bf16[2,256,128]{2,1,0:T(8,128)(2,1)S(1)}, u32[]{:S(2)}, u32[]{:S(2)}) collective-permute-start(bf16[2,256,128]{2,1,0:T(8,128)(2,1)S(1)} %get-tuple-element.50), channel_id=1, source_target_pairs={{0,96},{2,98},{4,100},{6,102},{8,104},{10,106},{12,108},{14,110},{... | collective-permute-start | bytes 393224 | tf_op jit(solution)/shard_map/ppermute | solution.py:213
  94.9 3.2 %collective-permute-start.28 = (bf16[2,128,128]{2,1,0:T(8,128)(2,1)S(1)}, bf16[2,128,128]{2,1,0:T(8,128)(2,1)S(1)}, u32[]{:S(2)}, u32[]{:S(2)}) collective-permute-start(bf16[2,128,128]{2,1,0:T(8,128)(2,1)S(1)} %select_bitcast_fusion), channel_id=1, source_target_pairs={{0,2},{2,0},{4,6},{6,4},{8,10},{10,8},{12,14},{14,12},{16,18},{18,... | collective-permute-start | bytes 196616 | tf_op jit(solution)/shard_map/ppermute | solution.py:213
  98.2 3.7 %collective-permute-start.29 = (bf16[128,128]{1,0:T(8,128)(2,1)S(1)}, bf16[128,128]{1,0:T(8,128)(2,1)S(1)}, u32[]{:S(2)}, u32[]{:S(2)}) collective-permute-start(bf16[128,128]{1,0:T(8,128)(2,1)S(1)} %select_bitcast_fusion.1), channel_id=1, source_target_pairs={{0,16},{2,18},{4,20},{6,22},{8,24},{10,26},{12,28},{14,30},{16,0},... | collective-permute-start | bytes 98312 | tf_op jit(solution)/shard_map/ppermute | solution.py:213

commit v4 on v3

--- a/solution.py
+++ b/solution.py
@@ -27,8 +27,8 @@
     nz, nx = sizes
     lines = nz
     place_ref, q_ref, g_ref = refs[:3]
-    pieces = (refs[3 : 3 + lines], refs[3 + lines : 3 + 2 * lines])
-    refs = refs[3 + 2 * lines :]
+    pieces = (refs[3 : 4 + lines], refs[4 + lines : 5 + 2 * lines])
+    refs = refs[5 + 2 * lines :]
     dq_ref = refs[0]
     sums = (refs[1 : 1 + lines], refs[1 + lines : 1 + 2 * lines])
     q_rows, g_rows, q_cols, g_cols, docs_all, kv_all, scores, dprobs, totals = refs[1 + 2 * lines :]
@@ -57,15 +57,22 @@
 
     spots = (places(core), places(1 - core))
 
+    def unit_of(arrived, i, j):
+        if i < 2:
+            return arrived[i].at[j]
+        if i == 2:
+            return arrived[2 + j // 2].at[j % 2]
+        return arrived[4].at[j]
+
     for which, arrived, spot in ((core, pieces[0], spots[0]), (1 - core, pieces[1], spots[1])):
         for i in steps:
             for j in steps:
                 for c in range(2):
-                    rows_of = arrived[i][j, 2 * c * BLOCK : 2 * (c + 1) * BLOCK]
+                    rows_of = unit_of(arrived, i, j)[2 * c * BLOCK : 2 * (c + 1) * BLOCK]
                     kv_all[which, pl.ds(spot[-i][-j] + 2 * nx * c, 2)] = rows_of.reshape(2, BLOCK, HEAD)
     for i in steps:
         for j in steps:
-            docs_all[i * lines + j] = pieces[0][i][j, 4 * BLOCK :].astype(jnp.float32)
+            docs_all[i * lines + j] = unit_of(pieces[0], i, j)[4 * BLOCK :].astype(jnp.float32)
     totals[...] = jnp.zeros_like(totals)
     row_token = z * part + lax.rem(lax.broadcasted_iota(jnp.int32, (CHUNK, rows), 1), part)
     key_token = lax.broadcasted_iota(jnp.int32, (CHUNK, rows), 0)
@@ -160,9 +167,9 @@
     return pl.pallas_call(
         lambda *refs: attention_grads(sizes, *refs),
         name="attention_grads",
-        out_shape=(jax.ShapeDtypeStruct(q.shape, jnp.bfloat16),) + (sums_shape,) * len(pieces),
+        out_shape=(jax.ShapeDtypeStruct(q.shape, jnp.bfloat16),) + (sums_shape,) * (2 * nz),
         in_specs=[pl.BlockSpec(memory_space=pltpu.SMEM)] + [whole] * (2 + len(pieces)),
-        out_specs=(whole,) * (1 + len(pieces)),
+        out_specs=(whole,) * (1 + 2 * nz),
         scratch_shapes=[
             pltpu.VMEM((rows, HEAD), jnp.bfloat16),
             pltpu.VMEM((rows, HEAD), jnp.bfloat16),
@@ -244,6 +251,7 @@
     given = jnp.where(core == 0, v_rows, k_rows)
     unit = in_order(core, kept, other_core(given), 0)
     unit = in_order(y, unit, other_y(unit), 1)
+    unit, pieces[1], pieces[3] = lax.optimization_barrier((unit, pieces[1], pieces[3]))
     unit = jnp.concatenate(
         [unit[:, :, :BLOCK].reshape(4 * BLOCK, HEAD), unit[:, :, BLOCK : BLOCK + 4].reshape(DOC_ROWS, HEAD)]
     )
@@ -251,21 +259,28 @@
     line, *pieces = lax.optimization_barrier((line, *pieces))
     q = jnp.stack([piece[:, :width] for piece in pieces])
     g = jnp.stack([piece[:, width:] for piece in pieces])
-    mine = [line] + [along_second(line, by) for by in range(1, lines)]
+    before, after = along_second(line, 1), along_second(line, -1)
+    mine = [line, before, along_second(before[:2], 1), along_second(after[2:], -1), after]
     theirs = [other_core(piece) for piece in mine]
 
     place = jnp.stack([z, x, y, core]).astype(jnp.int32)
     dq, *sums = grads_call((nz, nx), place, q, g, mine, theirs)
     keep, send = sums[:lines], sums[lines:]
 
-    totals = [None] * lines
-    for by in [*range(1, lines), 0]:
-        totals[by] = low(added([keep[by], other_core(send[by])]))
-    arrived = [along_second(totals[by], by) for by in range(1, lines)]
-    dq, totals[0] = lax.optimization_barrier((dq, totals[0]))
+    swapped = [None] * lines
+    for by in (2, 1, 3, 0):
+        swapped[by] = other_core(send[by])
+    far_up = low(added([keep[2][:2], swapped[2][:2]]))
+    far_down = low(added([keep[2][2:], swapped[2][2:]]))
+    far_up, far_down = along_second(far_up, 1), along_second(far_down, -1)
+    rest = ((0, 0),) * 3
+    up = low(added([keep[1], swapped[1], jnp.pad(far_up, ((0, 2),) + rest)]))
+    down = low(added([keep[3], swapped[3], jnp.pad(far_down, ((2, 0),) + rest)]))
+    dq, up, down = lax.optimization_barrier((dq, up, down))
+    arrived = [along_second(up, 1), along_second(down, -1)]
     returned = [dq[0]] + [along_z(dq[by], -by) for by in range(1, nz)]
     arrived, returned = lax.optimization_barrier((arrived, returned))
-    total = low(added([totals[0]] + arrived))
+    total = low(added([keep[0], swapped[0]] + arrived))
     total = low(added([total[0]] + [along_first(total[by], by) for by in range(1, lines)]))
     total = total.reshape(2, 2, BLOCK, HEAD)
     ours = jnp.where(y == 0, total[:, 0], total[:, 1])

time: 103 us -> 107 us (1.039)
  starting transfers between devices: 39.8 us -> 48.2 us
  Pallas kernels: 16.4 us -> 14 us
    ppermute x30 -> x33, starting transfers between devices: 39.8 us -> 48.2 us  [moved(): return lax.ppermute(value, CONTEXT, hops)]
    pallas_call x1, Pallas kernels: 16.4 us -> 14 us  [grads_call(): pl.pallas_call(lambda *refs: attention_grads(sizes, *refs), name='attenti...]
    ppermute x30 -> x33, waiting for transfers between devices: 38.3 us -> 37.3 us  [moved(): return lax.ppermute(value, CONTEXT, hops)]
  transfers between devices with their start and end apart: 30 -> 33, of which waited for: 16 -> 17; matrix products, arithmetic and copies ran while one was open for 3% -> 2% of each run, Pallas kernels for 0% -> 0%
where the time goes in v4:
time: 107 us
  starting transfers between devices  48.2 us (45%)
  waiting for transfers between devices  37.3 us (35%)
  Pallas kernels  14 us (13%)
  other arithmetic  3.47 us (3%)
  local copies, waits for them, and re-layouts  1.9 us (2%)
  between operations  1.69 us (2%)
    ppermute x33, starting transfers between devices, moved(): return lax.ppermute(value, CONTEXT, hops)  48.2 us
    ppermute x33, waiting for transfers between devices, moved(): return lax.ppermute(value, CONTEXT, hops)  37.3 us
    pallas_call x1, Pallas kernels, grads_call(): pl.pallas_call(lambda *refs: attention_grads(sizes, *refs), name='attenti...  14 us
  transfers between devices with their start and end apart: 33, of which 17 were waited for; matrix products, arithmetic and copies ran while one was open for 2% of the time, Pallas kernels for 0%

profile of v4, /device:TPU:1, one launch (start us, length us, event | category | flops | bytes accessed | tf_op | source)
XLA Modules:
  0.0 106.5 jit_solution(1277659730400775382)
XLA Ops:
  1.3 0.8 fusion.5
  2.1 1.5 %collective-permute-start = (bf16[144,128]{1,0:T(8,128)(2,1)S(1)}, bf16[144,128]{1,0:T(8,128)(2,1)S(1)}, u32[]{:S(2)}, u32[]{:S(2)}) collective-permute-start(bf16[144,128]{1,0:T(8,128)(2,1)S(1)} %get-tuple-element.82), channel_id=1, source_target_pairs={{0,16},{2,18},{4,20},{6,22},{8,24},{10,26},{12,28},{14,30},{16,0},... | collective-permute-start | bytes 110600 | tf_op jit(solution)/shard_map/ppermute | solution.py:220
  3.7 0.9 copy-done.2
  4.7 1.8 %collective-permute-start.2 = (bf16[32,2048]{1,0:T(8,128)(2,1)S(1)}, bf16[32,2048]{1,0:T(8,128)(2,1)S(1)}, u32[]{:S(2)}, u32[]{:S(2)}) collective-permute-start(bf16[32,2048]{1,0:T(8,128)(2,1)S(1)} %get-tuple-element.63), channel_id=1, source_target_pairs={{0,32},{2,34},{4,36},{6,38},{8,40},{10,42},{12,44},{14,46},{16,48}... | collective-permute-start | bytes 393224 | tf_op jit(solution)/shard_map/ppermute | solution.py:220
  6.5 2.2 %collective-permute-start.3 = (bf16[32,2048]{1,0:T(8,128)(2,1)S(1)}, bf16[32,2048]{1,0:T(8,128)(2,1)S(1)}, u32[]{:S(2)}, u32[]{:S(2)}) collective-permute-start(bf16[32,2048]{1,0:T(8,128)(2,1)S(1)} %get-tuple-element.62), channel_id=1, source_target_pairs={{0,96},{2,98},{4,100},{6,102},{8,104},{10,106},{12,108},{14,110},{... | collective-permute-start | bytes 393224 | tf_op jit(solution)/shard_map/ppermute | solution.py:220
  8.7 1.4 %collective-permute-start.1 = (bf16[2,144,128]{2,1,0:T(8,128)(2,1)S(1)}, bf16[2,144,128]{2,1,0:T(8,128)(2,1)S(1)}, u32[]{:S(2)}, u32[]{:S(2)}) collective-permute-start(bf16[2,144,128]{2,1,0:T(8,128)(2,1)S(1)} %maximum_select_fusion.2), channel_id=1, source_target_pairs={{0,2},{2,0},{4,6},{6,4},{8,10},{10,8},{12,14},{14,12},{16,18},{18,... | collective-permute-start | bytes 221192 | tf_op jit(solution)/shard_map/ppermute | solution.py:220
  10.1 2.2 %collective-permute-done.1 = bf16[2,144,128]{2,1,0:T(8,128)(2,1)S(1)} collective-permute-done((bf16[2,144,128]{2,1,0:T(8,128)(2,1)S(1)}, bf16[2,144,128]{2,1,0:T(8,128)(2,1)S(1)}, u32[]{:S(2)}, u32[]{:S(2)}) %collective-permute-start.1) | collective-permute-done | bytes 73760 | tf_op jit(solution)/shard_map/ppermute | solution.py:220
  12.5 1.3 %collective-permute-start.4 = (bf16[528,128]{1,0:T(8,128)(2,1)S(1)}, bf16[528,128]{1,0:T(8,128)(2,1)S(1)}, u32[]{:S(2)}, u32[]{:S(2)}) collective-permute-start(bf16[528,128]{1,0:T(8,128)(2,1)S(1)} %get-tuple-element.69), channel_id=1, source_target_pairs={{0,32},{2,34},{4,36},{6,38},{8,40},{10,42},{12,44},{14,46},{16,20}... | collective-permute-start | bytes 405512 | tf_op jit(solution)/shard_map/ppermute | solution.py:220
  13.7 2.5 %collective-permute-start.5 = (bf16[528,128]{1,0:T(8,128)(2,1)S(1)}, bf16[528,128]{1,0:T(8,128)(2,1)S(1)}, u32[]{:S(2)}, u32[]{:S(2)}) collective-permute-start(bf16[528,128]{1,0:T(8,128)(2,1)S(1)} %get-tuple-element.69), channel_id=1, source_target_pairs={{0,64},{2,66},{4,68},{6,70},{8,72},{10,74},{12,76},{14,78},{16,24}... | collective-permute-start | bytes 405512 | tf_op jit(solution)/shard_map/ppermute | solution.py:220
  16.2 1.2 %collective-permute-start.6 = (bf16[528,128]{1,0:T(8,128)(2,1)S(1)}, bf16[528,128]{1,0:T(8,128)(2,1)S(1)}, u32[]{:S(2)}, u32[]{:S(2)}) collective-permute-start(bf16[528,128]{1,0:T(8,128)(2,1)S(1)} %get-tuple-element.69), channel_id=1, source_target_pairs={{0,96},{2,98},{4,100},{6,102},{8,104},{10,106},{12,108},{14,110},{... | collective-permute-start | bytes 405512 | tf_op jit(solution)/shard_map/ppermute | solution.py:220
  17.4 2.1 %collective-permute-start.7 = (bf16[32,2048]{1,0:T(8,128)(2,1)S(1)}, bf16[32,2048]{1,0:T(8,128)(2,1)S(1)}, u32[]{:S(2)}, u32[]{:S(2)}) collective-permute-start(bf16[32,2048]{1,0:T(8,128)(2,1)S(1)} %get-tuple-element.60), channel_id=1, source_target_pairs={{0,64},{2,66},{4,68},{6,70},{8,72},{10,74},{12,76},{14,78},{16,80}... | collective-permute-start | bytes 393224 | tf_op jit(solution)/shard_map/ppermute | solution.py:220
  19.5 0.9 collective-permute-done.5
  20.4 2.4 %collective-permute-done.7 = bf16[32,2048]{1,0:T(8,128)(2,1)S(1)} collective-permute-done((bf16[32,2048]{1,0:T(8,128)(2,1)S(1)}, bf16[32,2048]{1,0:T(8,128)(2,1)S(1)}, u32[]{:S(2)}, u32[]{:S(2)}) %collective-permute-start.7) | collective-permute-done | bytes 131104 | tf_op jit(solution)/shard_map/ppermute | solution.py:220
  22.8 2.1 %collective-permute-start.8 = (bf16[4,528,128]{2,1,0:T(8,128)(2,1)S(1)}, bf16[4,528,128]{2,1,0:T(8,128)(2,1)S(1)}, u32[]{:S(2)}, u32[]{:S(2)}) collective-permute-start(bf16[4,528,128]{2,1,0:T(8,128)(2,1)S(1)} %pad_maximum_fusion.refs_3_), channel_id=1, source_target_pairs={{0,4},{2,6},{4,8},{6,10},{8,12},{10,14},{12,0},{14,2},{16,48},{18,... | collective-permute-start | bytes 1622024 | tf_op jit(solution)/shard_map/ppermute | solution.py:220
  24.9 2.0 %collective-permute-start.10 = (bf16[4,528,128]{2,1,0:T(8,128)(2,1)S(1)}, bf16[4,528,128]{2,1,0:T(8,128)(2,1)S(1)}, u32[]{:S(2)}, u32[]{:S(2)}) collective-permute-start(bf16[4,528,128]{2,1,0:T(8,128)(2,1)S(1)} %pad_maximum_fusion.refs_3_), channel_id=1, source_target_pairs={{0,12},{2,14},{4,0},{6,2},{8,4},{10,6},{12,8},{14,10},{16,112},{18... | collective-permute-start | bytes 1622024 | tf_op jit(solution)/shard_map/ppermute | solution.py:220
  26.9 7.0 %collective-permute-done.8.refs_4_ = bf16[4,528,128]{2,1,0:T(8,128)(2,1)S(1)} collective-permute-done((bf16[4,528,128]{2,1,0:T(8,128)(2,1)S(1)}, bf16[4,528,128]{2,1,0:T(8,128)(2,1)S(1)}, u32[]{:S(2)}, u32[]{:S(2)}) %collective-permute-start.8) | collective-permute-done | bytes 540704 | tf_op jit(solution)/shard_map/ppermute | solution.py:220
  34.1 2.7 %collective-permute-start.11 = (bf16[2,528,128]{2,1,0:T(8,128)(2,1)S(1)}, bf16[2,528,128]{2,1,0:T(8,128)(2,1)S(1)}, u32[]{:S(2)}, u32[]{:S(2)}) collective-permute-start(bf16[2,528,128]{2,1,0:T(8,128)(2,1)S(1)} %slice.119), channel_id=1, source_target_pairs={{0,12},{2,14},{4,0},{6,2},{8,4},{10,6},{12,8},{14,10},{16,112},{18... | collective-permute-start | bytes 811016 | tf_op jit(solution)/shard_map/ppermute | solution.py:220
  36.9 2.4 %collective-permute-start.12 = (bf16[4,528,128]{2,1,0:T(8,128)(2,1)S(1)}, bf16[4,528,128]{2,1,0:T(8,128)(2,1)S(1)}, u32[]{:S(2)}, u32[]{:S(2)}) collective-permute-start(bf16[4,528,128]{2,1,0:T(8,128)(2,1)S(1)} %pad_maximum_fusion.refs_3_), channel_id=1, source_target_pairs={{0,16},{2,18},{4,20},{6,22},{8,24},{10,26},{12,28},{14,30},{16,0},... | collective-permute-start | bytes 1622024 | tf_op jit(solution)/shard_map/ppermute | solution.py:220
  39.4 0.4 collective-permute-start.16
  39.8 1.0 collective-permute-done.9.refs_5_
  40.8 2.7 %collective-permute-start.14 = (bf16[2,528,128]{2,1,0:T(8,128)(2,1)S(1)}, bf16[2,528,128]{2,1,0:T(8,128)(2,1)S(1)}, u32[]{:S(2)}, u32[]{:S(2)}) collective-permute-start(bf16[2,528,128]{2,1,0:T(8,128)(2,1)S(1)} %collective-permute-done.9.refs_5_), channel_id=1, source_target_pairs={{0,16},{2,18},{4,20},{6,22},{8,24},{10,26},{12,28},{14,30},{16,0},... | collective-permute-start | bytes 811016 | tf_op jit(solution)/shard_map/ppermute | solution.py:220
  43.7 1.0 collective-permute-done.14.refs_10_
  44.7 0.4 collective-permute-done.15.refs_11_
  45.1 14.0 %attention_grads.1 = (bf16[4,32,1024]{2,1,0:T(8,128)(2,1)S(1)}, bf16[4,2,256,128]{3,2,1,0:T(8,128)(2,1)S(1)}, bf16[4,2,256,128]{3,2,1,0:T(8,128)(2,1)S(1)}, bf16...) custom-call(s32[4]{0:T(128)S(1)} %pad_add_fusion.refs_0_, ...), custom_call_target="tpu_custom_call" | custom-call | flops 3355443200 | bytes 16777216 | tf_op jit(solution)/shard_map/attention_grads/pallas_call | solution.py:167
  59.1 2.8 %collective-permute-start.18 = (bf16[4,2,256,128]{3,2,1,0:T(8,128)(2,1)S(1)}, bf16[4,2,256,128]{3,2,1,0:T(8,128)(2,1)S(1)}, u32[]{:S(2)}, u32[]{:S(2)}) collective-permute-start(bf16[4,2,256,128]{3,2,1,0:T(8,128)(2,1)S(1)} %get-tuple-element.41), channel_id=1, source_target_pairs={{0,16},{2,18},{4,20},{6,22},{8,24},{10,26},{12,28},{14,30},{16,0},... | collective-permute-start | bytes 1572872 | tf_op jit(solution)/shard_map/ppermute | solution.py:220
  62.1 1.4 %collective-permute-done.18 = bf16[4,2,256,128]{3,2,1,0:T(8,128)(2,1)S(1)} collective-permute-done((bf16[4,2,256,128]{3,2,1,0:T(8,128)(2,1)S(1)}, bf16[4,2,256,128]{3,2,1,0:T(8,128)(2,1)S(1)}, u32[]{:S(2)}, u32[]{:S(2)}) %collective-permute-start.18) | collective-permute-done | bytes 524320 | tf_op jit(solution)/shard_map/ppermute | solution.py:220
  63.7 2.8 %collective-permute-start.21 = (bf16[2,2,256,128]{3,2,1,0:T(8,128)(2,1)S(1)}, bf16[2,2,256,128]{3,2,1,0:T(8,128)(2,1)S(1)}, u32[]{:S(2)}, u32[]{:S(2)}) collective-permute-start(bf16[2,2,256,128]{3,2,1,0:T(8,128)(2,1)S(1)} %get-tuple-element.55), channel_id=1, source_target_pairs={{0,12},{2,14},{4,0},{6,2},{8,4},{10,6},{12,8},{14,10},{16,112},{18... | collective-permute-start | bytes 786440 | tf_op jit(solution)/shard_map/ppermute | solution.py:220
  66.4 0.5 collective-permute-start.17
  66.9 1.4 %collective-permute-start.19 = (bf16[2,2,256,128]{3,2,1,0:T(8,128)(2,1)S(1)}, bf16[2,2,256,128]{3,2,1,0:T(8,128)(2,1)S(1)}, u32[]{:S(2)}, u32[]{:S(2)}) collective-permute-start(bf16[2,2,256,128]{3,2,1,0:T(8,128)(2,1)S(1)} %get-tuple-element.56), channel_id=1, source_target_pairs={{0,4},{2,6},{4,8},{6,10},{8,12},{10,14},{12,0},{14,2},{16,48},{18,... | collective-permute-start | bytes 786440 | tf_op jit(solution)/shard_map/ppermute | solution.py:220
  68.3 1.5 %collective-permute-done.21 = bf16[2,2,256,128]{3,2,1,0:T(8,128)(2,1)S(1)} collective-permute-done((bf16[2,2,256,128]{3,2,1,0:T(8,128)(2,1)S(1)}, bf16[2,2,256,128]{3,2,1,0:T(8,128)(2,1)S(1)}, u32[]{:S(2)}, u32[]{:S(2)}) %collective-permute-start.21) | collective-permute-done | bytes 262176 | tf_op jit(solution)/shard_map/ppermute | solution.py:220
  69.9 3.7 %collective-permute-done.19 = bf16[2,2,256,128]{3,2,1,0:T(8,128)(2,1)S(1)} collective-permute-done((bf16[2,2,256,128]{3,2,1,0:T(8,128)(2,1)S(1)}, bf16[2,2,256,128]{3,2,1,0:T(8,128)(2,1)S(1)}, u32[]{:S(2)}, u32[]{:S(2)}) %collective-permute-start.19) | collective-permute-done | bytes 262176 | tf_op jit(solution)/shard_map/ppermute | solution.py:220
  74.0 2.5 %collective-permute-start.23 = (bf16[4,2,256,128]{3,2,1,0:T(8,128)(2,1)S(1)}, bf16[4,2,256,128]{3,2,1,0:T(8,128)(2,1)S(1)}, u32[]{:S(2)}, u32[]{:S(2)}) collective-permute-start(bf16[4,2,256,128]{3,2,1,0:T(8,128)(2,1)S(1)} %add_convert_fusion.1), channel_id=1, source_target_pairs={{0,12},{2,14},{4,0},{6,2},{8,4},{10,6},{12,8},{14,10},{16,112},{18... | collective-permute-start | bytes 1572872 | tf_op jit(solution)/shard_map/ppermute | solution.py:220
  76.6 1.4 %collective-permute-start.27 = (bf16[4,2,256,128]{3,2,1,0:T(8,128)(2,1)S(1)}, bf16[4,2,256,128]{3,2,1,0:T(8,128)(2,1)S(1)}, u32[]{:S(2)}, u32[]{:S(2)}) collective-permute-start(bf16[4,2,256,128]{3,2,1,0:T(8,128)(2,1)S(1)} %get-tuple-element.52), channel_id=1, source_target_pairs={{0,16},{2,18},{4,20},{6,22},{8,24},{10,26},{12,28},{14,30},{16,0},... | collective-permute-start | bytes 1572872 | tf_op jit(solution)/shard_map/ppermute | solution.py:220
  78.0 2.7 %collective-permute-start.24 = (bf16[32,1024]{1,0:T(8,128)(2,1)S(1)}, bf16[32,1024]{1,0:T(8,128)(2,1)S(1)}, u32[]{:S(2)}, u32[]{:S(2)}) collective-permute-start(bf16[32,1024]{1,0:T(8,128)(2,1)S(1)} %get-tuple-element.66), channel_id=1, source_target_pairs={{0,96},{2,98},{4,100},{6,102},{8,104},{10,106},{12,108},{14,110},{... | collective-permute-start | bytes 196616 | tf_op jit(solution)/shard_map/ppermute | solution.py:220
  80.7 0.5 collective-permute-start.25
  81.2 4.3 %collective-permute-done.24 = bf16[32,1024]{1,0:T(8,128)(2,1)S(1)} collective-permute-done((bf16[32,1024]{1,0:T(8,128)(2,1)S(1)}, bf16[32,1024]{1,0:T(8,128)(2,1)S(1)}, u32[]{:S(2)}, u32[]{:S(2)}) %collective-permute-start.24) | collective-permute-done | bytes 65568 | tf_op jit(solution)/shard_map/ppermute | solution.py:220
  85.5 5.7 %collective-permute-done.26 = bf16[32,1024]{1,0:T(8,128)(2,1)S(1)} collective-permute-done((bf16[32,1024]{1,0:T(8,128)(2,1)S(1)}, bf16[32,1024]{1,0:T(8,128)(2,1)S(1)}, u32[]{:S(2)}, u32[]{:S(2)}) %collective-permute-start.26) | collective-permute-done | bytes 65568 | tf_op jit(solution)/shard_map/ppermute | solution.py:220
  91.2 0.3 add_convert_fusion
  91.6 2.2 %collective-permute-start.29 = (bf16[2,256,128]{2,1,0:T(8,128)(2,1)S(1)}, bf16[2,256,128]{2,1,0:T(8,128)(2,1)S(1)}, u32[]{:S(2)}, u32[]{:S(2)}) collective-permute-start(bf16[2,256,128]{2,1,0:T(8,128)(2,1)S(1)} %get-tuple-element.59), channel_id=1, source_target_pairs={{0,64},{2,66},{4,68},{6,70},{8,72},{10,74},{12,76},{14,78},{16,24}... | collective-permute-start | bytes 393224 | tf_op jit(solution)/shard_map/ppermute | solution.py:220
  93.8 0.4 collective-permute-start.30
  94.5 3.9 %collective-permute-done.28 = bf16[2,256,128]{2,1,0:T(8,128)(2,1)S(1)} collective-permute-done((bf16[2,256,128]{2,1,0:T(8,128)(2,1)S(1)}, bf16[2,256,128]{2,1,0:T(8,128)(2,1)S(1)}, u32[]{:S(2)}, u32[]{:S(2)}) %collective-permute-start.28) | collective-permute-done | bytes 131104 | tf_op jit(solution)/shard_map/ppermute | solution.py:220
  98.3 0.6 collective-permute-done.30
  99.0 1.4 %collective-permute-start.31 = (bf16[2,128,128]{2,1,0:T(8,128)(2,1)S(1)}, bf16[2,128,128]{2,1,0:T(8,128)(2,1)S(1)}, u32[]{:S(2)}, u32[]{:S(2)}) collective-permute-start(bf16[2,128,128]{2,1,0:T(8,128)(2,1)S(1)} %select_bitcast_fusion), channel_id=1, source_target_pairs={{0,2},{2,0},{4,6},{6,4},{8,10},{10,8},{12,14},{14,12},{16,18},{18,... | collective-permute-start | bytes 196616 | tf_op jit(solution)/shard_map/ppermute | solution.py:220
  100.5 0.6 gather_fusion
  101.0 1.2 %collective-permute-done.31 = bf16[2,128,128]{2,1,0:T(8,128)(2,1)S(1)} collective-permute-done((bf16[2,128,128]{2,1,0:T(8,128)(2,1)S(1)}, bf16[2,128,128]{2,1,0:T(8,128)(2,1)S(1)}, u32[]{:S(2)}, u32[]{:S(2)}) %collective-permute-start.31) | collective-permute-done | bytes 65568 | tf_op jit(solution)/shard_map/ppermute | solution.py:220
  102.3 2.8 %collective-permute-start.32 = (bf16[128,128]{1,0:T(8,128)(2,1)S(1)}, bf16[128,128]{1,0:T(8,128)(2,1)S(1)}, u32[]{:S(2)}, u32[]{:S(2)}) collective-permute-start(bf16[128,128]{1,0:T(8,128)(2,1)S(1)} %select_bitcast_fusion.1), channel_id=1, source_target_pairs={{0,16},{2,18},{4,20},{6,22},{8,24},{10,26},{12,28},{14,30},{16,0},... | collective-permute-start | bytes 98312 | tf_op jit(solution)/shard_map/ppermute | solution.py:220
  105.0 0.8 bitcast_select_fusion
  105.9 0.6 bitcast_select_fusion.1
  (74 shorter events, 2.2 us)
Async XLA Ops:
  0.6 3.0 %copy-start.1 = (bf16[128,1024]{1,0:T(8,128)(2,1)S(1)}, bf16[128,1024]{1,0:T(8,128)(2,1)}, u32[]{:S(2)}) copy-start(bf16[128,1024]{1,0:T(8,128)(2,1)} %param.5) | copy-start | bytes 786436
  2.1 6.5 %collective-permute-start = (bf16[144,128]{1,0:T(8,128)(2,1)S(1)}, bf16[144,128]{1,0:T(8,128)(2,1)S(1)}, u32[]{:S(2)}, u32[]{:S(2)}) collective-permute-start(bf16[144,128]{1,0:T(8,128)(2,1)S(1)} %get-tuple-element.82), channel_id=1, source_target_pairs={{0,16},{2,18},{4,20},{6,22},{8,24},{10,26},{12,28},{14,30},{16,0},... | collective-permute-start | bytes 110600 | tf_op jit(solution)/shard_map/ppermute | solution.py:220
  3.6 1.0 copy-start.2
  4.7 7.7 %collective-permute-start.2 = (bf16[32,2048]{1,0:T(8,128)(2,1)S(1)}, bf16[32,2048]{1,0:T(8,128)(2,1)S(1)}, u32[]{:S(2)}, u32[]{:S(2)}) collective-permute-start(bf16[32,2048]{1,0:T(8,128)(2,1)S(1)} %get-tuple-element.63), channel_id=1, source_target_pairs={{0,32},{2,34},{4,36},{6,38},{8,40},{10,42},{12,44},{14,46},{16,48}... | collective-permute-start | bytes 393224 | tf_op jit(solution)/shard_map/ppermute | solution.py:220
  6.5 5.9 %collective-permute-start.3 = (bf16[32,2048]{1,0:T(8,128)(2,1)S(1)}, bf16[32,2048]{1,0:T(8,128)(2,1)S(1)}, u32[]{:S(2)}, u32[]{:S(2)}) collective-permute-start(bf16[32,2048]{1,0:T(8,128)(2,1)S(1)} %get-tuple-element.62), channel_id=1, source_target_pairs={{0,96},{2,98},{4,100},{6,102},{8,104},{10,106},{12,108},{14,110},{... | collective-permute-start | bytes 393224 | tf_op jit(solution)/shard_map/ppermute | solution.py:220
  8.7 3.6 %collective-permute-start.1 = (bf16[2,144,128]{2,1,0:T(8,128)(2,1)S(1)}, bf16[2,144,128]{2,1,0:T(8,128)(2,1)S(1)}, u32[]{:S(2)}, u32[]{:S(2)}) collective-permute-start(bf16[2,144,128]{2,1,0:T(8,128)(2,1)S(1)} %maximum_select_fusion.2), channel_id=1, source_target_pairs={{0,2},{2,0},{4,6},{6,4},{8,10},{10,8},{12,14},{14,12},{16,18},{18,... | collective-permute-start | bytes 221192 | tf_op jit(solution)/shard_map/ppermute | solution.py:220
  12.5 7.0 %collective-permute-start.4 = (bf16[528,128]{1,0:T(8,128)(2,1)S(1)}, bf16[528,128]{1,0:T(8,128)(2,1)S(1)}, u32[]{:S(2)}, u32[]{:S(2)}) collective-permute-start(bf16[528,128]{1,0:T(8,128)(2,1)S(1)} %get-tuple-element.69), channel_id=1, source_target_pairs={{0,32},{2,34},{4,36},{6,38},{8,40},{10,42},{12,44},{14,46},{16,20}... | collective-permute-start | bytes 405512 | tf_op jit(solution)/shard_map/ppermute | solution.py:220
  13.7 6.6 %collective-permute-start.5 = (bf16[528,128]{1,0:T(8,128)(2,1)S(1)}, bf16[528,128]{1,0:T(8,128)(2,1)S(1)}, u32[]{:S(2)}, u32[]{:S(2)}) collective-permute-start(bf16[528,128]{1,0:T(8,128)(2,1)S(1)} %get-tuple-element.69), channel_id=1, source_target_pairs={{0,64},{2,66},{4,68},{6,70},{8,72},{10,74},{12,76},{14,78},{16,24}... | collective-permute-start | bytes 405512 | tf_op jit(solution)/shard_map/ppermute | solution.py:220
  16.2 4.2 %collective-permute-start.6 = (bf16[528,128]{1,0:T(8,128)(2,1)S(1)}, bf16[528,128]{1,0:T(8,128)(2,1)S(1)}, u32[]{:S(2)}, u32[]{:S(2)}) collective-permute-start(bf16[528,128]{1,0:T(8,128)(2,1)S(1)} %get-tuple-element.69), channel_id=1, source_target_pairs={{0,96},{2,98},{4,100},{6,102},{8,104},{10,106},{12,108},{14,110},{... | collective-permute-start | bytes 405512 | tf_op jit(solution)/shard_map/ppermute | solution.py:220
  17.4 5.5 %collective-permute-start.7 = (bf16[32,2048]{1,0:T(8,128)(2,1)S(1)}, bf16[32,2048]{1,0:T(8,128)(2,1)S(1)}, u32[]{:S(2)}, u32[]{:S(2)}) collective-permute-start(bf16[32,2048]{1,0:T(8,128)(2,1)S(1)} %get-tuple-element.60), channel_id=1, source_target_pairs={{0,64},{2,66},{4,68},{6,70},{8,72},{10,74},{12,76},{14,78},{16,80}... | collective-permute-start | bytes 393224 | tf_op jit(solution)/shard_map/ppermute | solution.py:220
  20.4 16.4 %copy-start = (bf16[4,528,128]{2,1,0:T(8,128)(2,1)}, bf16[4,528,128]{2,1,0:T(8,128)(2,1)S(1)}, u32[]{:S(2)}) copy-start(bf16[4,528,128]{2,1,0:T(8,128)(2,1)S(1)} %pad_maximum_fusion.refs_3_) | copy-start | bytes 1622020
  22.8 11.1 %collective-permute-start.8 = (bf16[4,528,128]{2,1,0:T(8,128)(2,1)S(1)}, bf16[4,528,128]{2,1,0:T(8,128)(2,1)S(1)}, u32[]{:S(2)}, u32[]{:S(2)}) collective-permute-start(bf16[4,528,128]{2,1,0:T(8,128)(2,1)S(1)} %pad_maximum_fusion.refs_3_), channel_id=1, source_target_pairs={{0,4},{2,6},{4,8},{6,10},{8,12},{10,14},{12,0},{14,2},{16,48},{18,... | collective-permute-start | bytes 1622024 | tf_op jit(solution)/shard_map/ppermute | solution.py:220
  24.9 9.2 %collective-permute-start.10 = (bf16[4,528,128]{2,1,0:T(8,128)(2,1)S(1)}, bf16[4,528,128]{2,1,0:T(8,128)(2,1)S(1)}, u32[]{:S(2)}, u32[]{:S(2)}) collective-permute-start(bf16[4,528,128]{2,1,0:T(8,128)(2,1)S(1)} %pad_maximum_fusion.refs_3_), channel_id=1, source_target_pairs={{0,12},{2,14},{4,0},{6,2},{8,4},{10,6},{12,8},{14,10},{16,112},{18... | collective-permute-start | bytes 1622024 | tf_op jit(solution)/shard_map/ppermute | solution.py:220
  33.9 5.4 %copy-start.3 = (bf16[4,528,128]{2,1,0:T(8,128)(2,1)}, bf16[4,528,128]{2,1,0:T(8,128)(2,1)S(1)}, u32[]{:S(2)}) copy-start(bf16[4,528,128]{2,1,0:T(8,128)(2,1)S(1)} %collective-permute-done.8.refs_4_) | copy-start | bytes 1622020
  34.0 6.9 %collective-permute-start.9 = (bf16[2,528,128]{2,1,0:T(8,128)(2,1)S(1)}, bf16[2,528,128]{2,1,0:T(8,128)(2,1)S(1)}, u32[]{:S(2)}, u32[]{:S(2)}) collective-permute-start(bf16[2,528,128]{2,1,0:T(8,128)(2,1)S(1)} %slice.118), channel_id=1, source_target_pairs={{0,4},{2,6},{4,8},{6,10},{8,12},{10,14},{12,0},{14,2},{16,48},{18,... | collective-permute-start | bytes 811016 | tf_op jit(solution)/shard_map/ppermute | solution.py:220
  34.0 9.5 %copy-start.4 = (bf16[4,528,128]{2,1,0:T(8,128)(2,1)}, bf16[4,528,128]{2,1,0:T(8,128)(2,1)S(1)}, u32[]{:S(2)}) copy-start(bf16[4,528,128]{2,1,0:T(8,128)(2,1)S(1)} %collective-permute-done.10.refs_7_) | copy-start | bytes 1622020
  34.1 9.5 %collective-permute-start.11 = (bf16[2,528,128]{2,1,0:T(8,128)(2,1)S(1)}, bf16[2,528,128]{2,1,0:T(8,128)(2,1)S(1)}, u32[]{:S(2)}, u32[]{:S(2)}) collective-permute-start(bf16[2,528,128]{2,1,0:T(8,128)(2,1)S(1)} %slice.119), channel_id=1, source_target_pairs={{0,12},{2,14},{4,0},{6,2},{8,4},{10,6},{12,8},{14,10},{16,112},{18... | collective-permute-start | bytes 811016 | tf_op jit(solution)/shard_map/ppermute | solution.py:220
  36.9 6.8 %collective-permute-start.12 = (bf16[4,528,128]{2,1,0:T(8,128)(2,1)S(1)}, bf16[4,528,128]{2,1,0:T(8,128)(2,1)S(1)}, u32[]{:S(2)}, u32[]{:S(2)}) collective-permute-start(bf16[4,528,128]{2,1,0:T(8,128)(2,1)S(1)} %pad_maximum_fusion.refs_3_), channel_id=1, source_target_pairs={{0,16},{2,18},{4,20},{6,22},{8,24},{10,26},{12,28},{14,30},{16,0},... | collective-permute-start | bytes 1622024 | tf_op jit(solution)/shard_map/ppermute | solution.py:220
  39.3 4.4 %collective-permute-start.13 = (bf16[4,528,128]{2,1,0:T(8,128)(2,1)S(1)}, bf16[4,528,128]{2,1,0:T(8,128)(2,1)S(1)}, u32[]{:S(2)}, u32[]{:S(2)}) collective-permute-start(bf16[4,528,128]{2,1,0:T(8,128)(2,1)S(1)} %collective-permute-done.8.refs_4_), channel_id=1, source_target_pairs={{0,16},{2,18},{4,20},{6,22},{8,24},{10,26},{12,28},{14,30},{16,0},... | collective-permute-start | bytes 1622024 | tf_op jit(solution)/shard_map/ppermute | solution.py:220
  39.4 4.3 %collective-permute-start.16 = (bf16[4,528,128]{2,1,0:T(8,128)(2,1)S(1)}, bf16[4,528,128]{2,1,0:T(8,128)(2,1)S(1)}, u32[]{:S(2)}, u32[]{:S(2)}) collective-permute-start(bf16[4,528,128]{2,1,0:T(8,128)(2,1)S(1)} %collective-permute-done.10.refs_7_), channel_id=1, source_target_pairs={{0,16},{2,18},{4,20},{6,22},{8,24},{10,26},{12,28},{14,30},{16,0},... | collective-permute-start | bytes 1622024 | tf_op jit(solution)/shard_map/ppermute | solution.py:220
  40.8 3.9 %collective-permute-start.14 = (bf16[2,528,128]{2,1,0:T(8,128)(2,1)S(1)}, bf16[2,528,128]{2,1,0:T(8,128)(2,1)S(1)}, u32[]{:S(2)}, u32[]{:S(2)}) collective-permute-start(bf16[2,528,128]{2,1,0:T(8,128)(2,1)S(1)} %collective-permute-done.9.refs_5_), channel_id=1, source_target_pairs={{0,16},{2,18},{4,20},{6,22},{8,24},{10,26},{12,28},{14,30},{16,0},... | collective-permute-start | bytes 811016 | tf_op jit(solution)/shard_map/ppermute | solution.py:220
  43.6 1.6 %collective-permute-start.15 = (bf16[2,528,128]{2,1,0:T(8,128)(2,1)S(1)}, bf16[2,528,128]{2,1,0:T(8,128)(2,1)S(1)}, u32[]{:S(2)}, u32[]{:S(2)}) collective-permute-start(bf16[2,528,128]{2,1,0:T(8,128)(2,1)S(1)} %collective-permute-done.11.refs_6_), channel_id=1, source_target_pairs={{0,16},{2,18},{4,20},{6,22},{8,24},{10,26},{12,28},{14,30},{16,0},... | collective-permute-start | bytes 811016 | tf_op jit(solution)/shard_map/ppermute | solution.py:220
  43.7 1.4 %copy-start.5 = (bf16[4,528,128]{2,1,0:T(8,128)(2,1)}, bf16[4,528,128]{2,1,0:T(8,128)(2,1)S(1)}, u32[]{:S(2)}) copy-start(bf16[4,528,128]{2,1,0:T(8,128)(2,1)S(1)} %collective-permute-done.12.refs_8_) | copy-start | bytes 1622020
  43.7 1.4 %copy-start.6 = (bf16[4,528,128]{2,1,0:T(8,128)(2,1)}, bf16[4,528,128]{2,1,0:T(8,128)(2,1)S(1)}, u32[]{:S(2)}) copy-start(bf16[4,528,128]{2,1,0:T(8,128)(2,1)S(1)} %collective-permute-done.13.refs_9_) | copy-start | bytes 1622020
  43.7 1.4 %copy-start.7 = (bf16[4,528,128]{2,1,0:T(8,128)(2,1)}, bf16[4,528,128]{2,1,0:T(8,128)(2,1)S(1)}, u32[]{:S(2)}) copy-start(bf16[4,528,128]{2,1,0:T(8,128)(2,1)S(1)} %collective-permute-done.16.refs_12_) | copy-start | bytes 1622020
  59.1 4.4 %collective-permute-start.18 = (bf16[4,2,256,128]{3,2,1,0:T(8,128)(2,1)S(1)}, bf16[4,2,256,128]{3,2,1,0:T(8,128)(2,1)S(1)}, u32[]{:S(2)}, u32[]{:S(2)}) collective-permute-start(bf16[4,2,256,128]{3,2,1,0:T(8,128)(2,1)S(1)} %get-tuple-element.41), channel_id=1, source_target_pairs={{0,16},{2,18},{4,20},{6,22},{8,24},{10,26},{12,28},{14,30},{16,0},... | collective-permute-start | bytes 1572872 | tf_op jit(solution)/shard_map/ppermute | solution.py:220
  62.0 6.3 %collective-permute-start.20 = (bf16[4,2,256,128]{3,2,1,0:T(8,128)(2,1)S(1)}, bf16[4,2,256,128]{3,2,1,0:T(8,128)(2,1)S(1)}, u32[]{:S(2)}, u32[]{:S(2)}) collective-permute-start(bf16[4,2,256,128]{3,2,1,0:T(8,128)(2,1)S(1)} %get-tuple-element.43), channel_id=1, source_target_pairs={{0,16},{2,18},{4,20},{6,22},{8,24},{10,26},{12,28},{14,30},{16,0},... | collective-permute-start | bytes 1572872 | tf_op jit(solution)/shard_map/ppermute | solution.py:220
  63.7 6.1 %collective-permute-start.21 = (bf16[2,2,256,128]{3,2,1,0:T(8,128)(2,1)S(1)}, bf16[2,2,256,128]{3,2,1,0:T(8,128)(2,1)S(1)}, u32[]{:S(2)}, u32[]{:S(2)}) collective-permute-start(bf16[2,2,256,128]{3,2,1,0:T(8,128)(2,1)S(1)} %get-tuple-element.55), channel_id=1, source_target_pairs={{0,12},{2,14},{4,0},{6,2},{8,4},{10,6},{12,8},{14,10},{16,112},{18... | collective-permute-start | bytes 786440 | tf_op jit(solution)/shard_map/ppermute | solution.py:220
  66.4 3.5 %collective-permute-start.17 = (bf16[4,2,256,128]{3,2,1,0:T(8,128)(2,1)S(1)}, bf16[4,2,256,128]{3,2,1,0:T(8,128)(2,1)S(1)}, u32[]{:S(2)}, u32[]{:S(2)}) collective-permute-start(bf16[4,2,256,128]{3,2,1,0:T(8,128)(2,1)S(1)} %get-tuple-element.39), channel_id=1, source_target_pairs={{0,16},{2,18},{4,20},{6,22},{8,24},{10,26},{12,28},{14,30},{16,0},... | collective-permute-start | bytes 1572872 | tf_op jit(solution)/shard_map/ppermute | solution.py:220
  66.9 6.7 %collective-permute-start.19 = (bf16[2,2,256,128]{3,2,1,0:T(8,128)(2,1)S(1)}, bf16[2,2,256,128]{3,2,1,0:T(8,128)(2,1)S(1)}, u32[]{:S(2)}, u32[]{:S(2)}) collective-permute-start(bf16[2,2,256,128]{3,2,1,0:T(8,128)(2,1)S(1)} %get-tuple-element.56), channel_id=1, source_target_pairs={{0,4},{2,6},{4,8},{6,10},{8,12},{10,14},{12,0},{14,2},{16,48},{18,... | collective-permute-start | bytes 786440 | tf_op jit(solution)/shard_map/ppermute | solution.py:220
  73.8 17.4 %collective-permute-start.22 = (bf16[4,2,256,128]{3,2,1,0:T(8,128)(2,1)S(1)}, bf16[4,2,256,128]{3,2,1,0:T(8,128)(2,1)S(1)}, u32[]{:S(2)}, u32[]{:S(2)}) collective-permute-start(bf16[4,2,256,128]{3,2,1,0:T(8,128)(2,1)S(1)} %add_convert_fusion.2), channel_id=1, source_target_pairs={{0,4},{2,6},{4,8},{6,10},{8,12},{10,14},{12,0},{14,2},{16,48},{18,... | collective-permute-start | bytes 1572872 | tf_op jit(solution)/shard_map/ppermute | solution.py:220
  74.0 17.1 %collective-permute-start.23 = (bf16[4,2,256,128]{3,2,1,0:T(8,128)(2,1)S(1)}, bf16[4,2,256,128]{3,2,1,0:T(8,128)(2,1)S(1)}, u32[]{:S(2)}, u32[]{:S(2)}) collective-permute-start(bf16[4,2,256,128]{3,2,1,0:T(8,128)(2,1)S(1)} %add_convert_fusion.1), channel_id=1, source_target_pairs={{0,12},{2,14},{4,0},{6,2},{8,4},{10,6},{12,8},{14,10},{16,112},{18... | collective-permute-start | bytes 1572872 | tf_op jit(solution)/shard_map/ppermute | solution.py:220
  76.6 14.6 %collective-permute-start.27 = (bf16[4,2,256,128]{3,2,1,0:T(8,128)(2,1)S(1)}, bf16[4,2,256,128]{3,2,1,0:T(8,128)(2,1)S(1)}, u32[]{:S(2)}, u32[]{:S(2)}) collective-permute-start(bf16[4,2,256,128]{3,2,1,0:T(8,128)(2,1)S(1)} %get-tuple-element.52), channel_id=1, source_target_pairs={{0,16},{2,18},{4,20},{6,22},{8,24},{10,26},{12,28},{14,30},{16,0},... | collective-permute-start | bytes 1572872 | tf_op jit(solution)/shard_map/ppermute | solution.py:220
  78.0 7.5 %collective-permute-start.24 = (bf16[32,1024]{1,0:T(8,128)(2,1)S(1)}, bf16[32,1024]{1,0:T(8,128)(2,1)S(1)}, u32[]{:S(2)}, u32[]{:S(2)}) collective-permute-start(bf16[32,1024]{1,0:T(8,128)(2,1)S(1)} %get-tuple-element.66), channel_id=1, source_target_pairs={{0,96},{2,98},{4,100},{6,102},{8,104},{10,106},{12,108},{14,110},{... | collective-permute-start | bytes 196616 | tf_op jit(solution)/shard_map/ppermute | solution.py:220
  80.7 4.8 %collective-permute-start.25 = (bf16[32,1024]{1,0:T(8,128)(2,1)S(1)}, bf16[32,1024]{1,0:T(8,128)(2,1)S(1)}, u32[]{:S(2)}, u32[]{:S(2)}) collective-permute-start(bf16[32,1024]{1,0:T(8,128)(2,1)S(1)} %get-tuple-element.65), channel_id=1, source_target_pairs={{0,64},{2,66},{4,68},{6,70},{8,72},{10,74},{12,76},{14,78},{16,80}... | collective-permute-start | bytes 196616 | tf_op jit(solution)/shard_map/ppermute | solution.py:220
  85.5 5.7 %collective-permute-start.26 = (bf16[32,1024]{1,0:T(8,128)(2,1)S(1)}, bf16[32,1024]{1,0:T(8,128)(2,1)S(1)}, u32[]{:S(2)}, u32[]{:S(2)}) collective-permute-start(bf16[32,1024]{1,0:T(8,128)(2,1)S(1)} %get-tuple-element.64), channel_id=1, source_target_pairs={{0,32},{2,34},{4,36},{6,38},{8,40},{10,42},{12,44},{14,46},{16,48}... | collective-permute-start | bytes 196616 | tf_op jit(solution)/shard_map/ppermute | solution.py:220
  91.5 6.8 %collective-permute-start.28 = (bf16[2,256,128]{2,1,0:T(8,128)(2,1)S(1)}, bf16[2,256,128]{2,1,0:T(8,128)(2,1)S(1)}, u32[]{:S(2)}, u32[]{:S(2)}) collective-permute-start(bf16[2,256,128]{2,1,0:T(8,128)(2,1)S(1)} %get-tuple-element.57), channel_id=1, source_target_pairs={{0,32},{2,34},{4,36},{6,38},{8,40},{10,42},{12,44},{14,46},{16,20}... | collective-permute-start | bytes 393224 | tf_op jit(solution)/shard_map/ppermute | solution.py:220
  91.6 6.7 %collective-permute-start.29 = (bf16[2,256,128]{2,1,0:T(8,128)(2,1)S(1)}, bf16[2,256,128]{2,1,0:T(8,128)(2,1)S(1)}, u32[]{:S(2)}, u32[]{:S(2)}) collective-permute-start(bf16[2,256,128]{2,1,0:T(8,128)(2,1)S(1)} %get-tuple-element.59), channel_id=1, source_target_pairs={{0,64},{2,66},{4,68},{6,70},{8,72},{10,74},{12,76},{14,78},{16,24}... | collective-permute-start | bytes 393224 | tf_op jit(solution)/shard_map/ppermute | solution.py:220
  93.8 5.1 %collective-permute-start.30 = (bf16[2,256,128]{2,1,0:T(8,128)(2,1)S(1)}, bf16[2,256,128]{2,1,0:T(8,128)(2,1)S(1)}, u32[]{:S(2)}, u32[]{:S(2)}) collective-permute-start(bf16[2,256,128]{2,1,0:T(8,128)(2,1)S(1)} %get-tuple-element.58), channel_id=1, source_target_pairs={{0,96},{2,98},{4,100},{6,102},{8,104},{10,106},{12,108},{14,110},{... | collective-permute-start | bytes 393224 | tf_op jit(solution)/shard_map/ppermute | solution.py:220
  99.0 3.2 %collective-permute-start.31 = (bf16[2,128,128]{2,1,0:T(8,128)(2,1)S(1)}, bf16[2,128,128]{2,1,0:T(8,128)(2,1)S(1)}, u32[]{:S(2)}, u32[]{:S(2)}) collective-permute-start(bf16[2,128,128]{2,1,0:T(8,128)(2,1)S(1)} %select_bitcast_fusion), channel_id=1, source_target_pairs={{0,2},{2,0},{4,6},{6,4},{8,10},{10,8},{12,14},{14,12},{16,18},{18,... | collective-permute-start | bytes 196616 | tf_op jit(solution)/shard_map/ppermute | solution.py:220
  102.3 3.6 %collective-permute-start.32 = (bf16[128,128]{1,0:T(8,128)(2,1)S(1)}, bf16[128,128]{1,0:T(8,128)(2,1)S(1)}, u32[]{:S(2)}, u32[]{:S(2)}) collective-permute-start(bf16[128,128]{1,0:T(8,128)(2,1)S(1)} %select_bitcast_fusion.1), channel_id=1, source_target_pairs={{0,16},{2,18},{4,20},{6,22},{8,24},{10,26},{12,28},{14,30},{16,0},... | collective-permute-start | bytes 98312 | tf_op jit(solution)/shard_map/ppermute | solution.py:220

commit v5 on v3

--- a/solution.py
+++ b/solution.py
@@ -14,6 +14,7 @@
 CHUNK_BLOCKS = 8
 CHUNK = CHUNK_BLOCKS * BLOCK
 LONGEST = 40
+PEERS = 2
 SCALE = float(HEAD) ** (-0.5)
 TO_EXP2 = SCALE * math.log2(math.e)
 CONTEXT = ("inner", "outer")
@@ -31,7 +32,7 @@
     refs = refs[3 + 2 * lines :]
     dq_ref = refs[0]
     sums = (refs[1 : 1 + lines], refs[1 + lines : 1 + 2 * lines])
-    q_rows, g_rows, q_cols, g_cols, docs_all, kv_all, scores, dprobs, totals = refs[1 + 2 * lines :]
+    q_rows, g_rows, q_cols, g_cols, docs_all, kv_all, scores, totals = refs[1 + 2 * lines :]
     blocks = kv_all.shape[1]
     tiles, part, width = q_ref.shape
     heads = width // HEAD
@@ -67,15 +68,17 @@
         for j in steps:
             docs_all[i * lines + j] = pieces[0][i][j, 4 * BLOCK :].astype(jnp.float32)
     totals[...] = jnp.zeros_like(totals)
-    row_token = z * part + lax.rem(lax.broadcasted_iota(jnp.int32, (CHUNK, rows), 1), part)
+    apart = nz // tiles
+    row_token = lax.div(z, apart) * part + lax.rem(lax.broadcasted_iota(jnp.int32, (CHUNK, rows), 1), part)
     key_token = lax.broadcasted_iota(jnp.int32, (CHUNK, rows), 0)
 
     def fold(value, combine):
         return combine(value.reshape(CHUNK // 8, 8, rows), axis=0)
 
     def tile(j, carry):
-        block = (lax.rem(z + nz - j, nz) * 2 + core) * (2 * nx) + x * 2 + y
-        doc = docs_all[jnp.where(core == 0, j, j * lines), pl.ds(4 * (2 * core + y), 1), :]
+        dz = j * apart
+        block = (lax.rem(z + nz - dz, nz) * 2 + core) * (2 * nx) + x * 2 + y
+        doc = docs_all[jnp.where(core == 0, dz, dz * lines), pl.ds(4 * (2 * core + y), 1), :]
         before = jnp.sum(jnp.where(docs_all[...] < doc, 0.25, 0.0), axis=(0, 1))
         first = jnp.max(before).astype(jnp.int32)
         for h in range(heads):
@@ -116,7 +119,6 @@
             scores[slot(t), :] = e
             value_rows = v_all[pl.ds(keys_at(t), CHUNK_BLOCKS)].reshape(CHUNK, HEAD)
             dp = dot(value_rows, g_cols[...], (1, 0))
-            dprobs[slot(t), :] = dp
             return norm + fold(e, jnp.sum), weighted + fold(e * dp, jnp.sum)
 
         zeros = jnp.zeros((8, rows), jnp.float32)
@@ -127,7 +129,8 @@
         def grads(t, dq):
             keys = pl.ds(pl.multiple_of(keys_at(t) * BLOCK, BLOCK), CHUNK)
             p = scores[slot(t), :] * inverse
-            ds = p * (dprobs[slot(t), :] - delta)
+            value_rows = v_all[pl.ds(keys_at(t), CHUNK_BLOCKS)].reshape(CHUNK, HEAD)
+            ds = p * (dot(value_rows, g_cols[...], (1, 0)) - delta)
             p_low = p.astype(jnp.bfloat16)
             ds_low = ds.astype(jnp.bfloat16)
             dk_total[keys, :] += dot(ds_low, q, (1, 0))
@@ -171,10 +174,9 @@
             pltpu.VMEM((nz * nx, DOC_ROWS, HEAD), jnp.float32),
             pltpu.VMEM((2, blocks, BLOCK, HEAD), jnp.bfloat16),
             pltpu.VMEM((LONGEST * BLOCK, rows), jnp.float32),
-            pltpu.VMEM((LONGEST * BLOCK, rows), jnp.float32),
             pltpu.VMEM((2, blocks * BLOCK, HEAD), jnp.float32),
         ],
-        compiler_params=pltpu.CompilerParams(vmem_limit_bytes=48 * 1024 * 1024),
+        compiler_params=pltpu.CompilerParams(vmem_limit_bytes=36 * 1024 * 1024),
         cost_estimate=pl.CostEstimate(
             flops=10 * 20 * 1024 * 128 * 128, bytes_accessed=16 * 1024 * 1024, transcendentals=0
         ),
@@ -199,7 +201,8 @@
     inner, outer = lax.axis_index("inner"), lax.axis_index("outer")
     z, core = lax.div(inner, 2), lax.rem(inner, 2)
     x, y = lax.div(outer, 2), lax.rem(outer, 2)
-    part = rows // nz
+    part = rows // PEERS
+    apart = nz // PEERS
     lines = nz
 
     def moved(value, step):
@@ -218,8 +221,11 @@
     def other_y(value):
         return moved(value, lambda c: (0, 0, 1, 0))
 
-    def along_z(value, by):
-        return moved(value, lambda c: (by, 0, 0, 0))
+    def diagonal(value):
+        return moved(value, lambda c: (0, 0, 1, 1))
+
+    def peer(value):
+        return moved(value, lambda c: (apart, 0, 0, 0))
 
     def along_first(value, by):
         return moved(value, lambda c: (0, by, 0, 0) if c else (by, 0, 0, 0))
@@ -232,18 +238,17 @@
             index == 0, jnp.stack([mine, theirs], axis=axis), jnp.stack([theirs, mine], axis=axis)
         )
 
-    both = jnp.concatenate([queries, grad_out], axis=1)
-
-    def piece_for(peer):
-        return lax.dynamic_slice_in_dim(both, lax.rem(peer, nz) * part, part, 0)
-
-    pieces = [piece_for(z)] + [along_z(piece_for(z + by), by) for by in range(1, nz)]
+    both = jnp.concatenate([queries, grad_out], axis=1).reshape(PEERS, part, 2 * width)
+    half = lax.div(z, apart)
+    pieces = [jnp.where(half == 0, both[0], both[1]), peer(jnp.where(half == 0, both[1], both[0]))]
+
     docs = jnp.broadcast_to(low(block_docs)[:, None], (DOC_ROWS, HEAD))
     k_rows, v_rows = jnp.concatenate([keys, docs]), jnp.concatenate([values, docs])
     kept = jnp.where(core == 0, k_rows, v_rows)
     given = jnp.where(core == 0, v_rows, k_rows)
-    unit = in_order(core, kept, other_core(given), 0)
-    unit = in_order(y, unit, other_y(unit), 1)
+    near = in_order(core, kept, other_core(given), 0)
+    far = in_order(core, other_y(kept), diagonal(given), 0)
+    unit = in_order(y, near, far, 1)
     unit = jnp.concatenate(
         [unit[:, :, :BLOCK].reshape(4 * BLOCK, HEAD), unit[:, :, BLOCK : BLOCK + 4].reshape(DOC_ROWS, HEAD)]
     )
@@ -263,22 +268,22 @@
         totals[by] = low(added([keep[by], other_core(send[by])]))
     arrived = [along_second(totals[by], by) for by in range(1, lines)]
     dq, totals[0] = lax.optimization_barrier((dq, totals[0]))
-    returned = [dq[0]] + [along_z(dq[by], -by) for by in range(1, nz)]
+    returned = peer(dq[1])
     arrived, returned = lax.optimization_barrier((arrived, returned))
     total = low(added([totals[0]] + arrived))
     total = low(added([total[0]] + [along_first(total[by], by) for by in range(1, lines)]))
     total = total.reshape(2, 2, BLOCK, HEAD)
-    ours = jnp.where(y == 0, total[:, 0], total[:, 1])
-    far = jnp.where(y == 0, total[:, 1], total[:, 0])
-    total = added([ours, other_y(far)])
-    total = low(jnp.where(core == 0, SCALE * total, total))
-    mine = jnp.where(core == 0, total[0], total[1])
-    theirs = other_core(jnp.where(core == 0, total[1], total[0]))
-    grad_keys = jnp.where(core == 0, mine, theirs)
-    grad_values = jnp.where(core == 0, theirs, mine)
-
-    order = lax.rem(jnp.arange(nz) - z + nz, nz)
-    grad_queries = jnp.take(jnp.stack(returned), order, axis=0).reshape(rows, width)
+
+    def block_at(other_of_core, other_of_y):
+        c = 1 - core if other_of_core else core
+        row = 1 - y if other_of_y else y
+        return lax.dynamic_slice(total, (c, row, 0, 0), (1, 1, BLOCK, HEAD))[0, 0]
+
+    first = added([block_at(False, False), other_y(block_at(False, True))])
+    second = added([other_core(block_at(True, False)), diagonal(block_at(True, True))])
+    grad_keys = low(SCALE * jnp.where(core == 0, first, second))
+    grad_values = low(jnp.where(core == 0, second, first))
+    grad_queries = in_order(half, dq[0], returned, 0).reshape(rows, width)
     return grad_queries, grad_keys, grad_values
 
 

time: 103 us -> 93.2 us (0.905)
  Pallas kernels: 16.4 us -> 11.2 us
  waiting for transfers between devices: 38.3 us -> 34.4 us
  starting transfers between devices: 39.8 us -> 41.5 us
  local copies, waits for them, and re-layouts: 2.84 us -> 1.16 us
    pallas_call x1, Pallas kernels: 16.4 us -> 11.2 us  [grads_call(): pl.pallas_call(lambda *refs: attention_grads(sizes, *refs), name='attenti...]
    ppermute x30 -> x28, waiting for transfers between devices: 38.3 us -> 34.4 us  [moved(): return lax.ppermute(value, CONTEXT, hops)]
    ppermute x30 -> x28, starting transfers between devices: 39.8 us -> 41.5 us  [moved(): return lax.ppermute(value, CONTEXT, hops)]
  transfers between devices with their start and end apart: 30 -> 28, of which waited for: 16 -> 12; matrix products, arithmetic and copies ran while one was open for 3% -> 3% of each run, Pallas kernels for 0% -> 0%
where the time goes in v5:
time: 93.2 us
  starting transfers between devices  41.5 us (45%)
  waiting for transfers between devices  34.4 us (37%)
  Pallas kernels  11.2 us (12%)
  other arithmetic  3.39 us (4%)
  between operations  1.52 us (2%)
  local copies, waits for them, and re-layouts  1.16 us (1%)
    ppermute x28, starting transfers between devices, moved(): return lax.ppermute(value, CONTEXT, hops)  41.5 us
    ppermute x28, waiting for transfers between devices, moved(): return lax.ppermute(value, CONTEXT, hops)  34.4 us
    pallas_call x1, Pallas kernels, grads_call(): pl.pallas_call(lambda *refs: attention_grads(sizes, *refs), name='attenti...  11.2 us
  transfers between devices with their start and end apart: 28, of which 12 were waited for; matrix products, arithmetic and copies ran while one was open for 3% of the time, Pallas kernels for 0%

profile of v5, /device:TPU:1, one launch (start us, length us, event | category | flops | bytes accessed | tf_op | source)
XLA Modules:
  0.0 93.2 jit_solution(9562051415883837045)
XLA Ops:
  1.3 0.8 broadcast_select_fusion.3
  2.1 1.5 %collective-permute-start = (bf16[144,128]{1,0:T(8,128)(2,1)S(1)}, bf16[144,128]{1,0:T(8,128)(2,1)S(1)}, u32[]{:S(2)}, u32[]{:S(2)}) collective-permute-start(bf16[144,128]{1,0:T(8,128)(2,1)S(1)} %get-tuple-element.58), channel_id=1, source_target_pairs={{0,16},{2,18},{4,20},{6,22},{8,24},{10,26},{12,28},{14,30},{16,0},... | collective-permute-start | bytes 110600 | tf_op jit(solution)/shard_map/ppermute | solution.py:216
  3.6 1.4 %collective-permute-start.2 = (bf16[144,128]{1,0:T(8,128)(2,1)S(1)}, bf16[144,128]{1,0:T(8,128)(2,1)S(1)}, u32[]{:S(2)}, u32[]{:S(2)}) collective-permute-start(bf16[144,128]{1,0:T(8,128)(2,1)S(1)} %get-tuple-element.58), channel_id=1, source_target_pairs={{0,18},{2,16},{4,22},{6,20},{8,26},{10,24},{12,30},{14,28},{16,2},... | collective-permute-start | bytes 110600 | tf_op jit(solution)/shard_map/ppermute | solution.py:216
  4.9 1.0 %constant_dynamic-update-slice_fusion.1 = bf16[128,2048]{1,0:T(8,128)(2,1)S(1)} fusion(bf16[128,1024]{1,0:T(8,128)(2,1)} %param.5), kind=kLoop, calls=%fused_computation.38 | loop fusion | bytes 524288
  6.0 3.7 %collective-permute-start.6 = (bf16[64,2048]{1,0:T(8,128)(2,1)S(1)}, bf16[64,2048]{1,0:T(8,128)(2,1)S(1)}, u32[]{:S(2)}, u32[]{:S(2)}) collective-permute-start(bf16[64,2048]{1,0:T(8,128)(2,1)S(1)} %get-tuple-element.42), channel_id=1, source_target_pairs={{0,64},{2,66},{4,68},{6,70},{8,72},{10,74},{12,76},{14,78},{16,80}... | collective-permute-start | bytes 786440 | tf_op jit(solution)/shard_map/ppermute | solution.py:216
  9.7 0.2 collective-permute-start.1
  9.9 2.9 %collective-permute-done.1 = bf16[144,128]{1,0:T(8,128)(2,1)S(1)} collective-permute-done((bf16[144,128]{1,0:T(8,128)(2,1)S(1)}, bf16[144,128]{1,0:T(8,128)(2,1)S(1)}, u32[]{:S(2)}, u32[]{:S(2)}) %collective-permute-start.1) | collective-permute-done | bytes 36896 | tf_op jit(solution)/shard_map/ppermute | solution.py:216
  12.9 1.3 %collective-permute-start.3 = (bf16[528,128]{1,0:T(8,128)(2,1)S(1)}, bf16[528,128]{1,0:T(8,128)(2,1)S(1)}, u32[]{:S(2)}, u32[]{:S(2)}) collective-permute-start(bf16[528,128]{1,0:T(8,128)(2,1)S(1)} %get-tuple-element.53), channel_id=1, source_target_pairs={{0,32},{2,34},{4,36},{6,38},{8,40},{10,42},{12,44},{14,46},{16,20}... | collective-permute-start | bytes 405512 | tf_op jit(solution)/shard_map/ppermute | solution.py:216
  14.2 2.5 %collective-permute-start.4 = (bf16[528,128]{1,0:T(8,128)(2,1)S(1)}, bf16[528,128]{1,0:T(8,128)(2,1)S(1)}, u32[]{:S(2)}, u32[]{:S(2)}) collective-permute-start(bf16[528,128]{1,0:T(8,128)(2,1)S(1)} %get-tuple-element.53), channel_id=1, source_target_pairs={{0,64},{2,66},{4,68},{6,70},{8,72},{10,74},{12,76},{14,78},{16,24}... | collective-permute-start | bytes 405512 | tf_op jit(solution)/shard_map/ppermute | solution.py:216
  16.7 1.2 %collective-permute-start.5 = (bf16[528,128]{1,0:T(8,128)(2,1)S(1)}, bf16[528,128]{1,0:T(8,128)(2,1)S(1)}, u32[]{:S(2)}, u32[]{:S(2)}) collective-permute-start(bf16[528,128]{1,0:T(8,128)(2,1)S(1)} %get-tuple-element.53), channel_id=1, source_target_pairs={{0,96},{2,98},{4,100},{6,102},{8,104},{10,106},{12,108},{14,110},{... | collective-permute-start | bytes 405512 | tf_op jit(solution)/shard_map/ppermute | solution.py:216
  17.8 0.3 collective-permute-done.3
  18.1 2.7 %collective-permute-done.4 = bf16[528,128]{1,0:T(8,128)(2,1)S(1)} collective-permute-done((bf16[528,128]{1,0:T(8,128)(2,1)S(1)}, bf16[528,128]{1,0:T(8,128)(2,1)S(1)}, u32[]{:S(2)}, u32[]{:S(2)}) %collective-permute-start.4) | collective-permute-done | bytes 135200 | tf_op jit(solution)/shard_map/ppermute | solution.py:216
  20.9 0.8 collective-permute-start.7
  21.7 0.3 collective-permute-start.8
  22.0 2.2 %collective-permute-start.9 = (bf16[4,528,128]{2,1,0:T(8,128)(2,1)S(1)}, bf16[4,528,128]{2,1,0:T(8,128)(2,1)S(1)}, u32[]{:S(2)}, u32[]{:S(2)}) collective-permute-start(bf16[4,528,128]{2,1,0:T(8,128)(2,1)S(1)} %pad_maximum_fusion.refs_3_), channel_id=1, source_target_pairs={{0,12},{2,14},{4,0},{6,2},{8,4},{10,6},{12,8},{14,10},{16,112},{18... | collective-permute-start | bytes 1622024 | tf_op jit(solution)/shard_map/ppermute | solution.py:216
  24.2 4.7 %collective-permute-start.10 = (bf16[4,528,128]{2,1,0:T(8,128)(2,1)S(1)}, bf16[4,528,128]{2,1,0:T(8,128)(2,1)S(1)}, u32[]{:S(2)}, u32[]{:S(2)}) collective-permute-start(bf16[4,528,128]{2,1,0:T(8,128)(2,1)S(1)} %pad_maximum_fusion.refs_3_), channel_id=1, source_target_pairs={{0,16},{2,18},{4,20},{6,22},{8,24},{10,26},{12,28},{14,30},{16,0},... | collective-permute-start | bytes 1622024 | tf_op jit(solution)/shard_map/ppermute | solution.py:216
  28.9 7.6 %collective-permute-done.7.refs_4_ = bf16[4,528,128]{2,1,0:T(8,128)(2,1)S(1)} collective-permute-done((bf16[4,528,128]{2,1,0:T(8,128)(2,1)S(1)}, bf16[4,528,128]{2,1,0:T(8,128)(2,1)S(1)}, u32[]{:S(2)}, u32[]{:S(2)}) %collective-permute-start.7) | collective-permute-done | bytes 540704 | tf_op jit(solution)/shard_map/ppermute | solution.py:216
  36.5 4.1 %collective-permute-start.12 = (bf16[4,528,128]{2,1,0:T(8,128)(2,1)S(1)}, bf16[4,528,128]{2,1,0:T(8,128)(2,1)S(1)}, u32[]{:S(2)}, u32[]{:S(2)}) collective-permute-start(bf16[4,528,128]{2,1,0:T(8,128)(2,1)S(1)} %collective-permute-done.8.refs_5_), channel_id=1, source_target_pairs={{0,16},{2,18},{4,20},{6,22},{8,24},{10,26},{12,28},{14,30},{16,0},... | collective-permute-start | bytes 1622024 | tf_op jit(solution)/shard_map/ppermute | solution.py:216
  40.8 1.3 %collective-permute-done.12.refs_9_ = bf16[4,528,128]{2,1,0:T(8,128)(2,1)S(1)} collective-permute-done((bf16[4,528,128]{2,1,0:T(8,128)(2,1)S(1)}, bf16[4,528,128]{2,1,0:T(8,128)(2,1)S(1)}, u32[]{:S(2)}, u32[]{:S(2)}) %collective-permute-start.12) | collective-permute-done | bytes 540704 | tf_op jit(solution)/shard_map/ppermute | solution.py:216
  42.2 0.8 collective-permute-done.13.refs_10_
  42.9 11.2 %attention_grads.1 = (bf16[2,64,1024]{2,1,0:T(8,128)(2,1)S(1)}, bf16[4,2,256,128]{3,2,1,0:T(8,128)(2,1)S(1)}, bf16[4,2,256,128]{3,2,1,0:T(8,128)(2,1)S(1)}, bf16...) custom-call(s32[4]{0:T(128)S(1)} %pad_add_fusion.refs_0_, ...), custom_call_target="tpu_custom_call" | custom-call | flops 3355443200 | bytes 16777216 | tf_op jit(solution)/shard_map/attention_grads/pallas_call | solution.py:163
  54.2 0.1 collective-permute-start.19
  54.3 0.5 collective-permute-start.17
  54.8 0.1 collective-permute-start.14
  54.9 0.4 collective-permute-start.15
  55.3 0.9 collective-permute-done.19
  56.2 0.1 add_convert_fusion.1
  56.3 6.7 %collective-permute-start.20 = (bf16[4,2,256,128]{3,2,1,0:T(8,128)(2,1)S(1)}, bf16[4,2,256,128]{3,2,1,0:T(8,128)(2,1)S(1)}, u32[]{:S(2)}, u32[]{:S(2)}) collective-permute-start(bf16[4,2,256,128]{3,2,1,0:T(8,128)(2,1)S(1)} %add_convert_fusion.1), channel_id=1, source_target_pairs={{0,12},{2,14},{4,0},{6,2},{8,4},{10,6},{12,8},{14,10},{16,112},{18... | collective-permute-start | bytes 1572872 | tf_op jit(solution)/shard_map/ppermute | solution.py:216
  63.0 0.1 add_convert_fusion.2
  63.2 0.1 collective-permute-start.18
  63.3 0.1 add_convert_fusion.3
  63.4 1.2 %collective-permute-start.16 = (bf16[4,2,256,128]{3,2,1,0:T(8,128)(2,1)S(1)}, bf16[4,2,256,128]{3,2,1,0:T(8,128)(2,1)S(1)}, u32[]{:S(2)}, u32[]{:S(2)}) collective-permute-start(bf16[4,2,256,128]{3,2,1,0:T(8,128)(2,1)S(1)} %add_convert_fusion.3), channel_id=1, source_target_pairs={{0,4},{2,6},{4,8},{6,10},{8,12},{10,14},{12,0},{14,2},{16,48},{18,... | collective-permute-start | bytes 1572872 | tf_op jit(solution)/shard_map/ppermute | solution.py:216
  64.6 0.1 add_convert_fusion.4
  64.7 2.1 %collective-permute-start.21 = (bf16[64,1024]{1,0:T(8,128)(2,1)S(1)}, bf16[64,1024]{1,0:T(8,128)(2,1)S(1)}, u32[]{:S(2)}, u32[]{:S(2)}) collective-permute-start(bf16[64,1024]{1,0:T(8,128)(2,1)S(1)} %get-tuple-element.45), channel_id=1, source_target_pairs={{0,64},{2,66},{4,68},{6,70},{8,72},{10,74},{12,76},{14,78},{16,80}... | collective-permute-start | bytes 393224 | tf_op jit(solution)/shard_map/ppermute | solution.py:216
  66.9 13.0 %collective-permute-done.21 = bf16[64,1024]{1,0:T(8,128)(2,1)S(1)} collective-permute-done((bf16[64,1024]{1,0:T(8,128)(2,1)S(1)}, bf16[64,1024]{1,0:T(8,128)(2,1)S(1)}, u32[]{:S(2)}, u32[]{:S(2)}) %collective-permute-start.21) | collective-permute-done | bytes 131104 | tf_op jit(solution)/shard_map/ppermute | solution.py:216
  79.9 0.3 add_convert_fusion
  80.2 1.1 %collective-permute-start.22 = (bf16[2,256,128]{2,1,0:T(8,128)(2,1)S(1)}, bf16[2,256,128]{2,1,0:T(8,128)(2,1)S(1)}, u32[]{:S(2)}, u32[]{:S(2)}) collective-permute-start(bf16[2,256,128]{2,1,0:T(8,128)(2,1)S(1)} %get-tuple-element.39), channel_id=1, source_target_pairs={{0,32},{2,34},{4,36},{6,38},{8,40},{10,42},{12,44},{14,46},{16,20}... | collective-permute-start | bytes 393224 | tf_op jit(solution)/shard_map/ppermute | solution.py:216
  81.2 2.4 %collective-permute-start.23 = (bf16[2,256,128]{2,1,0:T(8,128)(2,1)S(1)}, bf16[2,256,128]{2,1,0:T(8,128)(2,1)S(1)}, u32[]{:S(2)}, u32[]{:S(2)}) collective-permute-start(bf16[2,256,128]{2,1,0:T(8,128)(2,1)S(1)} %get-tuple-element.41), channel_id=1, source_target_pairs={{0,64},{2,66},{4,68},{6,70},{8,72},{10,74},{12,76},{14,78},{16,24}... | collective-permute-start | bytes 393224 | tf_op jit(solution)/shard_map/ppermute | solution.py:216
  83.6 0.6 collective-permute-start.24
  84.2 1.1 %collective-permute-done.22 = bf16[2,256,128]{2,1,0:T(8,128)(2,1)S(1)} collective-permute-done((bf16[2,256,128]{2,1,0:T(8,128)(2,1)S(1)}, bf16[2,256,128]{2,1,0:T(8,128)(2,1)S(1)}, u32[]{:S(2)}, u32[]{:S(2)}) %collective-permute-start.22) | collective-permute-done | bytes 131104 | tf_op jit(solution)/shard_map/ppermute | solution.py:216
  85.3 2.2 %collective-permute-done.23 = bf16[2,256,128]{2,1,0:T(8,128)(2,1)S(1)} collective-permute-done((bf16[2,256,128]{2,1,0:T(8,128)(2,1)S(1)}, bf16[2,256,128]{2,1,0:T(8,128)(2,1)S(1)}, u32[]{:S(2)}, u32[]{:S(2)}) %collective-permute-start.23) | collective-permute-done | bytes 131104 | tf_op jit(solution)/shard_map/ppermute | solution.py:216
  87.5 0.2 collective-permute-done.24
  87.8 0.2 collective-permute-start.25
  88.1 1.1 %collective-permute-start.26 = (bf16[128,128]{1,0:T(8,128)(2,1)S(1)}, bf16[128,128]{1,0:T(8,128)(2,1)S(1)}, u32[]{:S(2)}, u32[]{:S(2)}) collective-permute-start(bf16[128,128]{1,0:T(8,128)(2,1)S(1)} %get-tuple-element.56), channel_id=1, source_target_pairs={{0,16},{2,18},{4,20},{6,22},{8,24},{10,26},{12,28},{14,30},{16,0},... | collective-permute-start | bytes 98312 | tf_op jit(solution)/shard_map/ppermute | solution.py:216
  89.2 1.2 %collective-permute-start.27 = (bf16[128,128]{1,0:T(8,128)(2,1)S(1)}, bf16[128,128]{1,0:T(8,128)(2,1)S(1)}, u32[]{:S(2)}, u32[]{:S(2)}) collective-permute-start(bf16[128,128]{1,0:T(8,128)(2,1)S(1)} %get-tuple-element.55), channel_id=1, source_target_pairs={{0,18},{2,16},{4,22},{6,20},{8,26},{10,24},{12,30},{14,28},{16,2},... | collective-permute-start | bytes 98312 | tf_op jit(solution)/shard_map/ppermute | solution.py:216
  90.4 0.7 maximum_select_fusion
  91.1 1.4 %collective-permute-done.27 = bf16[128,128]{1,0:T(8,128)(2,1)S(1)} collective-permute-done((bf16[128,128]{1,0:T(8,128)(2,1)S(1)}, bf16[128,128]{1,0:T(8,128)(2,1)S(1)}, u32[]{:S(2)}, u32[]{:S(2)}) %collective-permute-start.27) | collective-permute-done | bytes 32800 | tf_op jit(solution)/shard_map/ppermute | solution.py:216
  92.5 0.7 select_convert_fusion
  (37 shorter events, 0.6 us)
Async XLA Ops:
  2.1 7.8 %collective-permute-start = (bf16[144,128]{1,0:T(8,128)(2,1)S(1)}, bf16[144,128]{1,0:T(8,128)(2,1)S(1)}, u32[]{:S(2)}, u32[]{:S(2)}) collective-permute-start(bf16[144,128]{1,0:T(8,128)(2,1)S(1)} %get-tuple-element.58), channel_id=1, source_target_pairs={{0,16},{2,18},{4,20},{6,22},{8,24},{10,26},{12,28},{14,30},{16,0},... | collective-permute-start | bytes 110600 | tf_op jit(solution)/shard_map/ppermute | solution.py:216
  3.6 9.2 %collective-permute-start.2 = (bf16[144,128]{1,0:T(8,128)(2,1)S(1)}, bf16[144,128]{1,0:T(8,128)(2,1)S(1)}, u32[]{:S(2)}, u32[]{:S(2)}) collective-permute-start(bf16[144,128]{1,0:T(8,128)(2,1)S(1)} %get-tuple-element.58), channel_id=1, source_target_pairs={{0,18},{2,16},{4,22},{6,20},{8,26},{10,24},{12,30},{14,28},{16,2},... | collective-permute-start | bytes 110600 | tf_op jit(solution)/shard_map/ppermute | solution.py:216
  4.9 1.0 %copy-start = (bf16[128,1024]{1,0:T(8,128)(2,1)S(1)}, bf16[128,1024]{1,0:T(8,128)(2,1)}, u32[]{:S(2)}) copy-start(bf16[128,1024]{1,0:T(8,128)(2,1)} %param.8) | copy-start | bytes 786436
  6.0 14.8 %collective-permute-start.6 = (bf16[64,2048]{1,0:T(8,128)(2,1)S(1)}, bf16[64,2048]{1,0:T(8,128)(2,1)S(1)}, u32[]{:S(2)}, u32[]{:S(2)}) collective-permute-start(bf16[64,2048]{1,0:T(8,128)(2,1)S(1)} %get-tuple-element.42), channel_id=1, source_target_pairs={{0,64},{2,66},{4,68},{6,70},{8,72},{10,74},{12,76},{14,78},{16,80}... | collective-permute-start | bytes 786440 | tf_op jit(solution)/shard_map/ppermute | solution.py:216
  9.7 3.1 %collective-permute-start.1 = (bf16[144,128]{1,0:T(8,128)(2,1)S(1)}, bf16[144,128]{1,0:T(8,128)(2,1)S(1)}, u32[]{:S(2)}, u32[]{:S(2)}) collective-permute-start(bf16[144,128]{1,0:T(8,128)(2,1)S(1)} %get-tuple-element.57), channel_id=1, source_target_pairs={{0,2},{2,0},{4,6},{6,4},{8,10},{10,8},{12,14},{14,12},{16,18},{18,... | collective-permute-start | bytes 110600 | tf_op jit(solution)/shard_map/ppermute | solution.py:216
  12.9 5.1 %collective-permute-start.3 = (bf16[528,128]{1,0:T(8,128)(2,1)S(1)}, bf16[528,128]{1,0:T(8,128)(2,1)S(1)}, u32[]{:S(2)}, u32[]{:S(2)}) collective-permute-start(bf16[528,128]{1,0:T(8,128)(2,1)S(1)} %get-tuple-element.53), channel_id=1, source_target_pairs={{0,32},{2,34},{4,36},{6,38},{8,40},{10,42},{12,44},{14,46},{16,20}... | collective-permute-start | bytes 405512 | tf_op jit(solution)/shard_map/ppermute | solution.py:216
  14.2 6.6 %collective-permute-start.4 = (bf16[528,128]{1,0:T(8,128)(2,1)S(1)}, bf16[528,128]{1,0:T(8,128)(2,1)S(1)}, u32[]{:S(2)}, u32[]{:S(2)}) collective-permute-start(bf16[528,128]{1,0:T(8,128)(2,1)S(1)} %get-tuple-element.53), channel_id=1, source_target_pairs={{0,64},{2,66},{4,68},{6,70},{8,72},{10,74},{12,76},{14,78},{16,24}... | collective-permute-start | bytes 405512 | tf_op jit(solution)/shard_map/ppermute | solution.py:216
  16.7 4.2 %collective-permute-start.5 = (bf16[528,128]{1,0:T(8,128)(2,1)S(1)}, bf16[528,128]{1,0:T(8,128)(2,1)S(1)}, u32[]{:S(2)}, u32[]{:S(2)}) collective-permute-start(bf16[528,128]{1,0:T(8,128)(2,1)S(1)} %get-tuple-element.53), channel_id=1, source_target_pairs={{0,96},{2,98},{4,100},{6,102},{8,104},{10,106},{12,108},{14,110},{... | collective-permute-start | bytes 405512 | tf_op jit(solution)/shard_map/ppermute | solution.py:216
  20.9 15.6 %collective-permute-start.7 = (bf16[4,528,128]{2,1,0:T(8,128)(2,1)S(1)}, bf16[4,528,128]{2,1,0:T(8,128)(2,1)S(1)}, u32[]{:S(2)}, u32[]{:S(2)}) collective-permute-start(bf16[4,528,128]{2,1,0:T(8,128)(2,1)S(1)} %pad_maximum_fusion.refs_3_), channel_id=1, source_target_pairs={{0,4},{2,6},{4,8},{6,10},{8,12},{10,14},{12,0},{14,2},{16,48},{18,... | collective-permute-start | bytes 1622024 | tf_op jit(solution)/shard_map/ppermute | solution.py:216
  21.7 14.8 %collective-permute-start.8 = (bf16[4,528,128]{2,1,0:T(8,128)(2,1)S(1)}, bf16[4,528,128]{2,1,0:T(8,128)(2,1)S(1)}, u32[]{:S(2)}, u32[]{:S(2)}) collective-permute-start(bf16[4,528,128]{2,1,0:T(8,128)(2,1)S(1)} %pad_maximum_fusion.refs_3_), channel_id=1, source_target_pairs={{0,8},{2,10},{4,12},{6,14},{8,0},{10,2},{12,4},{14,6},{16,80},{18,... | collective-permute-start | bytes 1622024 | tf_op jit(solution)/shard_map/ppermute | solution.py:216
  22.0 18.6 %collective-permute-start.9 = (bf16[4,528,128]{2,1,0:T(8,128)(2,1)S(1)}, bf16[4,528,128]{2,1,0:T(8,128)(2,1)S(1)}, u32[]{:S(2)}, u32[]{:S(2)}) collective-permute-start(bf16[4,528,128]{2,1,0:T(8,128)(2,1)S(1)} %pad_maximum_fusion.refs_3_), channel_id=1, source_target_pairs={{0,12},{2,14},{4,0},{6,2},{8,4},{10,6},{12,8},{14,10},{16,112},{18... | collective-permute-start | bytes 1622024 | tf_op jit(solution)/shard_map/ppermute | solution.py:216
  24.2 16.6 %collective-permute-start.10 = (bf16[4,528,128]{2,1,0:T(8,128)(2,1)S(1)}, bf16[4,528,128]{2,1,0:T(8,128)(2,1)S(1)}, u32[]{:S(2)}, u32[]{:S(2)}) collective-permute-start(bf16[4,528,128]{2,1,0:T(8,128)(2,1)S(1)} %pad_maximum_fusion.refs_3_), channel_id=1, source_target_pairs={{0,16},{2,18},{4,20},{6,22},{8,24},{10,26},{12,28},{14,30},{16,0},... | collective-permute-start | bytes 1622024 | tf_op jit(solution)/shard_map/ppermute | solution.py:216
  36.5 4.3 %collective-permute-start.11 = (bf16[4,528,128]{2,1,0:T(8,128)(2,1)S(1)}, bf16[4,528,128]{2,1,0:T(8,128)(2,1)S(1)}, u32[]{:S(2)}, u32[]{:S(2)}) collective-permute-start(bf16[4,528,128]{2,1,0:T(8,128)(2,1)S(1)} %collective-permute-done.7.refs_4_), channel_id=1, source_target_pairs={{0,16},{2,18},{4,20},{6,22},{8,24},{10,26},{12,28},{14,30},{16,0},... | collective-permute-start | bytes 1622024 | tf_op jit(solution)/shard_map/ppermute | solution.py:216
  36.5 5.7 %collective-permute-start.12 = (bf16[4,528,128]{2,1,0:T(8,128)(2,1)S(1)}, bf16[4,528,128]{2,1,0:T(8,128)(2,1)S(1)}, u32[]{:S(2)}, u32[]{:S(2)}) collective-permute-start(bf16[4,528,128]{2,1,0:T(8,128)(2,1)S(1)} %collective-permute-done.8.refs_5_), channel_id=1, source_target_pairs={{0,16},{2,18},{4,20},{6,22},{8,24},{10,26},{12,28},{14,30},{16,0},... | collective-permute-start | bytes 1622024 | tf_op jit(solution)/shard_map/ppermute | solution.py:216
  40.6 2.3 %collective-permute-start.13 = (bf16[4,528,128]{2,1,0:T(8,128)(2,1)S(1)}, bf16[4,528,128]{2,1,0:T(8,128)(2,1)S(1)}, u32[]{:S(2)}, u32[]{:S(2)}) collective-permute-start(bf16[4,528,128]{2,1,0:T(8,128)(2,1)S(1)} %collective-permute-done.9.refs_6_), channel_id=1, source_target_pairs={{0,16},{2,18},{4,20},{6,22},{8,24},{10,26},{12,28},{14,30},{16,0},... | collective-permute-start | bytes 1622024 | tf_op jit(solution)/shard_map/ppermute | solution.py:216
  54.2 2.0 %collective-permute-start.19 = (bf16[4,2,256,128]{3,2,1,0:T(8,128)(2,1)S(1)}, bf16[4,2,256,128]{3,2,1,0:T(8,128)(2,1)S(1)}, u32[]{:S(2)}, u32[]{:S(2)}) collective-permute-start(bf16[4,2,256,128]{3,2,1,0:T(8,128)(2,1)S(1)} %get-tuple-element.33), channel_id=1, source_target_pairs={{0,16},{2,18},{4,20},{6,22},{8,24},{10,26},{12,28},{14,30},{16,0},... | collective-permute-start | bytes 1572872 | tf_op jit(solution)/shard_map/ppermute | solution.py:216
  54.3 8.8 %collective-permute-start.17 = (bf16[4,2,256,128]{3,2,1,0:T(8,128)(2,1)S(1)}, bf16[4,2,256,128]{3,2,1,0:T(8,128)(2,1)S(1)}, u32[]{:S(2)}, u32[]{:S(2)}) collective-permute-start(bf16[4,2,256,128]{3,2,1,0:T(8,128)(2,1)S(1)} %get-tuple-element.31), channel_id=1, source_target_pairs={{0,16},{2,18},{4,20},{6,22},{8,24},{10,26},{12,28},{14,30},{16,0},... | collective-permute-start | bytes 1572872 | tf_op jit(solution)/shard_map/ppermute | solution.py:216
  54.8 9.8 %collective-permute-start.14 = (bf16[4,2,256,128]{3,2,1,0:T(8,128)(2,1)S(1)}, bf16[4,2,256,128]{3,2,1,0:T(8,128)(2,1)S(1)}, u32[]{:S(2)}, u32[]{:S(2)}) collective-permute-start(bf16[4,2,256,128]{3,2,1,0:T(8,128)(2,1)S(1)} %get-tuple-element.26), channel_id=1, source_target_pairs={{0,16},{2,18},{4,20},{6,22},{8,24},{10,26},{12,28},{14,30},{16,0},... | collective-permute-start | bytes 1572872 | tf_op jit(solution)/shard_map/ppermute | solution.py:216
  54.9 8.4 %collective-permute-start.15 = (bf16[4,2,256,128]{3,2,1,0:T(8,128)(2,1)S(1)}, bf16[4,2,256,128]{3,2,1,0:T(8,128)(2,1)S(1)}, u32[]{:S(2)}, u32[]{:S(2)}) collective-permute-start(bf16[4,2,256,128]{3,2,1,0:T(8,128)(2,1)S(1)} %get-tuple-element.29), channel_id=1, source_target_pairs={{0,16},{2,18},{4,20},{6,22},{8,24},{10,26},{12,28},{14,30},{16,0},... | collective-permute-start | bytes 1572872 | tf_op jit(solution)/shard_map/ppermute | solution.py:216
  56.3 23.5 %collective-permute-start.20 = (bf16[4,2,256,128]{3,2,1,0:T(8,128)(2,1)S(1)}, bf16[4,2,256,128]{3,2,1,0:T(8,128)(2,1)S(1)}, u32[]{:S(2)}, u32[]{:S(2)}) collective-permute-start(bf16[4,2,256,128]{3,2,1,0:T(8,128)(2,1)S(1)} %add_convert_fusion.1), channel_id=1, source_target_pairs={{0,12},{2,14},{4,0},{6,2},{8,4},{10,6},{12,8},{14,10},{16,112},{18... | collective-permute-start | bytes 1572872 | tf_op jit(solution)/shard_map/ppermute | solution.py:216
  63.2 16.7 %collective-permute-start.18 = (bf16[4,2,256,128]{3,2,1,0:T(8,128)(2,1)S(1)}, bf16[4,2,256,128]{3,2,1,0:T(8,128)(2,1)S(1)}, u32[]{:S(2)}, u32[]{:S(2)}) collective-permute-start(bf16[4,2,256,128]{3,2,1,0:T(8,128)(2,1)S(1)} %add_convert_fusion.2), channel_id=1, source_target_pairs={{0,8},{2,10},{4,12},{6,14},{8,0},{10,2},{12,4},{14,6},{16,80},{18,... | collective-permute-start | bytes 1572872 | tf_op jit(solution)/shard_map/ppermute | solution.py:216
  63.4 16.4 %collective-permute-start.16 = (bf16[4,2,256,128]{3,2,1,0:T(8,128)(2,1)S(1)}, bf16[4,2,256,128]{3,2,1,0:T(8,128)(2,1)S(1)}, u32[]{:S(2)}, u32[]{:S(2)}) collective-permute-start(bf16[4,2,256,128]{3,2,1,0:T(8,128)(2,1)S(1)} %add_convert_fusion.3), channel_id=1, source_target_pairs={{0,4},{2,6},{4,8},{6,10},{8,12},{10,14},{12,0},{14,2},{16,48},{18,... | collective-permute-start | bytes 1572872 | tf_op jit(solution)/shard_map/ppermute | solution.py:216
  64.7 15.1 %collective-permute-start.21 = (bf16[64,1024]{1,0:T(8,128)(2,1)S(1)}, bf16[64,1024]{1,0:T(8,128)(2,1)S(1)}, u32[]{:S(2)}, u32[]{:S(2)}) collective-permute-start(bf16[64,1024]{1,0:T(8,128)(2,1)S(1)} %get-tuple-element.45), channel_id=1, source_target_pairs={{0,64},{2,66},{4,68},{6,70},{8,72},{10,74},{12,76},{14,78},{16,80}... | collective-permute-start | bytes 393224 | tf_op jit(solution)/shard_map/ppermute | solution.py:216
  80.2 5.1 %collective-permute-start.22 = (bf16[2,256,128]{2,1,0:T(8,128)(2,1)S(1)}, bf16[2,256,128]{2,1,0:T(8,128)(2,1)S(1)}, u32[]{:S(2)}, u32[]{:S(2)}) collective-permute-start(bf16[2,256,128]{2,1,0:T(8,128)(2,1)S(1)} %get-tuple-element.39), channel_id=1, source_target_pairs={{0,32},{2,34},{4,36},{6,38},{8,40},{10,42},{12,44},{14,46},{16,20}... | collective-permute-start | bytes 393224 | tf_op jit(solution)/shard_map/ppermute | solution.py:216
  81.2 6.3 %collective-permute-start.23 = (bf16[2,256,128]{2,1,0:T(8,128)(2,1)S(1)}, bf16[2,256,128]{2,1,0:T(8,128)(2,1)S(1)}, u32[]{:S(2)}, u32[]{:S(2)}) collective-permute-start(bf16[2,256,128]{2,1,0:T(8,128)(2,1)S(1)} %get-tuple-element.41), channel_id=1, source_target_pairs={{0,64},{2,66},{4,68},{6,70},{8,72},{10,74},{12,76},{14,78},{16,24}... | collective-permute-start | bytes 393224 | tf_op jit(solution)/shard_map/ppermute | solution.py:216
  83.6 4.1 %collective-permute-start.24 = (bf16[2,256,128]{2,1,0:T(8,128)(2,1)S(1)}, bf16[2,256,128]{2,1,0:T(8,128)(2,1)S(1)}, u32[]{:S(2)}, u32[]{:S(2)}) collective-permute-start(bf16[2,256,128]{2,1,0:T(8,128)(2,1)S(1)} %get-tuple-element.40), channel_id=1, source_target_pairs={{0,96},{2,98},{4,100},{6,102},{8,104},{10,106},{12,108},{14,110},{... | collective-permute-start | bytes 393224 | tf_op jit(solution)/shard_map/ppermute | solution.py:216
  87.8 3.3 %collective-permute-start.25 = (bf16[128,128]{1,0:T(8,128)(2,1)S(1)}, bf16[128,128]{1,0:T(8,128)(2,1)S(1)}, u32[]{:S(2)}, u32[]{:S(2)}) collective-permute-start(bf16[128,128]{1,0:T(8,128)(2,1)S(1)} %get-tuple-element.54), channel_id=1, source_target_pairs={{0,2},{2,0},{4,6},{6,4},{8,10},{10,8},{12,14},{14,12},{16,18},{18,... | collective-permute-start | bytes 98312 | tf_op jit(solution)/shard_map/ppermute | solution.py:216
  88.1 3.0 %collective-permute-start.26 = (bf16[128,128]{1,0:T(8,128)(2,1)S(1)}, bf16[128,128]{1,0:T(8,128)(2,1)S(1)}, u32[]{:S(2)}, u32[]{:S(2)}) collective-permute-start(bf16[128,128]{1,0:T(8,128)(2,1)S(1)} %get-tuple-element.56), channel_id=1, source_target_pairs={{0,16},{2,18},{4,20},{6,22},{8,24},{10,26},{12,28},{14,30},{16,0},... | collective-permute-start | bytes 98312 | tf_op jit(solution)/shard_map/ppermute | solution.py:216
  89.2 3.4 %collective-permute-start.27 = (bf16[128,128]{1,0:T(8,128)(2,1)S(1)}, bf16[128,128]{1,0:T(8,128)(2,1)S(1)}, u32[]{:S(2)}, u32[]{:S(2)}) collective-permute-start(bf16[128,128]{1,0:T(8,128)(2,1)S(1)} %get-tuple-element.55), channel_id=1, source_target_pairs={{0,18},{2,16},{4,22},{6,20},{8,26},{10,24},{12,30},{14,28},{16,2},... | collective-permute-start | bytes 98312 | tf_op jit(solution)/shard_map/ppermute | solution.py:216

commit v6 on v5

v6 whole, which is shorter than its diff:
```python
import math

import jax
import jax.numpy as jnp
from jax import lax
from jax.experimental import pallas as pl
from jax.experimental.pallas import tpu as pltpu
from jax.sharding import PartitionSpec as P

NEG = -1e30
HEAD = 128
BLOCK = 128
DOC_ROWS = 16
CHUNK_BLOCKS = 5
CHUNK = CHUNK_BLOCKS * BLOCK
LONGEST = 20
TILES = 4
PEERS = 2
SCALE = float(HEAD) ** (-0.5)
TO_EXP2 = SCALE * math.log2(math.e)
CONTEXT = ("inner", "outer")


def dot(lhs, rhs, over):
    return lax.dot_general(lhs, rhs, ((over[:1], over[1:]), ((), ())), preferred_element_type=jnp.float32)


class Setting:
    def __init__(self, sizes, refs, kv_all, docs_all, tile_docs, cols, rows=None):
        self.nz, self.nx = nz, nx = sizes
        lines = nz
        place_ref, doc_ref, own_ref, peer_ref, far_ref = refs[:5]
        pieces = (refs[5 : 5 + lines], refs[5 + lines : 5 + 2 * lines])
        self.z, self.x, self.y, self.core = (place_ref[i] for i in range(4))
        self.part = own_ref.shape[0]
        self.width = own_ref.shape[1] // 2
        self.heads = self.width // HEAD
        self.rows = self.heads * self.part
        self.kv_all, self.docs_all, self.tile_docs = kv_all, docs_all, tile_docs
        self.blocks = kv_all.shape[1]
        self.steps = steps = range(lines)
        z_at = [lax.rem(self.z + by, nz) * (2 * nx) for by in steps]
        x_at = [lax.rem(self.x + by, nx) for by in steps]

        def places(which):
            return [
                [
                    jnp.where(which == 0, x_at[i], z_at[i]) + jnp.where(which == 0, z_at[j], x_at[j])
                    for j in steps
                ]
                for i in steps
            ]

        self.spots = (places(self.core), places(1 - self.core))
        for which, arrived, spot in ((self.core, pieces[0], self.spots[0]), (1 - self.core, pieces[1], self.spots[1])):
            for i in steps:
                for j in steps:
                    for c in range(2):
                        kv_all[which, spot[-i][-j] + nx * c] = arrived[i][j, c * BLOCK : (c + 1) * BLOCK]
        for i in steps:
            for j in steps:
                docs_all[i * lines + j] = pieces[0][i][j, 2 * BLOCK :].astype(jnp.float32)
        part, width = self.part, self.width
        tile_docs[0] = doc_ref[...].astype(jnp.float32)
        tile_docs[1] = peer_ref[part:, :HEAD].astype(jnp.float32)
        tile_docs[2] = far_ref[2 * part :, :HEAD].astype(jnp.float32)
        tile_docs[3] = far_ref[2 * part :, width : width + HEAD].astype(jnp.float32)
        sources = ((own_ref, 0), (peer_ref, 0), (far_ref, 0), (far_ref, part))
        for t, (source, begin) in enumerate(sources):
            for side in range(2):
                whole = jnp.concatenate(
                    [
                        source[begin : begin + part, side * width + h * HEAD : side * width + (h + 1) * HEAD]
                        for h in range(self.heads)
                    ]
                )
                if rows is not None:
                    rows[side, t] = whole
                cols[side, t] = whole.T
        apart = nz // PEERS
        self.apart = apart
        self.row_token = lax.div(self.z, apart) * part + lax.rem(
            lax.broadcasted_iota(jnp.int32, (CHUNK, self.rows), 1), part
        )
        key_row = lax.broadcasted_iota(jnp.int32, (CHUNK, self.rows), 0)
        self.key_row = key_row
        self.key_token = key_row + lax.div(key_row, BLOCK) * BLOCK

    def tile(self, t):
        dz = lax.rem(t, 2) * self.apart
        row = jnp.where(t < 2, self.y, 1 - self.y)
        block = (lax.rem(self.z + self.nz - dz, self.nz) * 2 + self.core) * (2 * self.nx) + self.x * 2 + row
        doc = self.tile_docs[t, :1, :]
        before = jnp.sum(jnp.where(self.docs_all[...] < doc, 0.125, 0.0), axis=(0, 1))
        first = jnp.max(before).astype(jnp.int32)
        held = lax.div(block - self.y + 2, 2) - first
        chunks = lax.div(held + CHUNK_BLOCKS - 1, CHUNK_BLOCKS)
        last = jnp.maximum(chunks - 1, 0)

        def keys_at(n):
            return jnp.minimum(first + n * CHUNK_BLOCKS, self.blocks - CHUNK_BLOCKS)

        begin = keys_at(last)
        skipped = (first + last * CHUNK_BLOCKS - begin) * BLOCK
        reach = (block - 2 * begin - self.y) * BLOCK
        mask = (self.key_token <= self.row_token + reach) & (self.key_row >= skipped)
        return chunks, last, keys_at, mask

    def key_rows(self, which, at):
        return self.kv_all[which, pl.ds(at, CHUNK_BLOCKS)].reshape(CHUNK, HEAD)


def statistics(sizes, *refs):
    count = 5 + 2 * sizes[0]
    stats_ref = refs[count]
    kv_all, docs_all, tile_docs, cols, scores = refs[count + 1 :]
    s = Setting(sizes, refs, kv_all, docs_all, tile_docs, cols)
    rows = s.rows

    def fold(value, combine):
        return combine(value.reshape(CHUNK // 8, 8, rows), axis=0)

    def slot(n):
        return pl.ds(pl.multiple_of(n * CHUNK, CHUNK), CHUNK)

    def tile(t, carry):
        chunks, last, keys_at, mask = s.tile(t)

        def score(n, top, masked):
            value = dot(s.key_rows(0, keys_at(n)), cols[0, t], (1, 0))
            if masked:
                value = jnp.where(mask, value, NEG)
            scores[slot(n), :] = value
            return jnp.maximum(top, fold(value, jnp.max))

        top = jnp.full((8, rows), NEG, jnp.float32)
        top = lax.fori_loop(0, last, lambda n, top: score(n, top, False), top)
        top = lax.fori_loop(last, chunks, lambda n, top: score(n, top, True), top)
        top = jnp.max(top, axis=0, keepdims=True) * TO_EXP2

        def sums(n, state):
            norm, weighted = state
            e = jnp.exp2(scores[slot(n), :] * TO_EXP2 - top)
            dp = dot(s.key_rows(1, keys_at(n)), cols[1, t], (1, 0))
            return norm + fold(e, jnp.sum), weighted + fold(e * dp, jnp.sum)

        zeros = jnp.zeros((8, rows), jnp.float32)
        norm, weighted = lax.fori_loop(0, chunks, sums, (zeros, zeros))
        stats_ref[t, 0:1, :] = top
        stats_ref[t, 1:2, :] = jnp.sum(norm, axis=0, keepdims=True)
        stats_ref[t, 2:3, :] = jnp.sum(weighted, axis=0, keepdims=True)
        return carry

    stats_ref[...] = jnp.zeros_like(stats_ref)
    lax.fori_loop(0, TILES, tile, 0)


def gradients(sizes, *refs):
    lines = sizes[0]
    count = 5 + 2 * lines
    here_ref, there_ref, dq_ref = refs[count : count + 3]
    outs = refs[count + 3 : count + 3 + 2 * lines]
    kv_all, docs_all, tile_docs, cols, tile_rows, totals = refs[count + 3 + 2 * lines :]
    totals[...] = jnp.zeros_like(totals)
    s = Setting(sizes, refs, kv_all, docs_all, tile_docs, cols, tile_rows)
    part, rows = s.part, s.rows

    def tile(t, carry):
        chunks, last, keys_at, mask = s.tile(t)
        other = lax.rem(t + 2, TILES)
        top_here, top_there = here_ref[t, 0:1, :], there_ref[other, 0:1, :]
        top = jnp.maximum(top_here, top_there)
        weight_here, weight_there = jnp.exp2(top_here - top), jnp.exp2(top_there - top)
        norm = here_ref[t, 1:2, :] * weight_here + there_ref[other, 1:2, :] * weight_there
        weighted = here_ref[t, 2:3, :] * weight_here + there_ref[other, 2:3, :] * weight_there
        inverse = 1.0 / norm
        delta = weighted * inverse

        def work(n, dq, masked):
            at = keys_at(n)
            keys = pl.ds(pl.multiple_of(at * BLOCK, BLOCK), CHUNK)
            value = dot(s.key_rows(0, at), cols[0, t], (1, 0))
            if masked:
                value = jnp.where(mask, value, NEG)
            p = jnp.exp2(value * TO_EXP2 - top) * inverse
            ds = p * (dot(s.key_rows(1, at), cols[1, t], (1, 0)) - delta)
            p_low = p.astype(jnp.bfloat16)
            ds_low = ds.astype(jnp.bfloat16)
            totals[0, keys, :] += dot(ds_low, tile_rows[0, t], (1, 0))
            totals[1, keys, :] += dot(p_low, tile_rows[1, t], (1, 0))
            return dq + dot(s.key_rows(0, at), ds_low, (0, 0))

        dq = jnp.zeros((HEAD, rows), jnp.float32)
        dq = lax.fori_loop(0, last, lambda n, dq: work(n, dq, False), dq)
        dq = lax.fori_loop(last, chunks, lambda n, dq: work(n, dq, True), dq)
        dq = (dq * SCALE).T
        for h in range(s.heads):
            dq_ref[t, :, h * HEAD : (h + 1) * HEAD] = dq[h * part : (h + 1) * part, :]
        return carry

    lax.fori_loop(0, TILES, tile, 0)
    keep, send = outs[:lines], outs[lines:]
    for which, out, spot in ((s.core, keep, s.spots[0]), (1 - s.core, send, s.spots[1])):
        for i in s.steps:
            for j in s.steps:
                for c in range(2):
                    begin = pl.multiple_of((spot[i][j] + s.nx * c) * BLOCK, BLOCK)
                    out[i][j, c] = totals[which, pl.ds(begin, BLOCK), :].astype(jnp.bfloat16)


def kernel_call(kernel, sizes, operands, outs, extra, pairs):
    nz, nx = sizes
    part, width = operands[2].shape
    rows = part * width // (2 * HEAD)
    blocks = 2 * nz * nx
    whole = pl.BlockSpec(memory_space=pltpu.VMEM)
    return pl.pallas_call(
        lambda *refs: kernel(sizes, *refs),
        name=kernel.__name__,
        out_shape=outs,
        in_specs=[pl.BlockSpec(memory_space=pltpu.SMEM)] + [whole] * (len(operands) - 1),
        out_specs=(whole,) * len(outs),
        scratch_shapes=[
            pltpu.VMEM((2, blocks, BLOCK, HEAD), jnp.bfloat16),
            pltpu.VMEM((nz * nx, DOC_ROWS, HEAD), jnp.float32),
            pltpu.VMEM((TILES, DOC_ROWS, HEAD), jnp.float32),
            pltpu.VMEM((2, TILES, HEAD, rows), jnp.bfloat16),
        ]
        + extra(rows, blocks),
        compiler_params=pltpu.CompilerParams(vmem_limit_bytes=36 * 1024 * 1024),
        cost_estimate=pl.CostEstimate(
            flops=pairs * 2 * 24 * 1024 * 128 * 128, bytes_accessed=8 * 1024 * 1024, transcendentals=0
        ),
    )(*operands)


def statistics_call(sizes, *operands):
    rows = operands[2].shape[0] * operands[2].shape[1] // (2 * HEAD)
    slots = -(-LONGEST // CHUNK_BLOCKS) * CHUNK
    outs = (jax.ShapeDtypeStruct((TILES, 8, rows), jnp.float32),)
    return kernel_call(
        statistics, sizes, operands, outs, lambda rows, blocks: [pltpu.VMEM((slots, rows), jnp.float32)], 2
    )[0]


def gradients_call(sizes, *operands):
    nz, nx = sizes
    part, width = operands[2].shape
    outs = (jax.ShapeDtypeStruct((TILES, part, width // 2), jnp.float32),)
    outs += (jax.ShapeDtypeStruct((nx, 2, BLOCK, HEAD), jnp.bfloat16),) * (2 * nz)
    return kernel_call(
        gradients,
        sizes,
        operands,
        outs,
        lambda rows, blocks: [
            pltpu.VMEM((2, TILES, rows, HEAD), jnp.bfloat16),
            pltpu.VMEM((2, blocks * BLOCK, HEAD), jnp.float32),
        ],
        5,
    )


def low(value):
    return value.astype(jnp.bfloat16)


def added(terms):
    total = terms[0].astype(jnp.float32)
    for term in terms[1:]:
        total = total + term.astype(jnp.float32)
    return total


def per_device(queries, keys, values, grad_out, block_docs):
    rows, width = queries.shape
    inner_size, outer_size = lax.axis_size("inner"), lax.axis_size("outer")
    nz, nx = inner_size // 2, outer_size // 2
    inner, outer = lax.axis_index("inner"), lax.axis_index("outer")
    z, core = lax.div(inner, 2), lax.rem(inner, 2)
    x, y = lax.div(outer, 2), lax.rem(outer, 2)
    part = rows // PEERS
    apart = nz // PEERS
    lines = nz

    def moved(value, step):
        hops = []
        for source in range(inner_size * outer_size):
            i, o = divmod(source, outer_size)
            dz, dx, dy, dc = step(i % 2)
            to_inner = (i // 2 + dz) % nz * 2 + (i % 2 + dc) % 2
            to_outer = (o // 2 + dx) % nx * 2 + (o % 2 + dy) % 2
            hops.append((source, to_inner * outer_size + to_outer))
        return lax.ppermute(value, CONTEXT, hops)

    def other_core(value):
        return moved(value, lambda c: (0, 0, 0, 1))

    def other_y(value):
        return moved(value, lambda c: (0, 0, 1, 0))

    def peer(value):
        return moved(value, lambda c: (apart, 0, 0, 0))

    def along_first(value, by):
        return moved(value, lambda c: (0, by, 0, 0) if c else (by, 0, 0, 0))

    def along_second(value, by):
        return moved(value, lambda c: (by, 0, 0, 0) if c else (0, by, 0, 0))

    def in_order(index, mine, theirs, axis):
        return jnp.where(
            index == 0, jnp.stack([mine, theirs], axis=axis), jnp.stack([theirs, mine], axis=axis)
        )

    doc = jnp.broadcast_to(low(block_docs)[:, None], (DOC_ROWS, HEAD))
    both = jnp.concatenate([queries, grad_out], axis=1).reshape(PEERS, part, 2 * width)
    half = lax.div(z, apart)
    own = jnp.where(half == 0, both[0], both[1])
    lent = jnp.where(half == 0, both[1], both[0])
    wide_doc = jnp.broadcast_to(low(block_docs)[:, None], (DOC_ROWS, 2 * width))
    borrowed = peer(jnp.concatenate([lent, wide_doc]))
    docs_of_both = jnp.concatenate([wide_doc[:, :width], borrowed[part:, width:]], axis=1)
    far = other_y(jnp.concatenate([own, borrowed[:part], docs_of_both]))

    given = other_core(jnp.where(core == 0, values, keys))
    kept = jnp.where(core == 0, keys, values)
    unit_docs = other_core(doc)
    rows_in_order = in_order(core, kept, given, 0).reshape(2 * BLOCK, HEAD)
    docs_in_order = in_order(core, doc[:8], unit_docs[:8], 0).reshape(DOC_ROWS, HEAD)
    unit = jnp.concatenate([rows_in_order, docs_in_order])
    line = jnp.stack([unit] + [along_first(unit, by) for by in range(1, lines)])
    mine = [line] + [along_second(line, by) for by in range(1, lines)]
    theirs = [other_core(piece) for piece in mine]

    place = jnp.stack([z, x, y, core]).astype(jnp.int32)
    sizes = (nz, nx)
    operands = (place, doc, own, borrowed, far, *mine, *theirs)
    here = statistics_call(sizes, *operands)
    dq, *sums = gradients_call(sizes, *operands, here, other_y(here))
    keep, send = sums[:lines], sums[lines:]

    totals = [None] * lines
    for by in [*range(1, lines), 0]:
        totals[by] = low(added([keep[by], other_core(send[by])]))
    arrived = [along_second(totals[by], by) for by in range(1, lines)]
    dq, totals[0] = lax.optimization_barrier((dq, totals[0]))
    rest = other_y(low(dq[2:]))
    arrived, rest = lax.optimization_barrier((arrived, rest))
    dq = low(dq[:2] + rest.astype(jnp.float32))
    returned = peer(dq[1])
    total = low(added([totals[0]] + arrived))
    total = added([total[0]] + [along_first(total[by], by) for by in range(1, lines)])
    total = low(jnp.where(core == 0, SCALE * total, total))
    ours = jnp.where(core == 0, total[0], total[1])
    theirs = other_core(jnp.where(core == 0, total[1], total[0]))
    grad_keys = jnp.where(core == 0, ours, theirs)
    grad_values = jnp.where(core == 0, theirs, ours)
    grad_queries = in_order(half, dq[0], returned, 0).reshape(rows, width)
    return grad_queries, grad_keys, grad_values


def solution(mesh):
    wide = P(CONTEXT, "head")
    return jax.shard_map(
        per_device,
        mesh=mesh,
        in_specs=(wide, wide, wide, wide, P(CONTEXT)),
        out_specs=(wide, wide, wide),
        check_vma=False,
    )
```

time: 93.2 us -> 92.9 us (level)
  Pallas kernels: 11.2 us -> 22.4 us
  waiting for transfers between devices: 34.4 us -> 24.2 us
  starting transfers between devices: 41.5 us -> 39.1 us
    pallas_call x1 -> x2, Pallas kernels: 11.2 us -> 22.4 us  [kernel_call(): pl.pallas_call(lambda *refs: kernel(sizes, *refs), name=kernel.__name__,...]
    ppermute x28, waiting for transfers between devices: 34.4 us -> 24.2 us  [moved(): return lax.ppermute(value, CONTEXT, hops)]
    ppermute x28, starting transfers between devices: 41.5 us -> 39.1 us  [moved(): return lax.ppermute(value, CONTEXT, hops)]
    convert_element_type x7, other arithmetic: 1.57 us -> 0.55 us  [low(): return value.astype(jnp.bfloat16)]
    concatenate x1, local copies, waits for them, and re-layouts: 0.02 us -> 0.97 us  [per_device(): jnp.concatenate([queries, grad_out], axis=1).reshape(PEERS, part, 2 * width)]
  transfers between devices with their start and end apart: 28 -> 28, of which waited for: 12 -> 12; matrix products, arithmetic and copies ran while one was open for 3% -> 5% of each run, Pallas kernels for 0% -> 0%
where the time goes in v6:
time: 92.9 us; the launch traced here: 93 us
  starting transfers between devices  39.1 us (42%)
  waiting for transfers between devices  24.2 us (26%)
  Pallas kernels  22.4 us (24%)
  other arithmetic  3.77 us (4%)
  local copies, waits for them, and re-layouts  2.05 us (2%)
  between operations  1.48 us (2%)
    ppermute x28, starting transfers between devices, moved(): return lax.ppermute(value, CONTEXT, hops)  39.1 us
    ppermute x28, waiting for transfers between devices, moved(): return lax.ppermute(value, CONTEXT, hops)  24.2 us
    pallas_call x2, Pallas kernels, kernel_call(): pl.pallas_call(lambda *refs: kernel(sizes, *refs), name=kernel.__name__,...  22.4 us
  transfers between devices with their start and end apart: 28, of which 12 were waited for; matrix products, arithmetic and copies ran while one was open for 5% of the time, Pallas kernels for 0%

profile of v6, /device:TPU:1, one launch (start us, length us, event | category | flops | bytes accessed | tf_op | source)
XLA Modules:
  0.0 93.0 jit_solution(12934433132079490874)
XLA Ops:
  1.3 1.5 %collective-permute-start.3 = (bf16[16,128]{1,0:T(8,128)(2,1)S(1)}, bf16[16,128]{1,0:T(8,128)(2,1)S(1)}, u32[]{:S(2)}, u32[]{:S(2)}) collective-permute-start(bf16[16,128]{1,0:T(8,128)(2,1)S(1)} %broadcast_in_dim.5.refs_1_), channel_id=1, source_target_pairs={{0,16},{2,18},{4,20},{6,22},{8,24},{10,26},{12,28},{14,30},{16,0},... | collective-permute-start | bytes 12296 | tf_op jit(solution)/shard_map/ppermute | solution.py:294
  2.8 0.8 select_bitcast_fusion.1
  3.6 0.1 collective-permute-start.2
  3.7 1.0 %constant_dynamic-update-slice_fusion.1 = bf16[128,2048]{1,0:T(8,128)(2,1)S(1)} fusion(bf16[128,1024]{1,0:T(8,128)(2,1)} %param.5), kind=kLoop, calls=%fused_computation.33 | loop fusion | bytes 524288
  4.6 1.0 %constant_dynamic-update-slice_fusion = bf16[128,2048]{1,0:T(8,128)(2,1)S(1)} fusion(bf16[128,2048]{1,0:T(8,128)(2,1)S(1)} %constant_dynamic-update-slice_fusion.1, bf16[128,1024]{1,0:T(8,128)(2,1)} %param.8), kind=kLoop, calls=%fused_computation.32 | loop fusion | bytes 524288 | tf_op jit(solution)/shard_map/concatenate | solution.py:317
  5.7 3.8 %collective-permute-start = (bf16[80,2048]{1,0:T(8,128)(2,1)S(1)}, bf16[80,2048]{1,0:T(8,128)(2,1)S(1)}, u32[]{:S(2)}, u32[]{:S(2)}) collective-permute-start(bf16[80,2048]{1,0:T(8,128)(2,1)S(1)} %concatenate.16), channel_id=1, source_target_pairs={{0,64},{2,66},{4,68},{6,70},{8,72},{10,74},{12,76},{14,78},{16,80}... | collective-permute-start | bytes 983048 | tf_op jit(solution)/shard_map/ppermute | solution.py:294
  9.5 2.8 %collective-permute-start.5 = (bf16[272,128]{1,0:T(8,128)(2,1)S(1)}, bf16[272,128]{1,0:T(8,128)(2,1)S(1)}, u32[]{:S(2)}, u32[]{:S(2)}) collective-permute-start(bf16[272,128]{1,0:T(8,128)(2,1)S(1)} %get-tuple-element.43), channel_id=1, source_target_pairs={{0,64},{2,66},{4,68},{6,70},{8,72},{10,74},{12,76},{14,78},{16,24}... | collective-permute-start | bytes 208904 | tf_op jit(solution)/shard_map/ppermute | solution.py:294
  12.3 0.3 collective-permute-start.4
  12.7 2.4 %collective-permute-start.6 = (bf16[272,128]{1,0:T(8,128)(2,1)S(1)}, bf16[272,128]{1,0:T(8,128)(2,1)S(1)}, u32[]{:S(2)}, u32[]{:S(2)}) collective-permute-start(bf16[272,128]{1,0:T(8,128)(2,1)S(1)} %get-tuple-element.43), channel_id=1, source_target_pairs={{0,96},{2,98},{4,100},{6,102},{8,104},{10,106},{12,108},{14,110},{... | collective-permute-start | bytes 208904 | tf_op jit(solution)/shard_map/ppermute | solution.py:294
  15.0 2.1 %collective-permute-done.refs_3_ = bf16[80,2048]{1,0:T(8,128)(2,1)S(1)} collective-permute-done((bf16[80,2048]{1,0:T(8,128)(2,1)S(1)}, bf16[80,2048]{1,0:T(8,128)(2,1)S(1)}, u32[]{:S(2)}, u32[]{:S(2)}) %collective-permute-start) | collective-permute-done | bytes 327712 | tf_op jit(solution)/shard_map/ppermute | solution.py:294
  17.2 0.9 fusion.1
  18.1 1.3 %collective-permute-start.1 = (bf16[144,2048]{1,0:T(8,128)(2,1)}, bf16[144,2048]{1,0:T(8,128)(2,1)S(1)}, u32[]{:S(2)}, u32[]{:S(2)}) collective-permute-start(bf16[144,2048]{1,0:T(8,128)(2,1)} %fusion.1), channel_id=1, source_target_pairs={{0,2},{2,0},{4,6},{6,4},{8,10},{10,8},{12,14},{14,12},{16,18},{18,... | collective-permute-start | bytes 1769480 | tf_op jit(solution)/shard_map/ppermute | solution.py:294
  19.4 2.9 %collective-permute-start.9 = (bf16[4,272,128]{2,1,0:T(8,128)(2,1)S(1)}, bf16[4,272,128]{2,1,0:T(8,128)(2,1)S(1)}, u32[]{:S(2)}, u32[]{:S(2)}) collective-permute-start(bf16[4,272,128]{2,1,0:T(8,128)(2,1)S(1)} %pad_maximum_fusion.refs_5_), channel_id=1, source_target_pairs={{0,12},{2,14},{4,0},{6,2},{8,4},{10,6},{12,8},{14,10},{16,112},{18... | collective-permute-start | bytes 835592 | tf_op jit(solution)/shard_map/ppermute | solution.py:294
  22.3 0.7 collective-permute-start.7
  23.0 2.3 %collective-permute-start.10 = (bf16[4,272,128]{2,1,0:T(8,128)(2,1)S(1)}, bf16[4,272,128]{2,1,0:T(8,128)(2,1)S(1)}, u32[]{:S(2)}, u32[]{:S(2)}) collective-permute-start(bf16[4,272,128]{2,1,0:T(8,128)(2,1)S(1)} %pad_maximum_fusion.refs_5_), channel_id=1, source_target_pairs={{0,16},{2,18},{4,20},{6,22},{8,24},{10,26},{12,28},{14,30},{16,0},... | collective-permute-start | bytes 835592 | tf_op jit(solution)/shard_map/ppermute | solution.py:294
  25.3 3.5 %collective-permute-done.9.refs_8_ = bf16[4,272,128]{2,1,0:T(8,128)(2,1)S(1)} collective-permute-done((bf16[4,272,128]{2,1,0:T(8,128)(2,1)S(1)}, bf16[4,272,128]{2,1,0:T(8,128)(2,1)S(1)}, u32[]{:S(2)}, u32[]{:S(2)}) %collective-permute-start.9) | collective-permute-done | bytes 278560 | tf_op jit(solution)/shard_map/ppermute | solution.py:294
  28.8 1.9 %collective-permute-start.13 = (bf16[4,272,128]{2,1,0:T(8,128)(2,1)S(1)}, bf16[4,272,128]{2,1,0:T(8,128)(2,1)S(1)}, u32[]{:S(2)}, u32[]{:S(2)}) collective-permute-start(bf16[4,272,128]{2,1,0:T(8,128)(2,1)S(1)} %collective-permute-done.9.refs_8_), channel_id=1, source_target_pairs={{0,16},{2,18},{4,20},{6,22},{8,24},{10,26},{12,28},{14,30},{16,0},... | collective-permute-start | bytes 835592 | tf_op jit(solution)/shard_map/ppermute | solution.py:294
  30.7 1.1 %collective-permute-start.12 = (bf16[4,272,128]{2,1,0:T(8,128)(2,1)S(1)}, bf16[4,272,128]{2,1,0:T(8,128)(2,1)S(1)}, u32[]{:S(2)}, u32[]{:S(2)}) collective-permute-start(bf16[4,272,128]{2,1,0:T(8,128)(2,1)S(1)} %collective-permute-done.8.refs_7_), channel_id=1, source_target_pairs={{0,16},{2,18},{4,20},{6,22},{8,24},{10,26},{12,28},{14,30},{16,0},... | collective-permute-start | bytes 835592 | tf_op jit(solution)/shard_map/ppermute | solution.py:294
  31.7 0.4 collective-permute-done.7.refs_6_
  32.2 2.5 %collective-permute-start.11 = (bf16[4,272,128]{2,1,0:T(8,128)(2,1)S(1)}, bf16[4,272,128]{2,1,0:T(8,128)(2,1)S(1)}, u32[]{:S(2)}, u32[]{:S(2)}) collective-permute-start(bf16[4,272,128]{2,1,0:T(8,128)(2,1)S(1)} %collective-permute-done.7.refs_6_), channel_id=1, source_target_pairs={{0,16},{2,18},{4,20},{6,22},{8,24},{10,26},{12,28},{14,30},{16,0},... | collective-permute-start | bytes 835592 | tf_op jit(solution)/shard_map/ppermute | solution.py:294
  34.6 0.1 pad_add_fusion.refs_0_
  34.7 1.1 %collective-permute-done.11.refs_10_ = bf16[4,272,128]{2,1,0:T(8,128)(2,1)S(1)} collective-permute-done((bf16[4,272,128]{2,1,0:T(8,128)(2,1)S(1)}, bf16[4,272,128]{2,1,0:T(8,128)(2,1)S(1)}, u32[]{:S(2)}, u32[]{:S(2)}) %collective-permute-start.11) | collective-permute-done | bytes 278560 | tf_op jit(solution)/shard_map/ppermute | solution.py:294
  35.8 9.0 %statistics.1.refs_13_ = f32[4,8,512]{2,1,0:T(8,128)S(1)} custom-call(s32[4]{0:T(128)S(1)} %pad_add_fusion.refs_0_, bf16[16,128]{1,0:T(8,128)(2,1)S(1)} %broadcast_in_dim.5.refs_1_, bf16[64,2048]{1,0:T(8,128)(2,1)S(1)} %get-tuple-element.34.refs_2_, bf16[80,2048]{1,0:T(8,128)(2,1)S(1)} %collective-permute-done.refs_3_, ...), custom_call_target="tpu_custom_call" | custom-call | flops 1610612736 | bytes 8388608 | tf_op jit(solution)/shard_map/statistics/pallas_call | solution.py:217
  44.8 1.0 %collective-permute-start.14 = (f32[4,8,512]{2,1,0:T(8,128)S(1)}, f32[4,8,512]{2,1,0:T(8,128)S(1)}, u32[]{:S(2)}, u32[]{:S(2)}) collective-permute-start(f32[4,8,512]{2,1,0:T(8,128)S(1)} %statistics.1.refs_13_), channel_id=1, source_target_pairs={{0,2},{2,0},{4,6},{6,4},{8,10},{10,8},{12,14},{14,12},{16,18},{18,... | collective-permute-start | bytes 196616 | tf_op jit(solution)/shard_map/ppermute | solution.py:294
  45.8 2.3 %collective-permute-done.14.refs_14_ = f32[4,8,512]{2,1,0:T(8,128)S(1)} collective-permute-done((f32[4,8,512]{2,1,0:T(8,128)S(1)}, f32[4,8,512]{2,1,0:T(8,128)S(1)}, u32[]{:S(2)}, u32[]{:S(2)}) %collective-permute-start.14) | collective-permute-done | bytes 65568 | tf_op jit(solution)/shard_map/ppermute | solution.py:294
  48.1 13.4 %gradients.1 = (f32[4,64,1024]{2,1,0:T(8,128)S(1)}, bf16[4,2,128,128]{3,2,1,0:T(8,128)(2,1)S(1)}, bf16[4,2,128,128]{3,2,1,0:T(8,128)(2,1)S(1)}, bf16[4,2,128,128...) custom-call(s32[4]{0:T(128)S(1)} %pad_add_fusion.refs_0_, ...), custom_call_target="tpu_custom_call" | custom-call | flops 4026531840 | bytes 8388608 | tf_op jit(solution)/shard_map/gradients/pallas_call | solution.py:217
  61.6 0.1 collective-permute-start.15
  61.7 0.5 collective-permute-start.16
  62.2 0.1 collective-permute-start.18
  62.2 0.4 collective-permute-start.20
  62.7 0.5 collective-permute-done.15
  63.3 0.9 collective-permute-start.22
  64.4 2.6 %collective-permute-start.19 = (bf16[4,2,128,128]{3,2,1,0:T(8,128)(2,1)S(1)}, bf16[4,2,128,128]{3,2,1,0:T(8,128)(2,1)S(1)}, u32[]{:S(2)}, u32[]{:S(2)}) collective-permute-start(bf16[4,2,128,128]{3,2,1,0:T(8,128)(2,1)S(1)} %add_convert_fusion.3), channel_id=1, source_target_pairs={{0,8},{2,10},{4,12},{6,14},{8,0},{10,2},{12,4},{14,6},{16,80},{18,... | collective-permute-start | bytes 786440 | tf_op jit(solution)/shard_map/ppermute | solution.py:294
  67.1 1.9 %collective-permute-start.21 = (bf16[4,2,128,128]{3,2,1,0:T(8,128)(2,1)S(1)}, bf16[4,2,128,128]{3,2,1,0:T(8,128)(2,1)S(1)}, u32[]{:S(2)}, u32[]{:S(2)}) collective-permute-start(bf16[4,2,128,128]{3,2,1,0:T(8,128)(2,1)S(1)} %add_convert_fusion.2), channel_id=1, source_target_pairs={{0,12},{2,14},{4,0},{6,2},{8,4},{10,6},{12,8},{14,10},{16,112},{18... | collective-permute-start | bytes 786440 | tf_op jit(solution)/shard_map/ppermute | solution.py:294
  69.0 2.1 %collective-permute-done.22 = bf16[2,64,1024]{2,1,0:T(8,128)(2,1)S(1)} collective-permute-done((bf16[2,64,1024]{2,1,0:T(8,128)(2,1)S(1)}, bf16[2,64,1024]{2,1,0:T(8,128)(2,1)S(1)}, u32[]{:S(2)}, u32[]{:S(2)}) %collective-permute-start.22) | collective-permute-done | bytes 262176 | tf_op jit(solution)/shard_map/ppermute | solution.py:294
  71.1 2.7 %collective-permute-done.17 = bf16[4,2,128,128]{3,2,1,0:T(8,128)(2,1)S(1)} collective-permute-done((bf16[4,2,128,128]{3,2,1,0:T(8,128)(2,1)S(1)}, bf16[4,2,128,128]{3,2,1,0:T(8,128)(2,1)S(1)}, u32[]{:S(2)}, u32[]{:S(2)}) %collective-permute-start.17) | collective-permute-done | bytes 262176 | tf_op jit(solution)/shard_map/ppermute | solution.py:294
  73.9 0.7 collective-permute-done.21
  74.6 0.1 add_convert_fusion
  74.8 0.1 collective-permute-start.24
  74.9 2.7 %collective-permute-start.26 = (bf16[2,128,128]{2,1,0:T(8,128)(2,1)S(1)}, bf16[2,128,128]{2,1,0:T(8,128)(2,1)S(1)}, u32[]{:S(2)}, u32[]{:S(2)}) collective-permute-start(bf16[2,128,128]{2,1,0:T(8,128)(2,1)S(1)} %get-tuple-element.36), channel_id=1, source_target_pairs={{0,96},{2,98},{4,100},{6,102},{8,104},{10,106},{12,108},{14,110},{... | collective-permute-start | bytes 196616 | tf_op jit(solution)/shard_map/ppermute | solution.py:294
  77.5 0.8 collective-permute-start.25
  78.4 0.7 collective-permute-done.24
  79.2 3.0 %collective-permute-done.25 = bf16[2,128,128]{2,1,0:T(8,128)(2,1)S(1)} collective-permute-done((bf16[2,128,128]{2,1,0:T(8,128)(2,1)S(1)}, bf16[2,128,128]{2,1,0:T(8,128)(2,1)S(1)}, u32[]{:S(2)}, u32[]{:S(2)}) %collective-permute-start.25) | collective-permute-done | bytes 65568 | tf_op jit(solution)/shard_map/ppermute | solution.py:294
  82.2 3.4 %collective-permute-start.27 = (bf16[128,128]{1,0:T(8,128)(2,1)S(1)}, bf16[128,128]{1,0:T(8,128)(2,1)S(1)}, u32[]{:S(2)}, u32[]{:S(2)}) collective-permute-start(bf16[128,128]{1,0:T(8,128)(2,1)S(1)} %select_bitcast_fusion), channel_id=1, source_target_pairs={{0,16},{2,18},{4,20},{6,22},{8,24},{10,26},{12,28},{14,30},{16,0},... | collective-permute-start | bytes 98312 | tf_op jit(solution)/shard_map/ppermute | solution.py:294
  85.6 1.1 %collective-permute-start.23 = (bf16[64,1024]{1,0:T(8,128)(2,1)S(1)}, bf16[64,1024]{1,0:T(8,128)(2,1)S(1)}, u32[]{:S(2)}, u32[]{:S(2)}) collective-permute-start(bf16[64,1024]{1,0:T(8,128)(2,1)S(1)} %get-tuple-element.39), channel_id=1, source_target_pairs={{0,64},{2,66},{4,68},{6,70},{8,72},{10,74},{12,76},{14,78},{16,80}... | collective-permute-start | bytes 393224 | tf_op jit(solution)/shard_map/ppermute | solution.py:294
  86.7 0.6 bitcast_select_fusion
  87.3 5.0 %collective-permute-done.23 = bf16[64,1024]{1,0:T(8,128)(2,1)S(1)} collective-permute-done((bf16[64,1024]{1,0:T(8,128)(2,1)S(1)}, bf16[64,1024]{1,0:T(8,128)(2,1)S(1)}, u32[]{:S(2)}, u32[]{:S(2)}) %collective-permute-start.23) | collective-permute-done | bytes 131104 | tf_op jit(solution)/shard_map/ppermute | solution.py:294
  92.3 0.7 maximum_select_fusion
  (38 shorter events, 0.8 us)
Async XLA Ops:
  1.3 8.2 %collective-permute-start.3 = (bf16[16,128]{1,0:T(8,128)(2,1)S(1)}, bf16[16,128]{1,0:T(8,128)(2,1)S(1)}, u32[]{:S(2)}, u32[]{:S(2)}) collective-permute-start(bf16[16,128]{1,0:T(8,128)(2,1)S(1)} %broadcast_in_dim.5.refs_1_), channel_id=1, source_target_pairs={{0,16},{2,18},{4,20},{6,22},{8,24},{10,26},{12,28},{14,30},{16,0},... | collective-permute-start | bytes 12296 | tf_op jit(solution)/shard_map/ppermute | solution.py:294
  3.6 5.9 %collective-permute-start.2 = (bf16[128,128]{1,0:T(8,128)(2,1)S(1)}, bf16[128,128]{1,0:T(8,128)(2,1)S(1)}, u32[]{:S(2)}, u32[]{:S(2)}) collective-permute-start(bf16[128,128]{1,0:T(8,128)(2,1)S(1)} %get-tuple-element.45), channel_id=1, source_target_pairs={{0,16},{2,18},{4,20},{6,22},{8,24},{10,26},{12,28},{14,30},{16,0},... | collective-permute-start | bytes 98312 | tf_op jit(solution)/shard_map/ppermute | solution.py:294
  5.7 11.5 %collective-permute-start = (bf16[80,2048]{1,0:T(8,128)(2,1)S(1)}, bf16[80,2048]{1,0:T(8,128)(2,1)S(1)}, u32[]{:S(2)}, u32[]{:S(2)}) collective-permute-start(bf16[80,2048]{1,0:T(8,128)(2,1)S(1)} %concatenate.16), channel_id=1, source_target_pairs={{0,64},{2,66},{4,68},{6,70},{8,72},{10,74},{12,76},{14,78},{16,80}... | collective-permute-start | bytes 983048 | tf_op jit(solution)/shard_map/ppermute | solution.py:294
  9.5 9.8 %collective-permute-start.5 = (bf16[272,128]{1,0:T(8,128)(2,1)S(1)}, bf16[272,128]{1,0:T(8,128)(2,1)S(1)}, u32[]{:S(2)}, u32[]{:S(2)}) collective-permute-start(bf16[272,128]{1,0:T(8,128)(2,1)S(1)} %get-tuple-element.43), channel_id=1, source_target_pairs={{0,64},{2,66},{4,68},{6,70},{8,72},{10,74},{12,76},{14,78},{16,24}... | collective-permute-start | bytes 208904 | tf_op jit(solution)/shard_map/ppermute | solution.py:294
  12.3 7.0 %collective-permute-start.4 = (bf16[272,128]{1,0:T(8,128)(2,1)S(1)}, bf16[272,128]{1,0:T(8,128)(2,1)S(1)}, u32[]{:S(2)}, u32[]{:S(2)}) collective-permute-start(bf16[272,128]{1,0:T(8,128)(2,1)S(1)} %get-tuple-element.43), channel_id=1, source_target_pairs={{0,32},{2,34},{4,36},{6,38},{8,40},{10,42},{12,44},{14,46},{16,20}... | collective-permute-start | bytes 208904 | tf_op jit(solution)/shard_map/ppermute | solution.py:294
  12.7 6.7 %collective-permute-start.6 = (bf16[272,128]{1,0:T(8,128)(2,1)S(1)}, bf16[272,128]{1,0:T(8,128)(2,1)S(1)}, u32[]{:S(2)}, u32[]{:S(2)}) collective-permute-start(bf16[272,128]{1,0:T(8,128)(2,1)S(1)} %get-tuple-element.43), channel_id=1, source_target_pairs={{0,96},{2,98},{4,100},{6,102},{8,104},{10,106},{12,108},{14,110},{... | collective-permute-start | bytes 208904 | tf_op jit(solution)/shard_map/ppermute | solution.py:294
  18.1 17.8 %collective-permute-start.1 = (bf16[144,2048]{1,0:T(8,128)(2,1)}, bf16[144,2048]{1,0:T(8,128)(2,1)S(1)}, u32[]{:S(2)}, u32[]{:S(2)}) collective-permute-start(bf16[144,2048]{1,0:T(8,128)(2,1)} %fusion.1), channel_id=1, source_target_pairs={{0,2},{2,0},{4,6},{6,4},{8,10},{10,8},{12,14},{14,12},{16,18},{18,... | collective-permute-start | bytes 1769480 | tf_op jit(solution)/shard_map/ppermute | solution.py:294
  19.4 9.3 %collective-permute-start.9 = (bf16[4,272,128]{2,1,0:T(8,128)(2,1)S(1)}, bf16[4,272,128]{2,1,0:T(8,128)(2,1)S(1)}, u32[]{:S(2)}, u32[]{:S(2)}) collective-permute-start(bf16[4,272,128]{2,1,0:T(8,128)(2,1)S(1)} %pad_maximum_fusion.refs_5_), channel_id=1, source_target_pairs={{0,12},{2,14},{4,0},{6,2},{8,4},{10,6},{12,8},{14,10},{16,112},{18... | collective-permute-start | bytes 835592 | tf_op jit(solution)/shard_map/ppermute | solution.py:294
  22.3 8.4 %collective-permute-start.8 = (bf16[4,272,128]{2,1,0:T(8,128)(2,1)S(1)}, bf16[4,272,128]{2,1,0:T(8,128)(2,1)S(1)}, u32[]{:S(2)}, u32[]{:S(2)}) collective-permute-start(bf16[4,272,128]{2,1,0:T(8,128)(2,1)S(1)} %pad_maximum_fusion.refs_5_), channel_id=1, source_target_pairs={{0,8},{2,10},{4,12},{6,14},{8,0},{10,2},{12,4},{14,6},{16,80},{18,... | collective-permute-start | bytes 835592 | tf_op jit(solution)/shard_map/ppermute | solution.py:294
  22.3 9.9 %collective-permute-start.7 = (bf16[4,272,128]{2,1,0:T(8,128)(2,1)S(1)}, bf16[4,272,128]{2,1,0:T(8,128)(2,1)S(1)}, u32[]{:S(2)}, u32[]{:S(2)}) collective-permute-start(bf16[4,272,128]{2,1,0:T(8,128)(2,1)S(1)} %pad_maximum_fusion.refs_5_), channel_id=1, source_target_pairs={{0,4},{2,6},{4,8},{6,10},{8,12},{10,14},{12,0},{14,2},{16,48},{18,... | collective-permute-start | bytes 835592 | tf_op jit(solution)/shard_map/ppermute | solution.py:294
  23.0 11.7 %collective-permute-start.10 = (bf16[4,272,128]{2,1,0:T(8,128)(2,1)S(1)}, bf16[4,272,128]{2,1,0:T(8,128)(2,1)S(1)}, u32[]{:S(2)}, u32[]{:S(2)}) collective-permute-start(bf16[4,272,128]{2,1,0:T(8,128)(2,1)S(1)} %pad_maximum_fusion.refs_5_), channel_id=1, source_target_pairs={{0,16},{2,18},{4,20},{6,22},{8,24},{10,26},{12,28},{14,30},{16,0},... | collective-permute-start | bytes 835592 | tf_op jit(solution)/shard_map/ppermute | solution.py:294
  28.8 6.0 %collective-permute-start.13 = (bf16[4,272,128]{2,1,0:T(8,128)(2,1)S(1)}, bf16[4,272,128]{2,1,0:T(8,128)(2,1)S(1)}, u32[]{:S(2)}, u32[]{:S(2)}) collective-permute-start(bf16[4,272,128]{2,1,0:T(8,128)(2,1)S(1)} %collective-permute-done.9.refs_8_), channel_id=1, source_target_pairs={{0,16},{2,18},{4,20},{6,22},{8,24},{10,26},{12,28},{14,30},{16,0},... | collective-permute-start | bytes 835592 | tf_op jit(solution)/shard_map/ppermute | solution.py:294
  30.7 4.0 %collective-permute-start.12 = (bf16[4,272,128]{2,1,0:T(8,128)(2,1)S(1)}, bf16[4,272,128]{2,1,0:T(8,128)(2,1)S(1)}, u32[]{:S(2)}, u32[]{:S(2)}) collective-permute-start(bf16[4,272,128]{2,1,0:T(8,128)(2,1)S(1)} %collective-permute-done.8.refs_7_), channel_id=1, source_target_pairs={{0,16},{2,18},{4,20},{6,22},{8,24},{10,26},{12,28},{14,30},{16,0},... | collective-permute-start | bytes 835592 | tf_op jit(solution)/shard_map/ppermute | solution.py:294
  32.2 3.6 %collective-permute-start.11 = (bf16[4,272,128]{2,1,0:T(8,128)(2,1)S(1)}, bf16[4,272,128]{2,1,0:T(8,128)(2,1)S(1)}, u32[]{:S(2)}, u32[]{:S(2)}) collective-permute-start(bf16[4,272,128]{2,1,0:T(8,128)(2,1)S(1)} %collective-permute-done.7.refs_6_), channel_id=1, source_target_pairs={{0,16},{2,18},{4,20},{6,22},{8,24},{10,26},{12,28},{14,30},{16,0},... | collective-permute-start | bytes 835592 | tf_op jit(solution)/shard_map/ppermute | solution.py:294
  44.8 3.3 %collective-permute-start.14 = (f32[4,8,512]{2,1,0:T(8,128)S(1)}, f32[4,8,512]{2,1,0:T(8,128)S(1)}, u32[]{:S(2)}, u32[]{:S(2)}) collective-permute-start(f32[4,8,512]{2,1,0:T(8,128)S(1)} %statistics.1.refs_13_), channel_id=1, source_target_pairs={{0,2},{2,0},{4,6},{6,4},{8,10},{10,8},{12,14},{14,12},{16,18},{18,... | collective-permute-start | bytes 196616 | tf_op jit(solution)/shard_map/ppermute | solution.py:294
  61.6 1.6 %collective-permute-start.15 = (bf16[4,2,128,128]{3,2,1,0:T(8,128)(2,1)S(1)}, bf16[4,2,128,128]{3,2,1,0:T(8,128)(2,1)S(1)}, u32[]{:S(2)}, u32[]{:S(2)}) collective-permute-start(bf16[4,2,128,128]{3,2,1,0:T(8,128)(2,1)S(1)} %get-tuple-element.20), channel_id=1, source_target_pairs={{0,16},{2,18},{4,20},{6,22},{8,24},{10,26},{12,28},{14,30},{16,0},... | collective-permute-start | bytes 786440 | tf_op jit(solution)/shard_map/ppermute | solution.py:294
  61.7 2.5 %collective-permute-start.16 = (bf16[4,2,128,128]{3,2,1,0:T(8,128)(2,1)S(1)}, bf16[4,2,128,128]{3,2,1,0:T(8,128)(2,1)S(1)}, u32[]{:S(2)}, u32[]{:S(2)}) collective-permute-start(bf16[4,2,128,128]{3,2,1,0:T(8,128)(2,1)S(1)} %get-tuple-element.23), channel_id=1, source_target_pairs={{0,16},{2,18},{4,20},{6,22},{8,24},{10,26},{12,28},{14,30},{16,0},... | collective-permute-start | bytes 786440 | tf_op jit(solution)/shard_map/ppermute | solution.py:294
  62.2 2.2 %collective-permute-start.18 = (bf16[4,2,128,128]{3,2,1,0:T(8,128)(2,1)S(1)}, bf16[4,2,128,128]{3,2,1,0:T(8,128)(2,1)S(1)}, u32[]{:S(2)}, u32[]{:S(2)}) collective-permute-start(bf16[4,2,128,128]{3,2,1,0:T(8,128)(2,1)S(1)} %get-tuple-element.25), channel_id=1, source_target_pairs={{0,16},{2,18},{4,20},{6,22},{8,24},{10,26},{12,28},{14,30},{16,0},... | collective-permute-start | bytes 786440 | tf_op jit(solution)/shard_map/ppermute | solution.py:294
  62.2 4.8 %collective-permute-start.20 = (bf16[4,2,128,128]{3,2,1,0:T(8,128)(2,1)S(1)}, bf16[4,2,128,128]{3,2,1,0:T(8,128)(2,1)S(1)}, u32[]{:S(2)}, u32[]{:S(2)}) collective-permute-start(bf16[4,2,128,128]{3,2,1,0:T(8,128)(2,1)S(1)} %get-tuple-element.27), channel_id=1, source_target_pairs={{0,16},{2,18},{4,20},{6,22},{8,24},{10,26},{12,28},{14,30},{16,0},... | collective-permute-start | bytes 786440 | tf_op jit(solution)/shard_map/ppermute | solution.py:294
  63.3 7.8 %collective-permute-start.22 = (bf16[2,64,1024]{2,1,0:T(8,128)(2,1)S(1)}, bf16[2,64,1024]{2,1,0:T(8,128)(2,1)S(1)}, u32[]{:S(2)}, u32[]{:S(2)}) collective-permute-start(bf16[2,64,1024]{2,1,0:T(8,128)(2,1)S(1)} %slice.109), channel_id=1, source_target_pairs={{0,2},{2,0},{4,6},{6,4},{8,10},{10,8},{12,14},{14,12},{16,18},{18,... | collective-permute-start | bytes 786440 | tf_op jit(solution)/shard_map/ppermute | solution.py:294
  64.3 9.6 %collective-permute-start.17 = (bf16[4,2,128,128]{3,2,1,0:T(8,128)(2,1)S(1)}, bf16[4,2,128,128]{3,2,1,0:T(8,128)(2,1)S(1)}, u32[]{:S(2)}, u32[]{:S(2)}) collective-permute-start(bf16[4,2,128,128]{3,2,1,0:T(8,128)(2,1)S(1)} %add_convert_fusion.4), channel_id=1, source_target_pairs={{0,4},{2,6},{4,8},{6,10},{8,12},{10,14},{12,0},{14,2},{16,48},{18,... | collective-permute-start | bytes 786440 | tf_op jit(solution)/shard_map/ppermute | solution.py:294
  64.4 9.4 %collective-permute-start.19 = (bf16[4,2,128,128]{3,2,1,0:T(8,128)(2,1)S(1)}, bf16[4,2,128,128]{3,2,1,0:T(8,128)(2,1)S(1)}, u32[]{:S(2)}, u32[]{:S(2)}) collective-permute-start(bf16[4,2,128,128]{3,2,1,0:T(8,128)(2,1)S(1)} %add_convert_fusion.3), channel_id=1, source_target_pairs={{0,8},{2,10},{4,12},{6,14},{8,0},{10,2},{12,4},{14,6},{16,80},{18,... | collective-permute-start | bytes 786440 | tf_op jit(solution)/shard_map/ppermute | solution.py:294
  67.1 7.5 %collective-permute-start.21 = (bf16[4,2,128,128]{3,2,1,0:T(8,128)(2,1)S(1)}, bf16[4,2,128,128]{3,2,1,0:T(8,128)(2,1)S(1)}, u32[]{:S(2)}, u32[]{:S(2)}) collective-permute-start(bf16[4,2,128,128]{3,2,1,0:T(8,128)(2,1)S(1)} %add_convert_fusion.2), channel_id=1, source_target_pairs={{0,12},{2,14},{4,0},{6,2},{8,4},{10,6},{12,8},{14,10},{16,112},{18... | collective-permute-start | bytes 786440 | tf_op jit(solution)/shard_map/ppermute | solution.py:294
  74.8 4.4 %collective-permute-start.24 = (bf16[2,128,128]{2,1,0:T(8,128)(2,1)S(1)}, bf16[2,128,128]{2,1,0:T(8,128)(2,1)S(1)}, u32[]{:S(2)}, u32[]{:S(2)}) collective-permute-start(bf16[2,128,128]{2,1,0:T(8,128)(2,1)S(1)} %get-tuple-element.35), channel_id=1, source_target_pairs={{0,32},{2,34},{4,36},{6,38},{8,40},{10,42},{12,44},{14,46},{16,20}... | collective-permute-start | bytes 196616 | tf_op jit(solution)/shard_map/ppermute | solution.py:294
  74.9 4.3 %collective-permute-start.26 = (bf16[2,128,128]{2,1,0:T(8,128)(2,1)S(1)}, bf16[2,128,128]{2,1,0:T(8,128)(2,1)S(1)}, u32[]{:S(2)}, u32[]{:S(2)}) collective-permute-start(bf16[2,128,128]{2,1,0:T(8,128)(2,1)S(1)} %get-tuple-element.36), channel_id=1, source_target_pairs={{0,96},{2,98},{4,100},{6,102},{8,104},{10,106},{12,108},{14,110},{... | collective-permute-start | bytes 196616 | tf_op jit(solution)/shard_map/ppermute | solution.py:294
  77.5 4.6 %collective-permute-start.25 = (bf16[2,128,128]{2,1,0:T(8,128)(2,1)S(1)}, bf16[2,128,128]{2,1,0:T(8,128)(2,1)S(1)}, u32[]{:S(2)}, u32[]{:S(2)}) collective-permute-start(bf16[2,128,128]{2,1,0:T(8,128)(2,1)S(1)} %get-tuple-element.37), channel_id=1, source_target_pairs={{0,64},{2,66},{4,68},{6,70},{8,72},{10,74},{12,76},{14,78},{16,24}... | collective-permute-start | bytes 196616 | tf_op jit(solution)/shard_map/ppermute | solution.py:294
  82.2 4.5 %collective-permute-start.27 = (bf16[128,128]{1,0:T(8,128)(2,1)S(1)}, bf16[128,128]{1,0:T(8,128)(2,1)S(1)}, u32[]{:S(2)}, u32[]{:S(2)}) collective-permute-start(bf16[128,128]{1,0:T(8,128)(2,1)S(1)} %select_bitcast_fusion), channel_id=1, source_target_pairs={{0,16},{2,18},{4,20},{6,22},{8,24},{10,26},{12,28},{14,30},{16,0},... | collective-permute-start | bytes 98312 | tf_op jit(solution)/shard_map/ppermute | solution.py:294
  85.6 6.7 %collective-permute-start.23 = (bf16[64,1024]{1,0:T(8,128)(2,1)S(1)}, bf16[64,1024]{1,0:T(8,128)(2,1)S(1)}, u32[]{:S(2)}, u32[]{:S(2)}) collective-permute-start(bf16[64,1024]{1,0:T(8,128)(2,1)S(1)} %get-tuple-element.39), channel_id=1, source_target_pairs={{0,64},{2,66},{4,68},{6,70},{8,72},{10,74},{12,76},{14,78},{16,80}... | collective-permute-start | bytes 393224 | tf_op jit(solution)/shard_map/ppermute | solution.py:294

commit v7 on v6

--- a/solution.py
+++ b/solution.py
@@ -13,8 +13,8 @@
 DOC_ROWS = 16
 CHUNK_BLOCKS = 5
 CHUNK = CHUNK_BLOCKS * BLOCK
-LONGEST = 20
 TILES = 4
+VMEM_MIB = 36
 PEERS = 2
 SCALE = float(HEAD) ** (-0.5)
 TO_EXP2 = SCALE * math.log2(math.e)
@@ -26,16 +26,12 @@
 
 
 class Setting:
-    def __init__(self, sizes, refs, kv_all, docs_all, tile_docs, cols, rows=None):
+    def __init__(self, sizes, place_ref, kv_all, docs_all, tile_docs, rows, part):
         self.nz, self.nx = nz, nx = sizes
         lines = nz
-        place_ref, doc_ref, own_ref, peer_ref, far_ref = refs[:5]
-        pieces = (refs[5 : 5 + lines], refs[5 + lines : 5 + 2 * lines])
         self.z, self.x, self.y, self.core = (place_ref[i] for i in range(4))
-        self.part = own_ref.shape[0]
-        self.width = own_ref.shape[1] // 2
-        self.heads = self.width // HEAD
-        self.rows = self.heads * self.part
+        self.part, self.rows = part, rows
+        self.heads = rows // part
         self.kv_all, self.docs_all, self.tile_docs = kv_all, docs_all, tile_docs
         self.blocks = kv_all.shape[1]
         self.steps = steps = range(lines)
@@ -52,31 +48,6 @@
             ]
 
         self.spots = (places(self.core), places(1 - self.core))
-        for which, arrived, spot in ((self.core, pieces[0], self.spots[0]), (1 - self.core, pieces[1], self.spots[1])):
-            for i in steps:
-                for j in steps:
-                    for c in range(2):
-                        kv_all[which, spot[-i][-j] + nx * c] = arrived[i][j, c * BLOCK : (c + 1) * BLOCK]
-        for i in steps:
-            for j in steps:
-                docs_all[i * lines + j] = pieces[0][i][j, 2 * BLOCK :].astype(jnp.float32)
-        part, width = self.part, self.width
-        tile_docs[0] = doc_ref[...].astype(jnp.float32)
-        tile_docs[1] = peer_ref[part:, :HEAD].astype(jnp.float32)
-        tile_docs[2] = far_ref[2 * part :, :HEAD].astype(jnp.float32)
-        tile_docs[3] = far_ref[2 * part :, width : width + HEAD].astype(jnp.float32)
-        sources = ((own_ref, 0), (peer_ref, 0), (far_ref, 0), (far_ref, part))
-        for t, (source, begin) in enumerate(sources):
-            for side in range(2):
-                whole = jnp.concatenate(
-                    [
-                        source[begin : begin + part, side * width + h * HEAD : side * width + (h + 1) * HEAD]
-                        for h in range(self.heads)
-                    ]
-                )
-                if rows is not None:
-                    rows[side, t] = whole
-                cols[side, t] = whole.T
         apart = nz // PEERS
         self.apart = apart
         self.row_token = lax.div(self.z, apart) * part + lax.rem(
@@ -110,42 +81,67 @@
         return self.kv_all[which, pl.ds(at, CHUNK_BLOCKS)].reshape(CHUNK, HEAD)
 
 
+def place_all(s, refs, pieces, kv_all, docs_all, tile_docs, cols, rows):
+    doc_ref, own_ref, peer_ref, far_ref = refs
+    lines, nx, steps = s.nz, s.nx, s.steps
+    for which, arrived, spot in ((s.core, pieces[0], s.spots[0]), (1 - s.core, pieces[1], s.spots[1])):
+        for i in steps:
+            for j in steps:
+                for c in range(2):
+                    kv_all[which, spot[-i][-j] + nx * c] = arrived[i][j, c * BLOCK : (c + 1) * BLOCK]
+    for i in steps:
+        for j in steps:
+            docs_all[i * lines + j] = pieces[0][i][j, 2 * BLOCK :].astype(jnp.float32)
+    part, width = s.part, s.heads * HEAD
+    tile_docs[0] = doc_ref[...].astype(jnp.float32)
+    tile_docs[1] = peer_ref[part:, :HEAD].astype(jnp.float32)
+    tile_docs[2] = far_ref[2 * part :, :HEAD].astype(jnp.float32)
+    tile_docs[3] = far_ref[2 * part :, width : width + HEAD].astype(jnp.float32)
+    sources = ((own_ref, 0), (peer_ref, 0), (far_ref, 0), (far_ref, part))
+    for t, (source, begin) in enumerate(sources):
+        for side in range(2):
+            whole = jnp.concatenate(
+                [
+                    source[begin : begin + part, side * width + h * HEAD : side * width + (h + 1) * HEAD]
+                    for h in range(s.heads)
+                ]
+            )
+            rows[side, t] = whole
+            cols[side, t] = whole.T
+
+
 def statistics(sizes, *refs):
-    count = 5 + 2 * sizes[0]
-    stats_ref = refs[count]
-    kv_all, docs_all, tile_docs, cols, scores = refs[count + 1 :]
-    s = Setting(sizes, refs, kv_all, docs_all, tile_docs, cols)
+    lines = sizes[0]
+    count = 5 + 2 * lines
+    stats_ref, kv_all, docs_all, tile_docs, cols, tile_rows = refs[count : count + 6]
+    part = refs[2].shape[0]
+    s = Setting(sizes, refs[0], kv_all, docs_all, tile_docs, cols.shape[-1], part)
+    pieces = (refs[5 : 5 + lines], refs[5 + lines : count])
+    place_all(s, refs[1:5], pieces, kv_all, docs_all, tile_docs, cols, tile_rows)
     rows = s.rows
 
     def fold(value, combine):
         return combine(value.reshape(CHUNK // 8, 8, rows), axis=0)
 
-    def slot(n):
-        return pl.ds(pl.multiple_of(n * CHUNK, CHUNK), CHUNK)
-
     def tile(t, carry):
         chunks, last, keys_at, mask = s.tile(t)
 
-        def score(n, top, masked):
-            value = dot(s.key_rows(0, keys_at(n)), cols[0, t], (1, 0))
+        def step(n, state, masked):
+            top, norm, weighted = state
+            at = keys_at(n)
+            value = dot(s.key_rows(0, at), cols[0, t], (1, 0))
             if masked:
                 value = jnp.where(mask, value, NEG)
-            scores[slot(n), :] = value
-            return jnp.maximum(top, fold(value, jnp.max))
-
-        top = jnp.full((8, rows), NEG, jnp.float32)
-        top = lax.fori_loop(0, last, lambda n, top: score(n, top, False), top)
-        top = lax.fori_loop(last, chunks, lambda n, top: score(n, top, True), top)
-        top = jnp.max(top, axis=0, keepdims=True) * TO_EXP2
-
-        def sums(n, state):
-            norm, weighted = state
-            e = jnp.exp2(scores[slot(n), :] * TO_EXP2 - top)
-            dp = dot(s.key_rows(1, keys_at(n)), cols[1, t], (1, 0))
-            return norm + fold(e, jnp.sum), weighted + fold(e * dp, jnp.sum)
+            dp = dot(s.key_rows(1, at), cols[1, t], (1, 0))
+            raised = jnp.maximum(top, jnp.max(fold(value, jnp.max), axis=0, keepdims=True) * TO_EXP2)
+            e = jnp.exp2(value * TO_EXP2 - raised)
+            factor = jnp.exp2(top - raised)
+            return raised, norm * factor + fold(e, jnp.sum), weighted * factor + fold(e * dp, jnp.sum)
 
         zeros = jnp.zeros((8, rows), jnp.float32)
-        norm, weighted = lax.fori_loop(0, chunks, sums, (zeros, zeros))
+        state = (jnp.full((1, rows), NEG, jnp.float32), zeros, zeros)
+        state = lax.fori_loop(0, last, lambda n, state: step(n, state, False), state)
+        top, norm, weighted = lax.fori_loop(last, chunks, lambda n, state: step(n, state, True), state)
         stats_ref[t, 0:1, :] = top
         stats_ref[t, 1:2, :] = jnp.sum(norm, axis=0, keepdims=True)
         stats_ref[t, 2:3, :] = jnp.sum(weighted, axis=0, keepdims=True)
@@ -157,12 +153,11 @@
 
 def gradients(sizes, *refs):
     lines = sizes[0]
-    count = 5 + 2 * lines
-    here_ref, there_ref, dq_ref = refs[count : count + 3]
-    outs = refs[count + 3 : count + 3 + 2 * lines]
-    kv_all, docs_all, tile_docs, cols, tile_rows, totals = refs[count + 3 + 2 * lines :]
+    place_ref, here_ref, there_ref, kv_all, docs_all, tile_docs, cols, tile_rows, dq_ref = refs[:9]
+    outs = refs[9 : 9 + 2 * lines]
+    totals = refs[9 + 2 * lines]
     totals[...] = jnp.zeros_like(totals)
-    s = Setting(sizes, refs, kv_all, docs_all, tile_docs, cols, tile_rows)
+    s = Setting(sizes, place_ref, kv_all, docs_all, tile_docs, cols.shape[-1], dq_ref.shape[1])
     part, rows = s.part, s.rows
 
     def tile(t, carry):
@@ -173,8 +168,8 @@
         weight_here, weight_there = jnp.exp2(top_here - top), jnp.exp2(top_there - top)
         norm = here_ref[t, 1:2, :] * weight_here + there_ref[other, 1:2, :] * weight_there
         weighted = here_ref[t, 2:3, :] * weight_here + there_ref[other, 2:3, :] * weight_there
-        inverse = 1.0 / norm
-        delta = weighted * inverse
+        delta = weighted / norm
+        top = top + jnp.log2(norm)
 
         def work(n, dq, masked):
             at = keys_at(n)
@@ -182,7 +177,7 @@
             value = dot(s.key_rows(0, at), cols[0, t], (1, 0))
             if masked:
                 value = jnp.where(mask, value, NEG)
-            p = jnp.exp2(value * TO_EXP2 - top) * inverse
+            p = jnp.exp2(value * TO_EXP2 - top)
             ds = p * (dot(s.key_rows(1, at), cols[1, t], (1, 0)) - delta)
             p_low = p.astype(jnp.bfloat16)
             ds_low = ds.astype(jnp.bfloat16)
@@ -208,11 +203,7 @@
                     out[i][j, c] = totals[which, pl.ds(begin, BLOCK), :].astype(jnp.bfloat16)
 
 
-def kernel_call(kernel, sizes, operands, outs, extra, pairs):
-    nz, nx = sizes
-    part, width = operands[2].shape
-    rows = part * width // (2 * HEAD)
-    blocks = 2 * nz * nx
+def kernel_call(kernel, sizes, operands, outs, scratch, products):
     whole = pl.BlockSpec(memory_space=pltpu.VMEM)
     return pl.pallas_call(
         lambda *refs: kernel(sizes, *refs),
@@ -220,45 +211,37 @@
         out_shape=outs,
         in_specs=[pl.BlockSpec(memory_space=pltpu.SMEM)] + [whole] * (len(operands) - 1),
         out_specs=(whole,) * len(outs),
-        scratch_shapes=[
-            pltpu.VMEM((2, blocks, BLOCK, HEAD), jnp.bfloat16),
-            pltpu.VMEM((nz * nx, DOC_ROWS, HEAD), jnp.float32),
-            pltpu.VMEM((TILES, DOC_ROWS, HEAD), jnp.float32),
-            pltpu.VMEM((2, TILES, HEAD, rows), jnp.bfloat16),
-        ]
-        + extra(rows, blocks),
-        compiler_params=pltpu.CompilerParams(vmem_limit_bytes=36 * 1024 * 1024),
+        scratch_shapes=scratch,
+        compiler_params=pltpu.CompilerParams(vmem_limit_bytes=VMEM_MIB * 1024 * 1024),
         cost_estimate=pl.CostEstimate(
-            flops=pairs * 2 * 24 * 1024 * 128 * 128, bytes_accessed=8 * 1024 * 1024, transcendentals=0
+            flops=products * 2 * 24 * 1024 * 128 * 128, bytes_accessed=8 * 1024 * 1024, transcendentals=0
         ),
     )(*operands)
 
 
 def statistics_call(sizes, *operands):
-    rows = operands[2].shape[0] * operands[2].shape[1] // (2 * HEAD)
-    slots = -(-LONGEST // CHUNK_BLOCKS) * CHUNK
-    outs = (jax.ShapeDtypeStruct((TILES, 8, rows), jnp.float32),)
-    return kernel_call(
-        statistics, sizes, operands, outs, lambda rows, blocks: [pltpu.VMEM((slots, rows), jnp.float32)], 2
-    )[0]
-
-
-def gradients_call(sizes, *operands):
     nz, nx = sizes
     part, width = operands[2].shape
-    outs = (jax.ShapeDtypeStruct((TILES, part, width // 2), jnp.float32),)
+    rows = part * width // (2 * HEAD)
+    outs = (
+        jax.ShapeDtypeStruct((TILES, 8, rows), jnp.float32),
+        jax.ShapeDtypeStruct((2, 2 * nz * nx, BLOCK, HEAD), jnp.bfloat16),
+        jax.ShapeDtypeStruct((nz * nx, DOC_ROWS, HEAD), jnp.float32),
+        jax.ShapeDtypeStruct((TILES, DOC_ROWS, HEAD), jnp.float32),
+        jax.ShapeDtypeStruct((2, TILES, HEAD, rows), jnp.bfloat16),
+        jax.ShapeDtypeStruct((2, TILES, rows, HEAD), jnp.bfloat16),
+    )
+    return kernel_call(statistics, sizes, operands, outs, [], 2)
+
+
+def gradients_call(sizes, part, place, here, there, kv, docs, tile_docs, cols, rows):
+    nz, nx = sizes
+    width = rows.shape[2] * HEAD // part
+    outs = (jax.ShapeDtypeStruct((TILES, part, width), jnp.float32),)
     outs += (jax.ShapeDtypeStruct((nx, 2, BLOCK, HEAD), jnp.bfloat16),) * (2 * nz)
-    return kernel_call(
-        gradients,
-        sizes,
-        operands,
-        outs,
-        lambda rows, blocks: [
-            pltpu.VMEM((2, TILES, rows, HEAD), jnp.bfloat16),
-            pltpu.VMEM((2, blocks * BLOCK, HEAD), jnp.float32),
-        ],
-        5,
-    )
+    scratch = [pltpu.VMEM((2, kv.shape[1] * BLOCK, HEAD), jnp.float32)]
+    operands = (place, here, there, kv, docs, tile_docs, cols, rows)
+    return kernel_call(gradients, sizes, operands, outs, scratch, 5)
 
 
 def low(value):
@@ -336,8 +319,8 @@
     place = jnp.stack([z, x, y, core]).astype(jnp.int32)
     sizes = (nz, nx)
     operands = (place, doc, own, borrowed, far, *mine, *theirs)
-    here = statistics_call(sizes, *operands)
-    dq, *sums = gradients_call(sizes, *operands, here, other_y(here))
+    here, *placed = statistics_call(sizes, *operands)
+    dq, *sums = gradients_call(sizes, part, place, here, other_y(here), *placed)
     keep, send = sums[:lines], sums[lines:]
 
     totals = [None] * lines
@@ -350,7 +333,9 @@
     dq = low(dq[:2] + rest.astype(jnp.float32))
     returned = peer(dq[1])
     total = low(added([totals[0]] + arrived))
-    total = added([total[0]] + [along_first(total[by], by) for by in range(1, lines)])
+    short = [along_first(total[by], by) for by in range(1, lines)]
+    short, returned = lax.optimization_barrier((short, returned))
+    total = added([total[0]] + short)
     total = low(jnp.where(core == 0, SCALE * total, total))
     ours = jnp.where(core == 0, total[0], total[1])
     theirs = other_core(jnp.where(core == 0, total[1], total[0]))

time: 92.9 us -> 88.1 us (0.948); the launches traced: 93 us -> 86.4 us
  waiting for transfers between devices: 24.2 us -> 20.1 us
  Pallas kernels: 22.4 us -> 21.1 us
  starting transfers between devices: 39.1 us -> 37.9 us
    ppermute x28, waiting for transfers between devices: 24.2 us -> 20.1 us  [moved(): return lax.ppermute(value, CONTEXT, hops)]
    pallas_call x2, Pallas kernels: 22.4 us -> 21.1 us  [kernel_call(): pl.pallas_call(lambda *refs: kernel(sizes, *refs), name=kernel.__name__,...]
    ppermute x28, starting transfers between devices: 39.1 us -> 37.9 us  [moved(): return lax.ppermute(value, CONTEXT, hops)]
  transfers between devices with their start and end apart: 28 -> 28, of which waited for: 12 -> 13; matrix products, arithmetic and copies ran while one was open for 5% -> 6% of each run, Pallas kernels for 0% -> 0%
where the time goes in v7:
time: 88.1 us; the launch traced here: 86.4 us
  starting transfers between devices  37.9 us (43%)
  Pallas kernels  21.1 us (24%)
  waiting for transfers between devices  20.1 us (23%)
  other arithmetic  3.74 us (4%)
  local copies, waits for them, and re-layouts  2.06 us (2%)
  between operations  1.49 us (2%)
    ppermute x28, starting transfers between devices, moved(): return lax.ppermute(value, CONTEXT, hops)  37.9 us
    pallas_call x2, Pallas kernels, kernel_call(): pl.pallas_call(lambda *refs: kernel(sizes, *refs), name=kernel.__name__,...  21.1 us
    ppermute x28, waiting for transfers between devices, moved(): return lax.ppermute(value, CONTEXT, hops)  20.1 us
  transfers between devices with their start and end apart: 28, of which 13 were waited for; matrix products, arithmetic and copies ran while one was open for 6% of the time, Pallas kernels for 0%

profile of v7, /device:TPU:1, one launch (start us, length us, event | category | flops | bytes accessed | tf_op | source)
XLA Modules:
  0.0 86.4 jit_solution(14661041555787760744)
XLA Ops:
  1.3 1.5 %collective-permute-start.3 = (bf16[16,128]{1,0:T(8,128)(2,1)S(1)}, bf16[16,128]{1,0:T(8,128)(2,1)S(1)}, u32[]{:S(2)}, u32[]{:S(2)}) collective-permute-start(bf16[16,128]{1,0:T(8,128)(2,1)S(1)} %broadcast_in_dim.5.refs_1_), channel_id=1, source_target_pairs={{0,16},{2,18},{4,20},{6,22},{8,24},{10,26},{12,28},{14,30},{16,0},... | collective-permute-start | bytes 12296 | tf_op jit(solution)/shard_map/ppermute | solution.py:277
  2.8 0.8 select_bitcast_fusion.1
  3.6 0.1 collective-permute-start.2
  3.7 1.0 %constant_dynamic-update-slice_fusion.1 = bf16[128,2048]{1,0:T(8,128)(2,1)S(1)} fusion(bf16[128,1024]{1,0:T(8,128)(2,1)} %param.5), kind=kLoop, calls=%fused_computation.33 | loop fusion | bytes 524288
  4.6 1.0 %constant_dynamic-update-slice_fusion = bf16[128,2048]{1,0:T(8,128)(2,1)S(1)} fusion(bf16[128,2048]{1,0:T(8,128)(2,1)S(1)} %constant_dynamic-update-slice_fusion.1, bf16[128,1024]{1,0:T(8,128)(2,1)} %param.8), kind=kLoop, calls=%fused_computation.32 | loop fusion | bytes 524288 | tf_op jit(solution)/shard_map/concatenate | solution.py:300
  5.7 3.8 %collective-permute-start = (bf16[80,2048]{1,0:T(8,128)(2,1)S(1)}, bf16[80,2048]{1,0:T(8,128)(2,1)S(1)}, u32[]{:S(2)}, u32[]{:S(2)}) collective-permute-start(bf16[80,2048]{1,0:T(8,128)(2,1)S(1)} %concatenate.16), channel_id=1, source_target_pairs={{0,64},{2,66},{4,68},{6,70},{8,72},{10,74},{12,76},{14,78},{16,80}... | collective-permute-start | bytes 983048 | tf_op jit(solution)/shard_map/ppermute | solution.py:277
  9.5 2.8 %collective-permute-start.5 = (bf16[272,128]{1,0:T(8,128)(2,1)S(1)}, bf16[272,128]{1,0:T(8,128)(2,1)S(1)}, u32[]{:S(2)}, u32[]{:S(2)}) collective-permute-start(bf16[272,128]{1,0:T(8,128)(2,1)S(1)} %get-tuple-element.63), channel_id=1, source_target_pairs={{0,64},{2,66},{4,68},{6,70},{8,72},{10,74},{12,76},{14,78},{16,24}... | collective-permute-start | bytes 208904 | tf_op jit(solution)/shard_map/ppermute | solution.py:277
  12.3 0.3 collective-permute-start.4
  12.7 2.4 %collective-permute-start.6 = (bf16[272,128]{1,0:T(8,128)(2,1)S(1)}, bf16[272,128]{1,0:T(8,128)(2,1)S(1)}, u32[]{:S(2)}, u32[]{:S(2)}) collective-permute-start(bf16[272,128]{1,0:T(8,128)(2,1)S(1)} %get-tuple-element.63), channel_id=1, source_target_pairs={{0,96},{2,98},{4,100},{6,102},{8,104},{10,106},{12,108},{14,110},{... | collective-permute-start | bytes 208904 | tf_op jit(solution)/shard_map/ppermute | solution.py:277
  15.0 2.1 %collective-permute-done.refs_3_ = bf16[80,2048]{1,0:T(8,128)(2,1)S(1)} collective-permute-done((bf16[80,2048]{1,0:T(8,128)(2,1)S(1)}, bf16[80,2048]{1,0:T(8,128)(2,1)S(1)}, u32[]{:S(2)}, u32[]{:S(2)}) %collective-permute-start) | collective-permute-done | bytes 327712 | tf_op jit(solution)/shard_map/ppermute | solution.py:277
  17.2 0.9 fusion.1
  18.1 1.3 %collective-permute-start.1 = (bf16[144,2048]{1,0:T(8,128)(2,1)}, bf16[144,2048]{1,0:T(8,128)(2,1)S(1)}, u32[]{:S(2)}, u32[]{:S(2)}) collective-permute-start(bf16[144,2048]{1,0:T(8,128)(2,1)} %fusion.1), channel_id=1, source_target_pairs={{0,2},{2,0},{4,6},{6,4},{8,10},{10,8},{12,14},{14,12},{16,18},{18,... | collective-permute-start | bytes 1769480 | tf_op jit(solution)/shard_map/ppermute | solution.py:277
  19.4 2.9 %collective-permute-start.9 = (bf16[4,272,128]{2,1,0:T(8,128)(2,1)S(1)}, bf16[4,272,128]{2,1,0:T(8,128)(2,1)S(1)}, u32[]{:S(2)}, u32[]{:S(2)}) collective-permute-start(bf16[4,272,128]{2,1,0:T(8,128)(2,1)S(1)} %pad_maximum_fusion.refs_5_), channel_id=1, source_target_pairs={{0,12},{2,14},{4,0},{6,2},{8,4},{10,6},{12,8},{14,10},{16,112},{18... | collective-permute-start | bytes 835592 | tf_op jit(solution)/shard_map/ppermute | solution.py:277
  22.3 0.7 collective-permute-start.7
  23.0 2.3 %collective-permute-start.10 = (bf16[4,272,128]{2,1,0:T(8,128)(2,1)S(1)}, bf16[4,272,128]{2,1,0:T(8,128)(2,1)S(1)}, u32[]{:S(2)}, u32[]{:S(2)}) collective-permute-start(bf16[4,272,128]{2,1,0:T(8,128)(2,1)S(1)} %pad_maximum_fusion.refs_5_), channel_id=1, source_target_pairs={{0,16},{2,18},{4,20},{6,22},{8,24},{10,26},{12,28},{14,30},{16,0},... | collective-permute-start | bytes 835592 | tf_op jit(solution)/shard_map/ppermute | solution.py:277
  25.3 3.5 %collective-permute-done.9.refs_8_ = bf16[4,272,128]{2,1,0:T(8,128)(2,1)S(1)} collective-permute-done((bf16[4,272,128]{2,1,0:T(8,128)(2,1)S(1)}, bf16[4,272,128]{2,1,0:T(8,128)(2,1)S(1)}, u32[]{:S(2)}, u32[]{:S(2)}) %collective-permute-start.9) | collective-permute-done | bytes 278560 | tf_op jit(solution)/shard_map/ppermute | solution.py:277
  28.7 1.9 %collective-permute-start.13 = (bf16[4,272,128]{2,1,0:T(8,128)(2,1)S(1)}, bf16[4,272,128]{2,1,0:T(8,128)(2,1)S(1)}, u32[]{:S(2)}, u32[]{:S(2)}) collective-permute-start(bf16[4,272,128]{2,1,0:T(8,128)(2,1)S(1)} %collective-permute-done.9.refs_8_), channel_id=1, source_target_pairs={{0,16},{2,18},{4,20},{6,22},{8,24},{10,26},{12,28},{14,30},{16,0},... | collective-permute-start | bytes 835592 | tf_op jit(solution)/shard_map/ppermute | solution.py:277
  30.7 1.1 %collective-permute-start.12 = (bf16[4,272,128]{2,1,0:T(8,128)(2,1)S(1)}, bf16[4,272,128]{2,1,0:T(8,128)(2,1)S(1)}, u32[]{:S(2)}, u32[]{:S(2)}) collective-permute-start(bf16[4,272,128]{2,1,0:T(8,128)(2,1)S(1)} %collective-permute-done.8.refs_7_), channel_id=1, source_target_pairs={{0,16},{2,18},{4,20},{6,22},{8,24},{10,26},{12,28},{14,30},{16,0},... | collective-permute-start | bytes 835592 | tf_op jit(solution)/shard_map/ppermute | solution.py:277
  31.7 0.4 collective-permute-done.7.refs_6_
  32.2 2.5 %collective-permute-start.11 = (bf16[4,272,128]{2,1,0:T(8,128)(2,1)S(1)}, bf16[4,272,128]{2,1,0:T(8,128)(2,1)S(1)}, u32[]{:S(2)}, u32[]{:S(2)}) collective-permute-start(bf16[4,272,128]{2,1,0:T(8,128)(2,1)S(1)} %collective-permute-done.7.refs_6_), channel_id=1, source_target_pairs={{0,16},{2,18},{4,20},{6,22},{8,24},{10,26},{12,28},{14,30},{16,0},... | collective-permute-start | bytes 835592 | tf_op jit(solution)/shard_map/ppermute | solution.py:277
  34.6 0.1 pad_add_fusion.refs_0_
  34.7 1.1 %collective-permute-done.11.refs_10_ = bf16[4,272,128]{2,1,0:T(8,128)(2,1)S(1)} collective-permute-done((bf16[4,272,128]{2,1,0:T(8,128)(2,1)S(1)}, bf16[4,272,128]{2,1,0:T(8,128)(2,1)S(1)}, u32[]{:S(2)}, u32[]{:S(2)}) %collective-permute-start.11) | collective-permute-done | bytes 278560 | tf_op jit(solution)/shard_map/ppermute | solution.py:277
  35.8 8.1 %statistics.1 = (f32[4,8,512]{2,1,0:T(8,128)S(1)}, bf16[2,32,128,128]{3,2,1,0:T(8,128)(2,1)S(1)}, f32[16,16,128]{2,1,0:T(8,128)S(1)}, f32[4,16,128]{2,1,0:T(8,12...) custom-call(s32[4]{0:T(128)S(1)} %pad_add_fusion.refs_0_, ...), custom_call_target="tpu_custom_call" | custom-call | flops 1610612736 | bytes 8388608 | tf_op jit(solution)/shard_map/statistics/pallas_call | solution.py:208
  43.9 1.1 %collective-permute-start.14 = (f32[4,8,512]{2,1,0:T(8,128)S(1)}, f32[4,8,512]{2,1,0:T(8,128)S(1)}, u32[]{:S(2)}, u32[]{:S(2)}) collective-permute-start(f32[4,8,512]{2,1,0:T(8,128)S(1)} %get-tuple-element.28.refs_1_), channel_id=1, source_target_pairs={{0,2},{2,0},{4,6},{6,4},{8,10},{10,8},{12,14},{14,12},{16,18},{18,... | collective-permute-start | bytes 196616 | tf_op jit(solution)/shard_map/ppermute | solution.py:277
  45.0 2.5 %collective-permute-done.14.refs_2_ = f32[4,8,512]{2,1,0:T(8,128)S(1)} collective-permute-done((f32[4,8,512]{2,1,0:T(8,128)S(1)}, f32[4,8,512]{2,1,0:T(8,128)S(1)}, u32[]{:S(2)}, u32[]{:S(2)}) %collective-permute-start.14) | collective-permute-done | bytes 65568 | tf_op jit(solution)/shard_map/ppermute | solution.py:277
  47.5 12.9 %gradients.1 = (f32[4,64,1024]{2,1,0:T(8,128)S(1)}, bf16[4,2,128,128]{3,2,1,0:T(8,128)(2,1)S(1)}, bf16[4,2,128,128]{3,2,1,0:T(8,128)(2,1)S(1)}, bf16[4,2,128,128...) custom-call(s32[4]{0:T(128)S(1)} %pad_add_fusion.refs_0_, ...), custom_call_target="tpu_custom_call" | custom-call | flops 4026531840 | bytes 8388608 | tf_op jit(solution)/shard_map/gradients/pallas_call | solution.py:208
  60.4 0.1 collective-permute-start.15
  60.5 0.5 collective-permute-start.16
  61.0 0.1 collective-permute-start.18
  61.1 0.4 collective-permute-start.20
  61.5 0.5 collective-permute-done.15
  62.1 0.7 collective-permute-start.22
  63.1 2.8 %collective-permute-start.19 = (bf16[4,2,128,128]{3,2,1,0:T(8,128)(2,1)S(1)}, bf16[4,2,128,128]{3,2,1,0:T(8,128)(2,1)S(1)}, u32[]{:S(2)}, u32[]{:S(2)}) collective-permute-start(bf16[4,2,128,128]{3,2,1,0:T(8,128)(2,1)S(1)} %add_convert_fusion.3), channel_id=1, source_target_pairs={{0,8},{2,10},{4,12},{6,14},{8,0},{10,2},{12,4},{14,6},{16,80},{18,... | collective-permute-start | bytes 786440 | tf_op jit(solution)/shard_map/ppermute | solution.py:277
  66.0 1.9 %collective-permute-start.21 = (bf16[4,2,128,128]{3,2,1,0:T(8,128)(2,1)S(1)}, bf16[4,2,128,128]{3,2,1,0:T(8,128)(2,1)S(1)}, u32[]{:S(2)}, u32[]{:S(2)}) collective-permute-start(bf16[4,2,128,128]{3,2,1,0:T(8,128)(2,1)S(1)} %add_convert_fusion.2), channel_id=1, source_target_pairs={{0,12},{2,14},{4,0},{6,2},{8,4},{10,6},{12,8},{14,10},{16,112},{18... | collective-permute-start | bytes 786440 | tf_op jit(solution)/shard_map/ppermute | solution.py:277
  67.9 2.1 %collective-permute-done.22 = bf16[2,64,1024]{2,1,0:T(8,128)(2,1)S(1)} collective-permute-done((bf16[2,64,1024]{2,1,0:T(8,128)(2,1)S(1)}, bf16[2,64,1024]{2,1,0:T(8,128)(2,1)S(1)}, u32[]{:S(2)}, u32[]{:S(2)}) %collective-permute-start.22) | collective-permute-done | bytes 262176 | tf_op jit(solution)/shard_map/ppermute | solution.py:277
  70.0 2.6 %collective-permute-done.17 = bf16[4,2,128,128]{3,2,1,0:T(8,128)(2,1)S(1)} collective-permute-done((bf16[4,2,128,128]{3,2,1,0:T(8,128)(2,1)S(1)}, bf16[4,2,128,128]{3,2,1,0:T(8,128)(2,1)S(1)}, u32[]{:S(2)}, u32[]{:S(2)}) %collective-permute-start.17) | collective-permute-done | bytes 262176 | tf_op jit(solution)/shard_map/ppermute | solution.py:277
  72.6 0.7 collective-permute-done.21
  73.4 2.6 %collective-permute-start.26 = (bf16[64,1024]{1,0:T(8,128)(2,1)S(1)}, bf16[64,1024]{1,0:T(8,128)(2,1)S(1)}, u32[]{:S(2)}, u32[]{:S(2)}) collective-permute-start(bf16[64,1024]{1,0:T(8,128)(2,1)S(1)} %get-tuple-element.56), channel_id=1, source_target_pairs={{0,64},{2,66},{4,68},{6,70},{8,72},{10,74},{12,76},{14,78},{16,80}... | collective-permute-start | bytes 393224 | tf_op jit(solution)/shard_map/ppermute | solution.py:277
  76.0 0.1 add_convert_fusion
  76.2 2.0 %collective-permute-start.25 = (bf16[2,128,128]{2,1,0:T(8,128)(2,1)S(1)}, bf16[2,128,128]{2,1,0:T(8,128)(2,1)S(1)}, u32[]{:S(2)}, u32[]{:S(2)}) collective-permute-start(bf16[2,128,128]{2,1,0:T(8,128)(2,1)S(1)} %get-tuple-element.57), channel_id=1, source_target_pairs={{0,96},{2,98},{4,100},{6,102},{8,104},{10,106},{12,108},{14,110},{... | collective-permute-start | bytes 196616 | tf_op jit(solution)/shard_map/ppermute | solution.py:277
  78.1 0.7 collective-permute-start.23
  78.8 1.2 %collective-permute-done.25 = bf16[2,128,128]{2,1,0:T(8,128)(2,1)S(1)} collective-permute-done((bf16[2,128,128]{2,1,0:T(8,128)(2,1)S(1)}, bf16[2,128,128]{2,1,0:T(8,128)(2,1)S(1)}, u32[]{:S(2)}, u32[]{:S(2)}) %collective-permute-start.25) | collective-permute-done | bytes 65568 | tf_op jit(solution)/shard_map/ppermute | solution.py:277
  80.1 3.0 %collective-permute-done.24 = bf16[2,128,128]{2,1,0:T(8,128)(2,1)S(1)} collective-permute-done((bf16[2,128,128]{2,1,0:T(8,128)(2,1)S(1)}, bf16[2,128,128]{2,1,0:T(8,128)(2,1)S(1)}, u32[]{:S(2)}, u32[]{:S(2)}) %collective-permute-start.24) | collective-permute-done | bytes 65568 | tf_op jit(solution)/shard_map/ppermute | solution.py:277
  83.1 0.2 collective-permute-done.23
  83.4 1.6 %collective-permute-start.27 = (bf16[128,128]{1,0:T(8,128)(2,1)S(1)}, bf16[128,128]{1,0:T(8,128)(2,1)S(1)}, u32[]{:S(2)}, u32[]{:S(2)}) collective-permute-start(bf16[128,128]{1,0:T(8,128)(2,1)S(1)} %select_bitcast_fusion), channel_id=1, source_target_pairs={{0,16},{2,18},{4,20},{6,22},{8,24},{10,26},{12,28},{14,30},{16,0},... | collective-permute-start | bytes 98312 | tf_op jit(solution)/shard_map/ppermute | solution.py:277
  84.9 0.7 maximum_select_fusion
  85.6 0.1 collective-permute-done.27
  85.8 0.6 bitcast_select_fusion
  (38 shorter events, 0.7 us)
Async XLA Ops:
  1.3 8.2 %collective-permute-start.3 = (bf16[16,128]{1,0:T(8,128)(2,1)S(1)}, bf16[16,128]{1,0:T(8,128)(2,1)S(1)}, u32[]{:S(2)}, u32[]{:S(2)}) collective-permute-start(bf16[16,128]{1,0:T(8,128)(2,1)S(1)} %broadcast_in_dim.5.refs_1_), channel_id=1, source_target_pairs={{0,16},{2,18},{4,20},{6,22},{8,24},{10,26},{12,28},{14,30},{16,0},... | collective-permute-start | bytes 12296 | tf_op jit(solution)/shard_map/ppermute | solution.py:277
  3.6 5.9 %collective-permute-start.2 = (bf16[128,128]{1,0:T(8,128)(2,1)S(1)}, bf16[128,128]{1,0:T(8,128)(2,1)S(1)}, u32[]{:S(2)}, u32[]{:S(2)}) collective-permute-start(bf16[128,128]{1,0:T(8,128)(2,1)S(1)} %get-tuple-element.65), channel_id=1, source_target_pairs={{0,16},{2,18},{4,20},{6,22},{8,24},{10,26},{12,28},{14,30},{16,0},... | collective-permute-start | bytes 98312 | tf_op jit(solution)/shard_map/ppermute | solution.py:277
  5.7 11.5 %collective-permute-start = (bf16[80,2048]{1,0:T(8,128)(2,1)S(1)}, bf16[80,2048]{1,0:T(8,128)(2,1)S(1)}, u32[]{:S(2)}, u32[]{:S(2)}) collective-permute-start(bf16[80,2048]{1,0:T(8,128)(2,1)S(1)} %concatenate.16), channel_id=1, source_target_pairs={{0,64},{2,66},{4,68},{6,70},{8,72},{10,74},{12,76},{14,78},{16,80}... | collective-permute-start | bytes 983048 | tf_op jit(solution)/shard_map/ppermute | solution.py:277
  9.5 9.8 %collective-permute-start.5 = (bf16[272,128]{1,0:T(8,128)(2,1)S(1)}, bf16[272,128]{1,0:T(8,128)(2,1)S(1)}, u32[]{:S(2)}, u32[]{:S(2)}) collective-permute-start(bf16[272,128]{1,0:T(8,128)(2,1)S(1)} %get-tuple-element.63), channel_id=1, source_target_pairs={{0,64},{2,66},{4,68},{6,70},{8,72},{10,74},{12,76},{14,78},{16,24}... | collective-permute-start | bytes 208904 | tf_op jit(solution)/shard_map/ppermute | solution.py:277
  12.3 7.0 %collective-permute-start.4 = (bf16[272,128]{1,0:T(8,128)(2,1)S(1)}, bf16[272,128]{1,0:T(8,128)(2,1)S(1)}, u32[]{:S(2)}, u32[]{:S(2)}) collective-permute-start(bf16[272,128]{1,0:T(8,128)(2,1)S(1)} %get-tuple-element.63), channel_id=1, source_target_pairs={{0,32},{2,34},{4,36},{6,38},{8,40},{10,42},{12,44},{14,46},{16,20}... | collective-permute-start | bytes 208904 | tf_op jit(solution)/shard_map/ppermute | solution.py:277
  12.7 6.7 %collective-permute-start.6 = (bf16[272,128]{1,0:T(8,128)(2,1)S(1)}, bf16[272,128]{1,0:T(8,128)(2,1)S(1)}, u32[]{:S(2)}, u32[]{:S(2)}) collective-permute-start(bf16[272,128]{1,0:T(8,128)(2,1)S(1)} %get-tuple-element.63), channel_id=1, source_target_pairs={{0,96},{2,98},{4,100},{6,102},{8,104},{10,106},{12,108},{14,110},{... | collective-permute-start | bytes 208904 | tf_op jit(solution)/shard_map/ppermute | solution.py:277
  18.1 17.8 %collective-permute-start.1 = (bf16[144,2048]{1,0:T(8,128)(2,1)}, bf16[144,2048]{1,0:T(8,128)(2,1)S(1)}, u32[]{:S(2)}, u32[]{:S(2)}) collective-permute-start(bf16[144,2048]{1,0:T(8,128)(2,1)} %fusion.1), channel_id=1, source_target_pairs={{0,2},{2,0},{4,6},{6,4},{8,10},{10,8},{12,14},{14,12},{16,18},{18,... | collective-permute-start | bytes 1769480 | tf_op jit(solution)/shard_map/ppermute | solution.py:277
  19.4 9.3 %collective-permute-start.9 = (bf16[4,272,128]{2,1,0:T(8,128)(2,1)S(1)}, bf16[4,272,128]{2,1,0:T(8,128)(2,1)S(1)}, u32[]{:S(2)}, u32[]{:S(2)}) collective-permute-start(bf16[4,272,128]{2,1,0:T(8,128)(2,1)S(1)} %pad_maximum_fusion.refs_5_), channel_id=1, source_target_pairs={{0,12},{2,14},{4,0},{6,2},{8,4},{10,6},{12,8},{14,10},{16,112},{18... | collective-permute-start | bytes 835592 | tf_op jit(solution)/shard_map/ppermute | solution.py:277
  22.3 8.4 %collective-permute-start.8 = (bf16[4,272,128]{2,1,0:T(8,128)(2,1)S(1)}, bf16[4,272,128]{2,1,0:T(8,128)(2,1)S(1)}, u32[]{:S(2)}, u32[]{:S(2)}) collective-permute-start(bf16[4,272,128]{2,1,0:T(8,128)(2,1)S(1)} %pad_maximum_fusion.refs_5_), channel_id=1, source_target_pairs={{0,8},{2,10},{4,12},{6,14},{8,0},{10,2},{12,4},{14,6},{16,80},{18,... | collective-permute-start | bytes 835592 | tf_op jit(solution)/shard_map/ppermute | solution.py:277
  22.3 9.9 %collective-permute-start.7 = (bf16[4,272,128]{2,1,0:T(8,128)(2,1)S(1)}, bf16[4,272,128]{2,1,0:T(8,128)(2,1)S(1)}, u32[]{:S(2)}, u32[]{:S(2)}) collective-permute-start(bf16[4,272,128]{2,1,0:T(8,128)(2,1)S(1)} %pad_maximum_fusion.refs_5_), channel_id=1, source_target_pairs={{0,4},{2,6},{4,8},{6,10},{8,12},{10,14},{12,0},{14,2},{16,48},{18,... | collective-permute-start | bytes 835592 | tf_op jit(solution)/shard_map/ppermute | solution.py:277
  23.0 11.7 %collective-permute-start.10 = (bf16[4,272,128]{2,1,0:T(8,128)(2,1)S(1)}, bf16[4,272,128]{2,1,0:T(8,128)(2,1)S(1)}, u32[]{:S(2)}, u32[]{:S(2)}) collective-permute-start(bf16[4,272,128]{2,1,0:T(8,128)(2,1)S(1)} %pad_maximum_fusion.refs_5_), channel_id=1, source_target_pairs={{0,16},{2,18},{4,20},{6,22},{8,24},{10,26},{12,28},{14,30},{16,0},... | collective-permute-start | bytes 835592 | tf_op jit(solution)/shard_map/ppermute | solution.py:277
  28.7 6.0 %collective-permute-start.13 = (bf16[4,272,128]{2,1,0:T(8,128)(2,1)S(1)}, bf16[4,272,128]{2,1,0:T(8,128)(2,1)S(1)}, u32[]{:S(2)}, u32[]{:S(2)}) collective-permute-start(bf16[4,272,128]{2,1,0:T(8,128)(2,1)S(1)} %collective-permute-done.9.refs_8_), channel_id=1, source_target_pairs={{0,16},{2,18},{4,20},{6,22},{8,24},{10,26},{12,28},{14,30},{16,0},... | collective-permute-start | bytes 835592 | tf_op jit(solution)/shard_map/ppermute | solution.py:277
  30.7 4.0 %collective-permute-start.12 = (bf16[4,272,128]{2,1,0:T(8,128)(2,1)S(1)}, bf16[4,272,128]{2,1,0:T(8,128)(2,1)S(1)}, u32[]{:S(2)}, u32[]{:S(2)}) collective-permute-start(bf16[4,272,128]{2,1,0:T(8,128)(2,1)S(1)} %collective-permute-done.8.refs_7_), channel_id=1, source_target_pairs={{0,16},{2,18},{4,20},{6,22},{8,24},{10,26},{12,28},{14,30},{16,0},... | collective-permute-start | bytes 835592 | tf_op jit(solution)/shard_map/ppermute | solution.py:277
  32.2 3.6 %collective-permute-start.11 = (bf16[4,272,128]{2,1,0:T(8,128)(2,1)S(1)}, bf16[4,272,128]{2,1,0:T(8,128)(2,1)S(1)}, u32[]{:S(2)}, u32[]{:S(2)}) collective-permute-start(bf16[4,272,128]{2,1,0:T(8,128)(2,1)S(1)} %collective-permute-done.7.refs_6_), channel_id=1, source_target_pairs={{0,16},{2,18},{4,20},{6,22},{8,24},{10,26},{12,28},{14,30},{16,0},... | collective-permute-start | bytes 835592 | tf_op jit(solution)/shard_map/ppermute | solution.py:277
  43.9 3.5 %collective-permute-start.14 = (f32[4,8,512]{2,1,0:T(8,128)S(1)}, f32[4,8,512]{2,1,0:T(8,128)S(1)}, u32[]{:S(2)}, u32[]{:S(2)}) collective-permute-start(f32[4,8,512]{2,1,0:T(8,128)S(1)} %get-tuple-element.28.refs_1_), channel_id=1, source_target_pairs={{0,2},{2,0},{4,6},{6,4},{8,10},{10,8},{12,14},{14,12},{16,18},{18,... | collective-permute-start | bytes 196616 | tf_op jit(solution)/shard_map/ppermute | solution.py:277
  60.4 1.6 %collective-permute-start.15 = (bf16[4,2,128,128]{3,2,1,0:T(8,128)(2,1)S(1)}, bf16[4,2,128,128]{3,2,1,0:T(8,128)(2,1)S(1)}, u32[]{:S(2)}, u32[]{:S(2)}) collective-permute-start(bf16[4,2,128,128]{3,2,1,0:T(8,128)(2,1)S(1)} %get-tuple-element.36), channel_id=1, source_target_pairs={{0,16},{2,18},{4,20},{6,22},{8,24},{10,26},{12,28},{14,30},{16,0},... | collective-permute-start | bytes 786440 | tf_op jit(solution)/shard_map/ppermute | solution.py:277
  60.5 2.4 %collective-permute-start.16 = (bf16[4,2,128,128]{3,2,1,0:T(8,128)(2,1)S(1)}, bf16[4,2,128,128]{3,2,1,0:T(8,128)(2,1)S(1)}, u32[]{:S(2)}, u32[]{:S(2)}) collective-permute-start(bf16[4,2,128,128]{3,2,1,0:T(8,128)(2,1)S(1)} %get-tuple-element.39), channel_id=1, source_target_pairs={{0,16},{2,18},{4,20},{6,22},{8,24},{10,26},{12,28},{14,30},{16,0},... | collective-permute-start | bytes 786440 | tf_op jit(solution)/shard_map/ppermute | solution.py:277
  61.0 2.0 %collective-permute-start.18 = (bf16[4,2,128,128]{3,2,1,0:T(8,128)(2,1)S(1)}, bf16[4,2,128,128]{3,2,1,0:T(8,128)(2,1)S(1)}, u32[]{:S(2)}, u32[]{:S(2)}) collective-permute-start(bf16[4,2,128,128]{3,2,1,0:T(8,128)(2,1)S(1)} %get-tuple-element.41), channel_id=1, source_target_pairs={{0,16},{2,18},{4,20},{6,22},{8,24},{10,26},{12,28},{14,30},{16,0},... | collective-permute-start | bytes 786440 | tf_op jit(solution)/shard_map/ppermute | solution.py:277
  61.1 4.8 %collective-permute-start.20 = (bf16[4,2,128,128]{3,2,1,0:T(8,128)(2,1)S(1)}, bf16[4,2,128,128]{3,2,1,0:T(8,128)(2,1)S(1)}, u32[]{:S(2)}, u32[]{:S(2)}) collective-permute-start(bf16[4,2,128,128]{3,2,1,0:T(8,128)(2,1)S(1)} %get-tuple-element.43), channel_id=1, source_target_pairs={{0,16},{2,18},{4,20},{6,22},{8,24},{10,26},{12,28},{14,30},{16,0},... | collective-permute-start | bytes 786440 | tf_op jit(solution)/shard_map/ppermute | solution.py:277
  62.1 7.8 %collective-permute-start.22 = (bf16[2,64,1024]{2,1,0:T(8,128)(2,1)S(1)}, bf16[2,64,1024]{2,1,0:T(8,128)(2,1)S(1)}, u32[]{:S(2)}, u32[]{:S(2)}) collective-permute-start(bf16[2,64,1024]{2,1,0:T(8,128)(2,1)S(1)} %slice.109), channel_id=1, source_target_pairs={{0,2},{2,0},{4,6},{6,4},{8,10},{10,8},{12,14},{14,12},{16,18},{18,... | collective-permute-start | bytes 786440 | tf_op jit(solution)/shard_map/ppermute | solution.py:277
  62.9 9.6 %collective-permute-start.17 = (bf16[4,2,128,128]{3,2,1,0:T(8,128)(2,1)S(1)}, bf16[4,2,128,128]{3,2,1,0:T(8,128)(2,1)S(1)}, u32[]{:S(2)}, u32[]{:S(2)}) collective-permute-start(bf16[4,2,128,128]{3,2,1,0:T(8,128)(2,1)S(1)} %add_convert_fusion.4), channel_id=1, source_target_pairs={{0,4},{2,6},{4,8},{6,10},{8,12},{10,14},{12,0},{14,2},{16,48},{18,... | collective-permute-start | bytes 786440 | tf_op jit(solution)/shard_map/ppermute | solution.py:277
  63.1 9.4 %collective-permute-start.19 = (bf16[4,2,128,128]{3,2,1,0:T(8,128)(2,1)S(1)}, bf16[4,2,128,128]{3,2,1,0:T(8,128)(2,1)S(1)}, u32[]{:S(2)}, u32[]{:S(2)}) collective-permute-start(bf16[4,2,128,128]{3,2,1,0:T(8,128)(2,1)S(1)} %add_convert_fusion.3), channel_id=1, source_target_pairs={{0,8},{2,10},{4,12},{6,14},{8,0},{10,2},{12,4},{14,6},{16,80},{18,... | collective-permute-start | bytes 786440 | tf_op jit(solution)/shard_map/ppermute | solution.py:277
  66.0 7.3 %collective-permute-start.21 = (bf16[4,2,128,128]{3,2,1,0:T(8,128)(2,1)S(1)}, bf16[4,2,128,128]{3,2,1,0:T(8,128)(2,1)S(1)}, u32[]{:S(2)}, u32[]{:S(2)}) collective-permute-start(bf16[4,2,128,128]{3,2,1,0:T(8,128)(2,1)S(1)} %add_convert_fusion.2), channel_id=1, source_target_pairs={{0,12},{2,14},{4,0},{6,2},{8,4},{10,6},{12,8},{14,10},{16,112},{18... | collective-permute-start | bytes 786440 | tf_op jit(solution)/shard_map/ppermute | solution.py:277
  73.4 9.9 %collective-permute-start.26 = (bf16[64,1024]{1,0:T(8,128)(2,1)S(1)}, bf16[64,1024]{1,0:T(8,128)(2,1)S(1)}, u32[]{:S(2)}, u32[]{:S(2)}) collective-permute-start(bf16[64,1024]{1,0:T(8,128)(2,1)S(1)} %get-tuple-element.56), channel_id=1, source_target_pairs={{0,64},{2,66},{4,68},{6,70},{8,72},{10,74},{12,76},{14,78},{16,80}... | collective-permute-start | bytes 393224 | tf_op jit(solution)/shard_map/ppermute | solution.py:277
  76.2 3.9 %collective-permute-start.25 = (bf16[2,128,128]{2,1,0:T(8,128)(2,1)S(1)}, bf16[2,128,128]{2,1,0:T(8,128)(2,1)S(1)}, u32[]{:S(2)}, u32[]{:S(2)}) collective-permute-start(bf16[2,128,128]{2,1,0:T(8,128)(2,1)S(1)} %get-tuple-element.57), channel_id=1, source_target_pairs={{0,96},{2,98},{4,100},{6,102},{8,104},{10,106},{12,108},{14,110},{... | collective-permute-start | bytes 196616 | tf_op jit(solution)/shard_map/ppermute | solution.py:277
  78.1 4.9 %collective-permute-start.24 = (bf16[2,128,128]{2,1,0:T(8,128)(2,1)S(1)}, bf16[2,128,128]{2,1,0:T(8,128)(2,1)S(1)}, u32[]{:S(2)}, u32[]{:S(2)}) collective-permute-start(bf16[2,128,128]{2,1,0:T(8,128)(2,1)S(1)} %get-tuple-element.58), channel_id=1, source_target_pairs={{0,64},{2,66},{4,68},{6,70},{8,72},{10,74},{12,76},{14,78},{16,24}... | collective-permute-start | bytes 196616 | tf_op jit(solution)/shard_map/ppermute | solution.py:277
  78.1 5.1 %collective-permute-start.23 = (bf16[2,128,128]{2,1,0:T(8,128)(2,1)S(1)}, bf16[2,128,128]{2,1,0:T(8,128)(2,1)S(1)}, u32[]{:S(2)}, u32[]{:S(2)}) collective-permute-start(bf16[2,128,128]{2,1,0:T(8,128)(2,1)S(1)} %get-tuple-element.59), channel_id=1, source_target_pairs={{0,32},{2,34},{4,36},{6,38},{8,40},{10,42},{12,44},{14,46},{16,20}... | collective-permute-start | bytes 196616 | tf_op jit(solution)/shard_map/ppermute | solution.py:277
  83.4 2.4 %collective-permute-start.27 = (bf16[128,128]{1,0:T(8,128)(2,1)S(1)}, bf16[128,128]{1,0:T(8,128)(2,1)S(1)}, u32[]{:S(2)}, u32[]{:S(2)}) collective-permute-start(bf16[128,128]{1,0:T(8,128)(2,1)S(1)} %select_bitcast_fusion), channel_id=1, source_target_pairs={{0,16},{2,18},{4,20},{6,22},{8,24},{10,26},{12,28},{14,30},{16,0},... | collective-permute-start | bytes 98312 | tf_op jit(solution)/shard_map/ppermute | solution.py:277

commit v8 on v7

--- a/solution.py
+++ b/solution.py
@@ -13,7 +13,7 @@
 DOC_ROWS = 16
 CHUNK_BLOCKS = 5
 CHUNK = CHUNK_BLOCKS * BLOCK
-TILES = 4
+TILES = 2
 VMEM_MIB = 36
 PEERS = 2
 SCALE = float(HEAD) ** (-0.5)
@@ -26,12 +26,13 @@
 
 
 class Setting:
-    def __init__(self, sizes, place_ref, kv_all, docs_all, tile_docs, rows, part):
+    def __init__(self, sizes, place_ref, kv_all, docs_all, tile_docs, rows, part, far):
         self.nz, self.nx = nz, nx = sizes
         lines = nz
         self.z, self.x, self.y, self.core = (place_ref[i] for i in range(4))
         self.part, self.rows = part, rows
         self.heads = rows // part
+        self.row = 1 - self.y if far else self.y
         self.kv_all, self.docs_all, self.tile_docs = kv_all, docs_all, tile_docs
         self.blocks = kv_all.shape[1]
         self.steps = steps = range(lines)
@@ -58,9 +59,8 @@
         self.key_token = key_row + lax.div(key_row, BLOCK) * BLOCK
 
     def tile(self, t):
-        dz = lax.rem(t, 2) * self.apart
-        row = jnp.where(t < 2, self.y, 1 - self.y)
-        block = (lax.rem(self.z + self.nz - dz, self.nz) * 2 + self.core) * (2 * self.nx) + self.x * 2 + row
+        dz = t * self.apart
+        block = (lax.rem(self.z + self.nz - dz, self.nz) * 2 + self.core) * (2 * self.nx) + self.x * 2 + self.row
         doc = self.tile_docs[t, :1, :]
         before = jnp.sum(jnp.where(self.docs_all[...] < doc, 0.125, 0.0), axis=(0, 1))
         first = jnp.max(before).astype(jnp.int32)
@@ -81,24 +81,21 @@
         return self.kv_all[which, pl.ds(at, CHUNK_BLOCKS)].reshape(CHUNK, HEAD)
 
 
-def place_all(s, refs, pieces, kv_all, docs_all, tile_docs, cols, rows):
-    doc_ref, own_ref, peer_ref, far_ref = refs
-    lines, nx, steps = s.nz, s.nx, s.steps
+def place_keys(s, pieces, kv_all, docs_all):
     for which, arrived, spot in ((s.core, pieces[0], s.spots[0]), (1 - s.core, pieces[1], s.spots[1])):
-        for i in steps:
-            for j in steps:
+        for i in s.steps:
+            for j in s.steps:
                 for c in range(2):
-                    kv_all[which, spot[-i][-j] + nx * c] = arrived[i][j, c * BLOCK : (c + 1) * BLOCK]
-    for i in steps:
-        for j in steps:
-            docs_all[i * lines + j] = pieces[0][i][j, 2 * BLOCK :].astype(jnp.float32)
+                    kv_all[which, spot[-i][-j] + s.nx * c] = arrived[i][j, c * BLOCK : (c + 1) * BLOCK]
+    for i in s.steps:
+        for j in s.steps:
+            docs_all[i * s.nz + j] = pieces[0][i][j, 2 * BLOCK :].astype(jnp.float32)
+
+
+def place_rows(s, sources, tile_docs, cols, rows):
     part, width = s.part, s.heads * HEAD
-    tile_docs[0] = doc_ref[...].astype(jnp.float32)
-    tile_docs[1] = peer_ref[part:, :HEAD].astype(jnp.float32)
-    tile_docs[2] = far_ref[2 * part :, :HEAD].astype(jnp.float32)
-    tile_docs[3] = far_ref[2 * part :, width : width + HEAD].astype(jnp.float32)
-    sources = ((own_ref, 0), (peer_ref, 0), (far_ref, 0), (far_ref, part))
     for t, (source, begin) in enumerate(sources):
+        tile_docs[t] = source[begin : begin + DOC_ROWS, 2 * width :].astype(jnp.float32)
         for side in range(2):
             whole = jnp.concatenate(
                 [
@@ -110,14 +107,26 @@
             cols[side, t] = whole.T
 
 
-def statistics(sizes, *refs):
+def near_statistics(sizes, *refs):
     lines = sizes[0]
-    count = 5 + 2 * lines
-    stats_ref, kv_all, docs_all, tile_docs, cols, tile_rows = refs[count : count + 6]
-    part = refs[2].shape[0]
-    s = Setting(sizes, refs[0], kv_all, docs_all, tile_docs, cols.shape[-1], part)
-    pieces = (refs[5 : 5 + lines], refs[5 + lines : count])
-    place_all(s, refs[1:5], pieces, kv_all, docs_all, tile_docs, cols, tile_rows)
+    count = 3 + 2 * lines
+    place_ref, own_ref, peer_ref = refs[:3]
+    stats_ref, tile_docs, cols, tile_rows, kv_all, docs_all = refs[count:]
+    s = Setting(sizes, place_ref, kv_all, docs_all, tile_docs, cols.shape[-1], own_ref.shape[0], False)
+    place_keys(s, (refs[3 : 3 + lines], refs[3 + lines : count]), kv_all, docs_all)
+    place_rows(s, ((own_ref, 0), (peer_ref, 0)), tile_docs, cols, tile_rows)
+    statistics(s, stats_ref, cols)
+
+
+def far_statistics(sizes, *refs):
+    place_ref, far_ref, kv_all, docs_all, stats_ref, tile_docs, cols, tile_rows = refs
+    part = far_ref.shape[0] // TILES
+    s = Setting(sizes, place_ref, kv_all, docs_all, tile_docs, cols.shape[-1], part, True)
+    place_rows(s, ((far_ref, 0), (far_ref, part)), tile_docs, cols, tile_rows)
+    statistics(s, stats_ref, cols)
+
+
+def statistics(s, stats_ref, cols):
     rows = s.rows
 
     def fold(value, combine):
@@ -151,23 +160,39 @@
     lax.fori_loop(0, TILES, tile, 0)
 
 
-def gradients(sizes, *refs):
+def far_gradients(sizes, *refs):
+    place_ref, here_ref, there_ref, tile_docs, cols, tile_rows, kv_all, docs_all, dq_ref, totals = refs
+    s = Setting(sizes, place_ref, kv_all, docs_all, tile_docs, cols.shape[-1], dq_ref.shape[1], True)
+    totals[...] = jnp.zeros_like(totals)
+    gradients(s, here_ref, there_ref, cols, tile_rows, dq_ref, totals)
+
+
+def near_gradients(sizes, *refs):
     lines = sizes[0]
-    place_ref, here_ref, there_ref, kv_all, docs_all, tile_docs, cols, tile_rows, dq_ref = refs[:9]
-    outs = refs[9 : 9 + 2 * lines]
-    totals = refs[9 + 2 * lines]
-    totals[...] = jnp.zeros_like(totals)
-    s = Setting(sizes, place_ref, kv_all, docs_all, tile_docs, cols.shape[-1], dq_ref.shape[1])
+    place_ref, here_ref, there_ref, tile_docs, cols, tile_rows, kv_all, docs_all, so_far, dq_ref = refs[:10]
+    keep, send = refs[10 : 10 + lines], refs[10 + lines : 10 + 2 * lines]
+    totals = refs[10 + 2 * lines]
+    s = Setting(sizes, place_ref, kv_all, docs_all, tile_docs, cols.shape[-1], dq_ref.shape[1], False)
+    totals[...] = so_far[...]
+    gradients(s, here_ref, there_ref, cols, tile_rows, dq_ref, totals)
+    for which, out, spot in ((s.core, keep, s.spots[0]), (1 - s.core, send, s.spots[1])):
+        for i in s.steps:
+            for j in s.steps:
+                for c in range(2):
+                    begin = pl.multiple_of((spot[i][j] + s.nx * c) * BLOCK, BLOCK)
+                    out[i][j, c] = totals[which, pl.ds(begin, BLOCK), :].astype(jnp.bfloat16)
+
+
+def gradients(s, here_ref, there_ref, cols, tile_rows, dq_ref, totals):
     part, rows = s.part, s.rows
 
     def tile(t, carry):
         chunks, last, keys_at, mask = s.tile(t)
-        other = lax.rem(t + 2, TILES)
-        top_here, top_there = here_ref[t, 0:1, :], there_ref[other, 0:1, :]
+        top_here, top_there = here_ref[t, 0:1, :], there_ref[t, 0:1, :]
         top = jnp.maximum(top_here, top_there)
         weight_here, weight_there = jnp.exp2(top_here - top), jnp.exp2(top_there - top)
-        norm = here_ref[t, 1:2, :] * weight_here + there_ref[other, 1:2, :] * weight_there
-        weighted = here_ref[t, 2:3, :] * weight_here + there_ref[other, 2:3, :] * weight_there
+        norm = here_ref[t, 1:2, :] * weight_here + there_ref[t, 1:2, :] * weight_there
+        weighted = here_ref[t, 2:3, :] * weight_here + there_ref[t, 2:3, :] * weight_there
         delta = weighted / norm
         top = top + jnp.log2(norm)
 
@@ -190,18 +215,10 @@
         dq = lax.fori_loop(last, chunks, lambda n, dq: work(n, dq, True), dq)
         dq = (dq * SCALE).T
         for h in range(s.heads):
-            dq_ref[t, :, h * HEAD : (h + 1) * HEAD] = dq[h * part : (h + 1) * part, :]
+            dq_ref[t, :, h * HEAD : (h + 1) * HEAD] = dq[h * part : (h + 1) * part, :].astype(dq_ref.dtype)
         return carry
 
     lax.fori_loop(0, TILES, tile, 0)
-    keep, send = outs[:lines], outs[lines:]
-    for which, out, spot in ((s.core, keep, s.spots[0]), (1 - s.core, send, s.spots[1])):
-        for i in s.steps:
-            for j in s.steps:
-                for c in range(2):
-                    begin = pl.multiple_of((spot[i][j] + s.nx * c) * BLOCK, BLOCK)
-                    out[i][j, c] = totals[which, pl.ds(begin, BLOCK), :].astype(jnp.bfloat16)
-
 
 def kernel_call(kernel, sizes, operands, outs, scratch, products):
     whole = pl.BlockSpec(memory_space=pltpu.VMEM)
@@ -214,34 +231,48 @@
         scratch_shapes=scratch,
         compiler_params=pltpu.CompilerParams(vmem_limit_bytes=VMEM_MIB * 1024 * 1024),
         cost_estimate=pl.CostEstimate(
-            flops=products * 2 * 24 * 1024 * 128 * 128, bytes_accessed=8 * 1024 * 1024, transcendentals=0
+            flops=products * 2 * 12 * 1024 * 128 * 128, bytes_accessed=8 * 1024 * 1024, transcendentals=0
         ),
     )(*operands)
 
 
-def statistics_call(sizes, *operands):
-    nz, nx = sizes
-    part, width = operands[2].shape
-    rows = part * width // (2 * HEAD)
-    outs = (
+def tile_outs(rows):
+    return (
         jax.ShapeDtypeStruct((TILES, 8, rows), jnp.float32),
-        jax.ShapeDtypeStruct((2, 2 * nz * nx, BLOCK, HEAD), jnp.bfloat16),
-        jax.ShapeDtypeStruct((nz * nx, DOC_ROWS, HEAD), jnp.float32),
         jax.ShapeDtypeStruct((TILES, DOC_ROWS, HEAD), jnp.float32),
         jax.ShapeDtypeStruct((2, TILES, HEAD, rows), jnp.bfloat16),
         jax.ShapeDtypeStruct((2, TILES, rows, HEAD), jnp.bfloat16),
     )
-    return kernel_call(statistics, sizes, operands, outs, [], 2)
-
-
-def gradients_call(sizes, part, place, here, there, kv, docs, tile_docs, cols, rows):
+
+
+def near_statistics_call(sizes, rows, *operands):
     nz, nx = sizes
-    width = rows.shape[2] * HEAD // part
-    outs = (jax.ShapeDtypeStruct((TILES, part, width), jnp.float32),)
+    outs = tile_outs(rows) + (
+        jax.ShapeDtypeStruct((2, 2 * nz * nx, BLOCK, HEAD), jnp.bfloat16),
+        jax.ShapeDtypeStruct((nz * nx, DOC_ROWS, HEAD), jnp.float32),
+    )
+    outs = kernel_call(near_statistics, sizes, operands, outs, [], 2)
+    return outs[0], outs[1:4], outs[4:]
+
+
+def far_statistics_call(sizes, rows, *operands):
+    outs = kernel_call(far_statistics, sizes, operands, tile_outs(rows), [], 2)
+    return outs[0], outs[1:]
+
+
+def far_gradients_call(sizes, dq_shape, *operands):
+    nz, nx = sizes
+    totals = jax.ShapeDtypeStruct((2, 2 * nz * nx * BLOCK, HEAD), jnp.float32)
+    outs = (jax.ShapeDtypeStruct(dq_shape, jnp.bfloat16), totals)
+    return kernel_call(far_gradients, sizes, operands, outs, [], 5)
+
+
+def near_gradients_call(sizes, dq_shape, *operands):
+    nz, nx = sizes
+    outs = (jax.ShapeDtypeStruct(dq_shape, jnp.float32),)
     outs += (jax.ShapeDtypeStruct((nx, 2, BLOCK, HEAD), jnp.bfloat16),) * (2 * nz)
-    scratch = [pltpu.VMEM((2, kv.shape[1] * BLOCK, HEAD), jnp.float32)]
-    operands = (place, here, there, kv, docs, tile_docs, cols, rows)
-    return kernel_call(gradients, sizes, operands, outs, scratch, 5)
+    scratch = [pltpu.VMEM((2, 2 * nz * nx * BLOCK, HEAD), jnp.float32)]
+    return kernel_call(near_gradients, sizes, operands, outs, scratch, 5)
 
 
 def low(value):
@@ -297,14 +328,15 @@
         )
 
     doc = jnp.broadcast_to(low(block_docs)[:, None], (DOC_ROWS, HEAD))
-    both = jnp.concatenate([queries, grad_out], axis=1).reshape(PEERS, part, 2 * width)
     half = lax.div(z, apart)
-    own = jnp.where(half == 0, both[0], both[1])
-    lent = jnp.where(half == 0, both[1], both[0])
-    wide_doc = jnp.broadcast_to(low(block_docs)[:, None], (DOC_ROWS, 2 * width))
-    borrowed = peer(jnp.concatenate([lent, wide_doc]))
-    docs_of_both = jnp.concatenate([wide_doc[:, :width], borrowed[part:, width:]], axis=1)
-    far = other_y(jnp.concatenate([own, borrowed[:part], docs_of_both]))
+
+    def rows_of(which):
+        cut = [lax.dynamic_slice_in_dim(whole, which * part, part, 0) for whole in (queries, grad_out)]
+        return jnp.concatenate(cut + [jnp.broadcast_to(low(block_docs)[:, None], (part, HEAD))], axis=1)
+
+    own = rows_of(half)
+    borrowed = peer(rows_of(1 - half))
+    shared = jnp.concatenate([own, borrowed])
 
     given = other_core(jnp.where(core == 0, values, keys))
     kept = jnp.where(core == 0, keys, values)
@@ -313,14 +345,25 @@
     docs_in_order = in_order(core, doc[:8], unit_docs[:8], 0).reshape(DOC_ROWS, HEAD)
     unit = jnp.concatenate([rows_in_order, docs_in_order])
     line = jnp.stack([unit] + [along_first(unit, by) for by in range(1, lines)])
+    line, shared = lax.optimization_barrier((line, shared))
+    far = other_y(shared)
     mine = [line] + [along_second(line, by) for by in range(1, lines)]
     theirs = [other_core(piece) for piece in mine]
 
     place = jnp.stack([z, x, y, core]).astype(jnp.int32)
     sizes = (nz, nx)
-    operands = (place, doc, own, borrowed, far, *mine, *theirs)
-    here, *placed = statistics_call(sizes, *operands)
-    dq, *sums = gradients_call(sizes, part, place, here, other_y(here), *placed)
+    tile_rows = part * width // HEAD
+    near_here, near_tiles, keys_all = near_statistics_call(sizes, tile_rows, place, own, borrowed, *mine, *theirs)
+    far_there = other_y(near_here)
+    far_here, far_tiles = far_statistics_call(sizes, tile_rows, place, far, *keys_all)
+    near_there = other_y(far_here)
+    dq_shape = (TILES, part, width)
+    far_dq, so_far = far_gradients_call(sizes, dq_shape, place, far_here, far_there, *far_tiles, *keys_all)
+    rest = other_y(far_dq)
+    dq, *sums = near_gradients_call(
+        sizes, dq_shape, place, near_here, near_there, *near_tiles, *keys_all, so_far
+    )
+    rest, *sums = lax.optimization_barrier((rest, *sums))
     keep, send = sums[:lines], sums[lines:]
 
     totals = [None] * lines
@@ -328,13 +371,11 @@
         totals[by] = low(added([keep[by], other_core(send[by])]))
     arrived = [along_second(totals[by], by) for by in range(1, lines)]
     dq, totals[0] = lax.optimization_barrier((dq, totals[0]))
-    rest = other_y(low(dq[2:]))
-    arrived, rest = lax.optimization_barrier((arrived, rest))
-    dq = low(dq[:2] + rest.astype(jnp.float32))
+    dq = low(dq + rest.astype(jnp.float32))
     returned = peer(dq[1])
+    arrived, returned = lax.optimization_barrier((arrived, returned))
     total = low(added([totals[0]] + arrived))
     short = [along_first(total[by], by) for by in range(1, lines)]
-    short, returned = lax.optimization_barrier((short, returned))
     total = added([total[0]] + short)
     total = low(jnp.where(core == 0, SCALE * total, total))
     ours = jnp.where(core == 0, total[0], total[1])

time: 88.1 us -> 91.6 us (1.040); the launches traced: 86.4 us -> 91.1 us
  starting transfers between devices: 37.9 us -> 42.7 us
  waiting for transfers between devices: 20.1 us -> 22.7 us
  Pallas kernels: 21.1 us -> 19.4 us
    ppermute x28 -> x29, starting transfers between devices: 37.9 us -> 42.7 us  [moved(): return lax.ppermute(value, CONTEXT, hops)]
    ppermute x28 -> x29, waiting for transfers between devices: 20.1 us -> 22.7 us  [moved(): return lax.ppermute(value, CONTEXT, hops)]
    pallas_call x2 -> x4, Pallas kernels: 21.1 us -> 19.4 us  [kernel_call(): pl.pallas_call(lambda *refs: kernel(sizes, *refs), name=kernel.__name__,...]
    dynamic_slice x0 -> x1, local copies, waits for them, and re-layouts: none -> 1.14 us  [rows_of(): lax.dynamic_slice_in_dim(whole, which * part, part, 0)]
    concatenate x2 -> x0, local copies, waits for them, and re-layouts: 0.99 us -> none  [the longest x1 0.97 us: per_device(): jnp.concatenate([queries, grad_out], axis=1).reshape(PEERS, part, 2 * width)]
    unnamed x1 -> x0, local copies, waits for them, and re-layouts: 0.97 us -> none
  transfers between devices with their start and end apart: 28 -> 29, of which waited for: 13 -> 9; matrix products, arithmetic and copies ran while one was open for 6% -> 4% of each run, Pallas kernels for 0% -> 15%
where the time goes in v8:
time: 91.6 us; the launch traced here: 91.1 us
  starting transfers between devices  42.7 us (47%)
  waiting for transfers between devices  22.7 us (25%)
  Pallas kernels  19.4 us (21%)
  other arithmetic  3.72 us (4%)
  between operations  1.51 us (2%)
  local copies, waits for them, and re-layouts  1.18 us (1%)
    ppermute x29, starting transfers between devices, moved(): return lax.ppermute(value, CONTEXT, hops)  42.7 us
    ppermute x29, waiting for transfers between devices, moved(): return lax.ppermute(value, CONTEXT, hops)  22.7 us
    pallas_call x4, Pallas kernels, kernel_call(): pl.pallas_call(lambda *refs: kernel(sizes, *refs), name=kernel.__name__,...  19.4 us
  transfers between devices with their start and end apart: 29, of which 9 were waited for; matrix products, arithmetic and copies ran while one was open for 4% of the time, Pallas kernels for 15%

profile of v8, /device:TPU:1, one launch (start us, length us, event | category | flops | bytes accessed | tf_op | source)
XLA Modules:
  0.0 91.1 jit_solution(15611067484958352338)
XLA Ops:
  1.3 1.5 %collective-permute-start.2 = (bf16[16,128]{1,0:T(8,128)(2,1)S(1)}, bf16[16,128]{1,0:T(8,128)(2,1)S(1)}, u32[]{:S(2)}, u32[]{:S(2)}) collective-permute-start(bf16[16,128]{1,0:T(8,128)(2,1)S(1)} %broadcast_in_dim.8), channel_id=1, source_target_pairs={{0,16},{2,18},{4,20},{6,22},{8,24},{10,26},{12,28},{14,30},{16,0},... | collective-permute-start | bytes 12296 | tf_op jit(solution)/shard_map/ppermute | solution.py:308
  2.8 0.8 select_bitcast_fusion.1
  3.6 0.1 collective-permute-start.1
  3.7 1.1 %constant_dynamic-slice_fusion.2 = (bf16[64,1024]{1,0:T(8,128)(2,1)S(1)}, bf16[64,1024]{1,0:T(8,128)(2,1)S(1)}, bf16[64,1024]{1,0:T(8,128)(2,1)S(1)}, bf16[64,1024]{1,0:T(8,128)(2,1)S(1)}) fusion(bf16[128,1024]{1,0:T(8,128)(2,1)} %param.8, s32[]{:T(128)S(6)} %select_n.83, s32[]{:T(128)S(6)} %select_n.84, bf16[128,1024]{1,0:T(8,128)(2,1)} %param.5), kind=kLoop, calls=%fused_computation.33 | loop fusion | bytes 1048584 | tf_op jit(solution)/shard_map/dynamic_slice | solution.py:334
  4.9 3.8 %collective-permute-start = (bf16[64,2176]{1,0:T(8,128)(2,1)S(1)}, bf16[64,2176]{1,0:T(8,128)(2,1)S(1)}, u32[]{:S(2)}, u32[]{:S(2)}) collective-permute-start(bf16[64,2176]{1,0:T(8,128)(2,1)S(1)} %get-tuple-element.95), channel_id=1, source_target_pairs={{0,64},{2,66},{4,68},{6,70},{8,72},{10,74},{12,76},{14,78},{16,80}... | collective-permute-start | bytes 835592 | tf_op jit(solution)/shard_map/ppermute | solution.py:308
  8.7 2.8 %collective-permute-start.4 = (bf16[272,128]{1,0:T(8,128)(2,1)S(1)}, bf16[272,128]{1,0:T(8,128)(2,1)S(1)}, u32[]{:S(2)}, u32[]{:S(2)}) collective-permute-start(bf16[272,128]{1,0:T(8,128)(2,1)S(1)} %get-tuple-element.91), channel_id=1, source_target_pairs={{0,64},{2,66},{4,68},{6,70},{8,72},{10,74},{12,76},{14,78},{16,24}... | collective-permute-start | bytes 208904 | tf_op jit(solution)/shard_map/ppermute | solution.py:308
  11.5 0.3 collective-permute-start.3
  11.8 2.4 %collective-permute-start.5 = (bf16[272,128]{1,0:T(8,128)(2,1)S(1)}, bf16[272,128]{1,0:T(8,128)(2,1)S(1)}, u32[]{:S(2)}, u32[]{:S(2)}) collective-permute-start(bf16[272,128]{1,0:T(8,128)(2,1)S(1)} %get-tuple-element.91), channel_id=1, source_target_pairs={{0,96},{2,98},{4,100},{6,102},{8,104},{10,106},{12,108},{14,110},{... | collective-permute-start | bytes 208904 | tf_op jit(solution)/shard_map/ppermute | solution.py:308
  14.2 2.0 %collective-permute-done.3 = bf16[272,128]{1,0:T(8,128)(2,1)S(1)} collective-permute-done((bf16[272,128]{1,0:T(8,128)(2,1)S(1)}, bf16[272,128]{1,0:T(8,128)(2,1)S(1)}, u32[]{:S(2)}, u32[]{:S(2)}) %collective-permute-start.3) | collective-permute-done | bytes 69664 | tf_op jit(solution)/shard_map/ppermute | solution.py:308
  16.3 0.8 pad_maximum_fusion
  17.1 1.8 %collective-permute-start.8 = (bf16[4,272,128]{2,1,0:T(8,128)(2,1)S(1)}, bf16[4,272,128]{2,1,0:T(8,128)(2,1)S(1)}, u32[]{:S(2)}, u32[]{:S(2)}) collective-permute-start(bf16[4,272,128]{2,1,0:T(8,128)(2,1)S(1)} %pad_maximum_fusion.3.refs_3_), channel_id=1, source_target_pairs={{0,12},{2,14},{4,0},{6,2},{8,4},{10,6},{12,8},{14,10},{16,112},{18... | collective-permute-start | bytes 835592 | tf_op jit(solution)/shard_map/ppermute | solution.py:308
  18.9 0.6 collective-permute-start.7
  19.5 0.2 collective-permute-start.6
  19.7 1.3 %collective-permute-start.13 = (bf16[128,2176]{1,0:T(8,128)(2,1)}, bf16[128,2176]{1,0:T(8,128)(2,1)S(1)}, u32[]{:S(2)}, u32[]{:S(2)}) collective-permute-start(bf16[128,2176]{1,0:T(8,128)(2,1)} %pad_maximum_fusion), channel_id=1, source_target_pairs={{0,2},{2,0},{4,6},{6,4},{8,10},{10,8},{12,14},{14,12},{16,18},{18,... | collective-permute-start | bytes 1671176 | tf_op jit(solution)/shard_map/ppermute | solution.py:308
  21.0 4.5 %collective-permute-start.9 = (bf16[4,272,128]{2,1,0:T(8,128)(2,1)S(1)}, bf16[4,272,128]{2,1,0:T(8,128)(2,1)S(1)}, u32[]{:S(2)}, u32[]{:S(2)}) collective-permute-start(bf16[4,272,128]{2,1,0:T(8,128)(2,1)S(1)} %pad_maximum_fusion.3.refs_3_), channel_id=1, source_target_pairs={{0,16},{2,18},{4,20},{6,22},{8,24},{10,26},{12,28},{14,30},{16,0},... | collective-permute-start | bytes 835592 | tf_op jit(solution)/shard_map/ppermute | solution.py:308
  25.4 3.8 %collective-permute-start.12 = (bf16[4,272,128]{2,1,0:T(8,128)(2,1)S(1)}, bf16[4,272,128]{2,1,0:T(8,128)(2,1)S(1)}, u32[]{:S(2)}, u32[]{:S(2)}) collective-permute-start(bf16[4,272,128]{2,1,0:T(8,128)(2,1)S(1)} %collective-permute-done.8.refs_6_), channel_id=1, source_target_pairs={{0,16},{2,18},{4,20},{6,22},{8,24},{10,26},{12,28},{14,30},{16,0},... | collective-permute-start | bytes 835592 | tf_op jit(solution)/shard_map/ppermute | solution.py:308
  29.3 1.1 %collective-permute-start.11 = (bf16[4,272,128]{2,1,0:T(8,128)(2,1)S(1)}, bf16[4,272,128]{2,1,0:T(8,128)(2,1)S(1)}, u32[]{:S(2)}, u32[]{:S(2)}) collective-permute-start(bf16[4,272,128]{2,1,0:T(8,128)(2,1)S(1)} %collective-permute-done.7.refs_5_), channel_id=1, source_target_pairs={{0,16},{2,18},{4,20},{6,22},{8,24},{10,26},{12,28},{14,30},{16,0},... | collective-permute-start | bytes 835592 | tf_op jit(solution)/shard_map/ppermute | solution.py:308
  30.3 2.9 %collective-permute-start.10 = (bf16[4,272,128]{2,1,0:T(8,128)(2,1)S(1)}, bf16[4,272,128]{2,1,0:T(8,128)(2,1)S(1)}, u32[]{:S(2)}, u32[]{:S(2)}) collective-permute-start(bf16[4,272,128]{2,1,0:T(8,128)(2,1)S(1)} %collective-permute-done.6.refs_4_), channel_id=1, source_target_pairs={{0,16},{2,18},{4,20},{6,22},{8,24},{10,26},{12,28},{14,30},{16,0},... | collective-permute-start | bytes 835592 | tf_op jit(solution)/shard_map/ppermute | solution.py:308
  33.2 0.1 pad_add_fusion.refs_0_
  33.3 1.1 %collective-permute-done.10.refs_8_ = bf16[4,272,128]{2,1,0:T(8,128)(2,1)S(1)} collective-permute-done((bf16[4,272,128]{2,1,0:T(8,128)(2,1)S(1)}, bf16[4,272,128]{2,1,0:T(8,128)(2,1)S(1)}, u32[]{:S(2)}, u32[]{:S(2)}) %collective-permute-start.10) | collective-permute-done | bytes 278560 | tf_op jit(solution)/shard_map/ppermute | solution.py:308
  34.4 3.8 %near_statistics.1 = (f32[2,8,512]{2,1,0:T(8,128)S(1)}, f32[2,16,128]{2,1,0:T(8,128)S(1)}, bf16[2,2,128,512]{3,2,1,0:T(8,128)(2,1)S(1)}, bf16[2,2,512,128]{3,2,1...) custom-call(s32[4]{0:T(128)S(1)} %pad_add_fusion.refs_0_, ...), custom_call_target="tpu_custom_call" | custom-call | flops 805306368 | bytes 8388608 | tf_op jit(solution)/shard_map/near_statistics/pallas_call | solution.py:225
  38.2 1.4 %collective-permute-start.15 = (f32[2,8,512]{2,1,0:T(8,128)S(1)}, f32[2,8,512]{2,1,0:T(8,128)S(1)}, u32[]{:S(2)}, u32[]{:S(2)}) collective-permute-start(f32[2,8,512]{2,1,0:T(8,128)S(1)} %get-tuple-element.42.refs_1_), channel_id=1, source_target_pairs={{0,2},{2,0},{4,6},{6,4},{8,10},{10,8},{12,14},{14,12},{16,18},{18,... | collective-permute-start | bytes 98312 | tf_op jit(solution)/shard_map/ppermute | solution.py:308
  39.6 3.7 %far_statistics.1 = (f32[2,8,512]{2,1,0:T(8,128)S(1)}, f32[2,16,128]{2,1,0:T(8,128)S(1)}, bf16[2,2,128,512]{3,2,1,0:T(8,128)(2,1)S(1)}, bf16[2,2,512,128]{3,2,1,0:T(8,128)(2,1)S(1)}) custom-call(s32[4]{0:T(128)S(1)} %pad_add_fusion.refs_0_, bf16[128,2176]{1,0:T(8,128)(2,1)S(1)} %collective-permute-done.13.refs_1_, ...), custom_call_target="tpu_custom_call" | custom-call | flops 805306368 | bytes 8388608 | tf_op jit(solution)/shard_map/far_statistics/pallas_call | solution.py:225
  43.3 5.9 %far_gradients.1 = (bf16[2,64,1024]{2,1,0:T(8,128)(2,1)S(1)}, f32[2,4096,128]{2,1,0:T(8,128)S(1)}) custom-call(s32[4]{0:T(128)S(1)} %pad_add_fusion.refs_0_, f32[2,8,512]{2,1,0:T(8,128)S(1)} %get-tuple-element.46.refs_1_, f32[2,8,512]{2,1,0:T(8,128)S(1)} %collective-permute-done.15.refs_2_, f32[2,16,128]{2,1,0:T(8,128)S(1)} %get-tuple-element.50.refs_3_, ...), custom_call_target="tpu_custom_call" | custom-call | flops 2013265920 | bytes 8388608 | tf_op jit(solution)/shard_map/far_gradients/pallas_call | solution.py:225
  49.2 0.1 collective-permute-start.16
  49.3 1.5 %collective-permute-start.14 = (f32[2,8,512]{2,1,0:T(8,128)S(1)}, f32[2,8,512]{2,1,0:T(8,128)S(1)}, u32[]{:S(2)}, u32[]{:S(2)}) collective-permute-start(f32[2,8,512]{2,1,0:T(8,128)S(1)} %get-tuple-element.46.refs_1_), channel_id=1, source_target_pairs={{0,2},{2,0},{4,6},{6,4},{8,10},{10,8},{12,14},{14,12},{16,18},{18,... | collective-permute-start | bytes 98312 | tf_op jit(solution)/shard_map/ppermute | solution.py:308
  50.7 6.4 %collective-permute-done.14.refs_2_ = f32[2,8,512]{2,1,0:T(8,128)S(1)} collective-permute-done((f32[2,8,512]{2,1,0:T(8,128)S(1)}, f32[2,8,512]{2,1,0:T(8,128)S(1)}, u32[]{:S(2)}, u32[]{:S(2)}) %collective-permute-start.14) | collective-permute-done | bytes 32800 | tf_op jit(solution)/shard_map/ppermute | solution.py:308
  57.1 6.1 %near_gradients.1 = (f32[2,64,1024]{2,1,0:T(8,128)S(1)}, bf16[4,2,128,128]{3,2,1,0:T(8,128)(2,1)S(1)}, bf16[4,2,128,128]{3,2,1,0:T(8,128)(2,1)S(1)}, bf16[4,2,12...) custom-call(s32[4]{0:T(128)S(1)} %pad_add_fusion.refs_0_, ...), custom_call_target="tpu_custom_call" | custom-call | flops 2013265920 | bytes 8388608 | tf_op jit(solution)/shard_map/near_gradients/pallas_call | solution.py:225
  63.2 1.6 %collective-permute-start.17 = (bf16[4,2,128,128]{3,2,1,0:T(8,128)(2,1)S(1)}, bf16[4,2,128,128]{3,2,1,0:T(8,128)(2,1)S(1)}, u32[]{:S(2)}, u32[]{:S(2)}) collective-permute-start(bf16[4,2,128,128]{3,2,1,0:T(8,128)(2,1)S(1)} %get-tuple-element.65), channel_id=1, source_target_pairs={{0,16},{2,18},{4,20},{6,22},{8,24},{10,26},{12,28},{14,30},{16,0},... | collective-permute-start | bytes 786440 | tf_op jit(solution)/shard_map/ppermute | solution.py:308
  64.8 0.1 collective-permute-start.18
  64.9 0.4 collective-permute-start.20
  65.3 0.1 collective-permute-start.22
  65.4 0.6 collective-permute-done.17
  66.1 0.3 collective-permute-done.18
  66.4 1.9 %collective-permute-start.19 = (bf16[4,2,128,128]{3,2,1,0:T(8,128)(2,1)S(1)}, bf16[4,2,128,128]{3,2,1,0:T(8,128)(2,1)S(1)}, u32[]{:S(2)}, u32[]{:S(2)}) collective-permute-start(bf16[4,2,128,128]{3,2,1,0:T(8,128)(2,1)S(1)} %add_convert_fusion.3), channel_id=1, source_target_pairs={{0,4},{2,6},{4,8},{6,10},{8,12},{10,14},{12,0},{14,2},{16,48},{18,... | collective-permute-start | bytes 786440 | tf_op jit(solution)/shard_map/ppermute | solution.py:308
  68.4 2.9 %collective-permute-start.21 = (bf16[4,2,128,128]{3,2,1,0:T(8,128)(2,1)S(1)}, bf16[4,2,128,128]{3,2,1,0:T(8,128)(2,1)S(1)}, u32[]{:S(2)}, u32[]{:S(2)}) collective-permute-start(bf16[4,2,128,128]{3,2,1,0:T(8,128)(2,1)S(1)} %add_convert_fusion.2), channel_id=1, source_target_pairs={{0,8},{2,10},{4,12},{6,14},{8,0},{10,2},{12,4},{14,6},{16,80},{18,... | collective-permute-start | bytes 786440 | tf_op jit(solution)/shard_map/ppermute | solution.py:308
  71.4 0.1 collective-permute-start.23
  71.5 1.5 %collective-permute-start.24 = (bf16[64,1024]{1,0:T(8,128)(2,1)S(1)}, bf16[64,1024]{1,0:T(8,128)(2,1)S(1)}, u32[]{:S(2)}, u32[]{:S(2)}) collective-permute-start(bf16[64,1024]{1,0:T(8,128)(2,1)S(1)} %get-tuple-element.83), channel_id=1, source_target_pairs={{0,64},{2,66},{4,68},{6,70},{8,72},{10,74},{12,76},{14,78},{16,80}... | collective-permute-start | bytes 393224 | tf_op jit(solution)/shard_map/ppermute | solution.py:308
  73.0 7.5 %collective-permute-done.24 = bf16[64,1024]{1,0:T(8,128)(2,1)S(1)} collective-permute-done((bf16[64,1024]{1,0:T(8,128)(2,1)S(1)}, bf16[64,1024]{1,0:T(8,128)(2,1)S(1)}, u32[]{:S(2)}, u32[]{:S(2)}) %collective-permute-start.24) | collective-permute-done | bytes 131104 | tf_op jit(solution)/shard_map/ppermute | solution.py:308
  80.5 0.1 add_convert_fusion
  80.7 0.1 collective-permute-start.25
  80.8 2.7 %collective-permute-start.27 = (bf16[2,128,128]{2,1,0:T(8,128)(2,1)S(1)}, bf16[2,128,128]{2,1,0:T(8,128)(2,1)S(1)}, u32[]{:S(2)}, u32[]{:S(2)}) collective-permute-start(bf16[2,128,128]{2,1,0:T(8,128)(2,1)S(1)} %get-tuple-element.80), channel_id=1, source_target_pairs={{0,96},{2,98},{4,100},{6,102},{8,104},{10,106},{12,108},{14,110},{... | collective-permute-start | bytes 196616 | tf_op jit(solution)/shard_map/ppermute | solution.py:308
  83.4 1.9 %collective-permute-done.25 = bf16[2,128,128]{2,1,0:T(8,128)(2,1)S(1)} collective-permute-done((bf16[2,128,128]{2,1,0:T(8,128)(2,1)S(1)}, bf16[2,128,128]{2,1,0:T(8,128)(2,1)S(1)}, u32[]{:S(2)}, u32[]{:S(2)}) %collective-permute-start.25) | collective-permute-done | bytes 65568 | tf_op jit(solution)/shard_map/ppermute | solution.py:308
  85.4 2.7 %collective-permute-done.26 = bf16[2,128,128]{2,1,0:T(8,128)(2,1)S(1)} collective-permute-done((bf16[2,128,128]{2,1,0:T(8,128)(2,1)S(1)}, bf16[2,128,128]{2,1,0:T(8,128)(2,1)S(1)}, u32[]{:S(2)}, u32[]{:S(2)}) %collective-permute-start.26) | collective-permute-done | bytes 65568 | tf_op jit(solution)/shard_map/ppermute | solution.py:308
  88.1 1.5 %collective-permute-start.28 = (bf16[128,128]{1,0:T(8,128)(2,1)S(1)}, bf16[128,128]{1,0:T(8,128)(2,1)S(1)}, u32[]{:S(2)}, u32[]{:S(2)}) collective-permute-start(bf16[128,128]{1,0:T(8,128)(2,1)S(1)} %select_bitcast_fusion), channel_id=1, source_target_pairs={{0,16},{2,18},{4,20},{6,22},{8,24},{10,26},{12,28},{14,30},{16,0},... | collective-permute-start | bytes 98312 | tf_op jit(solution)/shard_map/ppermute | solution.py:308
  89.6 0.7 maximum_select_fusion
  90.4 0.1 collective-permute-done.28
  90.5 0.6 bitcast_select_fusion
  (38 shorter events, 0.6 us)
Async XLA Ops:
  1.3 7.4 %collective-permute-start.2 = (bf16[16,128]{1,0:T(8,128)(2,1)S(1)}, bf16[16,128]{1,0:T(8,128)(2,1)S(1)}, u32[]{:S(2)}, u32[]{:S(2)}) collective-permute-start(bf16[16,128]{1,0:T(8,128)(2,1)S(1)} %broadcast_in_dim.8), channel_id=1, source_target_pairs={{0,16},{2,18},{4,20},{6,22},{8,24},{10,26},{12,28},{14,30},{16,0},... | collective-permute-start | bytes 12296 | tf_op jit(solution)/shard_map/ppermute | solution.py:308
  3.6 5.1 %collective-permute-start.1 = (bf16[128,128]{1,0:T(8,128)(2,1)S(1)}, bf16[128,128]{1,0:T(8,128)(2,1)S(1)}, u32[]{:S(2)}, u32[]{:S(2)}) collective-permute-start(bf16[128,128]{1,0:T(8,128)(2,1)S(1)} %get-tuple-element.93), channel_id=1, source_target_pairs={{0,16},{2,18},{4,20},{6,22},{8,24},{10,26},{12,28},{14,30},{16,0},... | collective-permute-start | bytes 98312 | tf_op jit(solution)/shard_map/ppermute | solution.py:308
  4.9 11.4 %collective-permute-start = (bf16[64,2176]{1,0:T(8,128)(2,1)S(1)}, bf16[64,2176]{1,0:T(8,128)(2,1)S(1)}, u32[]{:S(2)}, u32[]{:S(2)}) collective-permute-start(bf16[64,2176]{1,0:T(8,128)(2,1)S(1)} %get-tuple-element.95), channel_id=1, source_target_pairs={{0,64},{2,66},{4,68},{6,70},{8,72},{10,74},{12,76},{14,78},{16,80}... | collective-permute-start | bytes 835592 | tf_op jit(solution)/shard_map/ppermute | solution.py:308
  8.7 5.5 %collective-permute-start.4 = (bf16[272,128]{1,0:T(8,128)(2,1)S(1)}, bf16[272,128]{1,0:T(8,128)(2,1)S(1)}, u32[]{:S(2)}, u32[]{:S(2)}) collective-permute-start(bf16[272,128]{1,0:T(8,128)(2,1)S(1)} %get-tuple-element.91), channel_id=1, source_target_pairs={{0,64},{2,66},{4,68},{6,70},{8,72},{10,74},{12,76},{14,78},{16,24}... | collective-permute-start | bytes 208904 | tf_op jit(solution)/shard_map/ppermute | solution.py:308
  11.5 4.7 %collective-permute-start.3 = (bf16[272,128]{1,0:T(8,128)(2,1)S(1)}, bf16[272,128]{1,0:T(8,128)(2,1)S(1)}, u32[]{:S(2)}, u32[]{:S(2)}) collective-permute-start(bf16[272,128]{1,0:T(8,128)(2,1)S(1)} %get-tuple-element.91), channel_id=1, source_target_pairs={{0,32},{2,34},{4,36},{6,38},{8,40},{10,42},{12,44},{14,46},{16,20}... | collective-permute-start | bytes 208904 | tf_op jit(solution)/shard_map/ppermute | solution.py:308
  11.8 4.4 %collective-permute-start.5 = (bf16[272,128]{1,0:T(8,128)(2,1)S(1)}, bf16[272,128]{1,0:T(8,128)(2,1)S(1)}, u32[]{:S(2)}, u32[]{:S(2)}) collective-permute-start(bf16[272,128]{1,0:T(8,128)(2,1)S(1)} %get-tuple-element.91), channel_id=1, source_target_pairs={{0,96},{2,98},{4,100},{6,102},{8,104},{10,106},{12,108},{14,110},{... | collective-permute-start | bytes 208904 | tf_op jit(solution)/shard_map/ppermute | solution.py:308
  17.1 8.3 %collective-permute-start.8 = (bf16[4,272,128]{2,1,0:T(8,128)(2,1)S(1)}, bf16[4,272,128]{2,1,0:T(8,128)(2,1)S(1)}, u32[]{:S(2)}, u32[]{:S(2)}) collective-permute-start(bf16[4,272,128]{2,1,0:T(8,128)(2,1)S(1)} %pad_maximum_fusion.3.refs_3_), channel_id=1, source_target_pairs={{0,12},{2,14},{4,0},{6,2},{8,4},{10,6},{12,8},{14,10},{16,112},{18... | collective-permute-start | bytes 835592 | tf_op jit(solution)/shard_map/ppermute | solution.py:308
  18.9 10.4 %collective-permute-start.7 = (bf16[4,272,128]{2,1,0:T(8,128)(2,1)S(1)}, bf16[4,272,128]{2,1,0:T(8,128)(2,1)S(1)}, u32[]{:S(2)}, u32[]{:S(2)}) collective-permute-start(bf16[4,272,128]{2,1,0:T(8,128)(2,1)S(1)} %pad_maximum_fusion.3.refs_3_), channel_id=1, source_target_pairs={{0,8},{2,10},{4,12},{6,14},{8,0},{10,2},{12,4},{14,6},{16,80},{18,... | collective-permute-start | bytes 835592 | tf_op jit(solution)/shard_map/ppermute | solution.py:308
  19.5 10.9 %collective-permute-start.6 = (bf16[4,272,128]{2,1,0:T(8,128)(2,1)S(1)}, bf16[4,272,128]{2,1,0:T(8,128)(2,1)S(1)}, u32[]{:S(2)}, u32[]{:S(2)}) collective-permute-start(bf16[4,272,128]{2,1,0:T(8,128)(2,1)S(1)} %pad_maximum_fusion.3.refs_3_), channel_id=1, source_target_pairs={{0,4},{2,6},{4,8},{6,10},{8,12},{10,14},{12,0},{14,2},{16,48},{18,... | collective-permute-start | bytes 835592 | tf_op jit(solution)/shard_map/ppermute | solution.py:308
  19.7 19.9 %collective-permute-start.13 = (bf16[128,2176]{1,0:T(8,128)(2,1)}, bf16[128,2176]{1,0:T(8,128)(2,1)S(1)}, u32[]{:S(2)}, u32[]{:S(2)}) collective-permute-start(bf16[128,2176]{1,0:T(8,128)(2,1)} %pad_maximum_fusion), channel_id=1, source_target_pairs={{0,2},{2,0},{4,6},{6,4},{8,10},{10,8},{12,14},{14,12},{16,18},{18,... | collective-permute-start | bytes 1671176 | tf_op jit(solution)/shard_map/ppermute | solution.py:308
  21.0 12.3 %collective-permute-start.9 = (bf16[4,272,128]{2,1,0:T(8,128)(2,1)S(1)}, bf16[4,272,128]{2,1,0:T(8,128)(2,1)S(1)}, u32[]{:S(2)}, u32[]{:S(2)}) collective-permute-start(bf16[4,272,128]{2,1,0:T(8,128)(2,1)S(1)} %pad_maximum_fusion.3.refs_3_), channel_id=1, source_target_pairs={{0,16},{2,18},{4,20},{6,22},{8,24},{10,26},{12,28},{14,30},{16,0},... | collective-permute-start | bytes 835592 | tf_op jit(solution)/shard_map/ppermute | solution.py:308
  25.4 7.9 %collective-permute-start.12 = (bf16[4,272,128]{2,1,0:T(8,128)(2,1)S(1)}, bf16[4,272,128]{2,1,0:T(8,128)(2,1)S(1)}, u32[]{:S(2)}, u32[]{:S(2)}) collective-permute-start(bf16[4,272,128]{2,1,0:T(8,128)(2,1)S(1)} %collective-permute-done.8.refs_6_), channel_id=1, source_target_pairs={{0,16},{2,18},{4,20},{6,22},{8,24},{10,26},{12,28},{14,30},{16,0},... | collective-permute-start | bytes 835592 | tf_op jit(solution)/shard_map/ppermute | solution.py:308
  29.3 4.0 %collective-permute-start.11 = (bf16[4,272,128]{2,1,0:T(8,128)(2,1)S(1)}, bf16[4,272,128]{2,1,0:T(8,128)(2,1)S(1)}, u32[]{:S(2)}, u32[]{:S(2)}) collective-permute-start(bf16[4,272,128]{2,1,0:T(8,128)(2,1)S(1)} %collective-permute-done.7.refs_5_), channel_id=1, source_target_pairs={{0,16},{2,18},{4,20},{6,22},{8,24},{10,26},{12,28},{14,30},{16,0},... | collective-permute-start | bytes 835592 | tf_op jit(solution)/shard_map/ppermute | solution.py:308
  30.3 4.1 %collective-permute-start.10 = (bf16[4,272,128]{2,1,0:T(8,128)(2,1)S(1)}, bf16[4,272,128]{2,1,0:T(8,128)(2,1)S(1)}, u32[]{:S(2)}, u32[]{:S(2)}) collective-permute-start(bf16[4,272,128]{2,1,0:T(8,128)(2,1)S(1)} %collective-permute-done.6.refs_4_), channel_id=1, source_target_pairs={{0,16},{2,18},{4,20},{6,22},{8,24},{10,26},{12,28},{14,30},{16,0},... | collective-permute-start | bytes 835592 | tf_op jit(solution)/shard_map/ppermute | solution.py:308
  38.2 5.1 %collective-permute-start.15 = (f32[2,8,512]{2,1,0:T(8,128)S(1)}, f32[2,8,512]{2,1,0:T(8,128)S(1)}, u32[]{:S(2)}, u32[]{:S(2)}) collective-permute-start(f32[2,8,512]{2,1,0:T(8,128)S(1)} %get-tuple-element.42.refs_1_), channel_id=1, source_target_pairs={{0,2},{2,0},{4,6},{6,4},{8,10},{10,8},{12,14},{14,12},{16,18},{18,... | collective-permute-start | bytes 98312 | tf_op jit(solution)/shard_map/ppermute | solution.py:308
  49.2 14.1 %collective-permute-start.16 = (bf16[2,64,1024]{2,1,0:T(8,128)(2,1)S(1)}, bf16[2,64,1024]{2,1,0:T(8,128)(2,1)S(1)}, u32[]{:S(2)}, u32[]{:S(2)}) collective-permute-start(bf16[2,64,1024]{2,1,0:T(8,128)(2,1)S(1)} %get-tuple-element.55), channel_id=1, source_target_pairs={{0,2},{2,0},{4,6},{6,4},{8,10},{10,8},{12,14},{14,12},{16,18},{18,... | collective-permute-start | bytes 786440 | tf_op jit(solution)/shard_map/ppermute | solution.py:308
  49.3 7.9 %collective-permute-start.14 = (f32[2,8,512]{2,1,0:T(8,128)S(1)}, f32[2,8,512]{2,1,0:T(8,128)S(1)}, u32[]{:S(2)}, u32[]{:S(2)}) collective-permute-start(f32[2,8,512]{2,1,0:T(8,128)S(1)} %get-tuple-element.46.refs_1_), channel_id=1, source_target_pairs={{0,2},{2,0},{4,6},{6,4},{8,10},{10,8},{12,14},{14,12},{16,18},{18,... | collective-permute-start | bytes 98312 | tf_op jit(solution)/shard_map/ppermute | solution.py:308
  63.2 2.8 %collective-permute-start.17 = (bf16[4,2,128,128]{3,2,1,0:T(8,128)(2,1)S(1)}, bf16[4,2,128,128]{3,2,1,0:T(8,128)(2,1)S(1)}, u32[]{:S(2)}, u32[]{:S(2)}) collective-permute-start(bf16[4,2,128,128]{3,2,1,0:T(8,128)(2,1)S(1)} %get-tuple-element.65), channel_id=1, source_target_pairs={{0,16},{2,18},{4,20},{6,22},{8,24},{10,26},{12,28},{14,30},{16,0},... | collective-permute-start | bytes 786440 | tf_op jit(solution)/shard_map/ppermute | solution.py:308
  64.8 1.5 %collective-permute-start.18 = (bf16[4,2,128,128]{3,2,1,0:T(8,128)(2,1)S(1)}, bf16[4,2,128,128]{3,2,1,0:T(8,128)(2,1)S(1)}, u32[]{:S(2)}, u32[]{:S(2)}) collective-permute-start(bf16[4,2,128,128]{3,2,1,0:T(8,128)(2,1)S(1)} %get-tuple-element.69), channel_id=1, source_target_pairs={{0,16},{2,18},{4,20},{6,22},{8,24},{10,26},{12,28},{14,30},{16,0},... | collective-permute-start | bytes 786440 | tf_op jit(solution)/shard_map/ppermute | solution.py:308
  64.9 3.4 %collective-permute-start.20 = (bf16[4,2,128,128]{3,2,1,0:T(8,128)(2,1)S(1)}, bf16[4,2,128,128]{3,2,1,0:T(8,128)(2,1)S(1)}, u32[]{:S(2)}, u32[]{:S(2)}) collective-permute-start(bf16[4,2,128,128]{3,2,1,0:T(8,128)(2,1)S(1)} %get-tuple-element.71), channel_id=1, source_target_pairs={{0,16},{2,18},{4,20},{6,22},{8,24},{10,26},{12,28},{14,30},{16,0},... | collective-permute-start | bytes 786440 | tf_op jit(solution)/shard_map/ppermute | solution.py:308
  65.3 6.0 %collective-permute-start.22 = (bf16[4,2,128,128]{3,2,1,0:T(8,128)(2,1)S(1)}, bf16[4,2,128,128]{3,2,1,0:T(8,128)(2,1)S(1)}, u32[]{:S(2)}, u32[]{:S(2)}) collective-permute-start(bf16[4,2,128,128]{3,2,1,0:T(8,128)(2,1)S(1)} %get-tuple-element.73), channel_id=1, source_target_pairs={{0,16},{2,18},{4,20},{6,22},{8,24},{10,26},{12,28},{14,30},{16,0},... | collective-permute-start | bytes 786440 | tf_op jit(solution)/shard_map/ppermute | solution.py:308
  66.4 14.1 %collective-permute-start.19 = (bf16[4,2,128,128]{3,2,1,0:T(8,128)(2,1)S(1)}, bf16[4,2,128,128]{3,2,1,0:T(8,128)(2,1)S(1)}, u32[]{:S(2)}, u32[]{:S(2)}) collective-permute-start(bf16[4,2,128,128]{3,2,1,0:T(8,128)(2,1)S(1)} %add_convert_fusion.3), channel_id=1, source_target_pairs={{0,4},{2,6},{4,8},{6,10},{8,12},{10,14},{12,0},{14,2},{16,48},{18,... | collective-permute-start | bytes 786440 | tf_op jit(solution)/shard_map/ppermute | solution.py:308
  68.4 12.1 %collective-permute-start.21 = (bf16[4,2,128,128]{3,2,1,0:T(8,128)(2,1)S(1)}, bf16[4,2,128,128]{3,2,1,0:T(8,128)(2,1)S(1)}, u32[]{:S(2)}, u32[]{:S(2)}) collective-permute-start(bf16[4,2,128,128]{3,2,1,0:T(8,128)(2,1)S(1)} %add_convert_fusion.2), channel_id=1, source_target_pairs={{0,8},{2,10},{4,12},{6,14},{8,0},{10,2},{12,4},{14,6},{16,80},{18,... | collective-permute-start | bytes 786440 | tf_op jit(solution)/shard_map/ppermute | solution.py:308
  71.4 9.1 %collective-permute-start.23 = (bf16[4,2,128,128]{3,2,1,0:T(8,128)(2,1)S(1)}, bf16[4,2,128,128]{3,2,1,0:T(8,128)(2,1)S(1)}, u32[]{:S(2)}, u32[]{:S(2)}) collective-permute-start(bf16[4,2,128,128]{3,2,1,0:T(8,128)(2,1)S(1)} %add_convert_fusion.1), channel_id=1, source_target_pairs={{0,12},{2,14},{4,0},{6,2},{8,4},{10,6},{12,8},{14,10},{16,112},{18... | collective-permute-start | bytes 786440 | tf_op jit(solution)/shard_map/ppermute | solution.py:308
  71.5 9.0 %collective-permute-start.24 = (bf16[64,1024]{1,0:T(8,128)(2,1)S(1)}, bf16[64,1024]{1,0:T(8,128)(2,1)S(1)}, u32[]{:S(2)}, u32[]{:S(2)}) collective-permute-start(bf16[64,1024]{1,0:T(8,128)(2,1)S(1)} %get-tuple-element.83), channel_id=1, source_target_pairs={{0,64},{2,66},{4,68},{6,70},{8,72},{10,74},{12,76},{14,78},{16,80}... | collective-permute-start | bytes 393224 | tf_op jit(solution)/shard_map/ppermute | solution.py:308
  80.7 4.7 %collective-permute-start.25 = (bf16[2,128,128]{2,1,0:T(8,128)(2,1)S(1)}, bf16[2,128,128]{2,1,0:T(8,128)(2,1)S(1)}, u32[]{:S(2)}, u32[]{:S(2)}) collective-permute-start(bf16[2,128,128]{2,1,0:T(8,128)(2,1)S(1)} %get-tuple-element.79), channel_id=1, source_target_pairs={{0,32},{2,34},{4,36},{6,38},{8,40},{10,42},{12,44},{14,46},{16,20}... | collective-permute-start | bytes 196616 | tf_op jit(solution)/shard_map/ppermute | solution.py:308
  80.8 4.6 %collective-permute-start.27 = (bf16[2,128,128]{2,1,0:T(8,128)(2,1)S(1)}, bf16[2,128,128]{2,1,0:T(8,128)(2,1)S(1)}, u32[]{:S(2)}, u32[]{:S(2)}) collective-permute-start(bf16[2,128,128]{2,1,0:T(8,128)(2,1)S(1)} %get-tuple-element.80), channel_id=1, source_target_pairs={{0,96},{2,98},{4,100},{6,102},{8,104},{10,106},{12,108},{14,110},{... | collective-permute-start | bytes 196616 | tf_op jit(solution)/shard_map/ppermute | solution.py:308
  83.4 4.6 %collective-permute-start.26 = (bf16[2,128,128]{2,1,0:T(8,128)(2,1)S(1)}, bf16[2,128,128]{2,1,0:T(8,128)(2,1)S(1)}, u32[]{:S(2)}, u32[]{:S(2)}) collective-permute-start(bf16[2,128,128]{2,1,0:T(8,128)(2,1)S(1)} %get-tuple-element.81), channel_id=1, source_target_pairs={{0,64},{2,66},{4,68},{6,70},{8,72},{10,74},{12,76},{14,78},{16,24}... | collective-permute-start | bytes 196616 | tf_op jit(solution)/shard_map/ppermute | solution.py:308
  88.1 2.4 %collective-permute-start.28 = (bf16[128,128]{1,0:T(8,128)(2,1)S(1)}, bf16[128,128]{1,0:T(8,128)(2,1)S(1)}, u32[]{:S(2)}, u32[]{:S(2)}) collective-permute-start(bf16[128,128]{1,0:T(8,128)(2,1)S(1)} %select_bitcast_fusion), channel_id=1, source_target_pairs={{0,16},{2,18},{4,20},{6,22},{8,24},{10,26},{12,28},{14,30},{16,0},... | collective-permute-start | bytes 98312 | tf_op jit(solution)/shard_map/ppermute | solution.py:308

commit v9 on v8

--- a/solution.py
+++ b/solution.py
@@ -359,6 +359,7 @@
     near_there = other_y(far_here)
     dq_shape = (TILES, part, width)
     far_dq, so_far = far_gradients_call(sizes, dq_shape, place, far_here, far_there, *far_tiles, *keys_all)
+    far_dq, near_there = lax.optimization_barrier((far_dq, near_there))
     rest = other_y(far_dq)
     dq, *sums = near_gradients_call(
         sizes, dq_shape, place, near_here, near_there, *near_tiles, *keys_all, so_far
@@ -373,9 +374,9 @@
     dq, totals[0] = lax.optimization_barrier((dq, totals[0]))
     dq = low(dq + rest.astype(jnp.float32))
     returned = peer(dq[1])
-    arrived, returned = lax.optimization_barrier((arrived, returned))
     total = low(added([totals[0]] + arrived))
     short = [along_first(total[by], by) for by in range(1, lines)]
+    short, returned = lax.optimization_barrier((short, returned))
     total = added([total[0]] + short)
     total = low(jnp.where(core == 0, SCALE * total, total))
     ours = jnp.where(core == 0, total[0], total[1])

time: 91.6 us -> 85.4 us (0.932); the launches traced: 91.1 us -> 86 us
  waiting for transfers between devices: 22.7 us -> 14.4 us
  starting transfers between devices: 42.7 us -> 47.6 us
  Pallas kernels: 19.4 us -> 17.6 us
    ppermute x29, waiting for transfers between devices: 22.7 us -> 14.4 us  [moved(): return lax.ppermute(value, CONTEXT, hops)]
    ppermute x29, starting transfers between devices: 42.7 us -> 47.6 us  [moved(): return lax.ppermute(value, CONTEXT, hops)]
    pallas_call x4, Pallas kernels: 19.4 us -> 17.6 us  [kernel_call(): pl.pallas_call(lambda *refs: kernel(sizes, *refs), name=kernel.__name__,...]
  transfers between devices with their start and end apart: 29 -> 29, of which waited for: 9 -> 10; matrix products, arithmetic and copies ran while one was open for 4% -> 4% of each run, Pallas kernels for 15% -> 20%
where the time goes in v9:
time: 85.4 us; the launch traced here: 86 us
  starting transfers between devices  47.6 us (56%)
  Pallas kernels  17.6 us (21%)
  waiting for transfers between devices  14.4 us (17%)
  other arithmetic  3.72 us (4%)
  between operations  1.48 us (2%)
  local copies, waits for them, and re-layouts  1.18 us (1%)
    ppermute x29, starting transfers between devices, moved(): return lax.ppermute(value, CONTEXT, hops)  47.6 us
    pallas_call x4, Pallas kernels, kernel_call(): pl.pallas_call(lambda *refs: kernel(sizes, *refs), name=kernel.__name__,...  17.6 us
    ppermute x29, waiting for transfers between devices, moved(): return lax.ppermute(value, CONTEXT, hops)  14.4 us
  transfers between devices with their start and end apart: 29, of which 10 were waited for; matrix products, arithmetic and copies ran while one was open for 4% of the time, Pallas kernels for 20%

profile of v9, /device:TPU:1, one launch (start us, length us, event | category | flops | bytes accessed | tf_op | source)
XLA Modules:
  0.0 86.0 jit_solution(2296677775874368745)
XLA Ops:
  1.3 1.5 %collective-permute-start.2 = (bf16[16,128]{1,0:T(8,128)(2,1)S(1)}, bf16[16,128]{1,0:T(8,128)(2,1)S(1)}, u32[]{:S(2)}, u32[]{:S(2)}) collective-permute-start(bf16[16,128]{1,0:T(8,128)(2,1)S(1)} %broadcast_in_dim.8), channel_id=1, source_target_pairs={{0,16},{2,18},{4,20},{6,22},{8,24},{10,26},{12,28},{14,30},{16,0},... | collective-permute-start | bytes 12296 | tf_op jit(solution)/shard_map/ppermute | solution.py:308
  2.8 0.8 select_bitcast_fusion.1
  3.6 0.1 collective-permute-start.1
  3.7 1.1 %constant_dynamic-slice_fusion.2 = (bf16[64,1024]{1,0:T(8,128)(2,1)S(1)}, bf16[64,1024]{1,0:T(8,128)(2,1)S(1)}, bf16[64,1024]{1,0:T(8,128)(2,1)S(1)}, bf16[64,1024]{1,0:T(8,128)(2,1)S(1)}) fusion(bf16[128,1024]{1,0:T(8,128)(2,1)} %param.8, s32[]{:T(128)S(6)} %select_n.83, s32[]{:T(128)S(6)} %select_n.84, bf16[128,1024]{1,0:T(8,128)(2,1)} %param.5), kind=kLoop, calls=%fused_computation.33 | loop fusion | bytes 1048584 | tf_op jit(solution)/shard_map/dynamic_slice | solution.py:334
  4.9 3.8 %collective-permute-start = (bf16[64,2176]{1,0:T(8,128)(2,1)S(1)}, bf16[64,2176]{1,0:T(8,128)(2,1)S(1)}, u32[]{:S(2)}, u32[]{:S(2)}) collective-permute-start(bf16[64,2176]{1,0:T(8,128)(2,1)S(1)} %get-tuple-element.99), channel_id=1, source_target_pairs={{0,64},{2,66},{4,68},{6,70},{8,72},{10,74},{12,76},{14,78},{16,80}... | collective-permute-start | bytes 835592 | tf_op jit(solution)/shard_map/ppermute | solution.py:308
  8.7 2.8 %collective-permute-start.4 = (bf16[272,128]{1,0:T(8,128)(2,1)S(1)}, bf16[272,128]{1,0:T(8,128)(2,1)S(1)}, u32[]{:S(2)}, u32[]{:S(2)}) collective-permute-start(bf16[272,128]{1,0:T(8,128)(2,1)S(1)} %get-tuple-element.95), channel_id=1, source_target_pairs={{0,64},{2,66},{4,68},{6,70},{8,72},{10,74},{12,76},{14,78},{16,24}... | collective-permute-start | bytes 208904 | tf_op jit(solution)/shard_map/ppermute | solution.py:308
  11.5 0.3 collective-permute-start.3
  11.8 2.4 %collective-permute-start.5 = (bf16[272,128]{1,0:T(8,128)(2,1)S(1)}, bf16[272,128]{1,0:T(8,128)(2,1)S(1)}, u32[]{:S(2)}, u32[]{:S(2)}) collective-permute-start(bf16[272,128]{1,0:T(8,128)(2,1)S(1)} %get-tuple-element.95), channel_id=1, source_target_pairs={{0,96},{2,98},{4,100},{6,102},{8,104},{10,106},{12,108},{14,110},{... | collective-permute-start | bytes 208904 | tf_op jit(solution)/shard_map/ppermute | solution.py:308
  14.2 2.0 %collective-permute-done.3 = bf16[272,128]{1,0:T(8,128)(2,1)S(1)} collective-permute-done((bf16[272,128]{1,0:T(8,128)(2,1)S(1)}, bf16[272,128]{1,0:T(8,128)(2,1)S(1)}, u32[]{:S(2)}, u32[]{:S(2)}) %collective-permute-start.3) | collective-permute-done | bytes 69664 | tf_op jit(solution)/shard_map/ppermute | solution.py:308
  16.3 0.8 pad_maximum_fusion
  17.1 1.8 %collective-permute-start.8 = (bf16[4,272,128]{2,1,0:T(8,128)(2,1)S(1)}, bf16[4,272,128]{2,1,0:T(8,128)(2,1)S(1)}, u32[]{:S(2)}, u32[]{:S(2)}) collective-permute-start(bf16[4,272,128]{2,1,0:T(8,128)(2,1)S(1)} %pad_maximum_fusion.3.refs_3_), channel_id=1, source_target_pairs={{0,12},{2,14},{4,0},{6,2},{8,4},{10,6},{12,8},{14,10},{16,112},{18... | collective-permute-start | bytes 835592 | tf_op jit(solution)/shard_map/ppermute | solution.py:308
  18.9 0.6 collective-permute-start.7
  19.5 0.2 collective-permute-start.6
  19.7 1.3 %collective-permute-start.13 = (bf16[128,2176]{1,0:T(8,128)(2,1)}, bf16[128,2176]{1,0:T(8,128)(2,1)S(1)}, u32[]{:S(2)}, u32[]{:S(2)}) collective-permute-start(bf16[128,2176]{1,0:T(8,128)(2,1)} %pad_maximum_fusion), channel_id=1, source_target_pairs={{0,2},{2,0},{4,6},{6,4},{8,10},{10,8},{12,14},{14,12},{16,18},{18,... | collective-permute-start | bytes 1671176 | tf_op jit(solution)/shard_map/ppermute | solution.py:308
  21.0 4.5 %collective-permute-start.9 = (bf16[4,272,128]{2,1,0:T(8,128)(2,1)S(1)}, bf16[4,272,128]{2,1,0:T(8,128)(2,1)S(1)}, u32[]{:S(2)}, u32[]{:S(2)}) collective-permute-start(bf16[4,272,128]{2,1,0:T(8,128)(2,1)S(1)} %pad_maximum_fusion.3.refs_3_), channel_id=1, source_target_pairs={{0,16},{2,18},{4,20},{6,22},{8,24},{10,26},{12,28},{14,30},{16,0},... | collective-permute-start | bytes 835592 | tf_op jit(solution)/shard_map/ppermute | solution.py:308
  25.4 3.8 %collective-permute-start.12 = (bf16[4,272,128]{2,1,0:T(8,128)(2,1)S(1)}, bf16[4,272,128]{2,1,0:T(8,128)(2,1)S(1)}, u32[]{:S(2)}, u32[]{:S(2)}) collective-permute-start(bf16[4,272,128]{2,1,0:T(8,128)(2,1)S(1)} %collective-permute-done.8.refs_6_), channel_id=1, source_target_pairs={{0,16},{2,18},{4,20},{6,22},{8,24},{10,26},{12,28},{14,30},{16,0},... | collective-permute-start | bytes 835592 | tf_op jit(solution)/shard_map/ppermute | solution.py:308
  29.3 1.1 %collective-permute-start.11 = (bf16[4,272,128]{2,1,0:T(8,128)(2,1)S(1)}, bf16[4,272,128]{2,1,0:T(8,128)(2,1)S(1)}, u32[]{:S(2)}, u32[]{:S(2)}) collective-permute-start(bf16[4,272,128]{2,1,0:T(8,128)(2,1)S(1)} %collective-permute-done.7.refs_5_), channel_id=1, source_target_pairs={{0,16},{2,18},{4,20},{6,22},{8,24},{10,26},{12,28},{14,30},{16,0},... | collective-permute-start | bytes 835592 | tf_op jit(solution)/shard_map/ppermute | solution.py:308
  30.3 2.9 %collective-permute-start.10 = (bf16[4,272,128]{2,1,0:T(8,128)(2,1)S(1)}, bf16[4,272,128]{2,1,0:T(8,128)(2,1)S(1)}, u32[]{:S(2)}, u32[]{:S(2)}) collective-permute-start(bf16[4,272,128]{2,1,0:T(8,128)(2,1)S(1)} %collective-permute-done.6.refs_4_), channel_id=1, source_target_pairs={{0,16},{2,18},{4,20},{6,22},{8,24},{10,26},{12,28},{14,30},{16,0},... | collective-permute-start | bytes 835592 | tf_op jit(solution)/shard_map/ppermute | solution.py:308
  33.2 0.1 pad_add_fusion.refs_0_
  33.3 1.1 %collective-permute-done.10.refs_8_ = bf16[4,272,128]{2,1,0:T(8,128)(2,1)S(1)} collective-permute-done((bf16[4,272,128]{2,1,0:T(8,128)(2,1)S(1)}, bf16[4,272,128]{2,1,0:T(8,128)(2,1)S(1)}, u32[]{:S(2)}, u32[]{:S(2)}) %collective-permute-start.10) | collective-permute-done | bytes 278560 | tf_op jit(solution)/shard_map/ppermute | solution.py:308
  34.4 3.8 %near_statistics.1 = (f32[2,8,512]{2,1,0:T(8,128)S(1)}, f32[2,16,128]{2,1,0:T(8,128)S(1)}, bf16[2,2,128,512]{3,2,1,0:T(8,128)(2,1)S(1)}, bf16[2,2,512,128]{3,2,1...) custom-call(s32[4]{0:T(128)S(1)} %pad_add_fusion.refs_0_, ...), custom_call_target="tpu_custom_call" | custom-call | flops 805306368 | bytes 8388608 | tf_op jit(solution)/shard_map/near_statistics/pallas_call | solution.py:225
  38.2 1.4 %collective-permute-start.14 = (f32[2,8,512]{2,1,0:T(8,128)S(1)}, f32[2,8,512]{2,1,0:T(8,128)S(1)}, u32[]{:S(2)}, u32[]{:S(2)}) collective-permute-start(f32[2,8,512]{2,1,0:T(8,128)S(1)} %get-tuple-element.44.refs_1_), channel_id=1, source_target_pairs={{0,2},{2,0},{4,6},{6,4},{8,10},{10,8},{12,14},{14,12},{16,18},{18,... | collective-permute-start | bytes 98312 | tf_op jit(solution)/shard_map/ppermute | solution.py:308
  39.6 3.1 %far_statistics.1 = (f32[2,8,512]{2,1,0:T(8,128)S(1)}, f32[2,16,128]{2,1,0:T(8,128)S(1)}, bf16[2,2,128,512]{3,2,1,0:T(8,128)(2,1)S(1)}, bf16[2,2,512,128]{3,2,1,0:T(8,128)(2,1)S(1)}) custom-call(s32[4]{0:T(128)S(1)} %pad_add_fusion.refs_0_, bf16[128,2176]{1,0:T(8,128)(2,1)S(1)} %collective-permute-done.13.refs_1_, ...), custom_call_target="tpu_custom_call" | custom-call | flops 805306368 | bytes 8388608 | tf_op jit(solution)/shard_map/far_statistics/pallas_call | solution.py:225
  42.7 0.9 %collective-permute-start.15 = (f32[2,8,512]{2,1,0:T(8,128)S(1)}, f32[2,8,512]{2,1,0:T(8,128)S(1)}, u32[]{:S(2)}, u32[]{:S(2)}) collective-permute-start(f32[2,8,512]{2,1,0:T(8,128)S(1)} %get-tuple-element.48.refs_1_), channel_id=1, source_target_pairs={{0,2},{2,0},{4,6},{6,4},{8,10},{10,8},{12,14},{14,12},{16,18},{18,... | collective-permute-start | bytes 98312 | tf_op jit(solution)/shard_map/ppermute | solution.py:308
  43.5 4.7 %far_gradients.1 = (bf16[2,64,1024]{2,1,0:T(8,128)(2,1)S(1)}, f32[2,4096,128]{2,1,0:T(8,128)S(1)}) custom-call(s32[4]{0:T(128)S(1)} %pad_add_fusion.refs_0_, f32[2,8,512]{2,1,0:T(8,128)S(1)} %get-tuple-element.48.refs_1_, f32[2,8,512]{2,1,0:T(8,128)S(1)} %collective-permute-done.14.refs_2_, f32[2,16,128]{2,1,0:T(8,128)S(1)} %get-tuple-element.49.refs_3_, ...), custom_call_target="tpu_custom_call" | custom-call | flops 2013265920 | bytes 8388608 | tf_op jit(solution)/shard_map/far_gradients/pallas_call | solution.py:225
  48.2 2.1 %collective-permute-start.16 = (bf16[2,64,1024]{2,1,0:T(8,128)(2,1)S(1)}, bf16[2,64,1024]{2,1,0:T(8,128)(2,1)S(1)}, u32[]{:S(2)}, u32[]{:S(2)}) collective-permute-start(bf16[2,64,1024]{2,1,0:T(8,128)(2,1)S(1)} %get-tuple-element.59), channel_id=1, source_target_pairs={{0,2},{2,0},{4,6},{6,4},{8,10},{10,8},{12,14},{14,12},{16,18},{18,... | collective-permute-start | bytes 786440 | tf_op jit(solution)/shard_map/ppermute | solution.py:308
  50.3 6.1 %near_gradients.1 = (f32[2,64,1024]{2,1,0:T(8,128)S(1)}, bf16[4,2,128,128]{3,2,1,0:T(8,128)(2,1)S(1)}, bf16[4,2,128,128]{3,2,1,0:T(8,128)(2,1)S(1)}, bf16[4,2,12...) custom-call(s32[4]{0:T(128)S(1)} %pad_add_fusion.refs_0_, ...), custom_call_target="tpu_custom_call" | custom-call | flops 2013265920 | bytes 8388608 | tf_op jit(solution)/shard_map/near_gradients/pallas_call | solution.py:225
  56.4 1.2 %collective-permute-start.17 = (bf16[4,2,128,128]{3,2,1,0:T(8,128)(2,1)S(1)}, bf16[4,2,128,128]{3,2,1,0:T(8,128)(2,1)S(1)}, u32[]{:S(2)}, u32[]{:S(2)}) collective-permute-start(bf16[4,2,128,128]{3,2,1,0:T(8,128)(2,1)S(1)} %get-tuple-element.69), channel_id=1, source_target_pairs={{0,16},{2,18},{4,20},{6,22},{8,24},{10,26},{12,28},{14,30},{16,0},... | collective-permute-start | bytes 786440 | tf_op jit(solution)/shard_map/ppermute | solution.py:308
  57.6 0.5 collective-permute-start.20
  58.1 0.6 collective-permute-done.17
  58.8 0.3 collective-permute-done.18
  59.2 4.7 %collective-permute-start.19 = (bf16[4,2,128,128]{3,2,1,0:T(8,128)(2,1)S(1)}, bf16[4,2,128,128]{3,2,1,0:T(8,128)(2,1)S(1)}, u32[]{:S(2)}, u32[]{:S(2)}) collective-permute-start(bf16[4,2,128,128]{3,2,1,0:T(8,128)(2,1)S(1)} %add_convert_fusion.3), channel_id=1, source_target_pairs={{0,4},{2,6},{4,8},{6,10},{8,12},{10,14},{12,0},{14,2},{16,48},{18,... | collective-permute-start | bytes 786440 | tf_op jit(solution)/shard_map/ppermute | solution.py:308
  64.0 2.9 %collective-permute-start.21 = (bf16[4,2,128,128]{3,2,1,0:T(8,128)(2,1)S(1)}, bf16[4,2,128,128]{3,2,1,0:T(8,128)(2,1)S(1)}, u32[]{:S(2)}, u32[]{:S(2)}) collective-permute-start(bf16[4,2,128,128]{3,2,1,0:T(8,128)(2,1)S(1)} %add_convert_fusion.2), channel_id=1, source_target_pairs={{0,8},{2,10},{4,12},{6,14},{8,0},{10,2},{12,4},{14,6},{16,80},{18,... | collective-permute-start | bytes 786440 | tf_op jit(solution)/shard_map/ppermute | solution.py:308
  66.9 0.1 collective-permute-start.23
  67.1 1.5 %collective-permute-start.27 = (bf16[64,1024]{1,0:T(8,128)(2,1)S(1)}, bf16[64,1024]{1,0:T(8,128)(2,1)S(1)}, u32[]{:S(2)}, u32[]{:S(2)}) collective-permute-start(bf16[64,1024]{1,0:T(8,128)(2,1)S(1)} %get-tuple-element.84), channel_id=1, source_target_pairs={{0,64},{2,66},{4,68},{6,70},{8,72},{10,74},{12,76},{14,78},{16,80}... | collective-permute-start | bytes 393224 | tf_op jit(solution)/shard_map/ppermute | solution.py:308
  68.6 1.0 %collective-permute-done.19 = bf16[4,2,128,128]{3,2,1,0:T(8,128)(2,1)S(1)} collective-permute-done((bf16[4,2,128,128]{3,2,1,0:T(8,128)(2,1)S(1)}, bf16[4,2,128,128]{3,2,1,0:T(8,128)(2,1)S(1)}, u32[]{:S(2)}, u32[]{:S(2)}) %collective-permute-start.19) | collective-permute-done | bytes 262176 | tf_op jit(solution)/shard_map/ppermute | solution.py:308
  69.5 5.1 %collective-permute-done.21 = bf16[4,2,128,128]{3,2,1,0:T(8,128)(2,1)S(1)} collective-permute-done((bf16[4,2,128,128]{3,2,1,0:T(8,128)(2,1)S(1)}, bf16[4,2,128,128]{3,2,1,0:T(8,128)(2,1)S(1)}, u32[]{:S(2)}, u32[]{:S(2)}) %collective-permute-start.21) | collective-permute-done | bytes 262176 | tf_op jit(solution)/shard_map/ppermute | solution.py:308
  74.6 0.1 add_convert_fusion
  74.8 0.1 collective-permute-start.26
  74.9 0.8 collective-permute-start.25
  75.7 0.7 collective-permute-start.24
  76.4 1.7 %collective-permute-done.26 = bf16[2,128,128]{2,1,0:T(8,128)(2,1)S(1)} collective-permute-done((bf16[2,128,128]{2,1,0:T(8,128)(2,1)S(1)}, bf16[2,128,128]{2,1,0:T(8,128)(2,1)S(1)}, u32[]{:S(2)}, u32[]{:S(2)}) %collective-permute-start.26) | collective-permute-done | bytes 65568 | tf_op jit(solution)/shard_map/ppermute | solution.py:308
  78.1 1.5 %collective-permute-done.25 = bf16[2,128,128]{2,1,0:T(8,128)(2,1)S(1)} collective-permute-done((bf16[2,128,128]{2,1,0:T(8,128)(2,1)S(1)}, bf16[2,128,128]{2,1,0:T(8,128)(2,1)S(1)}, u32[]{:S(2)}, u32[]{:S(2)}) %collective-permute-start.25) | collective-permute-done | bytes 65568 | tf_op jit(solution)/shard_map/ppermute | solution.py:308
  79.6 0.8 collective-permute-done.24
  80.5 4.0 %collective-permute-start.28 = (bf16[128,128]{1,0:T(8,128)(2,1)S(1)}, bf16[128,128]{1,0:T(8,128)(2,1)S(1)}, u32[]{:S(2)}, u32[]{:S(2)}) collective-permute-start(bf16[128,128]{1,0:T(8,128)(2,1)S(1)} %select_bitcast_fusion), channel_id=1, source_target_pairs={{0,16},{2,18},{4,20},{6,22},{8,24},{10,26},{12,28},{14,30},{16,0},... | collective-permute-start | bytes 98312 | tf_op jit(solution)/shard_map/ppermute | solution.py:308
  84.5 0.7 maximum_select_fusion
  85.2 0.1 collective-permute-done.28
  85.3 0.6 bitcast_select_fusion
  (38 shorter events, 0.6 us)
Async XLA Ops:
  1.3 7.4 %collective-permute-start.2 = (bf16[16,128]{1,0:T(8,128)(2,1)S(1)}, bf16[16,128]{1,0:T(8,128)(2,1)S(1)}, u32[]{:S(2)}, u32[]{:S(2)}) collective-permute-start(bf16[16,128]{1,0:T(8,128)(2,1)S(1)} %broadcast_in_dim.8), channel_id=1, source_target_pairs={{0,16},{2,18},{4,20},{6,22},{8,24},{10,26},{12,28},{14,30},{16,0},... | collective-permute-start | bytes 12296 | tf_op jit(solution)/shard_map/ppermute | solution.py:308
  3.6 5.1 %collective-permute-start.1 = (bf16[128,128]{1,0:T(8,128)(2,1)S(1)}, bf16[128,128]{1,0:T(8,128)(2,1)S(1)}, u32[]{:S(2)}, u32[]{:S(2)}) collective-permute-start(bf16[128,128]{1,0:T(8,128)(2,1)S(1)} %get-tuple-element.97), channel_id=1, source_target_pairs={{0,16},{2,18},{4,20},{6,22},{8,24},{10,26},{12,28},{14,30},{16,0},... | collective-permute-start | bytes 98312 | tf_op jit(solution)/shard_map/ppermute | solution.py:308
  4.9 11.4 %collective-permute-start = (bf16[64,2176]{1,0:T(8,128)(2,1)S(1)}, bf16[64,2176]{1,0:T(8,128)(2,1)S(1)}, u32[]{:S(2)}, u32[]{:S(2)}) collective-permute-start(bf16[64,2176]{1,0:T(8,128)(2,1)S(1)} %get-tuple-element.99), channel_id=1, source_target_pairs={{0,64},{2,66},{4,68},{6,70},{8,72},{10,74},{12,76},{14,78},{16,80}... | collective-permute-start | bytes 835592 | tf_op jit(solution)/shard_map/ppermute | solution.py:308
  8.7 5.5 %collective-permute-start.4 = (bf16[272,128]{1,0:T(8,128)(2,1)S(1)}, bf16[272,128]{1,0:T(8,128)(2,1)S(1)}, u32[]{:S(2)}, u32[]{:S(2)}) collective-permute-start(bf16[272,128]{1,0:T(8,128)(2,1)S(1)} %get-tuple-element.95), channel_id=1, source_target_pairs={{0,64},{2,66},{4,68},{6,70},{8,72},{10,74},{12,76},{14,78},{16,24}... | collective-permute-start | bytes 208904 | tf_op jit(solution)/shard_map/ppermute | solution.py:308
  11.5 4.7 %collective-permute-start.3 = (bf16[272,128]{1,0:T(8,128)(2,1)S(1)}, bf16[272,128]{1,0:T(8,128)(2,1)S(1)}, u32[]{:S(2)}, u32[]{:S(2)}) collective-permute-start(bf16[272,128]{1,0:T(8,128)(2,1)S(1)} %get-tuple-element.95), channel_id=1, source_target_pairs={{0,32},{2,34},{4,36},{6,38},{8,40},{10,42},{12,44},{14,46},{16,20}... | collective-permute-start | bytes 208904 | tf_op jit(solution)/shard_map/ppermute | solution.py:308
  11.8 4.4 %collective-permute-start.5 = (bf16[272,128]{1,0:T(8,128)(2,1)S(1)}, bf16[272,128]{1,0:T(8,128)(2,1)S(1)}, u32[]{:S(2)}, u32[]{:S(2)}) collective-permute-start(bf16[272,128]{1,0:T(8,128)(2,1)S(1)} %get-tuple-element.95), channel_id=1, source_target_pairs={{0,96},{2,98},{4,100},{6,102},{8,104},{10,106},{12,108},{14,110},{... | collective-permute-start | bytes 208904 | tf_op jit(solution)/shard_map/ppermute | solution.py:308
  17.1 8.3 %collective-permute-start.8 = (bf16[4,272,128]{2,1,0:T(8,128)(2,1)S(1)}, bf16[4,272,128]{2,1,0:T(8,128)(2,1)S(1)}, u32[]{:S(2)}, u32[]{:S(2)}) collective-permute-start(bf16[4,272,128]{2,1,0:T(8,128)(2,1)S(1)} %pad_maximum_fusion.3.refs_3_), channel_id=1, source_target_pairs={{0,12},{2,14},{4,0},{6,2},{8,4},{10,6},{12,8},{14,10},{16,112},{18... | collective-permute-start | bytes 835592 | tf_op jit(solution)/shard_map/ppermute | solution.py:308
  18.9 10.4 %collective-permute-start.7 = (bf16[4,272,128]{2,1,0:T(8,128)(2,1)S(1)}, bf16[4,272,128]{2,1,0:T(8,128)(2,1)S(1)}, u32[]{:S(2)}, u32[]{:S(2)}) collective-permute-start(bf16[4,272,128]{2,1,0:T(8,128)(2,1)S(1)} %pad_maximum_fusion.3.refs_3_), channel_id=1, source_target_pairs={{0,8},{2,10},{4,12},{6,14},{8,0},{10,2},{12,4},{14,6},{16,80},{18,... | collective-permute-start | bytes 835592 | tf_op jit(solution)/shard_map/ppermute | solution.py:308
  19.5 10.9 %collective-permute-start.6 = (bf16[4,272,128]{2,1,0:T(8,128)(2,1)S(1)}, bf16[4,272,128]{2,1,0:T(8,128)(2,1)S(1)}, u32[]{:S(2)}, u32[]{:S(2)}) collective-permute-start(bf16[4,272,128]{2,1,0:T(8,128)(2,1)S(1)} %pad_maximum_fusion.3.refs_3_), channel_id=1, source_target_pairs={{0,4},{2,6},{4,8},{6,10},{8,12},{10,14},{12,0},{14,2},{16,48},{18,... | collective-permute-start | bytes 835592 | tf_op jit(solution)/shard_map/ppermute | solution.py:308
  19.7 19.9 %collective-permute-start.13 = (bf16[128,2176]{1,0:T(8,128)(2,1)}, bf16[128,2176]{1,0:T(8,128)(2,1)S(1)}, u32[]{:S(2)}, u32[]{:S(2)}) collective-permute-start(bf16[128,2176]{1,0:T(8,128)(2,1)} %pad_maximum_fusion), channel_id=1, source_target_pairs={{0,2},{2,0},{4,6},{6,4},{8,10},{10,8},{12,14},{14,12},{16,18},{18,... | collective-permute-start | bytes 1671176 | tf_op jit(solution)/shard_map/ppermute | solution.py:308
  21.0 12.3 %collective-permute-start.9 = (bf16[4,272,128]{2,1,0:T(8,128)(2,1)S(1)}, bf16[4,272,128]{2,1,0:T(8,128)(2,1)S(1)}, u32[]{:S(2)}, u32[]{:S(2)}) collective-permute-start(bf16[4,272,128]{2,1,0:T(8,128)(2,1)S(1)} %pad_maximum_fusion.3.refs_3_), channel_id=1, source_target_pairs={{0,16},{2,18},{4,20},{6,22},{8,24},{10,26},{12,28},{14,30},{16,0},... | collective-permute-start | bytes 835592 | tf_op jit(solution)/shard_map/ppermute | solution.py:308
  25.4 7.9 %collective-permute-start.12 = (bf16[4,272,128]{2,1,0:T(8,128)(2,1)S(1)}, bf16[4,272,128]{2,1,0:T(8,128)(2,1)S(1)}, u32[]{:S(2)}, u32[]{:S(2)}) collective-permute-start(bf16[4,272,128]{2,1,0:T(8,128)(2,1)S(1)} %collective-permute-done.8.refs_6_), channel_id=1, source_target_pairs={{0,16},{2,18},{4,20},{6,22},{8,24},{10,26},{12,28},{14,30},{16,0},... | collective-permute-start | bytes 835592 | tf_op jit(solution)/shard_map/ppermute | solution.py:308
  29.3 4.0 %collective-permute-start.11 = (bf16[4,272,128]{2,1,0:T(8,128)(2,1)S(1)}, bf16[4,272,128]{2,1,0:T(8,128)(2,1)S(1)}, u32[]{:S(2)}, u32[]{:S(2)}) collective-permute-start(bf16[4,272,128]{2,1,0:T(8,128)(2,1)S(1)} %collective-permute-done.7.refs_5_), channel_id=1, source_target_pairs={{0,16},{2,18},{4,20},{6,22},{8,24},{10,26},{12,28},{14,30},{16,0},... | collective-permute-start | bytes 835592 | tf_op jit(solution)/shard_map/ppermute | solution.py:308
  30.3 4.1 %collective-permute-start.10 = (bf16[4,272,128]{2,1,0:T(8,128)(2,1)S(1)}, bf16[4,272,128]{2,1,0:T(8,128)(2,1)S(1)}, u32[]{:S(2)}, u32[]{:S(2)}) collective-permute-start(bf16[4,272,128]{2,1,0:T(8,128)(2,1)S(1)} %collective-permute-done.6.refs_4_), channel_id=1, source_target_pairs={{0,16},{2,18},{4,20},{6,22},{8,24},{10,26},{12,28},{14,30},{16,0},... | collective-permute-start | bytes 835592 | tf_op jit(solution)/shard_map/ppermute | solution.py:308
  38.2 5.3 %collective-permute-start.14 = (f32[2,8,512]{2,1,0:T(8,128)S(1)}, f32[2,8,512]{2,1,0:T(8,128)S(1)}, u32[]{:S(2)}, u32[]{:S(2)}) collective-permute-start(f32[2,8,512]{2,1,0:T(8,128)S(1)} %get-tuple-element.44.refs_1_), channel_id=1, source_target_pairs={{0,2},{2,0},{4,6},{6,4},{8,10},{10,8},{12,14},{14,12},{16,18},{18,... | collective-permute-start | bytes 98312 | tf_op jit(solution)/shard_map/ppermute | solution.py:308
  42.7 5.6 %collective-permute-start.15 = (f32[2,8,512]{2,1,0:T(8,128)S(1)}, f32[2,8,512]{2,1,0:T(8,128)S(1)}, u32[]{:S(2)}, u32[]{:S(2)}) collective-permute-start(f32[2,8,512]{2,1,0:T(8,128)S(1)} %get-tuple-element.48.refs_1_), channel_id=1, source_target_pairs={{0,2},{2,0},{4,6},{6,4},{8,10},{10,8},{12,14},{14,12},{16,18},{18,... | collective-permute-start | bytes 98312 | tf_op jit(solution)/shard_map/ppermute | solution.py:308
  48.2 8.2 %collective-permute-start.16 = (bf16[2,64,1024]{2,1,0:T(8,128)(2,1)S(1)}, bf16[2,64,1024]{2,1,0:T(8,128)(2,1)S(1)}, u32[]{:S(2)}, u32[]{:S(2)}) collective-permute-start(bf16[2,64,1024]{2,1,0:T(8,128)(2,1)S(1)} %get-tuple-element.59), channel_id=1, source_target_pairs={{0,2},{2,0},{4,6},{6,4},{8,10},{10,8},{12,14},{14,12},{16,18},{18,... | collective-permute-start | bytes 786440 | tf_op jit(solution)/shard_map/ppermute | solution.py:308
  56.4 2.3 %collective-permute-start.17 = (bf16[4,2,128,128]{3,2,1,0:T(8,128)(2,1)S(1)}, bf16[4,2,128,128]{3,2,1,0:T(8,128)(2,1)S(1)}, u32[]{:S(2)}, u32[]{:S(2)}) collective-permute-start(bf16[4,2,128,128]{3,2,1,0:T(8,128)(2,1)S(1)} %get-tuple-element.69), channel_id=1, source_target_pairs={{0,16},{2,18},{4,20},{6,22},{8,24},{10,26},{12,28},{14,30},{16,0},... | collective-permute-start | bytes 786440 | tf_op jit(solution)/shard_map/ppermute | solution.py:308
  57.6 1.5 %collective-permute-start.18 = (bf16[4,2,128,128]{3,2,1,0:T(8,128)(2,1)S(1)}, bf16[4,2,128,128]{3,2,1,0:T(8,128)(2,1)S(1)}, u32[]{:S(2)}, u32[]{:S(2)}) collective-permute-start(bf16[4,2,128,128]{3,2,1,0:T(8,128)(2,1)S(1)} %get-tuple-element.74), channel_id=1, source_target_pairs={{0,16},{2,18},{4,20},{6,22},{8,24},{10,26},{12,28},{14,30},{16,0},... | collective-permute-start | bytes 786440 | tf_op jit(solution)/shard_map/ppermute | solution.py:308
  57.6 6.3 %collective-permute-start.20 = (bf16[4,2,128,128]{3,2,1,0:T(8,128)(2,1)S(1)}, bf16[4,2,128,128]{3,2,1,0:T(8,128)(2,1)S(1)}, u32[]{:S(2)}, u32[]{:S(2)}) collective-permute-start(bf16[4,2,128,128]{3,2,1,0:T(8,128)(2,1)S(1)} %get-tuple-element.76), channel_id=1, source_target_pairs={{0,16},{2,18},{4,20},{6,22},{8,24},{10,26},{12,28},{14,30},{16,0},... | collective-permute-start | bytes 786440 | tf_op jit(solution)/shard_map/ppermute | solution.py:308
  58.1 8.7 %collective-permute-start.22 = (bf16[4,2,128,128]{3,2,1,0:T(8,128)(2,1)S(1)}, bf16[4,2,128,128]{3,2,1,0:T(8,128)(2,1)S(1)}, u32[]{:S(2)}, u32[]{:S(2)}) collective-permute-start(bf16[4,2,128,128]{3,2,1,0:T(8,128)(2,1)S(1)} %get-tuple-element.78), channel_id=1, source_target_pairs={{0,16},{2,18},{4,20},{6,22},{8,24},{10,26},{12,28},{14,30},{16,0},... | collective-permute-start | bytes 786440 | tf_op jit(solution)/shard_map/ppermute | solution.py:308
  59.2 10.3 %collective-permute-start.19 = (bf16[4,2,128,128]{3,2,1,0:T(8,128)(2,1)S(1)}, bf16[4,2,128,128]{3,2,1,0:T(8,128)(2,1)S(1)}, u32[]{:S(2)}, u32[]{:S(2)}) collective-permute-start(bf16[4,2,128,128]{3,2,1,0:T(8,128)(2,1)S(1)} %add_convert_fusion.3), channel_id=1, source_target_pairs={{0,4},{2,6},{4,8},{6,10},{8,12},{10,14},{12,0},{14,2},{16,48},{18,... | collective-permute-start | bytes 786440 | tf_op jit(solution)/shard_map/ppermute | solution.py:308
  64.0 10.7 %collective-permute-start.21 = (bf16[4,2,128,128]{3,2,1,0:T(8,128)(2,1)S(1)}, bf16[4,2,128,128]{3,2,1,0:T(8,128)(2,1)S(1)}, u32[]{:S(2)}, u32[]{:S(2)}) collective-permute-start(bf16[4,2,128,128]{3,2,1,0:T(8,128)(2,1)S(1)} %add_convert_fusion.2), channel_id=1, source_target_pairs={{0,8},{2,10},{4,12},{6,14},{8,0},{10,2},{12,4},{14,6},{16,80},{18,... | collective-permute-start | bytes 786440 | tf_op jit(solution)/shard_map/ppermute | solution.py:308
  66.9 7.7 %collective-permute-start.23 = (bf16[4,2,128,128]{3,2,1,0:T(8,128)(2,1)S(1)}, bf16[4,2,128,128]{3,2,1,0:T(8,128)(2,1)S(1)}, u32[]{:S(2)}, u32[]{:S(2)}) collective-permute-start(bf16[4,2,128,128]{3,2,1,0:T(8,128)(2,1)S(1)} %add_convert_fusion.1), channel_id=1, source_target_pairs={{0,12},{2,14},{4,0},{6,2},{8,4},{10,6},{12,8},{14,10},{16,112},{18... | collective-permute-start | bytes 786440 | tf_op jit(solution)/shard_map/ppermute | solution.py:308
  67.1 9.3 %collective-permute-start.27 = (bf16[64,1024]{1,0:T(8,128)(2,1)S(1)}, bf16[64,1024]{1,0:T(8,128)(2,1)S(1)}, u32[]{:S(2)}, u32[]{:S(2)}) collective-permute-start(bf16[64,1024]{1,0:T(8,128)(2,1)S(1)} %get-tuple-element.84), channel_id=1, source_target_pairs={{0,64},{2,66},{4,68},{6,70},{8,72},{10,74},{12,76},{14,78},{16,80}... | collective-permute-start | bytes 393224 | tf_op jit(solution)/shard_map/ppermute | solution.py:308
  74.8 3.3 %collective-permute-start.26 = (bf16[2,128,128]{2,1,0:T(8,128)(2,1)S(1)}, bf16[2,128,128]{2,1,0:T(8,128)(2,1)S(1)}, u32[]{:S(2)}, u32[]{:S(2)}) collective-permute-start(bf16[2,128,128]{2,1,0:T(8,128)(2,1)S(1)} %get-tuple-element.85), channel_id=1, source_target_pairs={{0,96},{2,98},{4,100},{6,102},{8,104},{10,106},{12,108},{14,110},{... | collective-permute-start | bytes 196616 | tf_op jit(solution)/shard_map/ppermute | solution.py:308
  74.9 4.7 %collective-permute-start.25 = (bf16[2,128,128]{2,1,0:T(8,128)(2,1)S(1)}, bf16[2,128,128]{2,1,0:T(8,128)(2,1)S(1)}, u32[]{:S(2)}, u32[]{:S(2)}) collective-permute-start(bf16[2,128,128]{2,1,0:T(8,128)(2,1)S(1)} %get-tuple-element.86), channel_id=1, source_target_pairs={{0,64},{2,66},{4,68},{6,70},{8,72},{10,74},{12,76},{14,78},{16,24}... | collective-permute-start | bytes 196616 | tf_op jit(solution)/shard_map/ppermute | solution.py:308
  75.7 4.7 %collective-permute-start.24 = (bf16[2,128,128]{2,1,0:T(8,128)(2,1)S(1)}, bf16[2,128,128]{2,1,0:T(8,128)(2,1)S(1)}, u32[]{:S(2)}, u32[]{:S(2)}) collective-permute-start(bf16[2,128,128]{2,1,0:T(8,128)(2,1)S(1)} %get-tuple-element.87), channel_id=1, source_target_pairs={{0,32},{2,34},{4,36},{6,38},{8,40},{10,42},{12,44},{14,46},{16,20}... | collective-permute-start | bytes 196616 | tf_op jit(solution)/shard_map/ppermute | solution.py:308
  80.5 4.8 %collective-permute-start.28 = (bf16[128,128]{1,0:T(8,128)(2,1)S(1)}, bf16[128,128]{1,0:T(8,128)(2,1)S(1)}, u32[]{:S(2)}, u32[]{:S(2)}) collective-permute-start(bf16[128,128]{1,0:T(8,128)(2,1)S(1)} %select_bitcast_fusion), channel_id=1, source_target_pairs={{0,16},{2,18},{4,20},{6,22},{8,24},{10,26},{12,28},{14,30},{16,0},... | collective-permute-start | bytes 98312 | tf_op jit(solution)/shard_map/ppermute | solution.py:308

commit v10 on v9

--- a/solution.py
+++ b/solution.py
@@ -28,27 +28,12 @@
 class Setting:
     def __init__(self, sizes, place_ref, kv_all, docs_all, tile_docs, rows, part, far):
         self.nz, self.nx = nz, nx = sizes
-        lines = nz
         self.z, self.x, self.y, self.core = (place_ref[i] for i in range(4))
         self.part, self.rows = part, rows
         self.heads = rows // part
         self.row = 1 - self.y if far else self.y
         self.kv_all, self.docs_all, self.tile_docs = kv_all, docs_all, tile_docs
         self.blocks = kv_all.shape[1]
-        self.steps = steps = range(lines)
-        z_at = [lax.rem(self.z + by, nz) * (2 * nx) for by in steps]
-        x_at = [lax.rem(self.x + by, nx) for by in steps]
-
-        def places(which):
-            return [
-                [
-                    jnp.where(which == 0, x_at[i], z_at[i]) + jnp.where(which == 0, z_at[j], x_at[j])
-                    for j in steps
-                ]
-                for i in steps
-            ]
-
-        self.spots = (places(self.core), places(1 - self.core))
         apart = nz // PEERS
         self.apart = apart
         self.row_token = lax.div(self.z, apart) * part + lax.rem(
@@ -82,24 +67,22 @@
 
 
 def place_keys(s, pieces, kv_all, docs_all):
-    for which, arrived, spot in ((s.core, pieces[0], s.spots[0]), (1 - s.core, pieces[1], s.spots[1])):
-        for i in s.steps:
-            for j in s.steps:
-                for c in range(2):
-                    kv_all[which, spot[-i][-j] + s.nx * c] = arrived[i][j, c * BLOCK : (c + 1) * BLOCK]
-    for i in s.steps:
-        for j in s.steps:
-            docs_all[i * s.nz + j] = pieces[0][i][j, 2 * BLOCK :].astype(jnp.float32)
+    for which, arrived in ((s.core, pieces[0]), (1 - s.core, pieces[1])):
+        for chip in range(s.nz * s.nx):
+            for c in range(2):
+                at = chip // s.nx * 2 * s.nx + c * s.nx + chip % s.nx
+                kv_all[which, at] = arrived[chip, c * BLOCK : (c + 1) * BLOCK]
+    docs_all[...] = pieces[0][:, 2 * BLOCK :].astype(jnp.float32)
 
 
 def place_rows(s, sources, tile_docs, cols, rows):
     part, width = s.part, s.heads * HEAD
-    for t, (source, begin) in enumerate(sources):
-        tile_docs[t] = source[begin : begin + DOC_ROWS, 2 * width :].astype(jnp.float32)
+    for t, source in enumerate(sources):
+        tile_docs[t] = source[:DOC_ROWS, 2 * width :].astype(jnp.float32)
         for side in range(2):
             whole = jnp.concatenate(
                 [
-                    source[begin : begin + part, side * width + h * HEAD : side * width + (h + 1) * HEAD]
+                    source[:, side * width + h * HEAD : side * width + (h + 1) * HEAD]
                     for h in range(s.heads)
                 ]
             )
@@ -108,21 +91,17 @@
 
 
 def near_statistics(sizes, *refs):
-    lines = sizes[0]
-    count = 3 + 2 * lines
-    place_ref, own_ref, peer_ref = refs[:3]
-    stats_ref, tile_docs, cols, tile_rows, kv_all, docs_all = refs[count:]
+    place_ref, own_ref, peer_ref, mine, theirs, stats_ref, tile_docs, cols, tile_rows, kv_all, docs_all = refs
     s = Setting(sizes, place_ref, kv_all, docs_all, tile_docs, cols.shape[-1], own_ref.shape[0], False)
-    place_keys(s, (refs[3 : 3 + lines], refs[3 + lines : count]), kv_all, docs_all)
-    place_rows(s, ((own_ref, 0), (peer_ref, 0)), tile_docs, cols, tile_rows)
+    place_keys(s, (mine, theirs), kv_all, docs_all)
+    place_rows(s, (own_ref, peer_ref), tile_docs, cols, tile_rows)
     statistics(s, stats_ref, cols)
 
 
 def far_statistics(sizes, *refs):
-    place_ref, far_ref, kv_all, docs_all, stats_ref, tile_docs, cols, tile_rows = refs
-    part = far_ref.shape[0] // TILES
-    s = Setting(sizes, place_ref, kv_all, docs_all, tile_docs, cols.shape[-1], part, True)
-    place_rows(s, ((far_ref, 0), (far_ref, part)), tile_docs, cols, tile_rows)
+    place_ref, own_ref, peer_ref, kv_all, docs_all, stats_ref, tile_docs, cols, tile_rows = refs
+    s = Setting(sizes, place_ref, kv_all, docs_all, tile_docs, cols.shape[-1], own_ref.shape[0], True)
+    place_rows(s, (own_ref, peer_ref), tile_docs, cols, tile_rows)
     statistics(s, stats_ref, cols)
 
 
@@ -168,19 +147,16 @@
 
 
 def near_gradients(sizes, *refs):
-    lines = sizes[0]
-    place_ref, here_ref, there_ref, tile_docs, cols, tile_rows, kv_all, docs_all, so_far, dq_ref = refs[:10]
-    keep, send = refs[10 : 10 + lines], refs[10 + lines : 10 + 2 * lines]
-    totals = refs[10 + 2 * lines]
+    place_ref, here_ref, there_ref, tile_docs, cols, tile_rows, kv_all, docs_all, so_far = refs[:9]
+    dq_ref, keep, send, totals = refs[9:]
     s = Setting(sizes, place_ref, kv_all, docs_all, tile_docs, cols.shape[-1], dq_ref.shape[1], False)
     totals[...] = so_far[...]
     gradients(s, here_ref, there_ref, cols, tile_rows, dq_ref, totals)
-    for which, out, spot in ((s.core, keep, s.spots[0]), (1 - s.core, send, s.spots[1])):
-        for i in s.steps:
-            for j in s.steps:
-                for c in range(2):
-                    begin = pl.multiple_of((spot[i][j] + s.nx * c) * BLOCK, BLOCK)
-                    out[i][j, c] = totals[which, pl.ds(begin, BLOCK), :].astype(jnp.bfloat16)
+    for which, out in ((s.core, keep), (1 - s.core, send)):
+        for chip in range(s.nz * s.nx):
+            for c in range(2):
+                begin = (chip // s.nx * 2 * s.nx + c * s.nx + chip % s.nx) * BLOCK
+                out[chip, c] = totals[which, begin : begin + BLOCK, :].astype(jnp.bfloat16)
 
 
 def gradients(s, here_ref, there_ref, cols, tile_rows, dq_ref, totals):
@@ -270,7 +246,7 @@
 def near_gradients_call(sizes, dq_shape, *operands):
     nz, nx = sizes
     outs = (jax.ShapeDtypeStruct(dq_shape, jnp.float32),)
-    outs += (jax.ShapeDtypeStruct((nx, 2, BLOCK, HEAD), jnp.bfloat16),) * (2 * nz)
+    outs += (jax.ShapeDtypeStruct((nz * nx, 2, BLOCK, HEAD), jnp.bfloat16),) * 2
     scratch = [pltpu.VMEM((2, 2 * nz * nx * BLOCK, HEAD), jnp.float32)]
     return kernel_call(near_gradients, sizes, operands, outs, scratch, 5)
 
@@ -295,7 +271,6 @@
     x, y = lax.div(outer, 2), lax.rem(outer, 2)
     part = rows // PEERS
     apart = nz // PEERS
-    lines = nz
 
     def moved(value, step):
         hops = []
@@ -316,11 +291,14 @@
     def peer(value):
         return moved(value, lambda c: (apart, 0, 0, 0))
 
-    def along_first(value, by):
-        return moved(value, lambda c: (0, by, 0, 0) if c else (by, 0, 0, 0))
-
-    def along_second(value, by):
-        return moved(value, lambda c: (by, 0, 0, 0) if c else (0, by, 0, 0))
+    members = [
+        [(iz * 2 + c) * outer_size + ix * 2 + iy for iz in range(nz) for ix in range(nx)]
+        for iy in range(2)
+        for c in range(2)
+    ]
+
+    def exchanged(value):
+        return lax.all_to_all(value, CONTEXT, 0, 0, tiled=True, axis_index_groups=members)
 
     def in_order(index, mine, theirs, axis):
         return jnp.where(
@@ -336,48 +314,39 @@
 
     own = rows_of(half)
     borrowed = peer(rows_of(1 - half))
-    shared = jnp.concatenate([own, borrowed])
-
-    given = other_core(jnp.where(core == 0, values, keys))
+    far_own = other_y(own)
+
+    given = other_core(jnp.concatenate([jnp.where(core == 0, values, keys), doc]))
     kept = jnp.where(core == 0, keys, values)
-    unit_docs = other_core(doc)
-    rows_in_order = in_order(core, kept, given, 0).reshape(2 * BLOCK, HEAD)
-    docs_in_order = in_order(core, doc[:8], unit_docs[:8], 0).reshape(DOC_ROWS, HEAD)
+    rows_in_order = in_order(core, kept, given[:BLOCK], 0).reshape(2 * BLOCK, HEAD)
+    docs_in_order = in_order(core, doc[:8], given[BLOCK : BLOCK + 8], 0).reshape(DOC_ROWS, HEAD)
     unit = jnp.concatenate([rows_in_order, docs_in_order])
-    line = jnp.stack([unit] + [along_first(unit, by) for by in range(1, lines)])
-    line, shared = lax.optimization_barrier((line, shared))
-    far = other_y(shared)
-    mine = [line] + [along_second(line, by) for by in range(1, lines)]
-    theirs = [other_core(piece) for piece in mine]
+    mine = exchanged(jnp.broadcast_to(unit, (nz * nx, *unit.shape)))
+    mine, borrowed, far_own = lax.optimization_barrier((mine, borrowed, far_own))
+    far_borrowed = other_y(borrowed)
+    theirs = other_core(mine)
 
     place = jnp.stack([z, x, y, core]).astype(jnp.int32)
     sizes = (nz, nx)
     tile_rows = part * width // HEAD
-    near_here, near_tiles, keys_all = near_statistics_call(sizes, tile_rows, place, own, borrowed, *mine, *theirs)
+    near_here, near_tiles, keys_all = near_statistics_call(sizes, tile_rows, place, own, borrowed, mine, theirs)
     far_there = other_y(near_here)
-    far_here, far_tiles = far_statistics_call(sizes, tile_rows, place, far, *keys_all)
+    far_here, far_tiles = far_statistics_call(sizes, tile_rows, place, far_own, far_borrowed, *keys_all)
     near_there = other_y(far_here)
     dq_shape = (TILES, part, width)
     far_dq, so_far = far_gradients_call(sizes, dq_shape, place, far_here, far_there, *far_tiles, *keys_all)
     far_dq, near_there = lax.optimization_barrier((far_dq, near_there))
     rest = other_y(far_dq)
-    dq, *sums = near_gradients_call(
+    dq, keep, send = near_gradients_call(
         sizes, dq_shape, place, near_here, near_there, *near_tiles, *keys_all, so_far
     )
-    rest, *sums = lax.optimization_barrier((rest, *sums))
-    keep, send = sums[:lines], sums[lines:]
-
-    totals = [None] * lines
-    for by in [*range(1, lines), 0]:
-        totals[by] = low(added([keep[by], other_core(send[by])]))
-    arrived = [along_second(totals[by], by) for by in range(1, lines)]
-    dq, totals[0] = lax.optimization_barrier((dq, totals[0]))
+    rest, dq, keep, send = lax.optimization_barrier((rest, dq, keep, send))
     dq = low(dq + rest.astype(jnp.float32))
     returned = peer(dq[1])
-    total = low(added([totals[0]] + arrived))
-    short = [along_first(total[by], by) for by in range(1, lines)]
-    short, returned = lax.optimization_barrier((short, returned))
-    total = added([total[0]] + short)
+
+    total = exchanged(low(added([keep, other_core(send)])))
+    total, returned = lax.optimization_barrier((total, returned))
+    total = jnp.sum(total.astype(jnp.float32), axis=0)
     total = low(jnp.where(core == 0, SCALE * total, total))
     ours = jnp.where(core == 0, total[0], total[1])
     theirs = other_core(jnp.where(core == 0, total[1], total[0]))

time: 85.4 us -> 94.6 us (1.11); the launches traced: 86 us -> 93.9 us
  waiting for transfers between devices: 14.4 us -> 36 us
  starting transfers between devices: 47.6 us -> 28.7 us
  Pallas kernels: 17.6 us -> 22.5 us
    ppermute x29 -> x11, starting transfers between devices: 47.6 us -> 16.6 us  [moved(): return lax.ppermute(value, CONTEXT, hops)]
    ppermute x29 -> x11, waiting for transfers between devices: 14.4 us -> 35.6 us  [moved(): return lax.ppermute(value, CONTEXT, hops)]
    all_to_all x0 -> x2, starting transfers between devices: none -> 12.2 us  [exchanged(): lax.all_to_all(value, CONTEXT, 0, 0, tiled=True, axis_index_groups=members)]
    pallas_call x4, Pallas kernels: 17.6 us -> 22.5 us  [kernel_call(): pl.pallas_call(lambda *refs: kernel(sizes, *refs), name=kernel.__name__,...]
    broadcast_in_dim x1, local copies, waits for them, and re-layouts: 0.01 us -> 1.18 us  [per_device(): mine = exchanged(jnp.broadcast_to(unit, (nz * nx, *unit.shape)))]
    dynamic_slice x1, local copies, waits for them, and re-layouts: 1.14 us -> 0.04 us  [rows_of(): lax.dynamic_slice_in_dim(whole, which * part, part, 0)]
  transfers between devices with their start and end apart: 29 -> 13, of which waited for: 10 -> 9; matrix products, arithmetic and copies ran while one was open for 4% -> 1% of each run, Pallas kernels for 20% -> 24%
where the time goes in v10:
time: 94.6 us; the launch traced here: 93.9 us
  waiting for transfers between devices  36 us (38%)
  starting transfers between devices  28.7 us (30%)
  Pallas kernels  22.5 us (24%)
  other arithmetic  3.95 us (4%)
  between operations  1.51 us (2%)
  local copies, waits for them, and re-layouts  1.27 us (1%)
    ppermute x11, waiting for transfers between devices, moved(): return lax.ppermute(value, CONTEXT, hops)  35.6 us
    pallas_call x4, Pallas kernels, kernel_call(): pl.pallas_call(lambda *refs: kernel(sizes, *refs), name=kernel.__name__,...  22.5 us
    ppermute x11, starting transfers between devices, moved(): return lax.ppermute(value, CONTEXT, hops)  16.6 us
    all_to_all x2, starting transfers between devices, exchanged(): lax.all_to_all(value, CONTEXT, 0, 0, tiled=True, axis_index_groups=members)  12.2 us
  transfers between devices with their start and end apart: 13, of which 9 were waited for; matrix products, arithmetic and copies ran while one was open for 1% of the time, Pallas kernels for 24%

profile of v10, /device:TPU:1, one launch (start us, length us, event | category | flops | bytes accessed | tf_op | source)
XLA Modules:
  0.0 93.9 jit_solution(234341057881331894)
XLA Ops:
  0.6 0.0 copy-start
  0.6 0.0 copy-start.1
  1.4 0.8 select_bitcast_fusion.1
  2.2 1.5 %collective-permute-start = (bf16[144,128]{1,0:T(8,128)(2,1)S(1)}, bf16[144,128]{1,0:T(8,128)(2,1)S(1)}, u32[]{:S(2)}, u32[]{:S(2)}) collective-permute-start(bf16[144,128]{1,0:T(8,128)(2,1)S(1)} %concatenate.12), channel_id=1, source_target_pairs={{0,16},{2,18},{4,20},{6,22},{8,24},{10,26},{12,28},{14,30},{16,0},... | collective-permute-start | bytes 110600 | tf_op jit(solution)/shard_map/ppermute | solution.py:283
  3.7 0.9 collective-permute-done
  4.6 1.2 %broadcast_in_dim.7 = bf16[16,272,128]{2,1,0:T(8,128)(2,1)} broadcast(bf16[272,128]{1,0:T(8,128)(2,1)S(1)} %pad_maximum_fusion), dimensions={1,2} | broadcast | bytes 1183744 | tf_op jit(solution)/shard_map/broadcast_in_dim | solution.py:324
  5.7 7.7 %all-to-all-start = ((bf16[16,272,128]{2,1,0:T(8,128)(2,1)}), bf16[16,272,128]{2,1,0:T(8,128)(2,1)S(1)}, u32[]{:S(2)}, u32[]{:S(2)}) async-start(bf16[16,272,128]{2,1,0:T(8,128)(2,1)} %broadcast_in_dim.7), calls=%async_computation | async-start | bytes 2228224 | tf_op jit(solution)/shard_map/all_to_all | solution.py:301
  13.4 0.0 copy-done
  13.4 0.0 copy-done.1
  13.5 0.1 maximum_maximum_fusion.1
  13.6 2.9 %collective-permute-start.1 = (bf16[64,2176]{1,0:T(8,128)(2,1)S(1)}, bf16[64,2176]{1,0:T(8,128)(2,1)S(1)}, u32[]{:S(2)}, u32[]{:S(2)}) collective-permute-start(bf16[64,2176]{1,0:T(8,128)(2,1)S(1)} %get-tuple-element.66), channel_id=1, source_target_pairs={{0,64},{2,66},{4,68},{6,70},{8,72},{10,74},{12,76},{14,78},{16,80}... | collective-permute-start | bytes 835592 | tf_op jit(solution)/shard_map/ppermute | solution.py:283
  16.6 1.3 %collective-permute-start.2 = (bf16[64,2176]{1,0:T(8,128)(2,1)S(1)}, bf16[64,2176]{1,0:T(8,128)(2,1)S(1)}, u32[]{:S(2)}, u32[]{:S(2)}) collective-permute-start(bf16[64,2176]{1,0:T(8,128)(2,1)S(1)} %get-tuple-element.65.refs_1_), channel_id=1, source_target_pairs={{0,2},{2,0},{4,6},{6,4},{8,10},{10,8},{12,14},{14,12},{16,18},{18,... | collective-permute-start | bytes 835592 | tf_op jit(solution)/shard_map/ppermute | solution.py:283
  17.9 16.8 %collective-permute-done.1.refs_2_ = bf16[64,2176]{1,0:T(8,128)(2,1)S(1)} collective-permute-done((bf16[64,2176]{1,0:T(8,128)(2,1)S(1)}, bf16[64,2176]{1,0:T(8,128)(2,1)S(1)}, u32[]{:S(2)}, u32[]{:S(2)}) %collective-permute-start.1) | collective-permute-done | bytes 278560 | tf_op jit(solution)/shard_map/ppermute | solution.py:283
  34.7 0.0 collective-permute-done.2.refs_1_
  34.7 0.0 all-to-all-done.refs_3_
  34.7 1.6 %collective-permute-start.4 = (bf16[16,272,128]{2,1,0:T(8,128)(2,1)S(1)}, bf16[16,272,128]{2,1,0:T(8,128)(2,1)S(1)}, u32[]{:S(2)}, u32[]{:S(2)}) collective-permute-start(bf16[16,272,128]{2,1,0:T(8,128)(2,1)S(1)} %all-to-all-done.refs_3_), channel_id=1, source_target_pairs={{0,16},{2,18},{4,20},{6,22},{8,24},{10,26},{12,28},{14,30},{16,0},... | collective-permute-start | bytes 3342344 | tf_op jit(solution)/shard_map/ppermute | solution.py:283
  36.3 1.3 %collective-permute-start.3 = (bf16[64,2176]{1,0:T(8,128)(2,1)S(1)}, bf16[64,2176]{1,0:T(8,128)(2,1)S(1)}, u32[]{:S(2)}, u32[]{:S(2)}) collective-permute-start(bf16[64,2176]{1,0:T(8,128)(2,1)S(1)} %collective-permute-done.1.refs_2_), channel_id=1, source_target_pairs={{0,2},{2,0},{4,6},{6,4},{8,10},{10,8},{12,14},{14,12},{16,18},{18,... | collective-permute-start | bytes 835592 | tf_op jit(solution)/shard_map/ppermute | solution.py:283
  37.6 0.1 pad_add_fusion.refs_0_
  37.7 1.0 %collective-permute-done.4.refs_4_ = bf16[16,272,128]{2,1,0:T(8,128)(2,1)S(1)} collective-permute-done((bf16[16,272,128]{2,1,0:T(8,128)(2,1)S(1)}, bf16[16,272,128]{2,1,0:T(8,128)(2,1)S(1)}, u32[]{:S(2)}, u32[]{:S(2)}) %collective-permute-start.4) | collective-permute-done | bytes 1114144 | tf_op jit(solution)/shard_map/ppermute | solution.py:283
  38.7 4.4 %near_statistics.1 = (f32[2,8,512]{2,1,0:T(8,128)S(1)}, f32[2,16,128]{2,1,0:T(8,128)S(1)}, bf16[2,2,128,512]{3,2,1,0:T(8,128)(2,1)S(1)}, bf16[2,2,512,128]{3,2,1...) custom-call(s32[4]{0:T(128)S(1)} %pad_add_fusion.refs_0_, ...), custom_call_target="tpu_custom_call" | custom-call | flops 805306368 | bytes 8388608 | tf_op jit(solution)/shard_map/near_statistics/pallas_call | solution.py:201
  43.0 1.4 %collective-permute-start.5 = (f32[2,8,512]{2,1,0:T(8,128)S(1)}, f32[2,8,512]{2,1,0:T(8,128)S(1)}, u32[]{:S(2)}, u32[]{:S(2)}) collective-permute-start(f32[2,8,512]{2,1,0:T(8,128)S(1)} %get-tuple-element.35.refs_1_), channel_id=1, source_target_pairs={{0,2},{2,0},{4,6},{6,4},{8,10},{10,8},{12,14},{14,12},{16,18},{18,... | collective-permute-start | bytes 98312 | tf_op jit(solution)/shard_map/ppermute | solution.py:283
  44.4 0.1 collective-permute-done.3.refs_2_
  44.5 4.3 %far_statistics.1 = (f32[2,8,512]{2,1,0:T(8,128)S(1)}, f32[2,16,128]{2,1,0:T(8,128)S(1)}, bf16[2,2,128,512]{3,2,1,0:T(8,128)(2,1)S(1)}, bf16[2,2,512,128]{3,2,1,0:T(8,128)(2,1)S(1)}) custom-call(s32[4]{0:T(128)S(1)} %pad_add_fusion.refs_0_, bf16[64,2176]{1,0:T(8,128)(2,1)S(1)} %collective-permute-done.2.refs_1_, ...), custom_call_target="tpu_custom_call" | custom-call | flops 805306368 | bytes 8388608 | tf_op jit(solution)/shard_map/far_statistics/pallas_call | solution.py:201
  48.8 0.8 collective-permute-start.6
  49.6 0.0 collective-permute-done.5.refs_2_
  49.6 6.8 %far_gradients.1 = (bf16[2,64,1024]{2,1,0:T(8,128)(2,1)S(1)}, f32[2,4096,128]{2,1,0:T(8,128)S(1)}) custom-call(s32[4]{0:T(128)S(1)} %pad_add_fusion.refs_0_, f32[2,8,512]{2,1,0:T(8,128)S(1)} %get-tuple-element.34.refs_1_, f32[2,8,512]{2,1,0:T(8,128)S(1)} %collective-permute-done.5.refs_2_, f32[2,16,128]{2,1,0:T(8,128)S(1)} %get-tuple-element.36.refs_3_, ...), custom_call_target="tpu_custom_call" | custom-call | flops 2013265920 | bytes 8388608 | tf_op jit(solution)/shard_map/far_gradients/pallas_call | solution.py:201
  56.4 0.0 collective-permute-done.6.refs_2_
  56.4 0.1 collective-permute-start.7
  56.5 7.0 %near_gradients.1 = (f32[2,64,1024]{2,1,0:T(8,128)S(1)}, bf16[16,2,128,128]{3,2,1,0:T(8,128)(2,1)S(1)}, bf16[16,2,128,128]{3,2,1,0:T(8,128)(2,1)S(1)}) custom-call(s32[4]{0:T(128)S(1)} %pad_add_fusion.refs_0_, f32[2,8,512]{2,1,0:T(8,128)S(1)} %get-tuple-element.35.refs_1_, f32[2,8,512]{2,1,0:T(8,128)S(1)} %collective-permute-done.6.refs_2_, ...), custom_call_target="tpu_custom_call" | custom-call | flops 2013265920 | bytes 8388608 | tf_op jit(solution)/shard_map/near_gradients/pallas_call | solution.py:201
  63.5 1.3 %collective-permute-done.7 = bf16[2,64,1024]{2,1,0:T(8,128)(2,1)S(1)} collective-permute-done((bf16[2,64,1024]{2,1,0:T(8,128)(2,1)S(1)}, bf16[2,64,1024]{2,1,0:T(8,128)(2,1)S(1)}, u32[]{:S(2)}, u32[]{:S(2)}) %collective-permute-start.7) | collective-permute-done | bytes 262176 | tf_op jit(solution)/shard_map/ppermute | solution.py:283
  64.8 0.4 collective-permute-start.8
  65.2 2.3 %collective-permute-done.8 = bf16[16,2,128,128]{3,2,1,0:T(8,128)(2,1)S(1)} collective-permute-done((bf16[16,2,128,128]{3,2,1,0:T(8,128)(2,1)S(1)}, bf16[16,2,128,128]{3,2,1,0:T(8,128)(2,1)S(1)}, u32[]{:S(2)}, u32[]{:S(2)}) %collective-permute-start.8) | collective-permute-done | bytes 1048608 | tf_op jit(solution)/shard_map/ppermute | solution.py:283
  67.5 1.4 %add_convert_fusion = bf16[16,2,128,128]{3,2,1,0:T(8,128)(2,1)} fusion(bf16[16,2,128,128]{3,2,1,0:T(8,128)(2,1)S(1)} %collective-permute-done.8, bf16[16,2,128,128]{3,2,1,0:T(8,128)(2,1)S(1)} %get-tuple-element.51), kind=kLoop, calls=%fused_computation.1 | loop fusion | flops 2097152 | bytes 3145728 | tf_op jit(solution)/shard_map/convert_element_type | solution.py:255
  68.9 4.5 %all-to-all-start.1 = ((bf16[16,2,128,128]{3,2,1,0:T(8,128)(2,1)}), bf16[16,2,128,128]{3,2,1,0:T(8,128)(2,1)S(1)}, u32[]{:S(2)}, u32[]{:S(2)}) async-start(bf16[16,2,128,128]{3,2,1,0:T(8,128)(2,1)} %add_convert_fusion), calls=%async_computation.1 | async-start | bytes 2097152 | tf_op jit(solution)/shard_map/all_to_all | solution.py:301
  73.3 0.1 add_convert_fusion.1
  73.4 3.0 %collective-permute-start.9 = (bf16[64,1024]{1,0:T(8,128)(2,1)S(1)}, bf16[64,1024]{1,0:T(8,128)(2,1)S(1)}, u32[]{:S(2)}, u32[]{:S(2)}) collective-permute-start(bf16[64,1024]{1,0:T(8,128)(2,1)S(1)} %get-tuple-element.56), channel_id=1, source_target_pairs={{0,64},{2,66},{4,68},{6,70},{8,72},{10,74},{12,76},{14,78},{16,80}... | collective-permute-start | bytes 393224 | tf_op jit(solution)/shard_map/ppermute | solution.py:283
  76.4 13.1 %collective-permute-done.9 = bf16[64,1024]{1,0:T(8,128)(2,1)S(1)} collective-permute-done((bf16[64,1024]{1,0:T(8,128)(2,1)S(1)}, bf16[64,1024]{1,0:T(8,128)(2,1)S(1)}, u32[]{:S(2)}, u32[]{:S(2)}) %collective-permute-start.9) | collective-permute-done | bytes 131104 | tf_op jit(solution)/shard_map/ppermute | solution.py:283
  89.5 0.3 all-to-all-done.1
  89.8 0.1 convert_reduce_fusion
  90.0 2.4 %collective-permute-start.10 = (bf16[128,128]{1,0:T(8,128)(2,1)S(1)}, bf16[128,128]{1,0:T(8,128)(2,1)S(1)}, u32[]{:S(2)}, u32[]{:S(2)}) collective-permute-start(bf16[128,128]{1,0:T(8,128)(2,1)S(1)} %select_bitcast_fusion), channel_id=1, source_target_pairs={{0,16},{2,18},{4,20},{6,22},{8,24},{10,26},{12,28},{14,30},{16,0},... | collective-permute-start | bytes 98312 | tf_op jit(solution)/shard_map/ppermute | solution.py:283
  92.4 0.7 maximum_select_fusion
  93.1 0.1 collective-permute-done.10
  93.2 0.6 bitcast_select_fusion
  (12 shorter events, 0.1 us)
Async XLA Ops:
  0.6 12.8 %copy-start = (bf16[128,1024]{1,0:T(8,128)(2,1)S(1)}, bf16[128,1024]{1,0:T(8,128)(2,1)}, u32[]{:S(2)}) copy-start(bf16[128,1024]{1,0:T(8,128)(2,1)} %param.8) | copy-start | bytes 786436
  0.6 12.8 %copy-start.1 = (bf16[128,1024]{1,0:T(8,128)(2,1)S(1)}, bf16[128,1024]{1,0:T(8,128)(2,1)}, u32[]{:S(2)}) copy-start(bf16[128,1024]{1,0:T(8,128)(2,1)} %param.5) | copy-start | bytes 786436
  2.2 2.4 %collective-permute-start = (bf16[144,128]{1,0:T(8,128)(2,1)S(1)}, bf16[144,128]{1,0:T(8,128)(2,1)S(1)}, u32[]{:S(2)}, u32[]{:S(2)}) collective-permute-start(bf16[144,128]{1,0:T(8,128)(2,1)S(1)} %concatenate.12), channel_id=1, source_target_pairs={{0,16},{2,18},{4,20},{6,22},{8,24},{10,26},{12,28},{14,30},{16,0},... | collective-permute-start | bytes 110600 | tf_op jit(solution)/shard_map/ppermute | solution.py:283
  5.7 29.0 %all-to-all-start = ((bf16[16,272,128]{2,1,0:T(8,128)(2,1)}), bf16[16,272,128]{2,1,0:T(8,128)(2,1)S(1)}, u32[]{:S(2)}, u32[]{:S(2)}) async-start(bf16[16,272,128]{2,1,0:T(8,128)(2,1)} %broadcast_in_dim.7), calls=%async_computation | async-start | bytes 2228224 | tf_op jit(solution)/shard_map/all_to_all | solution.py:301
  13.6 21.1 %collective-permute-start.1 = (bf16[64,2176]{1,0:T(8,128)(2,1)S(1)}, bf16[64,2176]{1,0:T(8,128)(2,1)S(1)}, u32[]{:S(2)}, u32[]{:S(2)}) collective-permute-start(bf16[64,2176]{1,0:T(8,128)(2,1)S(1)} %get-tuple-element.66), channel_id=1, source_target_pairs={{0,64},{2,66},{4,68},{6,70},{8,72},{10,74},{12,76},{14,78},{16,80}... | collective-permute-start | bytes 835592 | tf_op jit(solution)/shard_map/ppermute | solution.py:283
  16.6 18.1 %collective-permute-start.2 = (bf16[64,2176]{1,0:T(8,128)(2,1)S(1)}, bf16[64,2176]{1,0:T(8,128)(2,1)S(1)}, u32[]{:S(2)}, u32[]{:S(2)}) collective-permute-start(bf16[64,2176]{1,0:T(8,128)(2,1)S(1)} %get-tuple-element.65.refs_1_), channel_id=1, source_target_pairs={{0,2},{2,0},{4,6},{6,4},{8,10},{10,8},{12,14},{14,12},{16,18},{18,... | collective-permute-start | bytes 835592 | tf_op jit(solution)/shard_map/ppermute | solution.py:283
  34.7 3.9 %collective-permute-start.4 = (bf16[16,272,128]{2,1,0:T(8,128)(2,1)S(1)}, bf16[16,272,128]{2,1,0:T(8,128)(2,1)S(1)}, u32[]{:S(2)}, u32[]{:S(2)}) collective-permute-start(bf16[16,272,128]{2,1,0:T(8,128)(2,1)S(1)} %all-to-all-done.refs_3_), channel_id=1, source_target_pairs={{0,16},{2,18},{4,20},{6,22},{8,24},{10,26},{12,28},{14,30},{16,0},... | collective-permute-start | bytes 3342344 | tf_op jit(solution)/shard_map/ppermute | solution.py:283
  36.3 8.2 %collective-permute-start.3 = (bf16[64,2176]{1,0:T(8,128)(2,1)S(1)}, bf16[64,2176]{1,0:T(8,128)(2,1)S(1)}, u32[]{:S(2)}, u32[]{:S(2)}) collective-permute-start(bf16[64,2176]{1,0:T(8,128)(2,1)S(1)} %collective-permute-done.1.refs_2_), channel_id=1, source_target_pairs={{0,2},{2,0},{4,6},{6,4},{8,10},{10,8},{12,14},{14,12},{16,18},{18,... | collective-permute-start | bytes 835592 | tf_op jit(solution)/shard_map/ppermute | solution.py:283
  43.0 6.5 %collective-permute-start.5 = (f32[2,8,512]{2,1,0:T(8,128)S(1)}, f32[2,8,512]{2,1,0:T(8,128)S(1)}, u32[]{:S(2)}, u32[]{:S(2)}) collective-permute-start(f32[2,8,512]{2,1,0:T(8,128)S(1)} %get-tuple-element.35.refs_1_), channel_id=1, source_target_pairs={{0,2},{2,0},{4,6},{6,4},{8,10},{10,8},{12,14},{14,12},{16,18},{18,... | collective-permute-start | bytes 98312 | tf_op jit(solution)/shard_map/ppermute | solution.py:283
  48.8 7.6 %collective-permute-start.6 = (f32[2,8,512]{2,1,0:T(8,128)S(1)}, f32[2,8,512]{2,1,0:T(8,128)S(1)}, u32[]{:S(2)}, u32[]{:S(2)}) collective-permute-start(f32[2,8,512]{2,1,0:T(8,128)S(1)} %get-tuple-element.34.refs_1_), channel_id=1, source_target_pairs={{0,2},{2,0},{4,6},{6,4},{8,10},{10,8},{12,14},{14,12},{16,18},{18,... | collective-permute-start | bytes 98312 | tf_op jit(solution)/shard_map/ppermute | solution.py:283
  56.4 8.4 %collective-permute-start.7 = (bf16[2,64,1024]{2,1,0:T(8,128)(2,1)S(1)}, bf16[2,64,1024]{2,1,0:T(8,128)(2,1)S(1)}, u32[]{:S(2)}, u32[]{:S(2)}) collective-permute-start(bf16[2,64,1024]{2,1,0:T(8,128)(2,1)S(1)} %get-tuple-element.40), channel_id=1, source_target_pairs={{0,2},{2,0},{4,6},{6,4},{8,10},{10,8},{12,14},{14,12},{16,18},{18,... | collective-permute-start | bytes 786440 | tf_op jit(solution)/shard_map/ppermute | solution.py:283
  64.8 2.7 %collective-permute-start.8 = (bf16[16,2,128,128]{3,2,1,0:T(8,128)(2,1)S(1)}, bf16[16,2,128,128]{3,2,1,0:T(8,128)(2,1)S(1)}, u32[]{:S(2)}, u32[]{:S(2)}) collective-permute-start(bf16[16,2,128,128]{3,2,1,0:T(8,128)(2,1)S(1)} %get-tuple-element.52), channel_id=1, source_target_pairs={{0,16},{2,18},{4,20},{6,22},{8,24},{10,26},{12,28},{14,30},{16,0},... | collective-permute-start | bytes 3145736 | tf_op jit(solution)/shard_map/ppermute | solution.py:283
  68.9 21.0 %all-to-all-start.1 = ((bf16[16,2,128,128]{3,2,1,0:T(8,128)(2,1)}), bf16[16,2,128,128]{3,2,1,0:T(8,128)(2,1)S(1)}, u32[]{:S(2)}, u32[]{:S(2)}) async-start(bf16[16,2,128,128]{3,2,1,0:T(8,128)(2,1)} %add_convert_fusion), calls=%async_computation.1 | async-start | bytes 2097152 | tf_op jit(solution)/shard_map/all_to_all | solution.py:301
  73.4 16.0 %collective-permute-start.9 = (bf16[64,1024]{1,0:T(8,128)(2,1)S(1)}, bf16[64,1024]{1,0:T(8,128)(2,1)S(1)}, u32[]{:S(2)}, u32[]{:S(2)}) collective-permute-start(bf16[64,1024]{1,0:T(8,128)(2,1)S(1)} %get-tuple-element.56), channel_id=1, source_target_pairs={{0,64},{2,66},{4,68},{6,70},{8,72},{10,74},{12,76},{14,78},{16,80}... | collective-permute-start | bytes 393224 | tf_op jit(solution)/shard_map/ppermute | solution.py:283
  90.0 3.2 %collective-permute-start.10 = (bf16[128,128]{1,0:T(8,128)(2,1)S(1)}, bf16[128,128]{1,0:T(8,128)(2,1)S(1)}, u32[]{:S(2)}, u32[]{:S(2)}) collective-permute-start(bf16[128,128]{1,0:T(8,128)(2,1)S(1)} %select_bitcast_fusion), channel_id=1, source_target_pairs={{0,16},{2,18},{4,20},{6,22},{8,24},{10,26},{12,28},{14,30},{16,0},... | collective-permute-start | bytes 98312 | tf_op jit(solution)/shard_map/ppermute | solution.py:283

commit v11 on v9

--- a/solution.py
+++ b/solution.py
@@ -338,14 +338,12 @@
     borrowed = peer(rows_of(1 - half))
     shared = jnp.concatenate([own, borrowed])
 
-    given = other_core(jnp.where(core == 0, values, keys))
+    given = other_core(jnp.concatenate([jnp.where(core == 0, values, keys), doc]))
     kept = jnp.where(core == 0, keys, values)
-    unit_docs = other_core(doc)
-    rows_in_order = in_order(core, kept, given, 0).reshape(2 * BLOCK, HEAD)
-    docs_in_order = in_order(core, doc[:8], unit_docs[:8], 0).reshape(DOC_ROWS, HEAD)
+    rows_in_order = in_order(core, kept, given[:BLOCK], 0).reshape(2 * BLOCK, HEAD)
+    docs_in_order = in_order(core, doc[:8], given[BLOCK : BLOCK + 8], 0).reshape(DOC_ROWS, HEAD)
     unit = jnp.concatenate([rows_in_order, docs_in_order])
     line = jnp.stack([unit] + [along_first(unit, by) for by in range(1, lines)])
-    line, shared = lax.optimization_barrier((line, shared))
     far = other_y(shared)
     mine = [line] + [along_second(line, by) for by in range(1, lines)]
     theirs = [other_core(piece) for piece in mine]
@@ -368,9 +366,9 @@
     keep, send = sums[:lines], sums[lines:]
 
     totals = [None] * lines
-    for by in [*range(1, lines), 0]:
+    for by in (2, 1, 3, 0):
         totals[by] = low(added([keep[by], other_core(send[by])]))
-    arrived = [along_second(totals[by], by) for by in range(1, lines)]
+    arrived = [along_second(totals[by], by) for by in (2, 1, 3)]
     dq, totals[0] = lax.optimization_barrier((dq, totals[0]))
     dq = low(dq + rest.astype(jnp.float32))
     returned = peer(dq[1])

time: 85.4 us -> 82.3 us (0.964)
  Pallas kernels: 17.6 us -> 13.1 us
    pallas_call x4, Pallas kernels: 17.6 us -> 13.1 us  [kernel_call(): pl.pallas_call(lambda *refs: kernel(sizes, *refs), name=kernel.__name__,...]
    ppermute x29 -> x28, waiting for transfers between devices: 14.4 us -> 15.1 us  [moved(): return lax.ppermute(value, CONTEXT, hops)]
    ppermute x29 -> x28, starting transfers between devices: 47.6 us -> 47.5 us  [moved(): return lax.ppermute(value, CONTEXT, hops)]
  transfers between devices with their start and end apart: 29 -> 28, of which waited for: 10 -> 12; matrix products, arithmetic and copies ran while one was open for 4% -> 4% of each run, Pallas kernels for 20% -> 16%
where the time goes in v11:
time: 82.3 us; the launch traced here: 82.1 us
  starting transfers between devices  47.5 us (58%)
  waiting for transfers between devices  15.1 us (18%)
  Pallas kernels  13.1 us (16%)
  other arithmetic  3.72 us (5%)
  between operations  1.5 us (2%)
  local copies, waits for them, and re-layouts  1.18 us (1%)
    ppermute x28, starting transfers between devices, moved(): return lax.ppermute(value, CONTEXT, hops)  47.5 us
    ppermute x28, waiting for transfers between devices, moved(): return lax.ppermute(value, CONTEXT, hops)  15.1 us
    pallas_call x4, Pallas kernels, kernel_call(): pl.pallas_call(lambda *refs: kernel(sizes, *refs), name=kernel.__name__,...  13.1 us
  transfers between devices with their start and end apart: 28, of which 12 were waited for; matrix products, arithmetic and copies ran while one was open for 4% of the time, Pallas kernels for 16%

profile of v11, /device:TPU:1, one launch (start us, length us, event | category | flops | bytes accessed | tf_op | source)
XLA Modules:
  0.0 82.1 jit_solution(12904085435170810268)
XLA Ops:
  1.3 0.8 select_bitcast_fusion.1
  2.1 1.5 %collective-permute-start.1 = (bf16[144,128]{1,0:T(8,128)(2,1)S(1)}, bf16[144,128]{1,0:T(8,128)(2,1)S(1)}, u32[]{:S(2)}, u32[]{:S(2)}) collective-permute-start(bf16[144,128]{1,0:T(8,128)(2,1)S(1)} %concatenate.17), channel_id=1, source_target_pairs={{0,16},{2,18},{4,20},{6,22},{8,24},{10,26},{12,28},{14,30},{16,0},... | collective-permute-start | bytes 110600 | tf_op jit(solution)/shard_map/ppermute | solution.py:308
  3.6 1.1 %constant_dynamic-slice_fusion.2 = (bf16[64,1024]{1,0:T(8,128)(2,1)S(1)}, bf16[64,1024]{1,0:T(8,128)(2,1)S(1)}, bf16[64,1024]{1,0:T(8,128)(2,1)S(1)}, bf16[64,1024]{1,0:T(8,128)(2,1)S(1)}) fusion(bf16[128,1024]{1,0:T(8,128)(2,1)} %param.8, s32[]{:T(128)S(6)} %select_n.83, s32[]{:T(128)S(6)} %select_n.84, bf16[128,1024]{1,0:T(8,128)(2,1)} %param.5), kind=kLoop, calls=%fused_computation.34 | loop fusion | bytes 1048584 | tf_op jit(solution)/shard_map/dynamic_slice | solution.py:334
  4.8 3.8 %collective-permute-start = (bf16[64,2176]{1,0:T(8,128)(2,1)S(1)}, bf16[64,2176]{1,0:T(8,128)(2,1)S(1)}, u32[]{:S(2)}, u32[]{:S(2)}) collective-permute-start(bf16[64,2176]{1,0:T(8,128)(2,1)S(1)} %get-tuple-element.95), channel_id=1, source_target_pairs={{0,64},{2,66},{4,68},{6,70},{8,72},{10,74},{12,76},{14,78},{16,80}... | collective-permute-start | bytes 835592 | tf_op jit(solution)/shard_map/ppermute | solution.py:308
  8.6 2.8 %collective-permute-start.3 = (bf16[272,128]{1,0:T(8,128)(2,1)S(1)}, bf16[272,128]{1,0:T(8,128)(2,1)S(1)}, u32[]{:S(2)}, u32[]{:S(2)}) collective-permute-start(bf16[272,128]{1,0:T(8,128)(2,1)S(1)} %get-tuple-element.91), channel_id=1, source_target_pairs={{0,64},{2,66},{4,68},{6,70},{8,72},{10,74},{12,76},{14,78},{16,24}... | collective-permute-start | bytes 208904 | tf_op jit(solution)/shard_map/ppermute | solution.py:308
  11.4 0.3 collective-permute-start.2
  11.7 2.4 %collective-permute-start.4 = (bf16[272,128]{1,0:T(8,128)(2,1)S(1)}, bf16[272,128]{1,0:T(8,128)(2,1)S(1)}, u32[]{:S(2)}, u32[]{:S(2)}) collective-permute-start(bf16[272,128]{1,0:T(8,128)(2,1)S(1)} %get-tuple-element.91), channel_id=1, source_target_pairs={{0,96},{2,98},{4,100},{6,102},{8,104},{10,106},{12,108},{14,110},{... | collective-permute-start | bytes 208904 | tf_op jit(solution)/shard_map/ppermute | solution.py:308
  14.1 2.0 %collective-permute-done.2 = bf16[272,128]{1,0:T(8,128)(2,1)S(1)} collective-permute-done((bf16[272,128]{1,0:T(8,128)(2,1)S(1)}, bf16[272,128]{1,0:T(8,128)(2,1)S(1)}, u32[]{:S(2)}, u32[]{:S(2)}) %collective-permute-start.2) | collective-permute-done | bytes 69664 | tf_op jit(solution)/shard_map/ppermute | solution.py:308
  16.1 0.5 collective-permute-start.7
  16.6 1.9 %collective-permute-start.6 = (bf16[4,272,128]{2,1,0:T(8,128)(2,1)S(1)}, bf16[4,272,128]{2,1,0:T(8,128)(2,1)S(1)}, u32[]{:S(2)}, u32[]{:S(2)}) collective-permute-start(bf16[4,272,128]{2,1,0:T(8,128)(2,1)S(1)} %pad_maximum_fusion.3.refs_3_), channel_id=1, source_target_pairs={{0,8},{2,10},{4,12},{6,14},{8,0},{10,2},{12,4},{14,6},{16,80},{18,... | collective-permute-start | bytes 835592 | tf_op jit(solution)/shard_map/ppermute | solution.py:308
  18.6 0.8 %pad_maximum_fusion = bf16[128,2176]{1,0:T(8,128)(2,1)} fusion(bf16[64,2176]{1,0:T(8,128)(2,1)S(1)} %collective-permute-done.refs_2_, bf16[64,128]{1,0:T(8,128)(2,1)S(1)} %broadcast_in_dim.5, bf16[64,1024]{1,0:T(8,128)(2,1)S(1)} %get-tuple-element.86, bf16[64,1024]{1,0:T(8,128)(2,1)S(1)} %get-tuple-element.97), kind=kLoop, calls=%fused_computation | loop fusion | flops 2228224 | bytes 1114112 | tf_op jit(solution)/shard_map/concatenate | solution.py:339
  19.4 1.3 %collective-permute-start.12 = (bf16[128,2176]{1,0:T(8,128)(2,1)}, bf16[128,2176]{1,0:T(8,128)(2,1)S(1)}, u32[]{:S(2)}, u32[]{:S(2)}) collective-permute-start(bf16[128,2176]{1,0:T(8,128)(2,1)} %pad_maximum_fusion), channel_id=1, source_target_pairs={{0,2},{2,0},{4,6},{6,4},{8,10},{10,8},{12,14},{14,12},{16,18},{18,... | collective-permute-start | bytes 1671176 | tf_op jit(solution)/shard_map/ppermute | solution.py:308
  20.7 5.3 %collective-permute-start.8 = (bf16[4,272,128]{2,1,0:T(8,128)(2,1)S(1)}, bf16[4,272,128]{2,1,0:T(8,128)(2,1)S(1)}, u32[]{:S(2)}, u32[]{:S(2)}) collective-permute-start(bf16[4,272,128]{2,1,0:T(8,128)(2,1)S(1)} %pad_maximum_fusion.3.refs_3_), channel_id=1, source_target_pairs={{0,16},{2,18},{4,20},{6,22},{8,24},{10,26},{12,28},{14,30},{16,0},... | collective-permute-start | bytes 835592 | tf_op jit(solution)/shard_map/ppermute | solution.py:308
  26.0 2.4 %collective-permute-start.11 = (bf16[4,272,128]{2,1,0:T(8,128)(2,1)S(1)}, bf16[4,272,128]{2,1,0:T(8,128)(2,1)S(1)}, u32[]{:S(2)}, u32[]{:S(2)}) collective-permute-start(bf16[4,272,128]{2,1,0:T(8,128)(2,1)S(1)} %collective-permute-done.7.refs_6_), channel_id=1, source_target_pairs={{0,16},{2,18},{4,20},{6,22},{8,24},{10,26},{12,28},{14,30},{16,0},... | collective-permute-start | bytes 835592 | tf_op jit(solution)/shard_map/ppermute | solution.py:308
  28.4 1.1 %collective-permute-start.10 = (bf16[4,272,128]{2,1,0:T(8,128)(2,1)S(1)}, bf16[4,272,128]{2,1,0:T(8,128)(2,1)S(1)}, u32[]{:S(2)}, u32[]{:S(2)}) collective-permute-start(bf16[4,272,128]{2,1,0:T(8,128)(2,1)S(1)} %collective-permute-done.6.refs_5_), channel_id=1, source_target_pairs={{0,16},{2,18},{4,20},{6,22},{8,24},{10,26},{12,28},{14,30},{16,0},... | collective-permute-start | bytes 835592 | tf_op jit(solution)/shard_map/ppermute | solution.py:308
  29.4 2.9 %collective-permute-start.9 = (bf16[4,272,128]{2,1,0:T(8,128)(2,1)S(1)}, bf16[4,272,128]{2,1,0:T(8,128)(2,1)S(1)}, u32[]{:S(2)}, u32[]{:S(2)}) collective-permute-start(bf16[4,272,128]{2,1,0:T(8,128)(2,1)S(1)} %collective-permute-done.5.refs_4_), channel_id=1, source_target_pairs={{0,16},{2,18},{4,20},{6,22},{8,24},{10,26},{12,28},{14,30},{16,0},... | collective-permute-start | bytes 835592 | tf_op jit(solution)/shard_map/ppermute | solution.py:308
  32.4 1.1 %collective-permute-done.9.refs_8_ = bf16[4,272,128]{2,1,0:T(8,128)(2,1)S(1)} collective-permute-done((bf16[4,272,128]{2,1,0:T(8,128)(2,1)S(1)}, bf16[4,272,128]{2,1,0:T(8,128)(2,1)S(1)}, u32[]{:S(2)}, u32[]{:S(2)}) %collective-permute-start.9) | collective-permute-done | bytes 278560 | tf_op jit(solution)/shard_map/ppermute | solution.py:308
  33.5 2.6 %near_statistics.1 = (f32[2,8,512]{2,1,0:T(8,128)S(1)}, f32[2,16,128]{2,1,0:T(8,128)S(1)}, bf16[2,2,128,512]{3,2,1,0:T(8,128)(2,1)S(1)}, bf16[2,2,512,128]{3,2,1...) custom-call(s32[4]{0:T(128)S(1)} %pad_add_fusion.refs_0_, ...), custom_call_target="tpu_custom_call" | custom-call | flops 805306368 | bytes 8388608 | tf_op jit(solution)/shard_map/near_statistics/pallas_call | solution.py:225
  36.1 1.4 %collective-permute-start.13 = (f32[2,8,512]{2,1,0:T(8,128)S(1)}, f32[2,8,512]{2,1,0:T(8,128)S(1)}, u32[]{:S(2)}, u32[]{:S(2)}) collective-permute-start(f32[2,8,512]{2,1,0:T(8,128)S(1)} %get-tuple-element.41.refs_1_), channel_id=1, source_target_pairs={{0,2},{2,0},{4,6},{6,4},{8,10},{10,8},{12,14},{14,12},{16,18},{18,... | collective-permute-start | bytes 98312 | tf_op jit(solution)/shard_map/ppermute | solution.py:308
  37.5 2.5 %far_statistics.1 = (f32[2,8,512]{2,1,0:T(8,128)S(1)}, f32[2,16,128]{2,1,0:T(8,128)S(1)}, bf16[2,2,128,512]{3,2,1,0:T(8,128)(2,1)S(1)}, bf16[2,2,512,128]{3,2,1,0:T(8,128)(2,1)S(1)}) custom-call(s32[4]{0:T(128)S(1)} %pad_add_fusion.refs_0_, bf16[128,2176]{1,0:T(8,128)(2,1)S(1)} %collective-permute-done.12.refs_1_, ...), custom_call_target="tpu_custom_call" | custom-call | flops 805306368 | bytes 8388608 | tf_op jit(solution)/shard_map/far_statistics/pallas_call | solution.py:225
  40.0 0.1 collective-permute-start.14
  40.1 3.9 %far_gradients.1 = (bf16[2,64,1024]{2,1,0:T(8,128)(2,1)S(1)}, f32[2,4096,128]{2,1,0:T(8,128)S(1)}) custom-call(s32[4]{0:T(128)S(1)} %pad_add_fusion.refs_0_, f32[2,8,512]{2,1,0:T(8,128)S(1)} %get-tuple-element.44.refs_1_, f32[2,8,512]{2,1,0:T(8,128)S(1)} %collective-permute-done.13.refs_2_, f32[2,16,128]{2,1,0:T(8,128)S(1)} %get-tuple-element.45.refs_3_, ...), custom_call_target="tpu_custom_call" | custom-call | flops 2013265920 | bytes 8388608 | tf_op jit(solution)/shard_map/far_gradients/pallas_call | solution.py:225
  44.0 0.5 collective-permute-start.15
  44.5 4.1 %near_gradients.1 = (f32[2,64,1024]{2,1,0:T(8,128)S(1)}, bf16[4,2,128,128]{3,2,1,0:T(8,128)(2,1)S(1)}, bf16[4,2,128,128]{3,2,1,0:T(8,128)(2,1)S(1)}, bf16[4,2,12...) custom-call(s32[4]{0:T(128)S(1)} %pad_add_fusion.refs_0_, ...), custom_call_target="tpu_custom_call" | custom-call | flops 2013265920 | bytes 8388608 | tf_op jit(solution)/shard_map/near_gradients/pallas_call | solution.py:225
  48.6 1.2 %collective-permute-done.15 = bf16[2,64,1024]{2,1,0:T(8,128)(2,1)S(1)} collective-permute-done((bf16[2,64,1024]{2,1,0:T(8,128)(2,1)S(1)}, bf16[2,64,1024]{2,1,0:T(8,128)(2,1)S(1)}, u32[]{:S(2)}, u32[]{:S(2)}) %collective-permute-start.15) | collective-permute-done | bytes 262176 | tf_op jit(solution)/shard_map/ppermute | solution.py:308
  49.8 9.6 %collective-permute-start.16 = (bf16[4,2,128,128]{3,2,1,0:T(8,128)(2,1)S(1)}, bf16[4,2,128,128]{3,2,1,0:T(8,128)(2,1)S(1)}, u32[]{:S(2)}, u32[]{:S(2)}) collective-permute-start(bf16[4,2,128,128]{3,2,1,0:T(8,128)(2,1)S(1)} %get-tuple-element.65), channel_id=1, source_target_pairs={{0,16},{2,18},{4,20},{6,22},{8,24},{10,26},{12,28},{14,30},{16,0},... | collective-permute-start | bytes 786440 | tf_op jit(solution)/shard_map/ppermute | solution.py:308
  59.4 0.1 collective-permute-start.17
  59.5 0.4 collective-permute-start.19
  59.9 0.1 collective-permute-start.21
  60.0 0.6 collective-permute-done.16
  60.6 0.3 collective-permute-done.17
  61.0 2.3 %collective-permute-start.18 = (bf16[4,2,128,128]{3,2,1,0:T(8,128)(2,1)S(1)}, bf16[4,2,128,128]{3,2,1,0:T(8,128)(2,1)S(1)}, u32[]{:S(2)}, u32[]{:S(2)}) collective-permute-start(bf16[4,2,128,128]{3,2,1,0:T(8,128)(2,1)S(1)} %add_convert_fusion.3), channel_id=1, source_target_pairs={{0,8},{2,10},{4,12},{6,14},{8,0},{10,2},{12,4},{14,6},{16,80},{18,... | collective-permute-start | bytes 786440 | tf_op jit(solution)/shard_map/ppermute | solution.py:308
  63.5 2.7 %collective-permute-start.22 = (bf16[4,2,128,128]{3,2,1,0:T(8,128)(2,1)S(1)}, bf16[4,2,128,128]{3,2,1,0:T(8,128)(2,1)S(1)}, u32[]{:S(2)}, u32[]{:S(2)}) collective-permute-start(bf16[4,2,128,128]{3,2,1,0:T(8,128)(2,1)S(1)} %add_convert_fusion.1), channel_id=1, source_target_pairs={{0,12},{2,14},{4,0},{6,2},{8,4},{10,6},{12,8},{14,10},{16,112},{18... | collective-permute-start | bytes 786440 | tf_op jit(solution)/shard_map/ppermute | solution.py:308
  66.3 0.1 collective-permute-start.26
  66.4 1.7 %collective-permute-done.18 = bf16[4,2,128,128]{3,2,1,0:T(8,128)(2,1)S(1)} collective-permute-done((bf16[4,2,128,128]{3,2,1,0:T(8,128)(2,1)S(1)}, bf16[4,2,128,128]{3,2,1,0:T(8,128)(2,1)S(1)}, u32[]{:S(2)}, u32[]{:S(2)}) %collective-permute-start.18) | collective-permute-done | bytes 262176 | tf_op jit(solution)/shard_map/ppermute | solution.py:308
  68.1 2.8 %collective-permute-done.20 = bf16[4,2,128,128]{3,2,1,0:T(8,128)(2,1)S(1)} collective-permute-done((bf16[4,2,128,128]{3,2,1,0:T(8,128)(2,1)S(1)}, bf16[4,2,128,128]{3,2,1,0:T(8,128)(2,1)S(1)}, u32[]{:S(2)}, u32[]{:S(2)}) %collective-permute-start.20) | collective-permute-done | bytes 262176 | tf_op jit(solution)/shard_map/ppermute | solution.py:308
  70.9 1.5 %collective-permute-done.22 = bf16[4,2,128,128]{3,2,1,0:T(8,128)(2,1)S(1)} collective-permute-done((bf16[4,2,128,128]{3,2,1,0:T(8,128)(2,1)S(1)}, bf16[4,2,128,128]{3,2,1,0:T(8,128)(2,1)S(1)}, u32[]{:S(2)}, u32[]{:S(2)}) %collective-permute-start.22) | collective-permute-done | bytes 262176 | tf_op jit(solution)/shard_map/ppermute | solution.py:308
  72.4 0.1 add_convert_fusion
  72.5 1.5 %collective-permute-start.25 = (bf16[2,128,128]{2,1,0:T(8,128)(2,1)S(1)}, bf16[2,128,128]{2,1,0:T(8,128)(2,1)S(1)}, u32[]{:S(2)}, u32[]{:S(2)}) collective-permute-start(bf16[2,128,128]{2,1,0:T(8,128)(2,1)S(1)} %get-tuple-element.81), channel_id=1, source_target_pairs={{0,96},{2,98},{4,100},{6,102},{8,104},{10,106},{12,108},{14,110},{... | collective-permute-start | bytes 196616 | tf_op jit(solution)/shard_map/ppermute | solution.py:308
  74.0 1.0 %collective-permute-start.24 = (bf16[2,128,128]{2,1,0:T(8,128)(2,1)S(1)}, bf16[2,128,128]{2,1,0:T(8,128)(2,1)S(1)}, u32[]{:S(2)}, u32[]{:S(2)}) collective-permute-start(bf16[2,128,128]{2,1,0:T(8,128)(2,1)S(1)} %get-tuple-element.82), channel_id=1, source_target_pairs={{0,64},{2,66},{4,68},{6,70},{8,72},{10,74},{12,76},{14,78},{16,24}... | collective-permute-start | bytes 196616 | tf_op jit(solution)/shard_map/ppermute | solution.py:308
  75.1 0.8 collective-permute-start.23
  75.8 0.2 collective-permute-done.25
  76.0 2.6 %collective-permute-done.24 = bf16[2,128,128]{2,1,0:T(8,128)(2,1)S(1)} collective-permute-done((bf16[2,128,128]{2,1,0:T(8,128)(2,1)S(1)}, bf16[2,128,128]{2,1,0:T(8,128)(2,1)S(1)}, u32[]{:S(2)}, u32[]{:S(2)}) %collective-permute-start.24) | collective-permute-done | bytes 65568 | tf_op jit(solution)/shard_map/ppermute | solution.py:308
  78.7 1.0 %collective-permute-done.23 = bf16[2,128,128]{2,1,0:T(8,128)(2,1)S(1)} collective-permute-done((bf16[2,128,128]{2,1,0:T(8,128)(2,1)S(1)}, bf16[2,128,128]{2,1,0:T(8,128)(2,1)S(1)}, u32[]{:S(2)}, u32[]{:S(2)}) %collective-permute-start.23) | collective-permute-done | bytes 65568 | tf_op jit(solution)/shard_map/ppermute | solution.py:308
  79.7 0.8 %collective-permute-start.27 = (bf16[128,128]{1,0:T(8,128)(2,1)S(1)}, bf16[128,128]{1,0:T(8,128)(2,1)S(1)}, u32[]{:S(2)}, u32[]{:S(2)}) collective-permute-start(bf16[128,128]{1,0:T(8,128)(2,1)S(1)} %select_bitcast_fusion), channel_id=1, source_target_pairs={{0,16},{2,18},{4,20},{6,22},{8,24},{10,26},{12,28},{14,30},{16,0},... | collective-permute-start | bytes 98312 | tf_op jit(solution)/shard_map/ppermute | solution.py:308
  80.6 0.7 maximum_select_fusion
  81.3 0.1 collective-permute-done.27
  81.4 0.6 bitcast_select_fusion
  (37 shorter events, 0.8 us)
Async XLA Ops:
  2.1 6.5 %collective-permute-start.1 = (bf16[144,128]{1,0:T(8,128)(2,1)S(1)}, bf16[144,128]{1,0:T(8,128)(2,1)S(1)}, u32[]{:S(2)}, u32[]{:S(2)}) collective-permute-start(bf16[144,128]{1,0:T(8,128)(2,1)S(1)} %concatenate.17), channel_id=1, source_target_pairs={{0,16},{2,18},{4,20},{6,22},{8,24},{10,26},{12,28},{14,30},{16,0},... | collective-permute-start | bytes 110600 | tf_op jit(solution)/shard_map/ppermute | solution.py:308
  4.8 13.8 %collective-permute-start = (bf16[64,2176]{1,0:T(8,128)(2,1)S(1)}, bf16[64,2176]{1,0:T(8,128)(2,1)S(1)}, u32[]{:S(2)}, u32[]{:S(2)}) collective-permute-start(bf16[64,2176]{1,0:T(8,128)(2,1)S(1)} %get-tuple-element.95), channel_id=1, source_target_pairs={{0,64},{2,66},{4,68},{6,70},{8,72},{10,74},{12,76},{14,78},{16,80}... | collective-permute-start | bytes 835592 | tf_op jit(solution)/shard_map/ppermute | solution.py:308
  8.6 5.5 %collective-permute-start.3 = (bf16[272,128]{1,0:T(8,128)(2,1)S(1)}, bf16[272,128]{1,0:T(8,128)(2,1)S(1)}, u32[]{:S(2)}, u32[]{:S(2)}) collective-permute-start(bf16[272,128]{1,0:T(8,128)(2,1)S(1)} %get-tuple-element.91), channel_id=1, source_target_pairs={{0,64},{2,66},{4,68},{6,70},{8,72},{10,74},{12,76},{14,78},{16,24}... | collective-permute-start | bytes 208904 | tf_op jit(solution)/shard_map/ppermute | solution.py:308
  11.4 4.7 %collective-permute-start.2 = (bf16[272,128]{1,0:T(8,128)(2,1)S(1)}, bf16[272,128]{1,0:T(8,128)(2,1)S(1)}, u32[]{:S(2)}, u32[]{:S(2)}) collective-permute-start(bf16[272,128]{1,0:T(8,128)(2,1)S(1)} %get-tuple-element.91), channel_id=1, source_target_pairs={{0,32},{2,34},{4,36},{6,38},{8,40},{10,42},{12,44},{14,46},{16,20}... | collective-permute-start | bytes 208904 | tf_op jit(solution)/shard_map/ppermute | solution.py:308
  11.7 4.4 %collective-permute-start.4 = (bf16[272,128]{1,0:T(8,128)(2,1)S(1)}, bf16[272,128]{1,0:T(8,128)(2,1)S(1)}, u32[]{:S(2)}, u32[]{:S(2)}) collective-permute-start(bf16[272,128]{1,0:T(8,128)(2,1)S(1)} %get-tuple-element.91), channel_id=1, source_target_pairs={{0,96},{2,98},{4,100},{6,102},{8,104},{10,106},{12,108},{14,110},{... | collective-permute-start | bytes 208904 | tf_op jit(solution)/shard_map/ppermute | solution.py:308
  16.1 9.9 %collective-permute-start.7 = (bf16[4,272,128]{2,1,0:T(8,128)(2,1)S(1)}, bf16[4,272,128]{2,1,0:T(8,128)(2,1)S(1)}, u32[]{:S(2)}, u32[]{:S(2)}) collective-permute-start(bf16[4,272,128]{2,1,0:T(8,128)(2,1)S(1)} %pad_maximum_fusion.3.refs_3_), channel_id=1, source_target_pairs={{0,12},{2,14},{4,0},{6,2},{8,4},{10,6},{12,8},{14,10},{16,112},{18... | collective-permute-start | bytes 835592 | tf_op jit(solution)/shard_map/ppermute | solution.py:308
  16.6 11.7 %collective-permute-start.6 = (bf16[4,272,128]{2,1,0:T(8,128)(2,1)S(1)}, bf16[4,272,128]{2,1,0:T(8,128)(2,1)S(1)}, u32[]{:S(2)}, u32[]{:S(2)}) collective-permute-start(bf16[4,272,128]{2,1,0:T(8,128)(2,1)S(1)} %pad_maximum_fusion.3.refs_3_), channel_id=1, source_target_pairs={{0,8},{2,10},{4,12},{6,14},{8,0},{10,2},{12,4},{14,6},{16,80},{18,... | collective-permute-start | bytes 835592 | tf_op jit(solution)/shard_map/ppermute | solution.py:308
  18.6 10.9 %collective-permute-start.5 = (bf16[4,272,128]{2,1,0:T(8,128)(2,1)S(1)}, bf16[4,272,128]{2,1,0:T(8,128)(2,1)S(1)}, u32[]{:S(2)}, u32[]{:S(2)}) collective-permute-start(bf16[4,272,128]{2,1,0:T(8,128)(2,1)S(1)} %pad_maximum_fusion.3.refs_3_), channel_id=1, source_target_pairs={{0,4},{2,6},{4,8},{6,10},{8,12},{10,14},{12,0},{14,2},{16,48},{18,... | collective-permute-start | bytes 835592 | tf_op jit(solution)/shard_map/ppermute | solution.py:308
  19.4 18.1 %collective-permute-start.12 = (bf16[128,2176]{1,0:T(8,128)(2,1)}, bf16[128,2176]{1,0:T(8,128)(2,1)S(1)}, u32[]{:S(2)}, u32[]{:S(2)}) collective-permute-start(bf16[128,2176]{1,0:T(8,128)(2,1)} %pad_maximum_fusion), channel_id=1, source_target_pairs={{0,2},{2,0},{4,6},{6,4},{8,10},{10,8},{12,14},{14,12},{16,18},{18,... | collective-permute-start | bytes 1671176 | tf_op jit(solution)/shard_map/ppermute | solution.py:308
  20.7 11.7 %collective-permute-start.8 = (bf16[4,272,128]{2,1,0:T(8,128)(2,1)S(1)}, bf16[4,272,128]{2,1,0:T(8,128)(2,1)S(1)}, u32[]{:S(2)}, u32[]{:S(2)}) collective-permute-start(bf16[4,272,128]{2,1,0:T(8,128)(2,1)S(1)} %pad_maximum_fusion.3.refs_3_), channel_id=1, source_target_pairs={{0,16},{2,18},{4,20},{6,22},{8,24},{10,26},{12,28},{14,30},{16,0},... | collective-permute-start | bytes 835592 | tf_op jit(solution)/shard_map/ppermute | solution.py:308
  26.0 6.4 %collective-permute-start.11 = (bf16[4,272,128]{2,1,0:T(8,128)(2,1)S(1)}, bf16[4,272,128]{2,1,0:T(8,128)(2,1)S(1)}, u32[]{:S(2)}, u32[]{:S(2)}) collective-permute-start(bf16[4,272,128]{2,1,0:T(8,128)(2,1)S(1)} %collective-permute-done.7.refs_6_), channel_id=1, source_target_pairs={{0,16},{2,18},{4,20},{6,22},{8,24},{10,26},{12,28},{14,30},{16,0},... | collective-permute-start | bytes 835592 | tf_op jit(solution)/shard_map/ppermute | solution.py:308
  28.4 4.0 %collective-permute-start.10 = (bf16[4,272,128]{2,1,0:T(8,128)(2,1)S(1)}, bf16[4,272,128]{2,1,0:T(8,128)(2,1)S(1)}, u32[]{:S(2)}, u32[]{:S(2)}) collective-permute-start(bf16[4,272,128]{2,1,0:T(8,128)(2,1)S(1)} %collective-permute-done.6.refs_5_), channel_id=1, source_target_pairs={{0,16},{2,18},{4,20},{6,22},{8,24},{10,26},{12,28},{14,30},{16,0},... | collective-permute-start | bytes 835592 | tf_op jit(solution)/shard_map/ppermute | solution.py:308
  29.4 4.1 %collective-permute-start.9 = (bf16[4,272,128]{2,1,0:T(8,128)(2,1)S(1)}, bf16[4,272,128]{2,1,0:T(8,128)(2,1)S(1)}, u32[]{:S(2)}, u32[]{:S(2)}) collective-permute-start(bf16[4,272,128]{2,1,0:T(8,128)(2,1)S(1)} %collective-permute-done.5.refs_4_), channel_id=1, source_target_pairs={{0,16},{2,18},{4,20},{6,22},{8,24},{10,26},{12,28},{14,30},{16,0},... | collective-permute-start | bytes 835592 | tf_op jit(solution)/shard_map/ppermute | solution.py:308
  36.1 4.0 %collective-permute-start.13 = (f32[2,8,512]{2,1,0:T(8,128)S(1)}, f32[2,8,512]{2,1,0:T(8,128)S(1)}, u32[]{:S(2)}, u32[]{:S(2)}) collective-permute-start(f32[2,8,512]{2,1,0:T(8,128)S(1)} %get-tuple-element.41.refs_1_), channel_id=1, source_target_pairs={{0,2},{2,0},{4,6},{6,4},{8,10},{10,8},{12,14},{14,12},{16,18},{18,... | collective-permute-start | bytes 98312 | tf_op jit(solution)/shard_map/ppermute | solution.py:308
  40.0 4.0 %collective-permute-start.14 = (f32[2,8,512]{2,1,0:T(8,128)S(1)}, f32[2,8,512]{2,1,0:T(8,128)S(1)}, u32[]{:S(2)}, u32[]{:S(2)}) collective-permute-start(f32[2,8,512]{2,1,0:T(8,128)S(1)} %get-tuple-element.44.refs_1_), channel_id=1, source_target_pairs={{0,2},{2,0},{4,6},{6,4},{8,10},{10,8},{12,14},{14,12},{16,18},{18,... | collective-permute-start | bytes 98312 | tf_op jit(solution)/shard_map/ppermute | solution.py:308
  44.0 5.8 %collective-permute-start.15 = (bf16[2,64,1024]{2,1,0:T(8,128)(2,1)S(1)}, bf16[2,64,1024]{2,1,0:T(8,128)(2,1)S(1)}, u32[]{:S(2)}, u32[]{:S(2)}) collective-permute-start(bf16[2,64,1024]{2,1,0:T(8,128)(2,1)S(1)} %get-tuple-element.55), channel_id=1, source_target_pairs={{0,2},{2,0},{4,6},{6,4},{8,10},{10,8},{12,14},{14,12},{16,18},{18,... | collective-permute-start | bytes 786440 | tf_op jit(solution)/shard_map/ppermute | solution.py:308
  49.8 10.7 %collective-permute-start.16 = (bf16[4,2,128,128]{3,2,1,0:T(8,128)(2,1)S(1)}, bf16[4,2,128,128]{3,2,1,0:T(8,128)(2,1)S(1)}, u32[]{:S(2)}, u32[]{:S(2)}) collective-permute-start(bf16[4,2,128,128]{3,2,1,0:T(8,128)(2,1)S(1)} %get-tuple-element.65), channel_id=1, source_target_pairs={{0,16},{2,18},{4,20},{6,22},{8,24},{10,26},{12,28},{14,30},{16,0},... | collective-permute-start | bytes 786440 | tf_op jit(solution)/shard_map/ppermute | solution.py:308
  59.4 1.5 %collective-permute-start.17 = (bf16[4,2,128,128]{3,2,1,0:T(8,128)(2,1)S(1)}, bf16[4,2,128,128]{3,2,1,0:T(8,128)(2,1)S(1)}, u32[]{:S(2)}, u32[]{:S(2)}) collective-permute-start(bf16[4,2,128,128]{3,2,1,0:T(8,128)(2,1)S(1)} %get-tuple-element.70), channel_id=1, source_target_pairs={{0,16},{2,18},{4,20},{6,22},{8,24},{10,26},{12,28},{14,30},{16,0},... | collective-permute-start | bytes 786440 | tf_op jit(solution)/shard_map/ppermute | solution.py:308
  59.5 3.8 %collective-permute-start.19 = (bf16[4,2,128,128]{3,2,1,0:T(8,128)(2,1)S(1)}, bf16[4,2,128,128]{3,2,1,0:T(8,128)(2,1)S(1)}, u32[]{:S(2)}, u32[]{:S(2)}) collective-permute-start(bf16[4,2,128,128]{3,2,1,0:T(8,128)(2,1)S(1)} %get-tuple-element.72), channel_id=1, source_target_pairs={{0,16},{2,18},{4,20},{6,22},{8,24},{10,26},{12,28},{14,30},{16,0},... | collective-permute-start | bytes 786440 | tf_op jit(solution)/shard_map/ppermute | solution.py:308
  59.9 3.5 %collective-permute-start.21 = (bf16[4,2,128,128]{3,2,1,0:T(8,128)(2,1)S(1)}, bf16[4,2,128,128]{3,2,1,0:T(8,128)(2,1)S(1)}, u32[]{:S(2)}, u32[]{:S(2)}) collective-permute-start(bf16[4,2,128,128]{3,2,1,0:T(8,128)(2,1)S(1)} %get-tuple-element.74), channel_id=1, source_target_pairs={{0,16},{2,18},{4,20},{6,22},{8,24},{10,26},{12,28},{14,30},{16,0},... | collective-permute-start | bytes 786440 | tf_op jit(solution)/shard_map/ppermute | solution.py:308
  61.0 7.1 %collective-permute-start.18 = (bf16[4,2,128,128]{3,2,1,0:T(8,128)(2,1)S(1)}, bf16[4,2,128,128]{3,2,1,0:T(8,128)(2,1)S(1)}, u32[]{:S(2)}, u32[]{:S(2)}) collective-permute-start(bf16[4,2,128,128]{3,2,1,0:T(8,128)(2,1)S(1)} %add_convert_fusion.3), channel_id=1, source_target_pairs={{0,8},{2,10},{4,12},{6,14},{8,0},{10,2},{12,4},{14,6},{16,80},{18,... | collective-permute-start | bytes 786440 | tf_op jit(solution)/shard_map/ppermute | solution.py:308
  63.4 7.6 %collective-permute-start.20 = (bf16[4,2,128,128]{3,2,1,0:T(8,128)(2,1)S(1)}, bf16[4,2,128,128]{3,2,1,0:T(8,128)(2,1)S(1)}, u32[]{:S(2)}, u32[]{:S(2)}) collective-permute-start(bf16[4,2,128,128]{3,2,1,0:T(8,128)(2,1)S(1)} %add_convert_fusion.2), channel_id=1, source_target_pairs={{0,4},{2,6},{4,8},{6,10},{8,12},{10,14},{12,0},{14,2},{16,48},{18,... | collective-permute-start | bytes 786440 | tf_op jit(solution)/shard_map/ppermute | solution.py:308
  63.5 8.8 %collective-permute-start.22 = (bf16[4,2,128,128]{3,2,1,0:T(8,128)(2,1)S(1)}, bf16[4,2,128,128]{3,2,1,0:T(8,128)(2,1)S(1)}, u32[]{:S(2)}, u32[]{:S(2)}) collective-permute-start(bf16[4,2,128,128]{3,2,1,0:T(8,128)(2,1)S(1)} %add_convert_fusion.1), channel_id=1, source_target_pairs={{0,12},{2,14},{4,0},{6,2},{8,4},{10,6},{12,8},{14,10},{16,112},{18... | collective-permute-start | bytes 786440 | tf_op jit(solution)/shard_map/ppermute | solution.py:308
  66.3 9.5 %collective-permute-start.26 = (bf16[64,1024]{1,0:T(8,128)(2,1)S(1)}, bf16[64,1024]{1,0:T(8,128)(2,1)S(1)}, u32[]{:S(2)}, u32[]{:S(2)}) collective-permute-start(bf16[64,1024]{1,0:T(8,128)(2,1)S(1)} %get-tuple-element.80), channel_id=1, source_target_pairs={{0,64},{2,66},{4,68},{6,70},{8,72},{10,74},{12,76},{14,78},{16,80}... | collective-permute-start | bytes 393224 | tf_op jit(solution)/shard_map/ppermute | solution.py:308
  72.5 3.5 %collective-permute-start.25 = (bf16[2,128,128]{2,1,0:T(8,128)(2,1)S(1)}, bf16[2,128,128]{2,1,0:T(8,128)(2,1)S(1)}, u32[]{:S(2)}, u32[]{:S(2)}) collective-permute-start(bf16[2,128,128]{2,1,0:T(8,128)(2,1)S(1)} %get-tuple-element.81), channel_id=1, source_target_pairs={{0,96},{2,98},{4,100},{6,102},{8,104},{10,106},{12,108},{14,110},{... | collective-permute-start | bytes 196616 | tf_op jit(solution)/shard_map/ppermute | solution.py:308
  74.0 4.6 %collective-permute-start.24 = (bf16[2,128,128]{2,1,0:T(8,128)(2,1)S(1)}, bf16[2,128,128]{2,1,0:T(8,128)(2,1)S(1)}, u32[]{:S(2)}, u32[]{:S(2)}) collective-permute-start(bf16[2,128,128]{2,1,0:T(8,128)(2,1)S(1)} %get-tuple-element.82), channel_id=1, source_target_pairs={{0,64},{2,66},{4,68},{6,70},{8,72},{10,74},{12,76},{14,78},{16,24}... | collective-permute-start | bytes 196616 | tf_op jit(solution)/shard_map/ppermute | solution.py:308
  75.1 4.6 %collective-permute-start.23 = (bf16[2,128,128]{2,1,0:T(8,128)(2,1)S(1)}, bf16[2,128,128]{2,1,0:T(8,128)(2,1)S(1)}, u32[]{:S(2)}, u32[]{:S(2)}) collective-permute-start(bf16[2,128,128]{2,1,0:T(8,128)(2,1)S(1)} %get-tuple-element.83), channel_id=1, source_target_pairs={{0,32},{2,34},{4,36},{6,38},{8,40},{10,42},{12,44},{14,46},{16,20}... | collective-permute-start | bytes 196616 | tf_op jit(solution)/shard_map/ppermute | solution.py:308
  79.7 1.7 %collective-permute-start.27 = (bf16[128,128]{1,0:T(8,128)(2,1)S(1)}, bf16[128,128]{1,0:T(8,128)(2,1)S(1)}, u32[]{:S(2)}, u32[]{:S(2)}) collective-permute-start(bf16[128,128]{1,0:T(8,128)(2,1)S(1)} %select_bitcast_fusion), channel_id=1, source_target_pairs={{0,16},{2,18},{4,20},{6,22},{8,24},{10,26},{12,28},{14,30},{16,0},... | collective-permute-start | bytes 98312 | tf_op jit(solution)/shard_map/ppermute | solution.py:308

commit v12 on v11

--- a/solution.py
+++ b/solution.py
@@ -11,7 +11,7 @@
 HEAD = 128
 BLOCK = 128
 DOC_ROWS = 16
-CHUNK_BLOCKS = 5
+CHUNK_BLOCKS = 4
 CHUNK = CHUNK_BLOCKS * BLOCK
 TILES = 2
 VMEM_MIB = 36
@@ -345,8 +345,11 @@
     unit = jnp.concatenate([rows_in_order, docs_in_order])
     line = jnp.stack([unit] + [along_first(unit, by) for by in range(1, lines)])
     far = other_y(shared)
-    mine = [line] + [along_second(line, by) for by in range(1, lines)]
-    theirs = [other_core(piece) for piece in mine]
+    mine, theirs = [line] + [None] * (lines - 1), [None] * lines
+    for by in (2, 1, 3):
+        mine[by] = along_second(line, by)
+    for by in (0, 1, 3, 2):
+        theirs[by] = other_core(mine[by])
 
     place = jnp.stack([z, x, y, core]).astype(jnp.int32)
     sizes = (nz, nx)
@@ -373,7 +376,7 @@
     dq = low(dq + rest.astype(jnp.float32))
     returned = peer(dq[1])
     total = low(added([totals[0]] + arrived))
-    short = [along_first(total[by], by) for by in range(1, lines)]
+    short = [along_first(total[by], by) for by in (2, 1, 3)]
     short, returned = lax.optimization_barrier((short, returned))
     total = added([total[0]] + short)
     total = low(jnp.where(core == 0, SCALE * total, total))

time: 82.3 us -> 82.6 us (level)
  Pallas kernels: 13.1 us -> 19.6 us
  waiting for transfers between devices: 15.1 us -> 11.7 us
  starting transfers between devices: 47.5 us -> 44.5 us
    pallas_call x4, Pallas kernels: 13.1 us -> 19.6 us  [kernel_call(): pl.pallas_call(lambda *refs: kernel(sizes, *refs), name=kernel.__name__,...]
    ppermute x28, waiting for transfers between devices: 15.1 us -> 11.7 us  [moved(): return lax.ppermute(value, CONTEXT, hops)]
    ppermute x28, starting transfers between devices: 47.5 us -> 44.5 us  [moved(): return lax.ppermute(value, CONTEXT, hops)]
  transfers between devices with their start and end apart: 28 -> 28, of which waited for: 12 -> 10; matrix products, arithmetic and copies ran while one was open for 4% -> 4% of each run, Pallas kernels for 16% -> 24%
where the time goes in v12:
time: 82.6 us; the launch traced here: 82.2 us
  starting transfers between devices  44.5 us (54%)
  Pallas kernels  19.6 us (24%)
  waiting for transfers between devices  11.7 us (14%)
  other arithmetic  3.72 us (5%)
  between operations  1.48 us (2%)
  local copies, waits for them, and re-layouts  1.18 us (1%)
    ppermute x28, starting transfers between devices, moved(): return lax.ppermute(value, CONTEXT, hops)  44.5 us
    pallas_call x4, Pallas kernels, kernel_call(): pl.pallas_call(lambda *refs: kernel(sizes, *refs), name=kernel.__name__,...  19.6 us
    ppermute x28, waiting for transfers between devices, moved(): return lax.ppermute(value, CONTEXT, hops)  11.7 us
  transfers between devices with their start and end apart: 28, of which 10 were waited for; matrix products, arithmetic and copies ran while one was open for 4% of the time, Pallas kernels for 24%

profile of v12, /device:TPU:1, one launch (start us, length us, event | category | flops | bytes accessed | tf_op | source)
XLA Modules:
  0.0 82.2 jit_solution(5277074414425351037)
XLA Ops:
  1.3 0.8 select_bitcast_fusion.1
  2.1 1.5 %collective-permute-start.1 = (bf16[144,128]{1,0:T(8,128)(2,1)S(1)}, bf16[144,128]{1,0:T(8,128)(2,1)S(1)}, u32[]{:S(2)}, u32[]{:S(2)}) collective-permute-start(bf16[144,128]{1,0:T(8,128)(2,1)S(1)} %concatenate.17), channel_id=1, source_target_pairs={{0,16},{2,18},{4,20},{6,22},{8,24},{10,26},{12,28},{14,30},{16,0},... | collective-permute-start | bytes 110600 | tf_op jit(solution)/shard_map/ppermute | solution.py:308
  3.6 1.1 %constant_dynamic-slice_fusion.2 = (bf16[64,1024]{1,0:T(8,128)(2,1)S(1)}, bf16[64,1024]{1,0:T(8,128)(2,1)S(1)}, bf16[64,1024]{1,0:T(8,128)(2,1)S(1)}, bf16[64,1024]{1,0:T(8,128)(2,1)S(1)}) fusion(bf16[128,1024]{1,0:T(8,128)(2,1)} %param.8, s32[]{:T(128)S(6)} %select_n.83, s32[]{:T(128)S(6)} %select_n.84, bf16[128,1024]{1,0:T(8,128)(2,1)} %param.5), kind=kLoop, calls=%fused_computation.34 | loop fusion | bytes 1048584 | tf_op jit(solution)/shard_map/dynamic_slice | solution.py:334
  4.8 3.8 %collective-permute-start = (bf16[64,2176]{1,0:T(8,128)(2,1)S(1)}, bf16[64,2176]{1,0:T(8,128)(2,1)S(1)}, u32[]{:S(2)}, u32[]{:S(2)}) collective-permute-start(bf16[64,2176]{1,0:T(8,128)(2,1)S(1)} %get-tuple-element.95), channel_id=1, source_target_pairs={{0,64},{2,66},{4,68},{6,70},{8,72},{10,74},{12,76},{14,78},{16,80}... | collective-permute-start | bytes 835592 | tf_op jit(solution)/shard_map/ppermute | solution.py:308
  8.6 2.8 %collective-permute-start.3 = (bf16[272,128]{1,0:T(8,128)(2,1)S(1)}, bf16[272,128]{1,0:T(8,128)(2,1)S(1)}, u32[]{:S(2)}, u32[]{:S(2)}) collective-permute-start(bf16[272,128]{1,0:T(8,128)(2,1)S(1)} %get-tuple-element.91), channel_id=1, source_target_pairs={{0,64},{2,66},{4,68},{6,70},{8,72},{10,74},{12,76},{14,78},{16,24}... | collective-permute-start | bytes 208904 | tf_op jit(solution)/shard_map/ppermute | solution.py:308
  11.4 0.3 collective-permute-start.2
  11.7 2.4 %collective-permute-start.4 = (bf16[272,128]{1,0:T(8,128)(2,1)S(1)}, bf16[272,128]{1,0:T(8,128)(2,1)S(1)}, u32[]{:S(2)}, u32[]{:S(2)}) collective-permute-start(bf16[272,128]{1,0:T(8,128)(2,1)S(1)} %get-tuple-element.91), channel_id=1, source_target_pairs={{0,96},{2,98},{4,100},{6,102},{8,104},{10,106},{12,108},{14,110},{... | collective-permute-start | bytes 208904 | tf_op jit(solution)/shard_map/ppermute | solution.py:308
  14.1 2.0 %collective-permute-done.2 = bf16[272,128]{1,0:T(8,128)(2,1)S(1)} collective-permute-done((bf16[272,128]{1,0:T(8,128)(2,1)S(1)}, bf16[272,128]{1,0:T(8,128)(2,1)S(1)}, u32[]{:S(2)}, u32[]{:S(2)}) %collective-permute-start.2) | collective-permute-done | bytes 69664 | tf_op jit(solution)/shard_map/ppermute | solution.py:308
  16.1 0.5 collective-permute-start.7
  16.6 1.9 %collective-permute-start.6 = (bf16[4,272,128]{2,1,0:T(8,128)(2,1)S(1)}, bf16[4,272,128]{2,1,0:T(8,128)(2,1)S(1)}, u32[]{:S(2)}, u32[]{:S(2)}) collective-permute-start(bf16[4,272,128]{2,1,0:T(8,128)(2,1)S(1)} %pad_maximum_fusion.3.refs_3_), channel_id=1, source_target_pairs={{0,8},{2,10},{4,12},{6,14},{8,0},{10,2},{12,4},{14,6},{16,80},{18,... | collective-permute-start | bytes 835592 | tf_op jit(solution)/shard_map/ppermute | solution.py:308
  18.6 0.8 %pad_maximum_fusion = bf16[128,2176]{1,0:T(8,128)(2,1)} fusion(bf16[64,2176]{1,0:T(8,128)(2,1)S(1)} %collective-permute-done.refs_2_, bf16[64,128]{1,0:T(8,128)(2,1)S(1)} %broadcast_in_dim.5, bf16[64,1024]{1,0:T(8,128)(2,1)S(1)} %get-tuple-element.86, bf16[64,1024]{1,0:T(8,128)(2,1)S(1)} %get-tuple-element.97), kind=kLoop, calls=%fused_computation | loop fusion | flops 2228224 | bytes 1114112 | tf_op jit(solution)/shard_map/concatenate | solution.py:339
  19.4 1.3 %collective-permute-start.12 = (bf16[128,2176]{1,0:T(8,128)(2,1)}, bf16[128,2176]{1,0:T(8,128)(2,1)S(1)}, u32[]{:S(2)}, u32[]{:S(2)}) collective-permute-start(bf16[128,2176]{1,0:T(8,128)(2,1)} %pad_maximum_fusion), channel_id=1, source_target_pairs={{0,2},{2,0},{4,6},{6,4},{8,10},{10,8},{12,14},{14,12},{16,18},{18,... | collective-permute-start | bytes 1671176 | tf_op jit(solution)/shard_map/ppermute | solution.py:308
  20.7 5.3 %collective-permute-start.8 = (bf16[4,272,128]{2,1,0:T(8,128)(2,1)S(1)}, bf16[4,272,128]{2,1,0:T(8,128)(2,1)S(1)}, u32[]{:S(2)}, u32[]{:S(2)}) collective-permute-start(bf16[4,272,128]{2,1,0:T(8,128)(2,1)S(1)} %pad_maximum_fusion.3.refs_3_), channel_id=1, source_target_pairs={{0,16},{2,18},{4,20},{6,22},{8,24},{10,26},{12,28},{14,30},{16,0},... | collective-permute-start | bytes 835592 | tf_op jit(solution)/shard_map/ppermute | solution.py:308
  26.0 2.4 %collective-permute-start.11 = (bf16[4,272,128]{2,1,0:T(8,128)(2,1)S(1)}, bf16[4,272,128]{2,1,0:T(8,128)(2,1)S(1)}, u32[]{:S(2)}, u32[]{:S(2)}) collective-permute-start(bf16[4,272,128]{2,1,0:T(8,128)(2,1)S(1)} %collective-permute-done.7.refs_6_), channel_id=1, source_target_pairs={{0,16},{2,18},{4,20},{6,22},{8,24},{10,26},{12,28},{14,30},{16,0},... | collective-permute-start | bytes 835592 | tf_op jit(solution)/shard_map/ppermute | solution.py:308
  28.4 1.1 %collective-permute-start.10 = (bf16[4,272,128]{2,1,0:T(8,128)(2,1)S(1)}, bf16[4,272,128]{2,1,0:T(8,128)(2,1)S(1)}, u32[]{:S(2)}, u32[]{:S(2)}) collective-permute-start(bf16[4,272,128]{2,1,0:T(8,128)(2,1)S(1)} %collective-permute-done.6.refs_5_), channel_id=1, source_target_pairs={{0,16},{2,18},{4,20},{6,22},{8,24},{10,26},{12,28},{14,30},{16,0},... | collective-permute-start | bytes 835592 | tf_op jit(solution)/shard_map/ppermute | solution.py:308
  29.4 2.9 %collective-permute-start.9 = (bf16[4,272,128]{2,1,0:T(8,128)(2,1)S(1)}, bf16[4,272,128]{2,1,0:T(8,128)(2,1)S(1)}, u32[]{:S(2)}, u32[]{:S(2)}) collective-permute-start(bf16[4,272,128]{2,1,0:T(8,128)(2,1)S(1)} %collective-permute-done.5.refs_4_), channel_id=1, source_target_pairs={{0,16},{2,18},{4,20},{6,22},{8,24},{10,26},{12,28},{14,30},{16,0},... | collective-permute-start | bytes 835592 | tf_op jit(solution)/shard_map/ppermute | solution.py:308
  32.3 0.1 pad_add_fusion.refs_0_
  32.4 1.1 %collective-permute-done.9.refs_8_ = bf16[4,272,128]{2,1,0:T(8,128)(2,1)S(1)} collective-permute-done((bf16[4,272,128]{2,1,0:T(8,128)(2,1)S(1)}, bf16[4,272,128]{2,1,0:T(8,128)(2,1)S(1)}, u32[]{:S(2)}, u32[]{:S(2)}) %collective-permute-start.9) | collective-permute-done | bytes 278560 | tf_op jit(solution)/shard_map/ppermute | solution.py:308
  33.5 3.9 %near_statistics.1 = (f32[2,8,512]{2,1,0:T(8,128)S(1)}, f32[2,16,128]{2,1,0:T(8,128)S(1)}, bf16[2,2,128,512]{3,2,1,0:T(8,128)(2,1)S(1)}, bf16[2,2,512,128]{3,2,1...) custom-call(s32[4]{0:T(128)S(1)} %pad_add_fusion.refs_0_, ...), custom_call_target="tpu_custom_call" | custom-call | flops 805306368 | bytes 8388608 | tf_op jit(solution)/shard_map/near_statistics/pallas_call | solution.py:225
  37.4 1.4 %collective-permute-start.13 = (f32[2,8,512]{2,1,0:T(8,128)S(1)}, f32[2,8,512]{2,1,0:T(8,128)S(1)}, u32[]{:S(2)}, u32[]{:S(2)}) collective-permute-start(f32[2,8,512]{2,1,0:T(8,128)S(1)} %get-tuple-element.41.refs_1_), channel_id=1, source_target_pairs={{0,2},{2,0},{4,6},{6,4},{8,10},{10,8},{12,14},{14,12},{16,18},{18,... | collective-permute-start | bytes 98312 | tf_op jit(solution)/shard_map/ppermute | solution.py:308
  38.8 3.8 %far_statistics.1 = (f32[2,8,512]{2,1,0:T(8,128)S(1)}, f32[2,16,128]{2,1,0:T(8,128)S(1)}, bf16[2,2,128,512]{3,2,1,0:T(8,128)(2,1)S(1)}, bf16[2,2,512,128]{3,2,1,0:T(8,128)(2,1)S(1)}) custom-call(s32[4]{0:T(128)S(1)} %pad_add_fusion.refs_0_, bf16[128,2176]{1,0:T(8,128)(2,1)S(1)} %collective-permute-done.12.refs_1_, ...), custom_call_target="tpu_custom_call" | custom-call | flops 805306368 | bytes 8388608 | tf_op jit(solution)/shard_map/far_statistics/pallas_call | solution.py:225
  42.6 0.1 collective-permute-start.14
  42.7 5.8 %far_gradients.1 = (bf16[2,64,1024]{2,1,0:T(8,128)(2,1)S(1)}, f32[2,4096,128]{2,1,0:T(8,128)S(1)}) custom-call(s32[4]{0:T(128)S(1)} %pad_add_fusion.refs_0_, f32[2,8,512]{2,1,0:T(8,128)S(1)} %get-tuple-element.44.refs_1_, f32[2,8,512]{2,1,0:T(8,128)S(1)} %collective-permute-done.13.refs_2_, f32[2,16,128]{2,1,0:T(8,128)S(1)} %get-tuple-element.45.refs_3_, ...), custom_call_target="tpu_custom_call" | custom-call | flops 2013265920 | bytes 8388608 | tf_op jit(solution)/shard_map/far_gradients/pallas_call | solution.py:225
  48.6 0.9 %collective-permute-start.15 = (bf16[2,64,1024]{2,1,0:T(8,128)(2,1)S(1)}, bf16[2,64,1024]{2,1,0:T(8,128)(2,1)S(1)}, u32[]{:S(2)}, u32[]{:S(2)}) collective-permute-start(bf16[2,64,1024]{2,1,0:T(8,128)(2,1)S(1)} %get-tuple-element.55), channel_id=1, source_target_pairs={{0,2},{2,0},{4,6},{6,4},{8,10},{10,8},{12,14},{14,12},{16,18},{18,... | collective-permute-start | bytes 786440 | tf_op jit(solution)/shard_map/ppermute | solution.py:308
  49.5 6.1 %near_gradients.1 = (f32[2,64,1024]{2,1,0:T(8,128)S(1)}, bf16[4,2,128,128]{3,2,1,0:T(8,128)(2,1)S(1)}, bf16[4,2,128,128]{3,2,1,0:T(8,128)(2,1)S(1)}, bf16[4,2,12...) custom-call(s32[4]{0:T(128)S(1)} %pad_add_fusion.refs_0_, ...), custom_call_target="tpu_custom_call" | custom-call | flops 2013265920 | bytes 8388608 | tf_op jit(solution)/shard_map/near_gradients/pallas_call | solution.py:225
  55.6 0.6 collective-permute-done.15
  56.2 0.5 collective-permute-start.17
  56.7 0.5 collective-permute-start.21
  57.2 0.5 collective-permute-done.16
  57.7 0.1 add_convert_fusion.5
  57.8 0.3 collective-permute-done.17
  58.1 0.1 add_convert_fusion.3
  58.2 2.3 %collective-permute-start.18 = (bf16[4,2,128,128]{3,2,1,0:T(8,128)(2,1)S(1)}, bf16[4,2,128,128]{3,2,1,0:T(8,128)(2,1)S(1)}, u32[]{:S(2)}, u32[]{:S(2)}) collective-permute-start(bf16[4,2,128,128]{3,2,1,0:T(8,128)(2,1)S(1)} %add_convert_fusion.3), channel_id=1, source_target_pairs={{0,8},{2,10},{4,12},{6,14},{8,0},{10,2},{12,4},{14,6},{16,80},{18,... | collective-permute-start | bytes 786440 | tf_op jit(solution)/shard_map/ppermute | solution.py:308
  60.4 0.1 add_convert_fusion.2
  60.5 2.7 %collective-permute-start.20 = (bf16[4,2,128,128]{3,2,1,0:T(8,128)(2,1)S(1)}, bf16[4,2,128,128]{3,2,1,0:T(8,128)(2,1)S(1)}, u32[]{:S(2)}, u32[]{:S(2)}) collective-permute-start(bf16[4,2,128,128]{3,2,1,0:T(8,128)(2,1)S(1)} %add_convert_fusion.2), channel_id=1, source_target_pairs={{0,4},{2,6},{4,8},{6,10},{8,12},{10,14},{12,0},{14,2},{16,48},{18,... | collective-permute-start | bytes 786440 | tf_op jit(solution)/shard_map/ppermute | solution.py:308
  63.3 0.3 collective-permute-start.22
  63.7 1.7 %collective-permute-start.26 = (bf16[64,1024]{1,0:T(8,128)(2,1)S(1)}, bf16[64,1024]{1,0:T(8,128)(2,1)S(1)}, u32[]{:S(2)}, u32[]{:S(2)}) collective-permute-start(bf16[64,1024]{1,0:T(8,128)(2,1)S(1)} %get-tuple-element.80), channel_id=1, source_target_pairs={{0,64},{2,66},{4,68},{6,70},{8,72},{10,74},{12,76},{14,78},{16,80}... | collective-permute-start | bytes 393224 | tf_op jit(solution)/shard_map/ppermute | solution.py:308
  65.4 2.7 %collective-permute-done.20 = bf16[4,2,128,128]{3,2,1,0:T(8,128)(2,1)S(1)} collective-permute-done((bf16[4,2,128,128]{3,2,1,0:T(8,128)(2,1)S(1)}, bf16[4,2,128,128]{3,2,1,0:T(8,128)(2,1)S(1)}, u32[]{:S(2)}, u32[]{:S(2)}) %collective-permute-start.20) | collective-permute-done | bytes 262176 | tf_op jit(solution)/shard_map/ppermute | solution.py:308
  68.1 1.9 %collective-permute-done.22 = bf16[4,2,128,128]{3,2,1,0:T(8,128)(2,1)S(1)} collective-permute-done((bf16[4,2,128,128]{3,2,1,0:T(8,128)(2,1)S(1)}, bf16[4,2,128,128]{3,2,1,0:T(8,128)(2,1)S(1)}, u32[]{:S(2)}, u32[]{:S(2)}) %collective-permute-start.22) | collective-permute-done | bytes 262176 | tf_op jit(solution)/shard_map/ppermute | solution.py:308
  70.0 0.1 add_convert_fusion
  70.2 2.1 %collective-permute-start.25 = (bf16[2,128,128]{2,1,0:T(8,128)(2,1)S(1)}, bf16[2,128,128]{2,1,0:T(8,128)(2,1)S(1)}, u32[]{:S(2)}, u32[]{:S(2)}) collective-permute-start(bf16[2,128,128]{2,1,0:T(8,128)(2,1)S(1)} %get-tuple-element.81), channel_id=1, source_target_pairs={{0,96},{2,98},{4,100},{6,102},{8,104},{10,106},{12,108},{14,110},{... | collective-permute-start | bytes 196616 | tf_op jit(solution)/shard_map/ppermute | solution.py:308
  72.3 3.5 %collective-permute-start.23 = (bf16[2,128,128]{2,1,0:T(8,128)(2,1)S(1)}, bf16[2,128,128]{2,1,0:T(8,128)(2,1)S(1)}, u32[]{:S(2)}, u32[]{:S(2)}) collective-permute-start(bf16[2,128,128]{2,1,0:T(8,128)(2,1)S(1)} %get-tuple-element.83), channel_id=1, source_target_pairs={{0,64},{2,66},{4,68},{6,70},{8,72},{10,74},{12,76},{14,78},{16,24}... | collective-permute-start | bytes 196616 | tf_op jit(solution)/shard_map/ppermute | solution.py:308
  75.8 0.8 collective-permute-done.24
  76.6 1.6 %collective-permute-done.23 = bf16[2,128,128]{2,1,0:T(8,128)(2,1)S(1)} collective-permute-done((bf16[2,128,128]{2,1,0:T(8,128)(2,1)S(1)}, bf16[2,128,128]{2,1,0:T(8,128)(2,1)S(1)}, u32[]{:S(2)}, u32[]{:S(2)}) %collective-permute-start.23) | collective-permute-done | bytes 65568 | tf_op jit(solution)/shard_map/ppermute | solution.py:308
  78.2 2.5 %collective-permute-start.27 = (bf16[128,128]{1,0:T(8,128)(2,1)S(1)}, bf16[128,128]{1,0:T(8,128)(2,1)S(1)}, u32[]{:S(2)}, u32[]{:S(2)}) collective-permute-start(bf16[128,128]{1,0:T(8,128)(2,1)S(1)} %select_bitcast_fusion), channel_id=1, source_target_pairs={{0,16},{2,18},{4,20},{6,22},{8,24},{10,26},{12,28},{14,30},{16,0},... | collective-permute-start | bytes 98312 | tf_op jit(solution)/shard_map/ppermute | solution.py:308
  80.7 0.7 maximum_select_fusion
  81.4 0.1 collective-permute-done.27
  81.6 0.6 bitcast_select_fusion
  (37 shorter events, 0.5 us)
Async XLA Ops:
  2.1 6.5 %collective-permute-start.1 = (bf16[144,128]{1,0:T(8,128)(2,1)S(1)}, bf16[144,128]{1,0:T(8,128)(2,1)S(1)}, u32[]{:S(2)}, u32[]{:S(2)}) collective-permute-start(bf16[144,128]{1,0:T(8,128)(2,1)S(1)} %concatenate.17), channel_id=1, source_target_pairs={{0,16},{2,18},{4,20},{6,22},{8,24},{10,26},{12,28},{14,30},{16,0},... | collective-permute-start | bytes 110600 | tf_op jit(solution)/shard_map/ppermute | solution.py:308
  4.8 13.8 %collective-permute-start = (bf16[64,2176]{1,0:T(8,128)(2,1)S(1)}, bf16[64,2176]{1,0:T(8,128)(2,1)S(1)}, u32[]{:S(2)}, u32[]{:S(2)}) collective-permute-start(bf16[64,2176]{1,0:T(8,128)(2,1)S(1)} %get-tuple-element.95), channel_id=1, source_target_pairs={{0,64},{2,66},{4,68},{6,70},{8,72},{10,74},{12,76},{14,78},{16,80}... | collective-permute-start | bytes 835592 | tf_op jit(solution)/shard_map/ppermute | solution.py:308
  8.6 5.5 %collective-permute-start.3 = (bf16[272,128]{1,0:T(8,128)(2,1)S(1)}, bf16[272,128]{1,0:T(8,128)(2,1)S(1)}, u32[]{:S(2)}, u32[]{:S(2)}) collective-permute-start(bf16[272,128]{1,0:T(8,128)(2,1)S(1)} %get-tuple-element.91), channel_id=1, source_target_pairs={{0,64},{2,66},{4,68},{6,70},{8,72},{10,74},{12,76},{14,78},{16,24}... | collective-permute-start | bytes 208904 | tf_op jit(solution)/shard_map/ppermute | solution.py:308
  11.4 4.7 %collective-permute-start.2 = (bf16[272,128]{1,0:T(8,128)(2,1)S(1)}, bf16[272,128]{1,0:T(8,128)(2,1)S(1)}, u32[]{:S(2)}, u32[]{:S(2)}) collective-permute-start(bf16[272,128]{1,0:T(8,128)(2,1)S(1)} %get-tuple-element.91), channel_id=1, source_target_pairs={{0,32},{2,34},{4,36},{6,38},{8,40},{10,42},{12,44},{14,46},{16,20}... | collective-permute-start | bytes 208904 | tf_op jit(solution)/shard_map/ppermute | solution.py:308
  11.7 4.4 %collective-permute-start.4 = (bf16[272,128]{1,0:T(8,128)(2,1)S(1)}, bf16[272,128]{1,0:T(8,128)(2,1)S(1)}, u32[]{:S(2)}, u32[]{:S(2)}) collective-permute-start(bf16[272,128]{1,0:T(8,128)(2,1)S(1)} %get-tuple-element.91), channel_id=1, source_target_pairs={{0,96},{2,98},{4,100},{6,102},{8,104},{10,106},{12,108},{14,110},{... | collective-permute-start | bytes 208904 | tf_op jit(solution)/shard_map/ppermute | solution.py:308
  16.1 9.9 %collective-permute-start.7 = (bf16[4,272,128]{2,1,0:T(8,128)(2,1)S(1)}, bf16[4,272,128]{2,1,0:T(8,128)(2,1)S(1)}, u32[]{:S(2)}, u32[]{:S(2)}) collective-permute-start(bf16[4,272,128]{2,1,0:T(8,128)(2,1)S(1)} %pad_maximum_fusion.3.refs_3_), channel_id=1, source_target_pairs={{0,12},{2,14},{4,0},{6,2},{8,4},{10,6},{12,8},{14,10},{16,112},{18... | collective-permute-start | bytes 835592 | tf_op jit(solution)/shard_map/ppermute | solution.py:308
  16.6 11.7 %collective-permute-start.6 = (bf16[4,272,128]{2,1,0:T(8,128)(2,1)S(1)}, bf16[4,272,128]{2,1,0:T(8,128)(2,1)S(1)}, u32[]{:S(2)}, u32[]{:S(2)}) collective-permute-start(bf16[4,272,128]{2,1,0:T(8,128)(2,1)S(1)} %pad_maximum_fusion.3.refs_3_), channel_id=1, source_target_pairs={{0,8},{2,10},{4,12},{6,14},{8,0},{10,2},{12,4},{14,6},{16,80},{18,... | collective-permute-start | bytes 835592 | tf_op jit(solution)/shard_map/ppermute | solution.py:308
  18.6 10.9 %collective-permute-start.5 = (bf16[4,272,128]{2,1,0:T(8,128)(2,1)S(1)}, bf16[4,272,128]{2,1,0:T(8,128)(2,1)S(1)}, u32[]{:S(2)}, u32[]{:S(2)}) collective-permute-start(bf16[4,272,128]{2,1,0:T(8,128)(2,1)S(1)} %pad_maximum_fusion.3.refs_3_), channel_id=1, source_target_pairs={{0,4},{2,6},{4,8},{6,10},{8,12},{10,14},{12,0},{14,2},{16,48},{18,... | collective-permute-start | bytes 835592 | tf_op jit(solution)/shard_map/ppermute | solution.py:308
  19.4 19.4 %collective-permute-start.12 = (bf16[128,2176]{1,0:T(8,128)(2,1)}, bf16[128,2176]{1,0:T(8,128)(2,1)S(1)}, u32[]{:S(2)}, u32[]{:S(2)}) collective-permute-start(bf16[128,2176]{1,0:T(8,128)(2,1)} %pad_maximum_fusion), channel_id=1, source_target_pairs={{0,2},{2,0},{4,6},{6,4},{8,10},{10,8},{12,14},{14,12},{16,18},{18,... | collective-permute-start | bytes 1671176 | tf_op jit(solution)/shard_map/ppermute | solution.py:308
  20.7 11.7 %collective-permute-start.8 = (bf16[4,272,128]{2,1,0:T(8,128)(2,1)S(1)}, bf16[4,272,128]{2,1,0:T(8,128)(2,1)S(1)}, u32[]{:S(2)}, u32[]{:S(2)}) collective-permute-start(bf16[4,272,128]{2,1,0:T(8,128)(2,1)S(1)} %pad_maximum_fusion.3.refs_3_), channel_id=1, source_target_pairs={{0,16},{2,18},{4,20},{6,22},{8,24},{10,26},{12,28},{14,30},{16,0},... | collective-permute-start | bytes 835592 | tf_op jit(solution)/shard_map/ppermute | solution.py:308
  26.0 6.4 %collective-permute-start.11 = (bf16[4,272,128]{2,1,0:T(8,128)(2,1)S(1)}, bf16[4,272,128]{2,1,0:T(8,128)(2,1)S(1)}, u32[]{:S(2)}, u32[]{:S(2)}) collective-permute-start(bf16[4,272,128]{2,1,0:T(8,128)(2,1)S(1)} %collective-permute-done.7.refs_6_), channel_id=1, source_target_pairs={{0,16},{2,18},{4,20},{6,22},{8,24},{10,26},{12,28},{14,30},{16,0},... | collective-permute-start | bytes 835592 | tf_op jit(solution)/shard_map/ppermute | solution.py:308
  28.4 4.0 %collective-permute-start.10 = (bf16[4,272,128]{2,1,0:T(8,128)(2,1)S(1)}, bf16[4,272,128]{2,1,0:T(8,128)(2,1)S(1)}, u32[]{:S(2)}, u32[]{:S(2)}) collective-permute-start(bf16[4,272,128]{2,1,0:T(8,128)(2,1)S(1)} %collective-permute-done.6.refs_5_), channel_id=1, source_target_pairs={{0,16},{2,18},{4,20},{6,22},{8,24},{10,26},{12,28},{14,30},{16,0},... | collective-permute-start | bytes 835592 | tf_op jit(solution)/shard_map/ppermute | solution.py:308
  29.4 4.1 %collective-permute-start.9 = (bf16[4,272,128]{2,1,0:T(8,128)(2,1)S(1)}, bf16[4,272,128]{2,1,0:T(8,128)(2,1)S(1)}, u32[]{:S(2)}, u32[]{:S(2)}) collective-permute-start(bf16[4,272,128]{2,1,0:T(8,128)(2,1)S(1)} %collective-permute-done.5.refs_4_), channel_id=1, source_target_pairs={{0,16},{2,18},{4,20},{6,22},{8,24},{10,26},{12,28},{14,30},{16,0},... | collective-permute-start | bytes 835592 | tf_op jit(solution)/shard_map/ppermute | solution.py:308
  37.4 5.3 %collective-permute-start.13 = (f32[2,8,512]{2,1,0:T(8,128)S(1)}, f32[2,8,512]{2,1,0:T(8,128)S(1)}, u32[]{:S(2)}, u32[]{:S(2)}) collective-permute-start(f32[2,8,512]{2,1,0:T(8,128)S(1)} %get-tuple-element.41.refs_1_), channel_id=1, source_target_pairs={{0,2},{2,0},{4,6},{6,4},{8,10},{10,8},{12,14},{14,12},{16,18},{18,... | collective-permute-start | bytes 98312 | tf_op jit(solution)/shard_map/ppermute | solution.py:308
  42.6 6.0 %collective-permute-start.14 = (f32[2,8,512]{2,1,0:T(8,128)S(1)}, f32[2,8,512]{2,1,0:T(8,128)S(1)}, u32[]{:S(2)}, u32[]{:S(2)}) collective-permute-start(f32[2,8,512]{2,1,0:T(8,128)S(1)} %get-tuple-element.44.refs_1_), channel_id=1, source_target_pairs={{0,2},{2,0},{4,6},{6,4},{8,10},{10,8},{12,14},{14,12},{16,18},{18,... | collective-permute-start | bytes 98312 | tf_op jit(solution)/shard_map/ppermute | solution.py:308
  48.6 7.6 %collective-permute-start.15 = (bf16[2,64,1024]{2,1,0:T(8,128)(2,1)S(1)}, bf16[2,64,1024]{2,1,0:T(8,128)(2,1)S(1)}, u32[]{:S(2)}, u32[]{:S(2)}) collective-permute-start(bf16[2,64,1024]{2,1,0:T(8,128)(2,1)S(1)} %get-tuple-element.55), channel_id=1, source_target_pairs={{0,2},{2,0},{4,6},{6,4},{8,10},{10,8},{12,14},{14,12},{16,18},{18,... | collective-permute-start | bytes 786440 | tf_op jit(solution)/shard_map/ppermute | solution.py:308
  56.2 1.5 %collective-permute-start.16 = (bf16[4,2,128,128]{3,2,1,0:T(8,128)(2,1)S(1)}, bf16[4,2,128,128]{3,2,1,0:T(8,128)(2,1)S(1)}, u32[]{:S(2)}, u32[]{:S(2)}) collective-permute-start(bf16[4,2,128,128]{3,2,1,0:T(8,128)(2,1)S(1)} %get-tuple-element.65), channel_id=1, source_target_pairs={{0,16},{2,18},{4,20},{6,22},{8,24},{10,26},{12,28},{14,30},{16,0},... | collective-permute-start | bytes 786440 | tf_op jit(solution)/shard_map/ppermute | solution.py:308
  56.2 1.9 %collective-permute-start.17 = (bf16[4,2,128,128]{3,2,1,0:T(8,128)(2,1)S(1)}, bf16[4,2,128,128]{3,2,1,0:T(8,128)(2,1)S(1)}, u32[]{:S(2)}, u32[]{:S(2)}) collective-permute-start(bf16[4,2,128,128]{3,2,1,0:T(8,128)(2,1)S(1)} %get-tuple-element.70), channel_id=1, source_target_pairs={{0,16},{2,18},{4,20},{6,22},{8,24},{10,26},{12,28},{14,30},{16,0},... | collective-permute-start | bytes 786440 | tf_op jit(solution)/shard_map/ppermute | solution.py:308
  56.7 3.8 %collective-permute-start.19 = (bf16[4,2,128,128]{3,2,1,0:T(8,128)(2,1)S(1)}, bf16[4,2,128,128]{3,2,1,0:T(8,128)(2,1)S(1)}, u32[]{:S(2)}, u32[]{:S(2)}) collective-permute-start(bf16[4,2,128,128]{3,2,1,0:T(8,128)(2,1)S(1)} %get-tuple-element.72), channel_id=1, source_target_pairs={{0,16},{2,18},{4,20},{6,22},{8,24},{10,26},{12,28},{14,30},{16,0},... | collective-permute-start | bytes 786440 | tf_op jit(solution)/shard_map/ppermute | solution.py:308
  56.7 6.6 %collective-permute-start.21 = (bf16[4,2,128,128]{3,2,1,0:T(8,128)(2,1)S(1)}, bf16[4,2,128,128]{3,2,1,0:T(8,128)(2,1)S(1)}, u32[]{:S(2)}, u32[]{:S(2)}) collective-permute-start(bf16[4,2,128,128]{3,2,1,0:T(8,128)(2,1)S(1)} %get-tuple-element.74), channel_id=1, source_target_pairs={{0,16},{2,18},{4,20},{6,22},{8,24},{10,26},{12,28},{14,30},{16,0},... | collective-permute-start | bytes 786440 | tf_op jit(solution)/shard_map/ppermute | solution.py:308
  58.2 7.2 %collective-permute-start.18 = (bf16[4,2,128,128]{3,2,1,0:T(8,128)(2,1)S(1)}, bf16[4,2,128,128]{3,2,1,0:T(8,128)(2,1)S(1)}, u32[]{:S(2)}, u32[]{:S(2)}) collective-permute-start(bf16[4,2,128,128]{3,2,1,0:T(8,128)(2,1)S(1)} %add_convert_fusion.3), channel_id=1, source_target_pairs={{0,8},{2,10},{4,12},{6,14},{8,0},{10,2},{12,4},{14,6},{16,80},{18,... | collective-permute-start | bytes 786440 | tf_op jit(solution)/shard_map/ppermute | solution.py:308
  60.5 7.6 %collective-permute-start.20 = (bf16[4,2,128,128]{3,2,1,0:T(8,128)(2,1)S(1)}, bf16[4,2,128,128]{3,2,1,0:T(8,128)(2,1)S(1)}, u32[]{:S(2)}, u32[]{:S(2)}) collective-permute-start(bf16[4,2,128,128]{3,2,1,0:T(8,128)(2,1)S(1)} %add_convert_fusion.2), channel_id=1, source_target_pairs={{0,4},{2,6},{4,8},{6,10},{8,12},{10,14},{12,0},{14,2},{16,48},{18,... | collective-permute-start | bytes 786440 | tf_op jit(solution)/shard_map/ppermute | solution.py:308
  63.3 6.7 %collective-permute-start.22 = (bf16[4,2,128,128]{3,2,1,0:T(8,128)(2,1)S(1)}, bf16[4,2,128,128]{3,2,1,0:T(8,128)(2,1)S(1)}, u32[]{:S(2)}, u32[]{:S(2)}) collective-permute-start(bf16[4,2,128,128]{3,2,1,0:T(8,128)(2,1)S(1)} %add_convert_fusion.1), channel_id=1, source_target_pairs={{0,12},{2,14},{4,0},{6,2},{8,4},{10,6},{12,8},{14,10},{16,112},{18... | collective-permute-start | bytes 786440 | tf_op jit(solution)/shard_map/ppermute | solution.py:308
  63.7 12.0 %collective-permute-start.26 = (bf16[64,1024]{1,0:T(8,128)(2,1)S(1)}, bf16[64,1024]{1,0:T(8,128)(2,1)S(1)}, u32[]{:S(2)}, u32[]{:S(2)}) collective-permute-start(bf16[64,1024]{1,0:T(8,128)(2,1)S(1)} %get-tuple-element.80), channel_id=1, source_target_pairs={{0,64},{2,66},{4,68},{6,70},{8,72},{10,74},{12,76},{14,78},{16,80}... | collective-permute-start | bytes 393224 | tf_op jit(solution)/shard_map/ppermute | solution.py:308
  70.2 5.6 %collective-permute-start.25 = (bf16[2,128,128]{2,1,0:T(8,128)(2,1)S(1)}, bf16[2,128,128]{2,1,0:T(8,128)(2,1)S(1)}, u32[]{:S(2)}, u32[]{:S(2)}) collective-permute-start(bf16[2,128,128]{2,1,0:T(8,128)(2,1)S(1)} %get-tuple-element.81), channel_id=1, source_target_pairs={{0,96},{2,98},{4,100},{6,102},{8,104},{10,106},{12,108},{14,110},{... | collective-permute-start | bytes 196616 | tf_op jit(solution)/shard_map/ppermute | solution.py:308
  72.2 4.3 %collective-permute-start.24 = (bf16[2,128,128]{2,1,0:T(8,128)(2,1)S(1)}, bf16[2,128,128]{2,1,0:T(8,128)(2,1)S(1)}, u32[]{:S(2)}, u32[]{:S(2)}) collective-permute-start(bf16[2,128,128]{2,1,0:T(8,128)(2,1)S(1)} %get-tuple-element.82), channel_id=1, source_target_pairs={{0,32},{2,34},{4,36},{6,38},{8,40},{10,42},{12,44},{14,46},{16,20}... | collective-permute-start | bytes 196616 | tf_op jit(solution)/shard_map/ppermute | solution.py:308
  72.3 5.8 %collective-permute-start.23 = (bf16[2,128,128]{2,1,0:T(8,128)(2,1)S(1)}, bf16[2,128,128]{2,1,0:T(8,128)(2,1)S(1)}, u32[]{:S(2)}, u32[]{:S(2)}) collective-permute-start(bf16[2,128,128]{2,1,0:T(8,128)(2,1)S(1)} %get-tuple-element.83), channel_id=1, source_target_pairs={{0,64},{2,66},{4,68},{6,70},{8,72},{10,74},{12,76},{14,78},{16,24}... | collective-permute-start | bytes 196616 | tf_op jit(solution)/shard_map/ppermute | solution.py:308
  78.2 3.4 %collective-permute-start.27 = (bf16[128,128]{1,0:T(8,128)(2,1)S(1)}, bf16[128,128]{1,0:T(8,128)(2,1)S(1)}, u32[]{:S(2)}, u32[]{:S(2)}) collective-permute-start(bf16[128,128]{1,0:T(8,128)(2,1)S(1)} %select_bitcast_fusion), channel_id=1, source_target_pairs={{0,16},{2,18},{4,20},{6,22},{8,24},{10,26},{12,28},{14,30},{16,0},... | collective-permute-start | bytes 98312 | tf_op jit(solution)/shard_map/ppermute | solution.py:308

commit v13 on v12

--- a/solution.py
+++ b/solution.py
@@ -11,7 +11,7 @@
 HEAD = 128
 BLOCK = 128
 DOC_ROWS = 16
-CHUNK_BLOCKS = 4
+CHUNK_BLOCKS = 5
 CHUNK = CHUNK_BLOCKS * BLOCK
 TILES = 2
 VMEM_MIB = 36

time: 82.6 us -> 82.1 us (level)
  starting transfers between devices: 44.5 us -> 39.3 us
  Pallas kernels: 19.6 us -> 22.5 us
  waiting for transfers between devices: 11.7 us -> 13.7 us
    ppermute x28, starting transfers between devices: 44.5 us -> 39.3 us  [moved(): return lax.ppermute(value, CONTEXT, hops)]
    pallas_call x4, Pallas kernels: 19.6 us -> 22.5 us  [kernel_call(): pl.pallas_call(lambda *refs: kernel(sizes, *refs), name=kernel.__name__,...]
    ppermute x28, waiting for transfers between devices: 11.7 us -> 13.7 us  [moved(): return lax.ppermute(value, CONTEXT, hops)]
  transfers between devices with their start and end apart: 28 -> 28, of which waited for: 10 -> 11; matrix products, arithmetic and copies ran while one was open for 4% -> 4% of each run, Pallas kernels for 24% -> 28%
where the time goes in v13:
time: 82.1 us; the launch traced here: 81.9 us
  starting transfers between devices  39.3 us (48%)
  Pallas kernels  22.5 us (27%)
  waiting for transfers between devices  13.7 us (17%)
  other arithmetic  3.72 us (5%)
  between operations  1.51 us (2%)
  local copies, waits for them, and re-layouts  1.18 us (1%)
    ppermute x28, starting transfers between devices, moved(): return lax.ppermute(value, CONTEXT, hops)  39.3 us
    pallas_call x4, Pallas kernels, kernel_call(): pl.pallas_call(lambda *refs: kernel(sizes, *refs), name=kernel.__name__,...  22.5 us
    ppermute x28, waiting for transfers between devices, moved(): return lax.ppermute(value, CONTEXT, hops)  13.7 us
  transfers between devices with their start and end apart: 28, of which 11 were waited for; matrix products, arithmetic and copies ran while one was open for 4% of the time, Pallas kernels for 28%

profile of v13, /device:TPU:1, one launch (start us, length us, event | category | flops | bytes accessed | tf_op | source)
XLA Modules:
  0.0 81.9 jit_solution(4933529076351361502)
XLA Ops:
  1.3 0.8 select_bitcast_fusion.1
  2.1 1.5 %collective-permute-start.1 = (bf16[144,128]{1,0:T(8,128)(2,1)S(1)}, bf16[144,128]{1,0:T(8,128)(2,1)S(1)}, u32[]{:S(2)}, u32[]{:S(2)}) collective-permute-start(bf16[144,128]{1,0:T(8,128)(2,1)S(1)} %concatenate.17), channel_id=1, source_target_pairs={{0,16},{2,18},{4,20},{6,22},{8,24},{10,26},{12,28},{14,30},{16,0},... | collective-permute-start | bytes 110600 | tf_op jit(solution)/shard_map/ppermute | solution.py:308
  3.6 1.1 %constant_dynamic-slice_fusion.2 = (bf16[64,1024]{1,0:T(8,128)(2,1)S(1)}, bf16[64,1024]{1,0:T(8,128)(2,1)S(1)}, bf16[64,1024]{1,0:T(8,128)(2,1)S(1)}, bf16[64,1024]{1,0:T(8,128)(2,1)S(1)}) fusion(bf16[128,1024]{1,0:T(8,128)(2,1)} %param.8, s32[]{:T(128)S(6)} %select_n.83, s32[]{:T(128)S(6)} %select_n.84, bf16[128,1024]{1,0:T(8,128)(2,1)} %param.5), kind=kLoop, calls=%fused_computation.34 | loop fusion | bytes 1048584 | tf_op jit(solution)/shard_map/dynamic_slice | solution.py:334
  4.8 3.8 %collective-permute-start = (bf16[64,2176]{1,0:T(8,128)(2,1)S(1)}, bf16[64,2176]{1,0:T(8,128)(2,1)S(1)}, u32[]{:S(2)}, u32[]{:S(2)}) collective-permute-start(bf16[64,2176]{1,0:T(8,128)(2,1)S(1)} %get-tuple-element.95), channel_id=1, source_target_pairs={{0,64},{2,66},{4,68},{6,70},{8,72},{10,74},{12,76},{14,78},{16,80}... | collective-permute-start | bytes 835592 | tf_op jit(solution)/shard_map/ppermute | solution.py:308
  8.6 2.8 %collective-permute-start.3 = (bf16[272,128]{1,0:T(8,128)(2,1)S(1)}, bf16[272,128]{1,0:T(8,128)(2,1)S(1)}, u32[]{:S(2)}, u32[]{:S(2)}) collective-permute-start(bf16[272,128]{1,0:T(8,128)(2,1)S(1)} %get-tuple-element.91), channel_id=1, source_target_pairs={{0,64},{2,66},{4,68},{6,70},{8,72},{10,74},{12,76},{14,78},{16,24}... | collective-permute-start | bytes 208904 | tf_op jit(solution)/shard_map/ppermute | solution.py:308
  11.4 0.3 collective-permute-start.2
  11.7 2.4 %collective-permute-start.4 = (bf16[272,128]{1,0:T(8,128)(2,1)S(1)}, bf16[272,128]{1,0:T(8,128)(2,1)S(1)}, u32[]{:S(2)}, u32[]{:S(2)}) collective-permute-start(bf16[272,128]{1,0:T(8,128)(2,1)S(1)} %get-tuple-element.91), channel_id=1, source_target_pairs={{0,96},{2,98},{4,100},{6,102},{8,104},{10,106},{12,108},{14,110},{... | collective-permute-start | bytes 208904 | tf_op jit(solution)/shard_map/ppermute | solution.py:308
  14.1 2.0 %collective-permute-done.2 = bf16[272,128]{1,0:T(8,128)(2,1)S(1)} collective-permute-done((bf16[272,128]{1,0:T(8,128)(2,1)S(1)}, bf16[272,128]{1,0:T(8,128)(2,1)S(1)}, u32[]{:S(2)}, u32[]{:S(2)}) %collective-permute-start.2) | collective-permute-done | bytes 69664 | tf_op jit(solution)/shard_map/ppermute | solution.py:308
  16.1 0.5 collective-permute-start.7
  16.6 1.9 %collective-permute-start.6 = (bf16[4,272,128]{2,1,0:T(8,128)(2,1)S(1)}, bf16[4,272,128]{2,1,0:T(8,128)(2,1)S(1)}, u32[]{:S(2)}, u32[]{:S(2)}) collective-permute-start(bf16[4,272,128]{2,1,0:T(8,128)(2,1)S(1)} %pad_maximum_fusion.3.refs_3_), channel_id=1, source_target_pairs={{0,8},{2,10},{4,12},{6,14},{8,0},{10,2},{12,4},{14,6},{16,80},{18,... | collective-permute-start | bytes 835592 | tf_op jit(solution)/shard_map/ppermute | solution.py:308
  18.6 0.8 %pad_maximum_fusion = bf16[128,2176]{1,0:T(8,128)(2,1)} fusion(bf16[64,2176]{1,0:T(8,128)(2,1)S(1)} %collective-permute-done.refs_2_, bf16[64,128]{1,0:T(8,128)(2,1)S(1)} %broadcast_in_dim.5, bf16[64,1024]{1,0:T(8,128)(2,1)S(1)} %get-tuple-element.86, bf16[64,1024]{1,0:T(8,128)(2,1)S(1)} %get-tuple-element.97), kind=kLoop, calls=%fused_computation | loop fusion | flops 2228224 | bytes 1114112 | tf_op jit(solution)/shard_map/concatenate | solution.py:339
  19.4 1.3 %collective-permute-start.12 = (bf16[128,2176]{1,0:T(8,128)(2,1)}, bf16[128,2176]{1,0:T(8,128)(2,1)S(1)}, u32[]{:S(2)}, u32[]{:S(2)}) collective-permute-start(bf16[128,2176]{1,0:T(8,128)(2,1)} %pad_maximum_fusion), channel_id=1, source_target_pairs={{0,2},{2,0},{4,6},{6,4},{8,10},{10,8},{12,14},{14,12},{16,18},{18,... | collective-permute-start | bytes 1671176 | tf_op jit(solution)/shard_map/ppermute | solution.py:308
  20.7 5.3 %collective-permute-start.8 = (bf16[4,272,128]{2,1,0:T(8,128)(2,1)S(1)}, bf16[4,272,128]{2,1,0:T(8,128)(2,1)S(1)}, u32[]{:S(2)}, u32[]{:S(2)}) collective-permute-start(bf16[4,272,128]{2,1,0:T(8,128)(2,1)S(1)} %pad_maximum_fusion.3.refs_3_), channel_id=1, source_target_pairs={{0,16},{2,18},{4,20},{6,22},{8,24},{10,26},{12,28},{14,30},{16,0},... | collective-permute-start | bytes 835592 | tf_op jit(solution)/shard_map/ppermute | solution.py:308
  26.0 2.4 %collective-permute-start.11 = (bf16[4,272,128]{2,1,0:T(8,128)(2,1)S(1)}, bf16[4,272,128]{2,1,0:T(8,128)(2,1)S(1)}, u32[]{:S(2)}, u32[]{:S(2)}) collective-permute-start(bf16[4,272,128]{2,1,0:T(8,128)(2,1)S(1)} %collective-permute-done.7.refs_6_), channel_id=1, source_target_pairs={{0,16},{2,18},{4,20},{6,22},{8,24},{10,26},{12,28},{14,30},{16,0},... | collective-permute-start | bytes 835592 | tf_op jit(solution)/shard_map/ppermute | solution.py:308
  28.4 1.1 %collective-permute-start.10 = (bf16[4,272,128]{2,1,0:T(8,128)(2,1)S(1)}, bf16[4,272,128]{2,1,0:T(8,128)(2,1)S(1)}, u32[]{:S(2)}, u32[]{:S(2)}) collective-permute-start(bf16[4,272,128]{2,1,0:T(8,128)(2,1)S(1)} %collective-permute-done.6.refs_5_), channel_id=1, source_target_pairs={{0,16},{2,18},{4,20},{6,22},{8,24},{10,26},{12,28},{14,30},{16,0},... | collective-permute-start | bytes 835592 | tf_op jit(solution)/shard_map/ppermute | solution.py:308
  29.4 2.9 %collective-permute-start.9 = (bf16[4,272,128]{2,1,0:T(8,128)(2,1)S(1)}, bf16[4,272,128]{2,1,0:T(8,128)(2,1)S(1)}, u32[]{:S(2)}, u32[]{:S(2)}) collective-permute-start(bf16[4,272,128]{2,1,0:T(8,128)(2,1)S(1)} %collective-permute-done.5.refs_4_), channel_id=1, source_target_pairs={{0,16},{2,18},{4,20},{6,22},{8,24},{10,26},{12,28},{14,30},{16,0},... | collective-permute-start | bytes 835592 | tf_op jit(solution)/shard_map/ppermute | solution.py:308
  32.3 0.1 pad_add_fusion.refs_0_
  32.4 1.1 %collective-permute-done.9.refs_8_ = bf16[4,272,128]{2,1,0:T(8,128)(2,1)S(1)} collective-permute-done((bf16[4,272,128]{2,1,0:T(8,128)(2,1)S(1)}, bf16[4,272,128]{2,1,0:T(8,128)(2,1)S(1)}, u32[]{:S(2)}, u32[]{:S(2)}) %collective-permute-start.9) | collective-permute-done | bytes 278560 | tf_op jit(solution)/shard_map/ppermute | solution.py:308
  33.5 4.4 %near_statistics.1 = (f32[2,8,512]{2,1,0:T(8,128)S(1)}, f32[2,16,128]{2,1,0:T(8,128)S(1)}, bf16[2,2,128,512]{3,2,1,0:T(8,128)(2,1)S(1)}, bf16[2,2,512,128]{3,2,1...) custom-call(s32[4]{0:T(128)S(1)} %pad_add_fusion.refs_0_, ...), custom_call_target="tpu_custom_call" | custom-call | flops 805306368 | bytes 8388608 | tf_op jit(solution)/shard_map/near_statistics/pallas_call | solution.py:225
  37.9 1.4 %collective-permute-start.13 = (f32[2,8,512]{2,1,0:T(8,128)S(1)}, f32[2,8,512]{2,1,0:T(8,128)S(1)}, u32[]{:S(2)}, u32[]{:S(2)}) collective-permute-start(f32[2,8,512]{2,1,0:T(8,128)S(1)} %get-tuple-element.41.refs_1_), channel_id=1, source_target_pairs={{0,2},{2,0},{4,6},{6,4},{8,10},{10,8},{12,14},{14,12},{16,18},{18,... | collective-permute-start | bytes 98312 | tf_op jit(solution)/shard_map/ppermute | solution.py:308
  39.3 4.3 %far_statistics.1 = (f32[2,8,512]{2,1,0:T(8,128)S(1)}, f32[2,16,128]{2,1,0:T(8,128)S(1)}, bf16[2,2,128,512]{3,2,1,0:T(8,128)(2,1)S(1)}, bf16[2,2,512,128]{3,2,1,0:T(8,128)(2,1)S(1)}) custom-call(s32[4]{0:T(128)S(1)} %pad_add_fusion.refs_0_, bf16[128,2176]{1,0:T(8,128)(2,1)S(1)} %collective-permute-done.12.refs_1_, ...), custom_call_target="tpu_custom_call" | custom-call | flops 805306368 | bytes 8388608 | tf_op jit(solution)/shard_map/far_statistics/pallas_call | solution.py:225
  43.6 0.2 collective-permute-start.14
  43.8 6.8 %far_gradients.1 = (bf16[2,64,1024]{2,1,0:T(8,128)(2,1)S(1)}, f32[2,4096,128]{2,1,0:T(8,128)S(1)}) custom-call(s32[4]{0:T(128)S(1)} %pad_add_fusion.refs_0_, f32[2,8,512]{2,1,0:T(8,128)S(1)} %get-tuple-element.44.refs_1_, f32[2,8,512]{2,1,0:T(8,128)S(1)} %collective-permute-done.13.refs_2_, f32[2,16,128]{2,1,0:T(8,128)S(1)} %get-tuple-element.45.refs_3_, ...), custom_call_target="tpu_custom_call" | custom-call | flops 2013265920 | bytes 8388608 | tf_op jit(solution)/shard_map/far_gradients/pallas_call | solution.py:225
  50.7 1.6 %collective-permute-start.15 = (bf16[2,64,1024]{2,1,0:T(8,128)(2,1)S(1)}, bf16[2,64,1024]{2,1,0:T(8,128)(2,1)S(1)}, u32[]{:S(2)}, u32[]{:S(2)}) collective-permute-start(bf16[2,64,1024]{2,1,0:T(8,128)(2,1)S(1)} %get-tuple-element.55), channel_id=1, source_target_pairs={{0,2},{2,0},{4,6},{6,4},{8,10},{10,8},{12,14},{14,12},{16,18},{18,... | collective-permute-start | bytes 786440 | tf_op jit(solution)/shard_map/ppermute | solution.py:308
  52.2 7.0 %near_gradients.1 = (f32[2,64,1024]{2,1,0:T(8,128)S(1)}, bf16[4,2,128,128]{3,2,1,0:T(8,128)(2,1)S(1)}, bf16[4,2,128,128]{3,2,1,0:T(8,128)(2,1)S(1)}, bf16[4,2,12...) custom-call(s32[4]{0:T(128)S(1)} %pad_add_fusion.refs_0_, ...), custom_call_target="tpu_custom_call" | custom-call | flops 2013265920 | bytes 8388608 | tf_op jit(solution)/shard_map/near_gradients/pallas_call | solution.py:225
  59.3 0.1 collective-permute-start.16
  59.4 0.5 collective-permute-start.17
  59.9 0.1 collective-permute-start.19
  60.0 0.4 collective-permute-start.21
  60.4 0.5 collective-permute-done.16
  61.0 0.3 collective-permute-done.17
  61.3 2.3 %collective-permute-start.18 = (bf16[4,2,128,128]{3,2,1,0:T(8,128)(2,1)S(1)}, bf16[4,2,128,128]{3,2,1,0:T(8,128)(2,1)S(1)}, u32[]{:S(2)}, u32[]{:S(2)}) collective-permute-start(bf16[4,2,128,128]{3,2,1,0:T(8,128)(2,1)S(1)} %add_convert_fusion.3), channel_id=1, source_target_pairs={{0,8},{2,10},{4,12},{6,14},{8,0},{10,2},{12,4},{14,6},{16,80},{18,... | collective-permute-start | bytes 786440 | tf_op jit(solution)/shard_map/ppermute | solution.py:308
  63.9 2.7 %collective-permute-start.22 = (bf16[4,2,128,128]{3,2,1,0:T(8,128)(2,1)S(1)}, bf16[4,2,128,128]{3,2,1,0:T(8,128)(2,1)S(1)}, u32[]{:S(2)}, u32[]{:S(2)}) collective-permute-start(bf16[4,2,128,128]{3,2,1,0:T(8,128)(2,1)S(1)} %add_convert_fusion.1), channel_id=1, source_target_pairs={{0,12},{2,14},{4,0},{6,2},{8,4},{10,6},{12,8},{14,10},{16,112},{18... | collective-permute-start | bytes 786440 | tf_op jit(solution)/shard_map/ppermute | solution.py:308
  66.7 0.1 collective-permute-start.26
  66.8 1.7 %collective-permute-done.18 = bf16[4,2,128,128]{3,2,1,0:T(8,128)(2,1)S(1)} collective-permute-done((bf16[4,2,128,128]{3,2,1,0:T(8,128)(2,1)S(1)}, bf16[4,2,128,128]{3,2,1,0:T(8,128)(2,1)S(1)}, u32[]{:S(2)}, u32[]{:S(2)}) %collective-permute-start.18) | collective-permute-done | bytes 262176 | tf_op jit(solution)/shard_map/ppermute | solution.py:308
  68.4 2.8 %collective-permute-done.20 = bf16[4,2,128,128]{3,2,1,0:T(8,128)(2,1)S(1)} collective-permute-done((bf16[4,2,128,128]{3,2,1,0:T(8,128)(2,1)S(1)}, bf16[4,2,128,128]{3,2,1,0:T(8,128)(2,1)S(1)}, u32[]{:S(2)}, u32[]{:S(2)}) %collective-permute-start.20) | collective-permute-done | bytes 262176 | tf_op jit(solution)/shard_map/ppermute | solution.py:308
  71.3 1.1 %collective-permute-done.22 = bf16[4,2,128,128]{3,2,1,0:T(8,128)(2,1)S(1)} collective-permute-done((bf16[4,2,128,128]{3,2,1,0:T(8,128)(2,1)S(1)}, bf16[4,2,128,128]{3,2,1,0:T(8,128)(2,1)S(1)}, u32[]{:S(2)}, u32[]{:S(2)}) %collective-permute-start.22) | collective-permute-done | bytes 262176 | tf_op jit(solution)/shard_map/ppermute | solution.py:308
  72.4 0.1 add_convert_fusion
  72.5 0.1 collective-permute-start.25
  72.6 1.5 %collective-permute-start.24 = (bf16[2,128,128]{2,1,0:T(8,128)(2,1)S(1)}, bf16[2,128,128]{2,1,0:T(8,128)(2,1)S(1)}, u32[]{:S(2)}, u32[]{:S(2)}) collective-permute-start(bf16[2,128,128]{2,1,0:T(8,128)(2,1)S(1)} %get-tuple-element.82), channel_id=1, source_target_pairs={{0,32},{2,34},{4,36},{6,38},{8,40},{10,42},{12,44},{14,46},{16,20}... | collective-permute-start | bytes 196616 | tf_op jit(solution)/shard_map/ppermute | solution.py:308
  74.1 0.6 collective-permute-start.23
  74.6 1.4 %collective-permute-done.25 = bf16[2,128,128]{2,1,0:T(8,128)(2,1)S(1)} collective-permute-done((bf16[2,128,128]{2,1,0:T(8,128)(2,1)S(1)}, bf16[2,128,128]{2,1,0:T(8,128)(2,1)S(1)}, u32[]{:S(2)}, u32[]{:S(2)}) %collective-permute-start.25) | collective-permute-done | bytes 65568 | tf_op jit(solution)/shard_map/ppermute | solution.py:308
  76.0 1.3 %collective-permute-done.24 = bf16[2,128,128]{2,1,0:T(8,128)(2,1)S(1)} collective-permute-done((bf16[2,128,128]{2,1,0:T(8,128)(2,1)S(1)}, bf16[2,128,128]{2,1,0:T(8,128)(2,1)S(1)}, u32[]{:S(2)}, u32[]{:S(2)}) %collective-permute-start.24) | collective-permute-done | bytes 65568 | tf_op jit(solution)/shard_map/ppermute | solution.py:308
  77.3 1.4 %collective-permute-done.23 = bf16[2,128,128]{2,1,0:T(8,128)(2,1)S(1)} collective-permute-done((bf16[2,128,128]{2,1,0:T(8,128)(2,1)S(1)}, bf16[2,128,128]{2,1,0:T(8,128)(2,1)S(1)}, u32[]{:S(2)}, u32[]{:S(2)}) %collective-permute-start.23) | collective-permute-done | bytes 65568 | tf_op jit(solution)/shard_map/ppermute | solution.py:308
  78.8 1.7 %collective-permute-start.27 = (bf16[128,128]{1,0:T(8,128)(2,1)S(1)}, bf16[128,128]{1,0:T(8,128)(2,1)S(1)}, u32[]{:S(2)}, u32[]{:S(2)}) collective-permute-start(bf16[128,128]{1,0:T(8,128)(2,1)S(1)} %select_bitcast_fusion), channel_id=1, source_target_pairs={{0,16},{2,18},{4,20},{6,22},{8,24},{10,26},{12,28},{14,30},{16,0},... | collective-permute-start | bytes 98312 | tf_op jit(solution)/shard_map/ppermute | solution.py:308
  80.4 0.7 maximum_select_fusion
  81.2 0.1 collective-permute-done.27
  81.3 0.6 bitcast_select_fusion
  (37 shorter events, 0.7 us)
Async XLA Ops:
  2.1 6.5 %collective-permute-start.1 = (bf16[144,128]{1,0:T(8,128)(2,1)S(1)}, bf16[144,128]{1,0:T(8,128)(2,1)S(1)}, u32[]{:S(2)}, u32[]{:S(2)}) collective-permute-start(bf16[144,128]{1,0:T(8,128)(2,1)S(1)} %concatenate.17), channel_id=1, source_target_pairs={{0,16},{2,18},{4,20},{6,22},{8,24},{10,26},{12,28},{14,30},{16,0},... | collective-permute-start | bytes 110600 | tf_op jit(solution)/shard_map/ppermute | solution.py:308
  4.8 13.8 %collective-permute-start = (bf16[64,2176]{1,0:T(8,128)(2,1)S(1)}, bf16[64,2176]{1,0:T(8,128)(2,1)S(1)}, u32[]{:S(2)}, u32[]{:S(2)}) collective-permute-start(bf16[64,2176]{1,0:T(8,128)(2,1)S(1)} %get-tuple-element.95), channel_id=1, source_target_pairs={{0,64},{2,66},{4,68},{6,70},{8,72},{10,74},{12,76},{14,78},{16,80}... | collective-permute-start | bytes 835592 | tf_op jit(solution)/shard_map/ppermute | solution.py:308
  8.6 5.5 %collective-permute-start.3 = (bf16[272,128]{1,0:T(8,128)(2,1)S(1)}, bf16[272,128]{1,0:T(8,128)(2,1)S(1)}, u32[]{:S(2)}, u32[]{:S(2)}) collective-permute-start(bf16[272,128]{1,0:T(8,128)(2,1)S(1)} %get-tuple-element.91), channel_id=1, source_target_pairs={{0,64},{2,66},{4,68},{6,70},{8,72},{10,74},{12,76},{14,78},{16,24}... | collective-permute-start | bytes 208904 | tf_op jit(solution)/shard_map/ppermute | solution.py:308
  11.4 4.7 %collective-permute-start.2 = (bf16[272,128]{1,0:T(8,128)(2,1)S(1)}, bf16[272,128]{1,0:T(8,128)(2,1)S(1)}, u32[]{:S(2)}, u32[]{:S(2)}) collective-permute-start(bf16[272,128]{1,0:T(8,128)(2,1)S(1)} %get-tuple-element.91), channel_id=1, source_target_pairs={{0,32},{2,34},{4,36},{6,38},{8,40},{10,42},{12,44},{14,46},{16,20}... | collective-permute-start | bytes 208904 | tf_op jit(solution)/shard_map/ppermute | solution.py:308
  11.7 4.4 %collective-permute-start.4 = (bf16[272,128]{1,0:T(8,128)(2,1)S(1)}, bf16[272,128]{1,0:T(8,128)(2,1)S(1)}, u32[]{:S(2)}, u32[]{:S(2)}) collective-permute-start(bf16[272,128]{1,0:T(8,128)(2,1)S(1)} %get-tuple-element.91), channel_id=1, source_target_pairs={{0,96},{2,98},{4,100},{6,102},{8,104},{10,106},{12,108},{14,110},{... | collective-permute-start | bytes 208904 | tf_op jit(solution)/shard_map/ppermute | solution.py:308
  16.1 9.9 %collective-permute-start.7 = (bf16[4,272,128]{2,1,0:T(8,128)(2,1)S(1)}, bf16[4,272,128]{2,1,0:T(8,128)(2,1)S(1)}, u32[]{:S(2)}, u32[]{:S(2)}) collective-permute-start(bf16[4,272,128]{2,1,0:T(8,128)(2,1)S(1)} %pad_maximum_fusion.3.refs_3_), channel_id=1, source_target_pairs={{0,12},{2,14},{4,0},{6,2},{8,4},{10,6},{12,8},{14,10},{16,112},{18... | collective-permute-start | bytes 835592 | tf_op jit(solution)/shard_map/ppermute | solution.py:308
  16.6 11.7 %collective-permute-start.6 = (bf16[4,272,128]{2,1,0:T(8,128)(2,1)S(1)}, bf16[4,272,128]{2,1,0:T(8,128)(2,1)S(1)}, u32[]{:S(2)}, u32[]{:S(2)}) collective-permute-start(bf16[4,272,128]{2,1,0:T(8,128)(2,1)S(1)} %pad_maximum_fusion.3.refs_3_), channel_id=1, source_target_pairs={{0,8},{2,10},{4,12},{6,14},{8,0},{10,2},{12,4},{14,6},{16,80},{18,... | collective-permute-start | bytes 835592 | tf_op jit(solution)/shard_map/ppermute | solution.py:308
  18.6 10.9 %collective-permute-start.5 = (bf16[4,272,128]{2,1,0:T(8,128)(2,1)S(1)}, bf16[4,272,128]{2,1,0:T(8,128)(2,1)S(1)}, u32[]{:S(2)}, u32[]{:S(2)}) collective-permute-start(bf16[4,272,128]{2,1,0:T(8,128)(2,1)S(1)} %pad_maximum_fusion.3.refs_3_), channel_id=1, source_target_pairs={{0,4},{2,6},{4,8},{6,10},{8,12},{10,14},{12,0},{14,2},{16,48},{18,... | collective-permute-start | bytes 835592 | tf_op jit(solution)/shard_map/ppermute | solution.py:308
  19.4 19.9 %collective-permute-start.12 = (bf16[128,2176]{1,0:T(8,128)(2,1)}, bf16[128,2176]{1,0:T(8,128)(2,1)S(1)}, u32[]{:S(2)}, u32[]{:S(2)}) collective-permute-start(bf16[128,2176]{1,0:T(8,128)(2,1)} %pad_maximum_fusion), channel_id=1, source_target_pairs={{0,2},{2,0},{4,6},{6,4},{8,10},{10,8},{12,14},{14,12},{16,18},{18,... | collective-permute-start | bytes 1671176 | tf_op jit(solution)/shard_map/ppermute | solution.py:308
  20.7 11.7 %collective-permute-start.8 = (bf16[4,272,128]{2,1,0:T(8,128)(2,1)S(1)}, bf16[4,272,128]{2,1,0:T(8,128)(2,1)S(1)}, u32[]{:S(2)}, u32[]{:S(2)}) collective-permute-start(bf16[4,272,128]{2,1,0:T(8,128)(2,1)S(1)} %pad_maximum_fusion.3.refs_3_), channel_id=1, source_target_pairs={{0,16},{2,18},{4,20},{6,22},{8,24},{10,26},{12,28},{14,30},{16,0},... | collective-permute-start | bytes 835592 | tf_op jit(solution)/shard_map/ppermute | solution.py:308
  26.0 6.4 %collective-permute-start.11 = (bf16[4,272,128]{2,1,0:T(8,128)(2,1)S(1)}, bf16[4,272,128]{2,1,0:T(8,128)(2,1)S(1)}, u32[]{:S(2)}, u32[]{:S(2)}) collective-permute-start(bf16[4,272,128]{2,1,0:T(8,128)(2,1)S(1)} %collective-permute-done.7.refs_6_), channel_id=1, source_target_pairs={{0,16},{2,18},{4,20},{6,22},{8,24},{10,26},{12,28},{14,30},{16,0},... | collective-permute-start | bytes 835592 | tf_op jit(solution)/shard_map/ppermute | solution.py:308
  28.4 4.0 %collective-permute-start.10 = (bf16[4,272,128]{2,1,0:T(8,128)(2,1)S(1)}, bf16[4,272,128]{2,1,0:T(8,128)(2,1)S(1)}, u32[]{:S(2)}, u32[]{:S(2)}) collective-permute-start(bf16[4,272,128]{2,1,0:T(8,128)(2,1)S(1)} %collective-permute-done.6.refs_5_), channel_id=1, source_target_pairs={{0,16},{2,18},{4,20},{6,22},{8,24},{10,26},{12,28},{14,30},{16,0},... | collective-permute-start | bytes 835592 | tf_op jit(solution)/shard_map/ppermute | solution.py:308
  29.4 4.1 %collective-permute-start.9 = (bf16[4,272,128]{2,1,0:T(8,128)(2,1)S(1)}, bf16[4,272,128]{2,1,0:T(8,128)(2,1)S(1)}, u32[]{:S(2)}, u32[]{:S(2)}) collective-permute-start(bf16[4,272,128]{2,1,0:T(8,128)(2,1)S(1)} %collective-permute-done.5.refs_4_), channel_id=1, source_target_pairs={{0,16},{2,18},{4,20},{6,22},{8,24},{10,26},{12,28},{14,30},{16,0},... | collective-permute-start | bytes 835592 | tf_op jit(solution)/shard_map/ppermute | solution.py:308
  37.9 5.9 %collective-permute-start.13 = (f32[2,8,512]{2,1,0:T(8,128)S(1)}, f32[2,8,512]{2,1,0:T(8,128)S(1)}, u32[]{:S(2)}, u32[]{:S(2)}) collective-permute-start(f32[2,8,512]{2,1,0:T(8,128)S(1)} %get-tuple-element.41.refs_1_), channel_id=1, source_target_pairs={{0,2},{2,0},{4,6},{6,4},{8,10},{10,8},{12,14},{14,12},{16,18},{18,... | collective-permute-start | bytes 98312 | tf_op jit(solution)/shard_map/ppermute | solution.py:308
  43.6 7.1 %collective-permute-start.14 = (f32[2,8,512]{2,1,0:T(8,128)S(1)}, f32[2,8,512]{2,1,0:T(8,128)S(1)}, u32[]{:S(2)}, u32[]{:S(2)}) collective-permute-start(f32[2,8,512]{2,1,0:T(8,128)S(1)} %get-tuple-element.44.refs_1_), channel_id=1, source_target_pairs={{0,2},{2,0},{4,6},{6,4},{8,10},{10,8},{12,14},{14,12},{16,18},{18,... | collective-permute-start | bytes 98312 | tf_op jit(solution)/shard_map/ppermute | solution.py:308
  50.7 8.6 %collective-permute-start.15 = (bf16[2,64,1024]{2,1,0:T(8,128)(2,1)S(1)}, bf16[2,64,1024]{2,1,0:T(8,128)(2,1)S(1)}, u32[]{:S(2)}, u32[]{:S(2)}) collective-permute-start(bf16[2,64,1024]{2,1,0:T(8,128)(2,1)S(1)} %get-tuple-element.55), channel_id=1, source_target_pairs={{0,2},{2,0},{4,6},{6,4},{8,10},{10,8},{12,14},{14,12},{16,18},{18,... | collective-permute-start | bytes 786440 | tf_op jit(solution)/shard_map/ppermute | solution.py:308
  59.3 1.6 %collective-permute-start.16 = (bf16[4,2,128,128]{3,2,1,0:T(8,128)(2,1)S(1)}, bf16[4,2,128,128]{3,2,1,0:T(8,128)(2,1)S(1)}, u32[]{:S(2)}, u32[]{:S(2)}) collective-permute-start(bf16[4,2,128,128]{3,2,1,0:T(8,128)(2,1)S(1)} %get-tuple-element.65), channel_id=1, source_target_pairs={{0,16},{2,18},{4,20},{6,22},{8,24},{10,26},{12,28},{14,30},{16,0},... | collective-permute-start | bytes 786440 | tf_op jit(solution)/shard_map/ppermute | solution.py:308
  59.4 1.9 %collective-permute-start.17 = (bf16[4,2,128,128]{3,2,1,0:T(8,128)(2,1)S(1)}, bf16[4,2,128,128]{3,2,1,0:T(8,128)(2,1)S(1)}, u32[]{:S(2)}, u32[]{:S(2)}) collective-permute-start(bf16[4,2,128,128]{3,2,1,0:T(8,128)(2,1)S(1)} %get-tuple-element.70), channel_id=1, source_target_pairs={{0,16},{2,18},{4,20},{6,22},{8,24},{10,26},{12,28},{14,30},{16,0},... | collective-permute-start | bytes 786440 | tf_op jit(solution)/shard_map/ppermute | solution.py:308
  59.9 3.8 %collective-permute-start.19 = (bf16[4,2,128,128]{3,2,1,0:T(8,128)(2,1)S(1)}, bf16[4,2,128,128]{3,2,1,0:T(8,128)(2,1)S(1)}, u32[]{:S(2)}, u32[]{:S(2)}) collective-permute-start(bf16[4,2,128,128]{3,2,1,0:T(8,128)(2,1)S(1)} %get-tuple-element.72), channel_id=1, source_target_pairs={{0,16},{2,18},{4,20},{6,22},{8,24},{10,26},{12,28},{14,30},{16,0},... | collective-permute-start | bytes 786440 | tf_op jit(solution)/shard_map/ppermute | solution.py:308
  60.0 3.8 %collective-permute-start.21 = (bf16[4,2,128,128]{3,2,1,0:T(8,128)(2,1)S(1)}, bf16[4,2,128,128]{3,2,1,0:T(8,128)(2,1)S(1)}, u32[]{:S(2)}, u32[]{:S(2)}) collective-permute-start(bf16[4,2,128,128]{3,2,1,0:T(8,128)(2,1)S(1)} %get-tuple-element.74), channel_id=1, source_target_pairs={{0,16},{2,18},{4,20},{6,22},{8,24},{10,26},{12,28},{14,30},{16,0},... | collective-permute-start | bytes 786440 | tf_op jit(solution)/shard_map/ppermute | solution.py:308
  61.3 7.1 %collective-permute-start.18 = (bf16[4,2,128,128]{3,2,1,0:T(8,128)(2,1)S(1)}, bf16[4,2,128,128]{3,2,1,0:T(8,128)(2,1)S(1)}, u32[]{:S(2)}, u32[]{:S(2)}) collective-permute-start(bf16[4,2,128,128]{3,2,1,0:T(8,128)(2,1)S(1)} %add_convert_fusion.3), channel_id=1, source_target_pairs={{0,8},{2,10},{4,12},{6,14},{8,0},{10,2},{12,4},{14,6},{16,80},{18,... | collective-permute-start | bytes 786440 | tf_op jit(solution)/shard_map/ppermute | solution.py:308
  63.7 7.5 %collective-permute-start.20 = (bf16[4,2,128,128]{3,2,1,0:T(8,128)(2,1)S(1)}, bf16[4,2,128,128]{3,2,1,0:T(8,128)(2,1)S(1)}, u32[]{:S(2)}, u32[]{:S(2)}) collective-permute-start(bf16[4,2,128,128]{3,2,1,0:T(8,128)(2,1)S(1)} %add_convert_fusion.2), channel_id=1, source_target_pairs={{0,4},{2,6},{4,8},{6,10},{8,12},{10,14},{12,0},{14,2},{16,48},{18,... | collective-permute-start | bytes 786440 | tf_op jit(solution)/shard_map/ppermute | solution.py:308
  63.9 8.5 %collective-permute-start.22 = (bf16[4,2,128,128]{3,2,1,0:T(8,128)(2,1)S(1)}, bf16[4,2,128,128]{3,2,1,0:T(8,128)(2,1)S(1)}, u32[]{:S(2)}, u32[]{:S(2)}) collective-permute-start(bf16[4,2,128,128]{3,2,1,0:T(8,128)(2,1)S(1)} %add_convert_fusion.1), channel_id=1, source_target_pairs={{0,12},{2,14},{4,0},{6,2},{8,4},{10,6},{12,8},{14,10},{16,112},{18... | collective-permute-start | bytes 786440 | tf_op jit(solution)/shard_map/ppermute | solution.py:308
  66.7 8.0 %collective-permute-start.26 = (bf16[64,1024]{1,0:T(8,128)(2,1)S(1)}, bf16[64,1024]{1,0:T(8,128)(2,1)S(1)}, u32[]{:S(2)}, u32[]{:S(2)}) collective-permute-start(bf16[64,1024]{1,0:T(8,128)(2,1)S(1)} %get-tuple-element.80), channel_id=1, source_target_pairs={{0,64},{2,66},{4,68},{6,70},{8,72},{10,74},{12,76},{14,78},{16,80}... | collective-permute-start | bytes 393224 | tf_op jit(solution)/shard_map/ppermute | solution.py:308
  72.5 3.5 %collective-permute-start.25 = (bf16[2,128,128]{2,1,0:T(8,128)(2,1)S(1)}, bf16[2,128,128]{2,1,0:T(8,128)(2,1)S(1)}, u32[]{:S(2)}, u32[]{:S(2)}) collective-permute-start(bf16[2,128,128]{2,1,0:T(8,128)(2,1)S(1)} %get-tuple-element.81), channel_id=1, source_target_pairs={{0,96},{2,98},{4,100},{6,102},{8,104},{10,106},{12,108},{14,110},{... | collective-permute-start | bytes 196616 | tf_op jit(solution)/shard_map/ppermute | solution.py:308
  72.6 4.7 %collective-permute-start.24 = (bf16[2,128,128]{2,1,0:T(8,128)(2,1)S(1)}, bf16[2,128,128]{2,1,0:T(8,128)(2,1)S(1)}, u32[]{:S(2)}, u32[]{:S(2)}) collective-permute-start(bf16[2,128,128]{2,1,0:T(8,128)(2,1)S(1)} %get-tuple-element.82), channel_id=1, source_target_pairs={{0,32},{2,34},{4,36},{6,38},{8,40},{10,42},{12,44},{14,46},{16,20}... | collective-permute-start | bytes 196616 | tf_op jit(solution)/shard_map/ppermute | solution.py:308
  74.1 4.6 %collective-permute-start.23 = (bf16[2,128,128]{2,1,0:T(8,128)(2,1)S(1)}, bf16[2,128,128]{2,1,0:T(8,128)(2,1)S(1)}, u32[]{:S(2)}, u32[]{:S(2)}) collective-permute-start(bf16[2,128,128]{2,1,0:T(8,128)(2,1)S(1)} %get-tuple-element.83), channel_id=1, source_target_pairs={{0,64},{2,66},{4,68},{6,70},{8,72},{10,74},{12,76},{14,78},{16,24}... | collective-permute-start | bytes 196616 | tf_op jit(solution)/shard_map/ppermute | solution.py:308
  78.8 2.5 %collective-permute-start.27 = (bf16[128,128]{1,0:T(8,128)(2,1)S(1)}, bf16[128,128]{1,0:T(8,128)(2,1)S(1)}, u32[]{:S(2)}, u32[]{:S(2)}) collective-permute-start(bf16[128,128]{1,0:T(8,128)(2,1)S(1)} %select_bitcast_fusion), channel_id=1, source_target_pairs={{0,16},{2,18},{4,20},{6,22},{8,24},{10,26},{12,28},{14,30},{16,0},... | collective-permute-start | bytes 98312 | tf_op jit(solution)/shard_map/ppermute | solution.py:308
